TPU v7x, 512 devices: a whole 4x8x8 slice. The times are simulated.
512 devices in a mesh: outer: 16 (over z, y_hi), inner: 32 (over y_lo, x, core).
Axes of the slice: x: 4, y: 8 (y_hi: 2, y_lo: 4; y = y_hi * 4 + y_lo), z: 8, core: 2. Of those that a mesh axis runs over, the one named last changes fastest.
Arguments:
- image_embed: bfloat16 [65536, 768], P(('outer', 'inner')), may hold values from -0.21582031 to 0.21582031
- text_embed: bfloat16 [8192, 768], P(('outer', 'inner')), may hold values from -0.21582031 to 0.21582031
- log_scale: float32 [1], replicated, may hold values from 0.7 to 2.3
- logit_bias: float32 [1], replicated, may hold values from -4 to -1
- pair_index: int32 [8192], P(('outer', 'inner')), may hold values from 0 to 65535, as said below
Outputs:
- image_grad: bfloat16 [65536, 768], P(('outer', 'inner'))
- text_grad: bfloat16 [8192, 768], P(('outer', 'inner'))
Inputs may be any that keep to these rules, and one draw needn't show every extreme that they name: `pair_index`: no two text rows are paired with the same image row; images 0 and 65535 are always paired.
All inputs are finite; a program needn't handle non-finite values.
Results may differ from a plain program's by a relative error of at most 0.009.
Values may be sent and summed in bfloat16 or wider, within the bound.
No kernel may reach another device: no remote copies, remote signals or barrier semaphores. Data moves between devices by JAX's collectives and lax.ppermute only.
A program may use at most 64 MiB of HBM per device.

v0:
```python
import jax
import jax.numpy as jnp
from jax import lax
from jax.sharding import PartitionSpec as P


def shifted(array, axis, by):
    devices = lax.axis_size(axis)
    return lax.ppermute(array, axis, [(i, (i + by) % devices) for i in range(devices)])


def normalize(values):
    floats = values.astype(jnp.float32)
    inverse = lax.rsqrt(jnp.sum(floats * floats, axis=-1, keepdims=True) + 1e-06)
    return (floats * inverse, inverse)


def unit_backward(floats, inverse, grad):
    along = jnp.sum(floats * grad, axis=-1, keepdims=True)
    return ((grad - floats * along) * inverse).astype(jnp.bfloat16)


def on_device(image_embed, text_embed, log_scale, logit_bias, pair_index):
    rows = image_embed.shape[0]
    width = image_embed.shape[1]
    groups = lax.axis_size("outer")
    members = lax.axis_size("inner")
    image_float, image_inverse = normalize(image_embed)
    text_float, text_inverse = normalize(text_embed)
    image_unit = image_float.astype(jnp.bfloat16)
    text_unit = text_float.astype(jnp.bfloat16)
    scale = jnp.exp(log_scale[0])
    offset = logit_bias[0]
    group_id = lax.axis_index("outer")
    member_id = lax.axis_index("inner")
    pair_group = lax.all_gather(pair_index, "inner", axis=0, tiled=True)
    text_block = lax.all_gather(text_unit, "inner", axis=0, tiled=True)
    one = jnp.float32(1.0)

    def tile_terms(images, image_first):
        image_index = image_first + jnp.arange(images.shape[0], dtype=jnp.int32)
        label = jnp.where(pair_group[None, :] == image_index[:, None], one, -one)
        logits = scale * jnp.dot(images, text_block.T, preferred_element_type=jnp.float32) + offset
        weight = (-label * jax.nn.sigmoid(-label * logits) * scale).astype(jnp.bfloat16)
        image_term = jnp.dot(weight, text_block, preferred_element_type=jnp.float32)
        text_term = lax.dot_general(
            weight, images, (((0,), (0,)), ((), ())), preferred_element_type=jnp.float32
        )
        return (image_term, text_term)

    text_zero = jnp.zeros(text_block.shape, jnp.float32)
    partial_zero = jnp.zeros((rows, width), jnp.float32)

    def turn_step(turn, carry):
        block, partial_value, text_total = carry
        source = (group_id - turn + groups) % groups
        image_term, text_term = tile_terms(block, (source * members + member_id) * rows)
        partial_value = partial_value + image_term
        text_total = text_total + text_term
        block = shifted(block, "outer", 1)
        partial_value = shifted(partial_value, "outer", 1)
        return (block, partial_value, text_total)

    block, image_total, text_total = lax.fori_loop(
        0, groups, turn_step, (image_unit, partial_zero, text_zero)
    )
    text_own = lax.psum_scatter(text_total, "inner", scatter_dimension=0, tiled=True)
    return (
        unit_backward(image_float, image_inverse, image_total),
        unit_backward(text_float, text_inverse, text_own),
    )


def solution(mesh):
    in_specs = (
        P(("outer", "inner"), None),
        P(("outer", "inner"), None),
        P(),
        P(),
        P(("outer", "inner")),
    )
    out_specs = (P(("outer", "inner"), None), P(("outer", "inner"), None))
    return jax.shard_map(
        on_device, mesh=mesh, in_specs=in_specs, out_specs=out_specs, check_vma=False
    )
```

profile of v0, /device:TPU:64, one launch (start us, length us, event | category | flops | bytes accessed | tf_op | source)
XLA Modules:
  0.0 756.7 jit_solution(16483064161255738862)
XLA Ops:
  9.8 1.3 dynamic-slice
  12.6 16.6 %all-reduce = s32[512]{0:T(512)S(1)} all-reduce(s32[512]{0:T(512)S(1)} %dynamic-update-slice), channel_id=1, replica_groups=mesh['outer'=16,'inner'=32] {'inner'}, use_global_device_ids=true, to_apply=%add | all-reduce | flops 512 | bytes 4096
  30.0 1.7 fusion.11
  31.7 40.1 %all_gather.7 = bf16[512,768]{1,0:T(8,128)(2,1)S(1)} all-gather(bf16[16,768]{1,0:T(8,128)(2,1)S(1)} %fusion.19), channel_id=1, replica_groups=mesh['outer'=16,'inner'=32] {'inner'}, dimensions={0}, use_global_device_ids=true | all-gather | bytes 811008 | tf_op jit(solution)/shard_map/all_gather | solution.py:37
  71.9 495.7 %while.20 = (s32[]{:T(128)}, bf16[128,768]{1,0:T(8,128)(2,1)}, f32[128,768]{1,0:T(8,128)S(1)}, f32[512,768]{1,0:T(8,128)S(1)}, s32[512]{0:T(512)S(1)}, /*index=5...) while((s32[]{:T(128)}, bf16[128,768]{1,0:T(8,128)(2,1)}, ...), condition=%wide.region_3.4_spmd.clone, body=%wide.region_2.3_spmd.clone.sunk | while | flops 303661184 | bytes 9047460 | solution.py:64
  72.8 1.1 fusion.44
  74.3 7.7 %collective-permute-start.1 = (f32[128,768]{1,0:T(8,128)S(1)}, f32[128,768]{1,0:T(8,128)S(1)}, u32[]{:S(2)}, u32[]{:S(2)}) collective-permute-start(f32[128,768]{1,0:T(8,128)S(1)} %convolution_add_fusion.2), channel_id=1, source_target_pairs={{0,32},{32,64},{64,96},{96,128},{128,160},{160,192},{192,224},{224... | collective-permute-start | bytes 1179656 | tf_op jit(solution)/shard_map/while/body/eval_jaxpr/ppermute | solution.py:9
  82.0 3.8 collective-permute-start
  86.5 16.7 %collective-permute-done = bf16[128,768]{1,0:T(8,128)(2,1)} collective-permute-done((bf16[128,768]{1,0:T(8,128)(2,1)S(1)}, bf16[128,768]{1,0:T(8,128)(2,1)}, u32[]{:S(2)}, u32[]{:S(2)}) %collective-permute-start) | collective-permute-done | bytes 196640 | tf_op jit(solution)/shard_map/while/body/eval_jaxpr/ppermute | solution.py:9
  105.5 6.6 collective-permute-start.1
  112.1 5.0 collective-permute-start
  117.7 13.9 %collective-permute-done = bf16[128,768]{1,0:T(8,128)(2,1)} collective-permute-done((bf16[128,768]{1,0:T(8,128)(2,1)S(1)}, bf16[128,768]{1,0:T(8,128)(2,1)}, u32[]{:S(2)}, u32[]{:S(2)}) %collective-permute-start) | collective-permute-done | bytes 196640 | tf_op jit(solution)/shard_map/while/body/eval_jaxpr/ppermute | solution.py:9
  132.6 1.1 fusion.44
  134.0 5.0 collective-permute-start.1
  139.0 6.5 collective-permute-start
  146.2 14.9 %collective-permute-done = bf16[128,768]{1,0:T(8,128)(2,1)} collective-permute-done((bf16[128,768]{1,0:T(8,128)(2,1)S(1)}, bf16[128,768]{1,0:T(8,128)(2,1)}, u32[]{:S(2)}, u32[]{:S(2)}) %collective-permute-start) | collective-permute-done | bytes 196640 | tf_op jit(solution)/shard_map/while/body/eval_jaxpr/ppermute | solution.py:9
  163.4 4.1 collective-permute-start.1
  167.4 5.0 collective-permute-start
  173.1 35.9 %collective-permute-done = bf16[128,768]{1,0:T(8,128)(2,1)} collective-permute-done((bf16[128,768]{1,0:T(8,128)(2,1)S(1)}, bf16[128,768]{1,0:T(8,128)(2,1)}, u32[]{:S(2)}, u32[]{:S(2)}) %collective-permute-start) | collective-permute-done | bytes 196640 | tf_op jit(solution)/shard_map/while/body/eval_jaxpr/ppermute | solution.py:9
  211.3 1.9 collective-permute-start.1
  213.2 1.9 collective-permute-start
  215.8 27.1 %collective-permute-done = bf16[128,768]{1,0:T(8,128)(2,1)} collective-permute-done((bf16[128,768]{1,0:T(8,128)(2,1)S(1)}, bf16[128,768]{1,0:T(8,128)(2,1)}, u32[]{:S(2)}, u32[]{:S(2)}) %collective-permute-start) | collective-permute-done | bytes 196640 | tf_op jit(solution)/shard_map/while/body/eval_jaxpr/ppermute | solution.py:9
  245.2 8.5 %collective-permute-start.1 = (f32[128,768]{1,0:T(8,128)S(1)}, f32[128,768]{1,0:T(8,128)S(1)}, u32[]{:S(2)}, u32[]{:S(2)}) collective-permute-start(f32[128,768]{1,0:T(8,128)S(1)} %convolution_add_fusion.2), channel_id=1, source_target_pairs={{0,32},{32,64},{64,96},{96,128},{128,160},{160,192},{192,224},{224... | collective-permute-start | bytes 1179656 | tf_op jit(solution)/shard_map/while/body/eval_jaxpr/ppermute | solution.py:9
  253.7 1.9 collective-permute-start
  256.3 11.7 %collective-permute-done = bf16[128,768]{1,0:T(8,128)(2,1)} collective-permute-done((bf16[128,768]{1,0:T(8,128)(2,1)S(1)}, bf16[128,768]{1,0:T(8,128)(2,1)}, u32[]{:S(2)}, u32[]{:S(2)}) %collective-permute-start) | collective-permute-done | bytes 196640 | tf_op jit(solution)/shard_map/while/body/eval_jaxpr/ppermute | solution.py:9
  269.0 1.1 fusion.44
  270.4 11.5 %collective-permute-start.1 = (f32[128,768]{1,0:T(8,128)S(1)}, f32[128,768]{1,0:T(8,128)S(1)}, u32[]{:S(2)}, u32[]{:S(2)}) collective-permute-start(f32[128,768]{1,0:T(8,128)S(1)} %convolution_add_fusion.2), channel_id=1, source_target_pairs={{0,32},{32,64},{64,96},{96,128},{128,160},{160,192},{192,224},{224... | collective-permute-start | bytes 1179656 | tf_op jit(solution)/shard_map/while/body/eval_jaxpr/ppermute | solution.py:9
  281.9 1.9 collective-permute-start
  284.4 16.3 %collective-permute-done = bf16[128,768]{1,0:T(8,128)(2,1)} collective-permute-done((bf16[128,768]{1,0:T(8,128)(2,1)S(1)}, bf16[128,768]{1,0:T(8,128)(2,1)}, u32[]{:S(2)}, u32[]{:S(2)}) %collective-permute-start) | collective-permute-done | bytes 196640 | tf_op jit(solution)/shard_map/while/body/eval_jaxpr/ppermute | solution.py:9
  301.7 1.1 fusion.44
  303.1 1.9 collective-permute-start.1
  305.0 1.9 collective-permute-start
  307.6 13.3 %collective-permute-done = bf16[128,768]{1,0:T(8,128)(2,1)} collective-permute-done((bf16[128,768]{1,0:T(8,128)(2,1)S(1)}, bf16[128,768]{1,0:T(8,128)(2,1)}, u32[]{:S(2)}, u32[]{:S(2)}) %collective-permute-start) | collective-permute-done | bytes 196640 | tf_op jit(solution)/shard_map/while/body/eval_jaxpr/ppermute | solution.py:9
  321.8 1.1 fusion.44
  323.2 3.4 collective-permute-start.1
  326.7 5.6 collective-permute-start
  332.9 11.4 %collective-permute-done = bf16[128,768]{1,0:T(8,128)(2,1)} collective-permute-done((bf16[128,768]{1,0:T(8,128)(2,1)S(1)}, bf16[128,768]{1,0:T(8,128)(2,1)}, u32[]{:S(2)}, u32[]{:S(2)}) %collective-permute-start) | collective-permute-done | bytes 196640 | tf_op jit(solution)/shard_map/while/body/eval_jaxpr/ppermute | solution.py:9
  345.2 1.1 fusion.44
  346.6 7.5 collective-permute-start.1
  354.1 6.1 collective-permute-start
  360.9 13.1 %collective-permute-done = bf16[128,768]{1,0:T(8,128)(2,1)} collective-permute-done((bf16[128,768]{1,0:T(8,128)(2,1)S(1)}, bf16[128,768]{1,0:T(8,128)(2,1)}, u32[]{:S(2)}, u32[]{:S(2)}) %collective-permute-start) | collective-permute-done | bytes 196640 | tf_op jit(solution)/shard_map/while/body/eval_jaxpr/ppermute | solution.py:9
  375.0 1.1 fusion.44
  376.4 2.6 collective-permute-start.1
  378.9 6.6 collective-permute-start
  386.2 21.9 %collective-permute-done = bf16[128,768]{1,0:T(8,128)(2,1)} collective-permute-done((bf16[128,768]{1,0:T(8,128)(2,1)S(1)}, bf16[128,768]{1,0:T(8,128)(2,1)}, u32[]{:S(2)}, u32[]{:S(2)}) %collective-permute-start) | collective-permute-done | bytes 196640 | tf_op jit(solution)/shard_map/while/body/eval_jaxpr/ppermute | solution.py:9
  410.4 8.4 %collective-permute-start.1 = (f32[128,768]{1,0:T(8,128)S(1)}, f32[128,768]{1,0:T(8,128)S(1)}, u32[]{:S(2)}, u32[]{:S(2)}) collective-permute-start(f32[128,768]{1,0:T(8,128)S(1)} %convolution_add_fusion.2), channel_id=1, source_target_pairs={{0,32},{32,64},{64,96},{96,128},{128,160},{160,192},{192,224},{224... | collective-permute-start | bytes 1179656 | tf_op jit(solution)/shard_map/while/body/eval_jaxpr/ppermute | solution.py:9
  418.9 9.2 %collective-permute-start = (bf16[128,768]{1,0:T(8,128)(2,1)S(1)}, bf16[128,768]{1,0:T(8,128)(2,1)}, u32[]{:S(2)}, u32[]{:S(2)}) collective-permute-start(bf16[128,768]{1,0:T(8,128)(2,1)S(1)} %copy.13), channel_id=1, source_target_pairs={{0,32},{32,64},{64,96},{96,128},{128,160},{160,192},{192,224},{224... | collective-permute-start | bytes 589832 | tf_op jit(solution)/shard_map/while/body/eval_jaxpr/ppermute | solution.py:9
  428.7 15.9 %collective-permute-done = bf16[128,768]{1,0:T(8,128)(2,1)} collective-permute-done((bf16[128,768]{1,0:T(8,128)(2,1)S(1)}, bf16[128,768]{1,0:T(8,128)(2,1)}, u32[]{:S(2)}, u32[]{:S(2)}) %collective-permute-start) | collective-permute-done | bytes 196640 | tf_op jit(solution)/shard_map/while/body/eval_jaxpr/ppermute | solution.py:9
  447.0 8.2 %collective-permute-start.1 = (f32[128,768]{1,0:T(8,128)S(1)}, f32[128,768]{1,0:T(8,128)S(1)}, u32[]{:S(2)}, u32[]{:S(2)}) collective-permute-start(f32[128,768]{1,0:T(8,128)S(1)} %convolution_add_fusion.2), channel_id=1, source_target_pairs={{0,32},{32,64},{64,96},{96,128},{128,160},{160,192},{192,224},{224... | collective-permute-start | bytes 1179656 | tf_op jit(solution)/shard_map/while/body/eval_jaxpr/ppermute | solution.py:9
  455.2 1.9 collective-permute-start
  457.7 24.7 %collective-permute-done = bf16[128,768]{1,0:T(8,128)(2,1)} collective-permute-done((bf16[128,768]{1,0:T(8,128)(2,1)S(1)}, bf16[128,768]{1,0:T(8,128)(2,1)}, u32[]{:S(2)}, u32[]{:S(2)}) %collective-permute-start) | collective-permute-done | bytes 196640 | tf_op jit(solution)/shard_map/while/body/eval_jaxpr/ppermute | solution.py:9
  484.8 1.9 collective-permute-start.1
  486.7 1.9 collective-permute-start
  489.3 27.4 %collective-permute-done = bf16[128,768]{1,0:T(8,128)(2,1)} collective-permute-done((bf16[128,768]{1,0:T(8,128)(2,1)S(1)}, bf16[128,768]{1,0:T(8,128)(2,1)}, u32[]{:S(2)}, u32[]{:S(2)}) %collective-permute-start) | collective-permute-done | bytes 196640 | tf_op jit(solution)/shard_map/while/body/eval_jaxpr/ppermute | solution.py:9
  517.6 1.1 fusion.44
  519.1 1.9 collective-permute-start.1
  521.0 1.9 collective-permute-start
  523.5 17.3 %collective-permute-done = bf16[128,768]{1,0:T(8,128)(2,1)} collective-permute-done((bf16[128,768]{1,0:T(8,128)(2,1)S(1)}, bf16[128,768]{1,0:T(8,128)(2,1)}, u32[]{:S(2)}, u32[]{:S(2)}) %collective-permute-start) | collective-permute-done | bytes 196640 | tf_op jit(solution)/shard_map/while/body/eval_jaxpr/ppermute | solution.py:9
  543.2 4.2 collective-permute-start.1
  547.3 9.5 %collective-permute-start = (bf16[128,768]{1,0:T(8,128)(2,1)S(1)}, bf16[128,768]{1,0:T(8,128)(2,1)}, u32[]{:S(2)}, u32[]{:S(2)}) collective-permute-start(bf16[128,768]{1,0:T(8,128)(2,1)S(1)} %copy.13), channel_id=1, source_target_pairs={{0,32},{32,64},{64,96},{96,128},{128,160},{160,192},{192,224},{224... | collective-permute-start | bytes 589832 | tf_op jit(solution)/shard_map/while/body/eval_jaxpr/ppermute | solution.py:9
  557.5 10.0 %collective-permute-done = bf16[128,768]{1,0:T(8,128)(2,1)} collective-permute-done((bf16[128,768]{1,0:T(8,128)(2,1)S(1)}, bf16[128,768]{1,0:T(8,128)(2,1)}, u32[]{:S(2)}, u32[]{:S(2)}) %collective-permute-start) | collective-permute-done | bytes 196640 | tf_op jit(solution)/shard_map/while/body/eval_jaxpr/ppermute | solution.py:9
  567.6 1.1 copy-done
  569.8 177.6 %reduce-scatter.2.cloned.1.call-done = f32[16,768]{1,0:T(8,128)} async-done(((f32[512,768]{1,0:T(8,128)}), f32[16,768]{1,0:T(8,128)}) %reduce-scatter.2.cloned.1.call-update) | async-done | bytes 49168 | tf_op jit(solution)/shard_map/reduce_scatter | solution.py:67
  748.3 1.5 fusion.23
  (107 shorter events, 43.8 us)
Async XLA Ops:
  7.2 740.2 %reduce-scatter.2.cloned.1.call-start = ((), (), s32[]{:S(2)}) async-start(), calls=%async_computation.1 | async-start | bytes 1622016 | tf_op jit(solution)/shard_map/reduce_scatter | solution.py:67
  74.3 28.9 %collective-permute-start.1 = (f32[128,768]{1,0:T(8,128)S(1)}, f32[128,768]{1,0:T(8,128)S(1)}, u32[]{:S(2)}, u32[]{:S(2)}) collective-permute-start(f32[128,768]{1,0:T(8,128)S(1)} %convolution_add_fusion.2), channel_id=1, source_target_pairs={{0,32},{32,64},{64,96},{96,128},{128,160},{160,192},{192,224},{224... | collective-permute-start | bytes 1179656 | tf_op jit(solution)/shard_map/while/body/eval_jaxpr/ppermute | solution.py:9
  82.0 21.2 %collective-permute-start = (bf16[128,768]{1,0:T(8,128)(2,1)S(1)}, bf16[128,768]{1,0:T(8,128)(2,1)}, u32[]{:S(2)}, u32[]{:S(2)}) collective-permute-start(bf16[128,768]{1,0:T(8,128)(2,1)S(1)} %copy.13), channel_id=1, source_target_pairs={{0,32},{32,64},{64,96},{96,128},{128,160},{160,192},{192,224},{224... | collective-permute-start | bytes 589832 | tf_op jit(solution)/shard_map/while/body/eval_jaxpr/ppermute | solution.py:9
  105.5 26.1 %collective-permute-start.1 = (f32[128,768]{1,0:T(8,128)S(1)}, f32[128,768]{1,0:T(8,128)S(1)}, u32[]{:S(2)}, u32[]{:S(2)}) collective-permute-start(f32[128,768]{1,0:T(8,128)S(1)} %convolution_add_fusion.2), channel_id=1, source_target_pairs={{0,32},{32,64},{64,96},{96,128},{128,160},{160,192},{192,224},{224... | collective-permute-start | bytes 1179656 | tf_op jit(solution)/shard_map/while/body/eval_jaxpr/ppermute | solution.py:9
  112.1 19.6 %collective-permute-start = (bf16[128,768]{1,0:T(8,128)(2,1)S(1)}, bf16[128,768]{1,0:T(8,128)(2,1)}, u32[]{:S(2)}, u32[]{:S(2)}) collective-permute-start(bf16[128,768]{1,0:T(8,128)(2,1)S(1)} %copy.13), channel_id=1, source_target_pairs={{0,32},{32,64},{64,96},{96,128},{128,160},{160,192},{192,224},{224... | collective-permute-start | bytes 589832 | tf_op jit(solution)/shard_map/while/body/eval_jaxpr/ppermute | solution.py:9
  134.0 27.1 %collective-permute-start.1 = (f32[128,768]{1,0:T(8,128)S(1)}, f32[128,768]{1,0:T(8,128)S(1)}, u32[]{:S(2)}, u32[]{:S(2)}) collective-permute-start(f32[128,768]{1,0:T(8,128)S(1)} %convolution_add_fusion.2), channel_id=1, source_target_pairs={{0,32},{32,64},{64,96},{96,128},{128,160},{160,192},{192,224},{224... | collective-permute-start | bytes 1179656 | tf_op jit(solution)/shard_map/while/body/eval_jaxpr/ppermute | solution.py:9
  139.0 22.0 %collective-permute-start = (bf16[128,768]{1,0:T(8,128)(2,1)S(1)}, bf16[128,768]{1,0:T(8,128)(2,1)}, u32[]{:S(2)}, u32[]{:S(2)}) collective-permute-start(bf16[128,768]{1,0:T(8,128)(2,1)S(1)} %copy.13), channel_id=1, source_target_pairs={{0,32},{32,64},{64,96},{96,128},{128,160},{160,192},{192,224},{224... | collective-permute-start | bytes 589832 | tf_op jit(solution)/shard_map/while/body/eval_jaxpr/ppermute | solution.py:9
  163.4 45.6 %collective-permute-start.1 = (f32[128,768]{1,0:T(8,128)S(1)}, f32[128,768]{1,0:T(8,128)S(1)}, u32[]{:S(2)}, u32[]{:S(2)}) collective-permute-start(f32[128,768]{1,0:T(8,128)S(1)} %convolution_add_fusion.2), channel_id=1, source_target_pairs={{0,32},{32,64},{64,96},{96,128},{128,160},{160,192},{192,224},{224... | collective-permute-start | bytes 1179656 | tf_op jit(solution)/shard_map/while/body/eval_jaxpr/ppermute | solution.py:9
  167.4 41.5 %collective-permute-start = (bf16[128,768]{1,0:T(8,128)(2,1)S(1)}, bf16[128,768]{1,0:T(8,128)(2,1)}, u32[]{:S(2)}, u32[]{:S(2)}) collective-permute-start(bf16[128,768]{1,0:T(8,128)(2,1)S(1)} %copy.13), channel_id=1, source_target_pairs={{0,32},{32,64},{64,96},{96,128},{128,160},{160,192},{192,224},{224... | collective-permute-start | bytes 589832 | tf_op jit(solution)/shard_map/while/body/eval_jaxpr/ppermute | solution.py:9
  211.3 31.6 %collective-permute-start.1 = (f32[128,768]{1,0:T(8,128)S(1)}, f32[128,768]{1,0:T(8,128)S(1)}, u32[]{:S(2)}, u32[]{:S(2)}) collective-permute-start(f32[128,768]{1,0:T(8,128)S(1)} %convolution_add_fusion.2), channel_id=1, source_target_pairs={{0,32},{32,64},{64,96},{96,128},{128,160},{160,192},{192,224},{224... | collective-permute-start | bytes 1179656 | tf_op jit(solution)/shard_map/while/body/eval_jaxpr/ppermute | solution.py:9
  213.2 29.7 %collective-permute-start = (bf16[128,768]{1,0:T(8,128)(2,1)S(1)}, bf16[128,768]{1,0:T(8,128)(2,1)}, u32[]{:S(2)}, u32[]{:S(2)}) collective-permute-start(bf16[128,768]{1,0:T(8,128)(2,1)S(1)} %copy.13), channel_id=1, source_target_pairs={{0,32},{32,64},{64,96},{96,128},{128,160},{160,192},{192,224},{224... | collective-permute-start | bytes 589832 | tf_op jit(solution)/shard_map/while/body/eval_jaxpr/ppermute | solution.py:9
  245.2 22.8 %collective-permute-start.1 = (f32[128,768]{1,0:T(8,128)S(1)}, f32[128,768]{1,0:T(8,128)S(1)}, u32[]{:S(2)}, u32[]{:S(2)}) collective-permute-start(f32[128,768]{1,0:T(8,128)S(1)} %convolution_add_fusion.2), channel_id=1, source_target_pairs={{0,32},{32,64},{64,96},{96,128},{128,160},{160,192},{192,224},{224... | collective-permute-start | bytes 1179656 | tf_op jit(solution)/shard_map/while/body/eval_jaxpr/ppermute | solution.py:9
  253.7 14.3 %collective-permute-start = (bf16[128,768]{1,0:T(8,128)(2,1)S(1)}, bf16[128,768]{1,0:T(8,128)(2,1)}, u32[]{:S(2)}, u32[]{:S(2)}) collective-permute-start(bf16[128,768]{1,0:T(8,128)(2,1)S(1)} %copy.13), channel_id=1, source_target_pairs={{0,32},{32,64},{64,96},{96,128},{128,160},{160,192},{192,224},{224... | collective-permute-start | bytes 589832 | tf_op jit(solution)/shard_map/while/body/eval_jaxpr/ppermute | solution.py:9
  270.4 30.4 %collective-permute-start.1 = (f32[128,768]{1,0:T(8,128)S(1)}, f32[128,768]{1,0:T(8,128)S(1)}, u32[]{:S(2)}, u32[]{:S(2)}) collective-permute-start(f32[128,768]{1,0:T(8,128)S(1)} %convolution_add_fusion.2), channel_id=1, source_target_pairs={{0,32},{32,64},{64,96},{96,128},{128,160},{160,192},{192,224},{224... | collective-permute-start | bytes 1179656 | tf_op jit(solution)/shard_map/while/body/eval_jaxpr/ppermute | solution.py:9
  281.9 18.9 %collective-permute-start = (bf16[128,768]{1,0:T(8,128)(2,1)S(1)}, bf16[128,768]{1,0:T(8,128)(2,1)}, u32[]{:S(2)}, u32[]{:S(2)}) collective-permute-start(bf16[128,768]{1,0:T(8,128)(2,1)S(1)} %copy.13), channel_id=1, source_target_pairs={{0,32},{32,64},{64,96},{96,128},{128,160},{160,192},{192,224},{224... | collective-permute-start | bytes 589832 | tf_op jit(solution)/shard_map/while/body/eval_jaxpr/ppermute | solution.py:9
  303.1 17.8 %collective-permute-start.1 = (f32[128,768]{1,0:T(8,128)S(1)}, f32[128,768]{1,0:T(8,128)S(1)}, u32[]{:S(2)}, u32[]{:S(2)}) collective-permute-start(f32[128,768]{1,0:T(8,128)S(1)} %convolution_add_fusion.2), channel_id=1, source_target_pairs={{0,32},{32,64},{64,96},{96,128},{128,160},{160,192},{192,224},{224... | collective-permute-start | bytes 1179656 | tf_op jit(solution)/shard_map/while/body/eval_jaxpr/ppermute | solution.py:9
  305.0 15.9 %collective-permute-start = (bf16[128,768]{1,0:T(8,128)(2,1)S(1)}, bf16[128,768]{1,0:T(8,128)(2,1)}, u32[]{:S(2)}, u32[]{:S(2)}) collective-permute-start(bf16[128,768]{1,0:T(8,128)(2,1)S(1)} %copy.13), channel_id=1, source_target_pairs={{0,32},{32,64},{64,96},{96,128},{128,160},{160,192},{192,224},{224... | collective-permute-start | bytes 589832 | tf_op jit(solution)/shard_map/while/body/eval_jaxpr/ppermute | solution.py:9
  323.2 21.0 %collective-permute-start.1 = (f32[128,768]{1,0:T(8,128)S(1)}, f32[128,768]{1,0:T(8,128)S(1)}, u32[]{:S(2)}, u32[]{:S(2)}) collective-permute-start(f32[128,768]{1,0:T(8,128)S(1)} %convolution_add_fusion.2), channel_id=1, source_target_pairs={{0,32},{32,64},{64,96},{96,128},{128,160},{160,192},{192,224},{224... | collective-permute-start | bytes 1179656 | tf_op jit(solution)/shard_map/while/body/eval_jaxpr/ppermute | solution.py:9
  326.7 17.6 %collective-permute-start = (bf16[128,768]{1,0:T(8,128)(2,1)S(1)}, bf16[128,768]{1,0:T(8,128)(2,1)}, u32[]{:S(2)}, u32[]{:S(2)}) collective-permute-start(bf16[128,768]{1,0:T(8,128)(2,1)S(1)} %copy.13), channel_id=1, source_target_pairs={{0,32},{32,64},{64,96},{96,128},{128,160},{160,192},{192,224},{224... | collective-permute-start | bytes 589832 | tf_op jit(solution)/shard_map/while/body/eval_jaxpr/ppermute | solution.py:9
  346.6 27.4 %collective-permute-start.1 = (f32[128,768]{1,0:T(8,128)S(1)}, f32[128,768]{1,0:T(8,128)S(1)}, u32[]{:S(2)}, u32[]{:S(2)}) collective-permute-start(f32[128,768]{1,0:T(8,128)S(1)} %convolution_add_fusion.2), channel_id=1, source_target_pairs={{0,32},{32,64},{64,96},{96,128},{128,160},{160,192},{192,224},{224... | collective-permute-start | bytes 1179656 | tf_op jit(solution)/shard_map/while/body/eval_jaxpr/ppermute | solution.py:9
  354.1 19.9 %collective-permute-start = (bf16[128,768]{1,0:T(8,128)(2,1)S(1)}, bf16[128,768]{1,0:T(8,128)(2,1)}, u32[]{:S(2)}, u32[]{:S(2)}) collective-permute-start(bf16[128,768]{1,0:T(8,128)(2,1)S(1)} %copy.13), channel_id=1, source_target_pairs={{0,32},{32,64},{64,96},{96,128},{128,160},{160,192},{192,224},{224... | collective-permute-start | bytes 589832 | tf_op jit(solution)/shard_map/while/body/eval_jaxpr/ppermute | solution.py:9
  376.4 31.7 %collective-permute-start.1 = (f32[128,768]{1,0:T(8,128)S(1)}, f32[128,768]{1,0:T(8,128)S(1)}, u32[]{:S(2)}, u32[]{:S(2)}) collective-permute-start(f32[128,768]{1,0:T(8,128)S(1)} %convolution_add_fusion.2), channel_id=1, source_target_pairs={{0,32},{32,64},{64,96},{96,128},{128,160},{160,192},{192,224},{224... | collective-permute-start | bytes 1179656 | tf_op jit(solution)/shard_map/while/body/eval_jaxpr/ppermute | solution.py:9
  378.9 29.1 %collective-permute-start = (bf16[128,768]{1,0:T(8,128)(2,1)S(1)}, bf16[128,768]{1,0:T(8,128)(2,1)}, u32[]{:S(2)}, u32[]{:S(2)}) collective-permute-start(bf16[128,768]{1,0:T(8,128)(2,1)S(1)} %copy.13), channel_id=1, source_target_pairs={{0,32},{32,64},{64,96},{96,128},{128,160},{160,192},{192,224},{224... | collective-permute-start | bytes 589832 | tf_op jit(solution)/shard_map/while/body/eval_jaxpr/ppermute | solution.py:9
  410.4 34.2 %collective-permute-start.1 = (f32[128,768]{1,0:T(8,128)S(1)}, f32[128,768]{1,0:T(8,128)S(1)}, u32[]{:S(2)}, u32[]{:S(2)}) collective-permute-start(f32[128,768]{1,0:T(8,128)S(1)} %convolution_add_fusion.2), channel_id=1, source_target_pairs={{0,32},{32,64},{64,96},{96,128},{128,160},{160,192},{192,224},{224... | collective-permute-start | bytes 1179656 | tf_op jit(solution)/shard_map/while/body/eval_jaxpr/ppermute | solution.py:9
  418.9 25.8 %collective-permute-start = (bf16[128,768]{1,0:T(8,128)(2,1)S(1)}, bf16[128,768]{1,0:T(8,128)(2,1)}, u32[]{:S(2)}, u32[]{:S(2)}) collective-permute-start(bf16[128,768]{1,0:T(8,128)(2,1)S(1)} %copy.13), channel_id=1, source_target_pairs={{0,32},{32,64},{64,96},{96,128},{128,160},{160,192},{192,224},{224... | collective-permute-start | bytes 589832 | tf_op jit(solution)/shard_map/while/body/eval_jaxpr/ppermute | solution.py:9
  447.0 35.5 %collective-permute-start.1 = (f32[128,768]{1,0:T(8,128)S(1)}, f32[128,768]{1,0:T(8,128)S(1)}, u32[]{:S(2)}, u32[]{:S(2)}) collective-permute-start(f32[128,768]{1,0:T(8,128)S(1)} %convolution_add_fusion.2), channel_id=1, source_target_pairs={{0,32},{32,64},{64,96},{96,128},{128,160},{160,192},{192,224},{224... | collective-permute-start | bytes 1179656 | tf_op jit(solution)/shard_map/while/body/eval_jaxpr/ppermute | solution.py:9
  455.2 27.3 %collective-permute-start = (bf16[128,768]{1,0:T(8,128)(2,1)S(1)}, bf16[128,768]{1,0:T(8,128)(2,1)}, u32[]{:S(2)}, u32[]{:S(2)}) collective-permute-start(bf16[128,768]{1,0:T(8,128)(2,1)S(1)} %copy.13), channel_id=1, source_target_pairs={{0,32},{32,64},{64,96},{96,128},{128,160},{160,192},{192,224},{224... | collective-permute-start | bytes 589832 | tf_op jit(solution)/shard_map/while/body/eval_jaxpr/ppermute | solution.py:9
  484.8 31.9 %collective-permute-start.1 = (f32[128,768]{1,0:T(8,128)S(1)}, f32[128,768]{1,0:T(8,128)S(1)}, u32[]{:S(2)}, u32[]{:S(2)}) collective-permute-start(f32[128,768]{1,0:T(8,128)S(1)} %convolution_add_fusion.2), channel_id=1, source_target_pairs={{0,32},{32,64},{64,96},{96,128},{128,160},{160,192},{192,224},{224... | collective-permute-start | bytes 1179656 | tf_op jit(solution)/shard_map/while/body/eval_jaxpr/ppermute | solution.py:9
  486.7 30.0 %collective-permute-start = (bf16[128,768]{1,0:T(8,128)(2,1)S(1)}, bf16[128,768]{1,0:T(8,128)(2,1)}, u32[]{:S(2)}, u32[]{:S(2)}) collective-permute-start(bf16[128,768]{1,0:T(8,128)(2,1)S(1)} %copy.13), channel_id=1, source_target_pairs={{0,32},{32,64},{64,96},{96,128},{128,160},{160,192},{192,224},{224... | collective-permute-start | bytes 589832 | tf_op jit(solution)/shard_map/while/body/eval_jaxpr/ppermute | solution.py:9
  519.1 21.8 %collective-permute-start.1 = (f32[128,768]{1,0:T(8,128)S(1)}, f32[128,768]{1,0:T(8,128)S(1)}, u32[]{:S(2)}, u32[]{:S(2)}) collective-permute-start(f32[128,768]{1,0:T(8,128)S(1)} %convolution_add_fusion.2), channel_id=1, source_target_pairs={{0,32},{32,64},{64,96},{96,128},{128,160},{160,192},{192,224},{224... | collective-permute-start | bytes 1179656 | tf_op jit(solution)/shard_map/while/body/eval_jaxpr/ppermute | solution.py:9
  521.0 19.8 %collective-permute-start = (bf16[128,768]{1,0:T(8,128)(2,1)S(1)}, bf16[128,768]{1,0:T(8,128)(2,1)}, u32[]{:S(2)}, u32[]{:S(2)}) collective-permute-start(bf16[128,768]{1,0:T(8,128)(2,1)S(1)} %copy.13), channel_id=1, source_target_pairs={{0,32},{32,64},{64,96},{96,128},{128,160},{160,192},{192,224},{224... | collective-permute-start | bytes 589832 | tf_op jit(solution)/shard_map/while/body/eval_jaxpr/ppermute | solution.py:9
  543.2 24.4 %collective-permute-start.1 = (f32[128,768]{1,0:T(8,128)S(1)}, f32[128,768]{1,0:T(8,128)S(1)}, u32[]{:S(2)}, u32[]{:S(2)}) collective-permute-start(f32[128,768]{1,0:T(8,128)S(1)} %convolution_add_fusion.2), channel_id=1, source_target_pairs={{0,32},{32,64},{64,96},{96,128},{128,160},{160,192},{192,224},{224... | collective-permute-start | bytes 1179656 | tf_op jit(solution)/shard_map/while/body/eval_jaxpr/ppermute | solution.py:9
  547.3 20.2 %collective-permute-start = (bf16[128,768]{1,0:T(8,128)(2,1)S(1)}, bf16[128,768]{1,0:T(8,128)(2,1)}, u32[]{:S(2)}, u32[]{:S(2)}) collective-permute-start(bf16[128,768]{1,0:T(8,128)(2,1)S(1)} %copy.13), channel_id=1, source_target_pairs={{0,32},{32,64},{64,96},{96,128},{128,160},{160,192},{192,224},{224... | collective-permute-start | bytes 589832 | tf_op jit(solution)/shard_map/while/body/eval_jaxpr/ppermute | solution.py:9
  567.5 1.2 copy-start
  567.5 1.2 copy-start.1
  567.5 179.8 %copy-start.2 = (bf16[16,768]{1,0:T(8,128)(2,1)S(1)}, bf16[16,768]{1,0:T(8,128)(2,1)}, u32[]{:S(2)}) copy-start(bf16[16,768]{1,0:T(8,128)(2,1)} %param.8) | copy-start | bytes 73732
Sparse Core Ops, SparseCore 0:
  568.8 178.4 reduce-scatter.1
where the time goes:
time: 759 us; the launch traced here: 757 us
  waiting for transfers between devices  469 us (62%)
  starting transfers between devices  156 us (21%)
  blocking collectives  56.7 us (7%)
  matrix products  32.1 us (4%)
  local copies, waits for them, and re-layouts  18.2 us (2%)
  between operations  15.4 us (2%)
  other arithmetic  8.02 us (1%)
    ppermute x32, waiting for transfers between devices, shifted(): lax.ppermute(array, axis, [(i, (i + by) % devices) for i in range(devices)])  292 us
    reduce_scatter x1, waiting for transfers between devices, on_device(): lax.psum_scatter(text_total, 'inner', scatter_dimension=0, tiled=True)  178 us
    ppermute x32, starting transfers between devices, shifted(): lax.ppermute(array, axis, [(i, (i + by) % devices) for i in range(devices)])  156 us
    all_gather x1, blocking collectives, on_device(): text_block = lax.all_gather(text_unit, 'inner', axis=0, tiled=True)  40.1 us
    dot_general x16, matrix products, tile_terms(): jnp.dot(images, text_block.T, preferred_element_type=jnp.float32)  17.7 us
    unnamed x1, blocking collectives  16.6 us
  transfers between devices with their start and end apart: 33, of which 17 were waited for; matrix products, arithmetic and copies ran while one was open for 1% of the time, Pallas kernels for 0%

commit v1 on v0

v1 whole, which is shorter than its diff:
```python
import functools

import jax
import jax.numpy as jnp
from jax import lax
from jax.experimental import pallas as pl
from jax.experimental.pallas import tpu as pltpu
from jax.sharding import Mesh
from jax.sharding import PartitionSpec as P

AXES = ("z", "yh", "yl", "x", "c")
TEXT_AXES = ("z", "yh", "yl")
IMAGE_AXES = ("x", "c")
LANES = 128


def normalize(values):
    floats = values.astype(jnp.float32)
    inverse = lax.rsqrt(jnp.sum(floats * floats, axis=-1, keepdims=True) + 1e-06)
    return (floats * inverse, inverse)


def unit_backward(floats, inverse, grad):
    along = jnp.sum(floats * grad, axis=-1, keepdims=True)
    return ((grad - floats * along) * inverse).astype(jnp.bfloat16)


def pair_kernel(first_ref, scalars_ref, image_ref, text_ref, pair_ref, image_grad_ref, text_grad_ref, text_acc):
    step = pl.program_id(0)
    block = image_ref.shape[0]
    scale = scalars_ref[0]
    offset = scalars_ref[1]
    images = image_ref[...]
    texts = text_ref[...]
    dots = lax.dot_general(images, texts, (((1,), (1,)), ((), ())), preferred_element_type=jnp.float32)
    chance = 1.0 / (1.0 + jnp.exp(-(scale * dots + offset)))
    rows = first_ref[0] + step * block + lax.broadcasted_iota(jnp.int32, chance.shape, 0)
    paired = pair_ref[...] == rows
    weight = (scale * jnp.where(paired, chance - 1.0, chance)).astype(jnp.bfloat16)
    image_grad_ref[...] = jnp.dot(weight, texts, preferred_element_type=jnp.float32).astype(image_grad_ref.dtype)
    term = lax.dot_general(weight, images, (((0,), (0,)), ((), ())), preferred_element_type=jnp.float32)

    @pl.when(step == 0)
    def _():
        text_acc[...] = term

    @pl.when(step > 0)
    def _():
        text_acc[...] += term

    @pl.when(step == pl.num_programs(0) - 1)
    def _():
        text_grad_ref[...] = text_acc[...].astype(text_grad_ref.dtype)


def pair_block(first, scalars, images, texts, pairs, block):
    rows, width = images.shape
    count = texts.shape[0]
    return pl.pallas_call(
        pair_kernel,
        grid=(rows // block,),
        in_specs=[
            pl.BlockSpec(memory_space=pltpu.SMEM),
            pl.BlockSpec(memory_space=pltpu.SMEM),
            pl.BlockSpec((block, width), lambda i: (i, 0)),
            pl.BlockSpec((count, width), lambda i: (0, 0)),
            pl.BlockSpec((1, count), lambda i: (0, 0)),
        ],
        out_specs=[
            pl.BlockSpec((block, width), lambda i: (i, 0)),
            pl.BlockSpec((count, width), lambda i: (0, 0)),
        ],
        out_shape=[
            jax.ShapeDtypeStruct((rows, width), jnp.bfloat16),
            jax.ShapeDtypeStruct((count, width), jnp.bfloat16),
        ],
        scratch_shapes=[pltpu.VMEM((count, width), jnp.float32)],
        compiler_params=pltpu.CompilerParams(vmem_limit_bytes=40 * 1024 * 1024),
        cost_estimate=pl.CostEstimate(
            flops=6 * rows * count * width, bytes_accessed=8 * (rows + count) * width, transcendentals=2 * rows * count
        ),
    )(first, scalars, images, texts, pairs)


def on_device(image_embed, text_embed, log_scale, logit_bias, pair_index):
    own_images, width = image_embed.shape
    own_texts = text_embed.shape[0]
    peers = lax.axis_size(TEXT_AXES)
    members = lax.axis_size(IMAGE_AXES)
    image_float, image_inverse = normalize(image_embed)
    text_float, text_inverse = normalize(text_embed)
    scalars = jnp.concatenate([jnp.exp(log_scale), logit_bias])

    images = lax.all_gather(image_float.astype(jnp.bfloat16), IMAGE_AXES, axis=0, tiled=True)

    lane = lax.broadcasted_iota(jnp.int32, (own_texts, LANES), 1)
    digits = jnp.where(lane == 0, pair_index[:, None] // 256, jnp.where(lane == 1, pair_index[:, None] % 256, 0))
    packet = jnp.concatenate([text_float.astype(jnp.bfloat16), digits.astype(jnp.bfloat16)], axis=1)
    spread = jnp.broadcast_to(packet[None], (peers, own_texts, width + LANES))
    gathered = lax.all_to_all(spread, TEXT_AXES, split_axis=0, concat_axis=0, tiled=True)
    gathered = gathered.reshape(peers * own_texts, width + LANES)
    texts = gathered[:, :width]
    pairs = gathered[:, width].astype(jnp.int32) * 256 + gathered[:, width + 1].astype(jnp.int32)

    first = lax.axis_index(TEXT_AXES) * (own_images * members)
    image_part, text_part = pair_block(
        jnp.reshape(first, (1,)).astype(jnp.int32), scalars, images, texts, pairs[None, :], 256
    )
    image_total = lax.psum_scatter(image_part, IMAGE_AXES, scatter_dimension=0, tiled=True)
    text_parts = lax.all_to_all(
        text_part.reshape(peers, own_texts, width), TEXT_AXES, split_axis=0, concat_axis=0, tiled=True
    )
    text_total = jnp.sum(text_parts.astype(jnp.float32), axis=0)
    return (
        unit_backward(image_float, image_inverse, image_total.astype(jnp.float32)),
        unit_backward(text_float, text_inverse, text_total),
    )


def solution(mesh):
    split = Mesh(mesh.devices.reshape(8, 2, 4, 4, 2), AXES)
    rows = P(AXES, None)
    return jax.shard_map(
        on_device,
        mesh=split,
        in_specs=(rows, rows, P(), P(), P(AXES)),
        out_specs=(rows, rows),
        check_vma=False,
    )
```

time: 759 us -> 147 us (0.19)
  the two profiles are of different devices: /device:TPU:64 before, /device:TPU:6 now
where the time goes in v1:
time: 147 us; the launch traced here: 144 us
  waiting for transfers between devices  84 us (57%)
  starting transfers between devices  24.4 us (17%)
  between operations  15.5 us (11%)
  Pallas kernels  9.4 us (6%)
  other arithmetic  7.8 us (5%)
  local copies, waits for them, and re-layouts  2.91 us (2%)
    all_to_all x1, waiting for transfers between devices, on_device(): lax.all_to_all(spread, TEXT_AXES, split_axis=0, concat_axis=0, tiled=True)  44.6 us
    all_to_all x1, waiting for transfers between devices, on_device(): lax.all_to_all(text_part.reshape(peers, own_texts, width), TEXT_AXES, spl...  38.7 us
    all_to_all x1, starting transfers between devices, on_device(): lax.all_to_all(spread, TEXT_AXES, split_axis=0, concat_axis=0, tiled=True)  16.7 us
    pallas_call x1, Pallas kernels, pair_block(): pl.pallas_call(pair_kernel, grid=(rows // block,), in_specs=[pl.BlockSpec...  9.4 us
    all_to_all x1, starting transfers between devices, on_device(): lax.all_to_all(text_part.reshape(peers, own_texts, width), TEXT_AXES, spl...  7.6 us
  transfers between devices with their start and end apart: 4, of which 2 were waited for; matrix products, arithmetic and copies ran while one was open for 2% of the time, Pallas kernels for 0%

profile of v1, /device:TPU:6, one launch (start us, length us, event | category | flops | bytes accessed | tf_op | source)
XLA Modules:
  0.0 144.0 jit_solution(9654885935936234280)
XLA Ops:
  7.2 0.9 fusion.13
  8.0 0.7 and_select_fusion.1
  8.7 0.8 fusion.8
  9.5 0.1 select_convert_fusion
  9.6 1.4 broadcast_in_dim.22
  11.0 0.0 copy-start.1
  11.0 16.7 %all-to-all-start = ((bf16[64,16,896]{2,1,0:T(8,128)(2,1)}), bf16[64,16,896]{2,1,0:T(8,128)(2,1)S(1)}, u32[]{:S(2)}, u32[]{:S(2)}) async-start(bf16[64,16,896]{2,1,0:T(8,128)(2,1)} %broadcast_in_dim.22), calls=%async_computation | async-start | bytes 3670016 | tf_op jit(solution)/shard_map/all_to_all | solution.py:100
  27.7 0.0 all-gather.2.cloned.1.call-start
  27.8 0.0 copy-done.1
  27.8 0.1 fusion.2
  27.9 0.8 fusion.1
  28.7 0.0 all-gather.2.cloned.1.call-update
  30.1 0.1 pad_maximum_fusion.1.scalars_ref
  30.1 44.6 %all-to-all-done = bf16[64,16,896]{2,1,0:T(8,128)(2,1)S(1)} async-done(((bf16[64,16,896]{2,1,0:T(8,128)(2,1)}), bf16[64,16,896]{2,1,0:T(8,128)(2,1)S(1)}, u32[]{:S(2)}, u32[]{:S(2)}) %all-to-all-start) | async-done | bytes 1835040 | tf_op jit(solution)/shard_map/all_to_all | solution.py:100
  74.8 0.1 slice.12.text_ref
  74.9 0.3 add_reduce_fusion
  75.2 0.0 all-gather.2.cloned.1.call-done.image_ref
  75.2 0.0 copy-start
  75.2 1.4 copy-done
  76.6 9.4 %shard_map.68 = (bf16[1024,768]{1,0:T(8,128)(2,1)}, bf16[1024,768]{1,0:T(8,128)(2,1)}) custom-call(s32[1]{0:T(128)} %bitcast.first_ref, f32[2]{0:T(128)S(1)} %pad_maximum_fusion.1.scalars_ref, bf16[1024,768]{1,0:T(8,128)(2,1)S(1)} %copy-done, bf16[1024,768]{1,0:T(8,128)(2,1)S(1)} %slice.12.text_ref, s32[1,1024]{1,0:T(1,128)S(1)} %bitcast.4), custom_call_target="tpu_custom_call" | custom-call | flops 4831838208 | bytes 12582912 | tf_op jit(solution)/shard_map/pallas_call | solution.py:59
  86.0 7.6 %all-to-all-start.1 = ((bf16[64,16,768]{2,1,0:T(8,128)(2,1)}), bf16[64,16,768]{2,1,0:T(8,128)(2,1)S(1)}, u32[]{:S(2)}, u32[]{:S(2)}) async-start(bf16[64,16,768]{2,1,0:T(8,128)(2,1)} %bitcast.2), calls=%async_computation.2 | async-start | bytes 3145728 | tf_op jit(solution)/shard_map/all_to_all | solution.py:110
  93.6 0.0 reduce-scatter.2.cloned.1.call-start
  93.7 0.0 copy-start.3
  93.7 0.0 copy-start.2
  93.7 0.7 reduce-scatter.2.cloned.1.call-update
  94.4 38.7 %all-to-all-done.1 = bf16[64,16,768]{2,1,0:T(8,128)(2,1)S(1)} async-done(((bf16[64,16,768]{2,1,0:T(8,128)(2,1)}), bf16[64,16,768]{2,1,0:T(8,128)(2,1)S(1)}, u32[]{:S(2)}, u32[]{:S(2)}) %all-to-all-start.1) | async-done | bytes 1572896 | tf_op jit(solution)/shard_map/all_to_all | solution.py:110
  133.1 0.2 convert_reduce_fusion
  133.3 0.0 copy-done.3
  133.3 0.2 fusion.9
  133.5 0.7 fusion.12
  134.2 0.0 reduce-scatter.2.cloned.1.call-done
  134.2 0.0 copy-done.2
  134.2 1.1 fusion.3
  135.4 1.8 %fusion.5 = bf16[128,768]{1,0:T(8,128)(2,1)} fusion(bf16[128,768]{1,0:T(8,128)(2,1)S(1)} %copy-done.2, bf16[128,768]{1,0:T(8,128)(2,1)} %reduce-scatter.2.cloned.1.call-done, f32[128]{0:T(128)S(1)} %fusion.3, f32[128]{0:T(128)S(1)} %add_rsqrt_fusion.1), kind=kLoop, calls=%fused_computation.11 | loop fusion | flops 688128 | bytes 590848 | tf_op jit(solution)/shard_map/convert_element_type | solution.py:25
  (4 shorter events, 0.0 us)
Async XLA Ops:
  11.0 16.8 %copy-start.1 = (bf16[128,768]{1,0:T(8,128)(2,1)S(1)}, bf16[128,768]{1,0:T(8,128)(2,1)}, u32[]{:S(2)}) copy-start(bf16[128,768]{1,0:T(8,128)(2,1)} %param.5) | copy-start | bytes 589828
  11.0 63.8 %all-to-all-start = ((bf16[64,16,896]{2,1,0:T(8,128)(2,1)}), bf16[64,16,896]{2,1,0:T(8,128)(2,1)S(1)}, u32[]{:S(2)}, u32[]{:S(2)}) async-start(bf16[64,16,896]{2,1,0:T(8,128)(2,1)} %broadcast_in_dim.22), calls=%async_computation | async-start | bytes 3670016 | tf_op jit(solution)/shard_map/all_to_all | solution.py:100
  27.7 47.5 %all-gather.2.cloned.1.call-start = ((), (), s32[]{:S(2)}) async-start(), calls=%async_computation.3 | async-start | bytes 1769472 | tf_op jit(solution)/shard_map/all_gather | solution.py:94
  75.2 1.4 copy-start
  86.0 47.1 %all-to-all-start.1 = ((bf16[64,16,768]{2,1,0:T(8,128)(2,1)}), bf16[64,16,768]{2,1,0:T(8,128)(2,1)S(1)}, u32[]{:S(2)}, u32[]{:S(2)}) async-start(bf16[64,16,768]{2,1,0:T(8,128)(2,1)} %bitcast.2), calls=%async_computation.2 | async-start | bytes 3145728 | tf_op jit(solution)/shard_map/all_to_all | solution.py:110
  93.6 40.6 %reduce-scatter.2.cloned.1.call-start = ((), (), s32[]{:S(2)}) async-start(), calls=%async_computation.4 | async-start | bytes 1769472 | tf_op jit(solution)/shard_map/reduce_scatter | solution.py:109
  93.7 39.7 %copy-start.3 = (bf16[16,768]{1,0:T(8,128)(2,1)S(1)}, bf16[16,768]{1,0:T(8,128)(2,1)}, u32[]{:S(2)}) copy-start(bf16[16,768]{1,0:T(8,128)(2,1)} %param.6) | copy-start | bytes 73732
  93.7 40.6 %copy-start.2 = (bf16[128,768]{1,0:T(8,128)(2,1)S(1)}, bf16[128,768]{1,0:T(8,128)(2,1)}, u32[]{:S(2)}) copy-start(bf16[128,768]{1,0:T(8,128)(2,1)} %param.5) | copy-start | bytes 589828
Sparse Core Ops, SparseCore 0:
  31.3 28.9 all-gather.1
  97.3 36.0 reduce-scatter.1

commit v2 on v1

v2 whole, which is shorter than its diff:
```python
import jax
import jax.numpy as jnp
from jax import lax
from jax.experimental import pallas as pl
from jax.experimental.pallas import tpu as pltpu
from jax.sharding import Mesh
from jax.sharding import PartitionSpec as P

AXES = ("z", "yh", "yl", "x", "c")
FAR = ("z", "yh")
LANES = 128
BLOCK = 256
VMEM = 40 * 1024 * 1024


def normalize(values):
    floats = values.astype(jnp.float32)
    inverse = lax.rsqrt(jnp.sum(floats * floats, axis=-1, keepdims=True) + 1e-06)
    return (floats * inverse, inverse)


def unit_backward(floats, inverse, grad):
    along = jnp.sum(floats * grad, axis=-1, keepdims=True)
    return ((grad - floats * along) * inverse).astype(jnp.bfloat16)


def shifted(array, axis, by):
    devices = lax.axis_size(axis)
    return lax.ppermute(array, axis, [(i, (i + by) % devices) for i in range(devices)])


def chunk_kernel(first_ref, scalars_ref, own_ref, other_ref, packet_ref, weight_ref, grad_ref):
    width = own_ref.shape[1]
    scale = scalars_ref[0]
    offset = scalars_ref[1]
    texts = packet_ref[:, :width]
    digits = packet_ref[:, width:].astype(jnp.float32).T
    pairs = (digits[0:1] * 256.0 + digits[1:2]).astype(jnp.int32)
    half = own_ref.shape[0]
    pieces = BLOCK // 128
    total = None
    for block in range(2 * half // BLOCK):
        source, start = (own_ref, block * BLOCK) if block * BLOCK < half else (other_ref, block * BLOCK - half)
        images = source[start : start + BLOCK, :]
        dots = lax.dot_general(images, texts, (((1,), (1,)), ((), ())), preferred_element_type=jnp.float32)
        chance = 1.0 / (1.0 + jnp.exp(-(scale * dots + offset)))
        row = lax.broadcasted_iota(jnp.int32, (128, 1), 0)
        rows = jnp.concatenate([row + first_ref[block * pieces + p] for p in range(pieces)], axis=0)
        weight = (scale * jnp.where(pairs == rows, chance - 1.0, chance)).astype(jnp.bfloat16)
        weight_ref[block * BLOCK : (block + 1) * BLOCK, :] = weight
        term = lax.dot_general(weight, images, (((0,), (0,)), ((), ())), preferred_element_type=jnp.float32)
        total = term if total is None else total + term
    grad_ref[...] = total.astype(grad_ref.dtype)


def chunk_terms(first, scalars, own, other, packet, grad_type):
    half, width = own.shape
    count = packet.shape[0]
    smem = pl.BlockSpec(memory_space=pltpu.SMEM)
    vmem = pl.BlockSpec(memory_space=pltpu.VMEM)
    return pl.pallas_call(
        chunk_kernel,
        in_specs=[smem, smem, vmem, vmem, vmem],
        out_specs=[vmem, vmem],
        out_shape=[
            jax.ShapeDtypeStruct((2 * half, count), jnp.bfloat16),
            jax.ShapeDtypeStruct((count, width), grad_type),
        ],
        compiler_params=pltpu.CompilerParams(vmem_limit_bytes=VMEM),
        cost_estimate=pl.CostEstimate(
            flops=8 * half * count * width,
            bytes_accessed=4 * half * (width + count) + 4 * count * width,
            transcendentals=4 * half * count,
        ),
    )(first, scalars, own, other, packet)


def image_kernel(start, *refs):
    weights, packets, out_ref = refs[:4], refs[4:8], refs[8]
    width = out_ref.shape[1]
    for block in range(out_ref.shape[0] // BLOCK):
        total = None
        for weight_ref, packet_ref in zip(weights, packets):
            weight = weight_ref[start + block * BLOCK : start + (block + 1) * BLOCK, :]
            term = jnp.dot(weight, packet_ref[:, :width], preferred_element_type=jnp.float32)
            total = term if total is None else total + term
        out_ref[block * BLOCK : (block + 1) * BLOCK, :] = total.astype(out_ref.dtype)


def image_terms(weights, packets, start, half, width, out_type):
    vmem = pl.BlockSpec(memory_space=pltpu.VMEM)
    count = packets[0].shape[0]
    return pl.pallas_call(
        lambda *refs: image_kernel(start, *refs),
        in_specs=[vmem] * 8,
        out_specs=vmem,
        out_shape=jax.ShapeDtypeStruct((half, width), out_type),
        compiler_params=pltpu.CompilerParams(vmem_limit_bytes=VMEM),
        cost_estimate=pl.CostEstimate(
            flops=8 * half * count * width, bytes_accessed=16 * half * count + 8 * count * width, transcendentals=0
        ),
    )(*weights, *packets)


def on_device(image_embed, text_embed, log_scale, logit_bias, pair_index):
    own_images, width = image_embed.shape
    own_texts = text_embed.shape[0]
    peers = lax.axis_size(FAR)
    near = lax.axis_size("yl")
    ring = lax.axis_size("x")
    image_float, image_inverse = normalize(image_embed)
    text_float, text_inverse = normalize(text_embed)
    scalars = jnp.concatenate([jnp.exp(log_scale), logit_bias])

    lane = lax.broadcasted_iota(jnp.int32, (own_texts, LANES), 1)
    digits = jnp.where(lane == 0, pair_index[:, None] // 256, jnp.where(lane == 1, pair_index[:, None] % 256, 0))
    packet = jnp.concatenate([text_float.astype(jnp.bfloat16), digits.astype(jnp.bfloat16)], axis=1)
    spread = jnp.broadcast_to(packet[None], (peers, own_texts, width + LANES))
    packet = lax.all_to_all(spread, FAR, split_axis=0, concat_axis=0, tiled=True)
    packet = packet.reshape(peers * own_texts, width + LANES)

    image_unit = image_float.astype(jnp.bfloat16)
    own = jnp.concatenate([image_unit] + [shifted(image_unit, "yl", s) for s in range(1, near)], axis=0)
    other = shifted(own, "c", 1)

    far_id, yl, x, c = lax.axis_index(FAR), lax.axis_index("yl"), lax.axis_index("x"), lax.axis_index("c")
    group = lax.axis_size("x") * lax.axis_size("c")
    first = jnp.stack(
        [
            (((far_id * near + (yl - s) % near) * group) + x * 2 + core) * own_images
            for core in (c, 1 - c)
            for s in range(near)
        ]
    ).astype(jnp.int32)

    order = (0, 1, ring - 1, 2)
    packets = [packet] + [shifted(packet, "x", s) for s in order[1:]]
    weights, text_total = [], None
    for step, chunk in zip(order, packets):
        weight, part = chunk_terms(first, scalars, own, other, chunk, jnp.float32 if step == 0 else jnp.bfloat16)
        weights.append(weight)
        part = part if step == 0 else shifted(part, "x", -step).astype(jnp.float32)
        text_total = part if text_total is None else text_total + part

    half = near * own_images
    other_part = image_terms(weights, packets, half, half, width, jnp.bfloat16)
    own_part = image_terms(weights, packets, 0, half, width, jnp.float32)
    image_part = own_part + shifted(other_part, "c", 1).astype(jnp.float32)
    image_total = image_part[:own_images]
    for s in range(1, near):
        sent = image_part[s * own_images : (s + 1) * own_images].astype(jnp.bfloat16)
        image_total = image_total + shifted(sent, "yl", -s).astype(jnp.float32)

    text_parts = lax.all_to_all(
        text_total.astype(jnp.bfloat16).reshape(peers, own_texts, width), FAR, split_axis=0, concat_axis=0, tiled=True
    )
    text_own = jnp.sum(text_parts.astype(jnp.float32), axis=0)
    return (
        unit_backward(image_float, image_inverse, image_total),
        unit_backward(text_float, text_inverse, text_own),
    )


def solution(mesh):
    split = Mesh(mesh.devices.reshape(8, 2, 4, 4, 2), AXES)
    rows = P(AXES, None)
    return jax.shard_map(
        on_device,
        mesh=split,
        in_specs=(rows, rows, P(), P(), P(AXES)),
        out_specs=(rows, rows),
        check_vma=False,
    )
```

time: 147 us -> 152 us (1.034)
  starting transfers between devices: 24.4 us -> 67.6 us
  waiting for transfers between devices: 84 us -> 56.2 us
  between operations: 15.5 us -> 2.31 us
  Pallas kernels: 9.4 us -> 15.4 us
  local copies, waits for them, and re-layouts: 2.91 us -> 0.97 us
    all_to_all x2, waiting for transfers between devices: 83.3 us -> 0.01 us  [the longest x1 0.01 us: on_device(): lax.all_to_all(text_total.astype(jnp.bfloat16).reshape(peers, own_texts,...]
    ppermute x0 -> x14, waiting for transfers between devices: none -> 56.2 us  [shifted(): lax.ppermute(array, axis, [(i, (i + by) % devices) for i in range(devices)])]
    ppermute x0 -> x14, starting transfers between devices: none -> 40.4 us  [shifted(): lax.ppermute(array, axis, [(i, (i + by) % devices) for i in range(devices)])]
    pallas_call x1 -> x6, Pallas kernels: 9.4 us -> 15.4 us  [the longest x4 12.6 us: chunk_terms(): pl.pallas_call(chunk_kernel, in_specs=[smem, smem, vmem, vmem, vmem], out...]
    all_to_all x2, starting transfers between devices: 24.3 us -> 27.2 us  [the longest x1 15.7 us: on_device(): lax.all_to_all(spread, FAR, split_axis=0, concat_axis=0, tiled=True)]
  transfers between devices with their start and end apart: 4 -> 16, of which waited for: 2 -> 10; matrix products, arithmetic and copies ran while one was open for 2% -> 3% of each run, Pallas kernels for 0% -> 7%
where the time goes in v2:
time: 152 us; the launch traced here: 150 us
  starting transfers between devices  67.6 us (44%)
  waiting for transfers between devices  56.2 us (37%)
  Pallas kernels  15.4 us (10%)
  other arithmetic  7.15 us (5%)
  between operations  2.31 us (2%)
    ppermute x14, waiting for transfers between devices, shifted(): lax.ppermute(array, axis, [(i, (i + by) % devices) for i in range(devices)])  56.2 us
    ppermute x14, starting transfers between devices, shifted(): lax.ppermute(array, axis, [(i, (i + by) % devices) for i in range(devices)])  40.4 us
    all_to_all x1, starting transfers between devices, on_device(): lax.all_to_all(spread, FAR, split_axis=0, concat_axis=0, tiled=True)  15.7 us
    pallas_call x4, Pallas kernels, chunk_terms(): pl.pallas_call(chunk_kernel, in_specs=[smem, smem, vmem, vmem, vmem], out...  12.6 us
    all_to_all x1, starting transfers between devices, on_device(): lax.all_to_all(text_total.astype(jnp.bfloat16).reshape(peers, own_texts,...  11.5 us
  transfers between devices with their start and end apart: 16, of which 10 were waited for; matrix products, arithmetic and copies ran while one was open for 3% of the time, Pallas kernels for 7%

profile of v2, /device:TPU:6, one launch (start us, length us, event | category | flops | bytes accessed | tf_op | source)
XLA Modules:
  0.0 149.6 jit_solution(7017493448012327976)
XLA Ops:
  0.6 0.0 copy-start
  0.7 0.9 fusion.17
  1.6 0.7 and_select_fusion.1
  2.2 0.8 fusion.12
  3.0 0.1 select_convert_fusion
  3.1 0.8 broadcast_in_dim.22
  3.9 15.7 %all-to-all-start = ((bf16[16,16,896]{2,1,0:T(8,128)(2,1)}), bf16[16,16,896]{2,1,0:T(8,128)(2,1)S(1)}, u32[]{:S(2)}, u32[]{:S(2)}) async-start(bf16[16,16,896]{2,1,0:T(8,128)(2,1)} %broadcast_in_dim.22), calls=%async_computation | async-start | bytes 917504 | tf_op jit(solution)/shard_map/all_to_all | solution.py:119
  19.6 0.0 copy-done
  19.6 0.1 fusion.7
  19.8 0.1 fusion.2
  19.9 2.8 %collective-permute-start.2 = (bf16[128,768]{1,0:T(8,128)(2,1)S(1)}, bf16[128,768]{1,0:T(8,128)(2,1)S(1)}, u32[]{:S(2)}, u32[]{:S(2)}) collective-permute-start(bf16[128,768]{1,0:T(8,128)(2,1)S(1)} %fusion.2), channel_id=1, source_target_pairs={{0,24},{8,0},{16,8},{24,16},{1,25},{9,1},{17,9},{25,17},{2,26},{10... | collective-permute-start | bytes 589832 | tf_op jit(solution)/shard_map/ppermute | solution.py:29
  22.7 3.1 %collective-permute-start.1 = (bf16[128,768]{1,0:T(8,128)(2,1)S(1)}, bf16[128,768]{1,0:T(8,128)(2,1)S(1)}, u32[]{:S(2)}, u32[]{:S(2)}) collective-permute-start(bf16[128,768]{1,0:T(8,128)(2,1)S(1)} %fusion.2), channel_id=1, source_target_pairs={{0,16},{8,24},{16,0},{24,8},{1,17},{9,25},{17,1},{25,9},{2,18},{10... | collective-permute-start | bytes 589832 | tf_op jit(solution)/shard_map/ppermute | solution.py:29
  25.9 2.6 %collective-permute-start = (bf16[128,768]{1,0:T(8,128)(2,1)S(1)}, bf16[128,768]{1,0:T(8,128)(2,1)S(1)}, u32[]{:S(2)}, u32[]{:S(2)}) collective-permute-start(bf16[128,768]{1,0:T(8,128)(2,1)S(1)} %fusion.2), channel_id=1, source_target_pairs={{0,8},{8,16},{16,24},{24,0},{1,9},{9,17},{17,25},{25,1},{2,10},{10... | collective-permute-start | bytes 589832 | tf_op jit(solution)/shard_map/ppermute | solution.py:29
  28.5 6.4 %collective-permute-done.2 = bf16[128,768]{1,0:T(8,128)(2,1)S(1)} collective-permute-done((bf16[128,768]{1,0:T(8,128)(2,1)S(1)}, bf16[128,768]{1,0:T(8,128)(2,1)S(1)}, u32[]{:S(2)}, u32[]{:S(2)}) %collective-permute-start.2) | collective-permute-done | bytes 196640 | tf_op jit(solution)/shard_map/ppermute | solution.py:29
  34.9 12.9 %collective-permute-done.1 = bf16[128,768]{1,0:T(8,128)(2,1)S(1)} collective-permute-done((bf16[128,768]{1,0:T(8,128)(2,1)S(1)}, bf16[128,768]{1,0:T(8,128)(2,1)S(1)}, u32[]{:S(2)}, u32[]{:S(2)}) %collective-permute-start.1) | collective-permute-done | bytes 196640 | tf_op jit(solution)/shard_map/ppermute | solution.py:29
  47.8 0.0 collective-permute-done
  47.8 0.1 pad_maximum_fusion.own_ref
  47.9 1.9 %collective-permute-start.3 = (bf16[512,768]{1,0:T(8,128)(2,1)S(1)}, bf16[512,768]{1,0:T(8,128)(2,1)}, u32[]{:S(2)}, u32[]{:S(2)}) collective-permute-start(bf16[512,768]{1,0:T(8,128)(2,1)S(1)} %pad_maximum_fusion.own_ref), channel_id=1, source_target_pairs={{0,1},{1,0},{2,3},{3,2},{4,5},{5,4},{6,7},{7,6},{8,9},{9,8},{10,11... | collective-permute-start | bytes 2359304 | tf_op jit(solution)/shard_map/ppermute | solution.py:29
  49.8 0.0 all-to-all-done
  49.8 3.3 %collective-permute-start.6 = (bf16[256,896]{1,0:T(8,128)(2,1)S(1)}, bf16[256,896]{1,0:T(8,128)(2,1)S(1)}, u32[]{:S(2)}, u32[]{:S(2)}) collective-permute-start(bf16[256,896]{1,0:T(8,128)(2,1)S(1)} %bitcast.10), channel_id=1, source_target_pairs={{0,4},{2,6},{4,0},{6,2},{1,5},{3,7},{5,1},{7,3},{8,12},{10,14},{12... | collective-permute-start | bytes 1376264 | tf_op jit(solution)/shard_map/ppermute | solution.py:29
  53.1 1.9 %collective-permute-start.5 = (bf16[256,896]{1,0:T(8,128)(2,1)S(1)}, bf16[256,896]{1,0:T(8,128)(2,1)S(1)}, u32[]{:S(2)}, u32[]{:S(2)}) collective-permute-start(bf16[256,896]{1,0:T(8,128)(2,1)S(1)} %bitcast.11), channel_id=1, source_target_pairs={{0,6},{2,0},{4,2},{6,4},{1,7},{3,1},{5,3},{7,5},{8,14},{10,8},{12,... | collective-permute-start | bytes 1376264 | tf_op jit(solution)/shard_map/ppermute | solution.py:29
  55.1 5.1 %collective-permute-start.4 = (bf16[256,896]{1,0:T(8,128)(2,1)S(1)}, bf16[256,896]{1,0:T(8,128)(2,1)S(1)}, u32[]{:S(2)}, u32[]{:S(2)}) collective-permute-start(bf16[256,896]{1,0:T(8,128)(2,1)S(1)} %bitcast.12), channel_id=1, source_target_pairs={{0,2},{2,4},{4,6},{6,0},{1,3},{3,5},{5,7},{7,1},{8,10},{10,12},{12... | collective-permute-start | bytes 1376264 | tf_op jit(solution)/shard_map/ppermute | solution.py:29
  61.6 0.1 stack.35.first_ref
  61.7 0.1 pad_maximum_fusion.2.scalars_ref
  61.8 0.0 collective-permute-done.3.other_ref
  61.8 3.1 %shard_map.68 = (bf16[1024,256]{1,0:T(8,128)(2,1)S(1)}, f32[256,768]{1,0:T(8,128)S(1)}) custom-call(s32[8]{0:T(128)S(1)} %stack.35.first_ref, f32[2]{0:T(128)S(1)} %pad_maximum_fusion.2.scalars_ref, bf16[512,768]{1,0:T(8,128)(2,1)S(1)} %pad_maximum_fusion.own_ref, bf16[512,768]{1,0:T(8,128)(2,1)} %collective-permute-done.3.other_ref, ...), custom_call_target="tpu_custom_call" | custom-call | flops 805306368 | bytes 2883584 | tf_op jit(solution)/shard_map/pallas_call | solution.py:61
  64.9 1.6 %collective-permute-done.6.packet_ref.refs_7_ = bf16[256,896]{1,0:T(8,128)(2,1)S(1)} collective-permute-done((bf16[256,896]{1,0:T(8,128)(2,1)S(1)}, bf16[256,896]{1,0:T(8,128)(2,1)S(1)}, u32[]{:S(2)}, u32[]{:S(2)}) %collective-permute-start.6) | collective-permute-done | bytes 458784 | tf_op jit(solution)/shard_map/ppermute | solution.py:29
  66.6 3.1 %shard_map.71 = (bf16[1024,256]{1,0:T(8,128)(2,1)S(1)}, bf16[256,768]{1,0:T(8,128)(2,1)S(1)}) custom-call(s32[8]{0:T(128)S(1)} %stack.35.first_ref, f32[2]{0:T(128)S(1)} %pad_maximum_fusion.2.scalars_ref, bf16[512,768]{1,0:T(8,128)(2,1)S(1)} %pad_maximum_fusion.own_ref, bf16[512,768]{1,0:T(8,128)(2,1)} %collective-permute-done.3.other_ref, ...), custom_call_target="tpu_custom_call" | custom-call | flops 805306368 | bytes 2883584 | tf_op jit(solution)/shard_map/pallas_call | solution.py:61
  69.7 6.2 %collective-permute-done.5.packet_ref.refs_6_ = bf16[256,896]{1,0:T(8,128)(2,1)S(1)} collective-permute-done((bf16[256,896]{1,0:T(8,128)(2,1)S(1)}, bf16[256,896]{1,0:T(8,128)(2,1)S(1)}, u32[]{:S(2)}, u32[]{:S(2)}) %collective-permute-start.5) | collective-permute-done | bytes 458784 | tf_op jit(solution)/shard_map/ppermute | solution.py:29
  76.0 3.1 %shard_map.70 = (bf16[1024,256]{1,0:T(8,128)(2,1)S(1)}, bf16[256,768]{1,0:T(8,128)(2,1)S(1)}) custom-call(s32[8]{0:T(128)S(1)} %stack.35.first_ref, f32[2]{0:T(128)S(1)} %pad_maximum_fusion.2.scalars_ref, bf16[512,768]{1,0:T(8,128)(2,1)S(1)} %pad_maximum_fusion.own_ref, bf16[512,768]{1,0:T(8,128)(2,1)} %collective-permute-done.3.other_ref, ...), custom_call_target="tpu_custom_call" | custom-call | flops 805306368 | bytes 2883584 | tf_op jit(solution)/shard_map/pallas_call | solution.py:61
  79.1 0.0 collective-permute-done.4.packet_ref.refs_5_
  79.1 3.1 %shard_map.69 = (bf16[1024,256]{1,0:T(8,128)(2,1)S(1)}, bf16[256,768]{1,0:T(8,128)(2,1)S(1)}) custom-call(s32[8]{0:T(128)S(1)} %stack.35.first_ref, f32[2]{0:T(128)S(1)} %pad_maximum_fusion.2.scalars_ref, bf16[512,768]{1,0:T(8,128)(2,1)S(1)} %pad_maximum_fusion.own_ref, bf16[512,768]{1,0:T(8,128)(2,1)} %collective-permute-done.3.other_ref, ...), custom_call_target="tpu_custom_call" | custom-call | flops 805306368 | bytes 2883584 | tf_op jit(solution)/shard_map/pallas_call | solution.py:61
  82.3 1.9 %shard_map.73 = bf16[512,768]{1,0:T(8,128)(2,1)} custom-call(bf16[1024,256]{1,0:T(8,128)(2,1)S(1)} %get-tuple-element.10.refs_0_, bf16[1024,256]{1,0:T(8,128)(2,1)S(1)} %get-tuple-element.11.refs_1_, bf16[1024,256]{1,0:T(8,128)(2,1)S(1)} %get-tuple-element.12.refs_2_, bf16[1024,256]{1,0:T(8,128)(2,1)S(1)} %get-tuple-element.13.refs_3_, ...), custom_call_target="tpu_custom_call" | custom-call | flops 805306368 | bytes 3670016 | tf_op jit(solution)/shard_map/pallas_call | solution.py:93
  84.2 1.9 %collective-permute-start.7 = (bf16[512,768]{1,0:T(8,128)(2,1)}, bf16[512,768]{1,0:T(8,128)(2,1)}, u32[]{:S(2)}, u32[]{:S(2)}) collective-permute-start(bf16[512,768]{1,0:T(8,128)(2,1)} %shard_map.73), channel_id=1, source_target_pairs={{0,1},{1,0},{2,3},{3,2},{4,5},{5,4},{6,7},{7,6},{8,9},{9,8},{10,11... | collective-permute-start | bytes 2359304 | tf_op jit(solution)/shard_map/ppermute | solution.py:29
  86.1 3.3 %collective-permute-start.13 = (bf16[256,768]{1,0:T(8,128)(2,1)S(1)}, bf16[256,768]{1,0:T(8,128)(2,1)S(1)}, u32[]{:S(2)}, u32[]{:S(2)}) collective-permute-start(bf16[256,768]{1,0:T(8,128)(2,1)S(1)} %get-tuple-element.17), channel_id=1, source_target_pairs={{0,4},{2,6},{4,0},{6,2},{1,5},{3,7},{5,1},{7,3},{8,12},{10,14},{12... | collective-permute-start | bytes 1179656 | tf_op jit(solution)/shard_map/ppermute | solution.py:29
  89.4 3.1 %collective-permute-start.12 = (bf16[256,768]{1,0:T(8,128)(2,1)S(1)}, bf16[256,768]{1,0:T(8,128)(2,1)S(1)}, u32[]{:S(2)}, u32[]{:S(2)}) collective-permute-start(bf16[256,768]{1,0:T(8,128)(2,1)S(1)} %get-tuple-element.16), channel_id=1, source_target_pairs={{0,2},{2,4},{4,6},{6,0},{1,3},{3,5},{5,7},{7,1},{8,10},{10,12},{12... | collective-permute-start | bytes 1179656 | tf_op jit(solution)/shard_map/ppermute | solution.py:29
  92.5 2.8 %collective-permute-start.11 = (bf16[256,768]{1,0:T(8,128)(2,1)S(1)}, bf16[256,768]{1,0:T(8,128)(2,1)S(1)}, u32[]{:S(2)}, u32[]{:S(2)}) collective-permute-start(bf16[256,768]{1,0:T(8,128)(2,1)S(1)} %get-tuple-element.15), channel_id=1, source_target_pairs={{0,6},{2,0},{4,2},{6,4},{1,7},{3,1},{5,3},{7,5},{8,14},{10,8},{12,... | collective-permute-start | bytes 1179656 | tf_op jit(solution)/shard_map/ppermute | solution.py:29
  95.3 1.0 shard_map.72
  96.3 5.2 %collective-permute-done.13 = bf16[256,768]{1,0:T(8,128)(2,1)S(1)} collective-permute-done((bf16[256,768]{1,0:T(8,128)(2,1)S(1)}, bf16[256,768]{1,0:T(8,128)(2,1)S(1)}, u32[]{:S(2)}, u32[]{:S(2)}) %collective-permute-start.13) | collective-permute-done | bytes 393248 | tf_op jit(solution)/shard_map/ppermute | solution.py:29
  101.5 5.9 %collective-permute-done.12 = bf16[256,768]{1,0:T(8,128)(2,1)S(1)} collective-permute-done((bf16[256,768]{1,0:T(8,128)(2,1)S(1)}, bf16[256,768]{1,0:T(8,128)(2,1)S(1)}, u32[]{:S(2)}, u32[]{:S(2)}) %collective-permute-start.12) | collective-permute-done | bytes 393248 | tf_op jit(solution)/shard_map/ppermute | solution.py:29
  107.4 2.0 %collective-permute-done.11 = bf16[256,768]{1,0:T(8,128)(2,1)S(1)} collective-permute-done((bf16[256,768]{1,0:T(8,128)(2,1)S(1)}, bf16[256,768]{1,0:T(8,128)(2,1)S(1)}, u32[]{:S(2)}, u32[]{:S(2)}) %collective-permute-start.11) | collective-permute-done | bytes 393248 | tf_op jit(solution)/shard_map/ppermute | solution.py:29
  109.4 0.9 add_convert_fusion
  110.3 11.5 %all-to-all-start.1 = ((bf16[16,16,768]{2,1,0:T(8,128)(2,1)}), bf16[16,16,768]{2,1,0:T(8,128)(2,1)S(1)}, u32[]{:S(2)}, u32[]{:S(2)}) async-start(bf16[16,16,768]{2,1,0:T(8,128)(2,1)} %bitcast.9), calls=%async_computation.1 | async-start | bytes 786432 | tf_op jit(solution)/shard_map/all_to_all | solution.py:154
  121.9 0.0 copy-start.1
  121.9 0.0 collective-permute-done.7
  121.9 1.3 fusion.18
  123.3 0.0 copy-start.2
  123.3 1.9 %collective-permute-start.8 = (bf16[128,768]{1,0:T(8,128)(2,1)S(1)}, bf16[128,768]{1,0:T(8,128)(2,1)S(1)}, u32[]{:S(2)}, u32[]{:S(2)}) collective-permute-start(bf16[128,768]{1,0:T(8,128)(2,1)S(1)} %get-tuple-element.20), channel_id=1, source_target_pairs={{0,24},{8,0},{16,8},{24,16},{1,25},{9,1},{17,9},{25,17},{2,26},{10... | collective-permute-start | bytes 589832 | tf_op jit(solution)/shard_map/ppermute | solution.py:29
  125.2 3.9 %collective-permute-start.10 = (bf16[128,768]{1,0:T(8,128)(2,1)S(1)}, bf16[128,768]{1,0:T(8,128)(2,1)S(1)}, u32[]{:S(2)}, u32[]{:S(2)}) collective-permute-start(bf16[128,768]{1,0:T(8,128)(2,1)S(1)} %get-tuple-element.21), channel_id=1, source_target_pairs={{0,8},{8,16},{16,24},{24,0},{1,9},{9,17},{17,25},{25,1},{2,10},{10... | collective-permute-start | bytes 589832 | tf_op jit(solution)/shard_map/ppermute | solution.py:29
  129.2 2.6 %collective-permute-start.9 = (bf16[128,768]{1,0:T(8,128)(2,1)S(1)}, bf16[128,768]{1,0:T(8,128)(2,1)S(1)}, u32[]{:S(2)}, u32[]{:S(2)}) collective-permute-start(bf16[128,768]{1,0:T(8,128)(2,1)S(1)} %get-tuple-element.22), channel_id=1, source_target_pairs={{0,16},{8,24},{16,0},{24,8},{1,17},{9,25},{17,1},{25,9},{2,18},{10... | collective-permute-start | bytes 589832 | tf_op jit(solution)/shard_map/ppermute | solution.py:29
  131.8 3.1 %collective-permute-done.8 = bf16[128,768]{1,0:T(8,128)(2,1)S(1)} collective-permute-done((bf16[128,768]{1,0:T(8,128)(2,1)S(1)}, bf16[128,768]{1,0:T(8,128)(2,1)S(1)}, u32[]{:S(2)}, u32[]{:S(2)}) %collective-permute-start.8) | collective-permute-done | bytes 196640 | tf_op jit(solution)/shard_map/ppermute | solution.py:29
  134.9 6.7 %collective-permute-done.10 = bf16[128,768]{1,0:T(8,128)(2,1)S(1)} collective-permute-done((bf16[128,768]{1,0:T(8,128)(2,1)S(1)}, bf16[128,768]{1,0:T(8,128)(2,1)S(1)}, u32[]{:S(2)}, u32[]{:S(2)}) %collective-permute-start.10) | collective-permute-done | bytes 196640 | tf_op jit(solution)/shard_map/ppermute | solution.py:29
  141.6 6.0 %collective-permute-done.9 = bf16[128,768]{1,0:T(8,128)(2,1)S(1)} collective-permute-done((bf16[128,768]{1,0:T(8,128)(2,1)S(1)}, bf16[128,768]{1,0:T(8,128)(2,1)S(1)}, u32[]{:S(2)}, u32[]{:S(2)}) %collective-permute-start.9) | collective-permute-done | bytes 196640 | tf_op jit(solution)/shard_map/ppermute | solution.py:29
  147.6 0.0 copy-done.1
  147.6 0.2 fusion.3
  147.8 0.9 fusion.6
  148.7 0.0 all-to-all-done.1
  148.7 0.1 convert_reduce_fusion
  148.8 0.0 copy-done.2
  148.8 0.2 fusion.13
  149.0 0.7 fusion.16
  (5 shorter events, 0.1 us)
Async XLA Ops:
  0.6 19.0 %copy-start = (bf16[128,768]{1,0:T(8,128)(2,1)S(1)}, bf16[128,768]{1,0:T(8,128)(2,1)}, u32[]{:S(2)}) copy-start(bf16[128,768]{1,0:T(8,128)(2,1)} %param.5) | copy-start | bytes 589828
  3.9 45.9 %all-to-all-start = ((bf16[16,16,896]{2,1,0:T(8,128)(2,1)}), bf16[16,16,896]{2,1,0:T(8,128)(2,1)S(1)}, u32[]{:S(2)}, u32[]{:S(2)}) async-start(bf16[16,16,896]{2,1,0:T(8,128)(2,1)} %broadcast_in_dim.22), calls=%async_computation | async-start | bytes 917504 | tf_op jit(solution)/shard_map/all_to_all | solution.py:119
  19.9 15.0 %collective-permute-start.2 = (bf16[128,768]{1,0:T(8,128)(2,1)S(1)}, bf16[128,768]{1,0:T(8,128)(2,1)S(1)}, u32[]{:S(2)}, u32[]{:S(2)}) collective-permute-start(bf16[128,768]{1,0:T(8,128)(2,1)S(1)} %fusion.2), channel_id=1, source_target_pairs={{0,24},{8,0},{16,8},{24,16},{1,25},{9,1},{17,9},{25,17},{2,26},{10... | collective-permute-start | bytes 589832 | tf_op jit(solution)/shard_map/ppermute | solution.py:29
  22.7 25.1 %collective-permute-start.1 = (bf16[128,768]{1,0:T(8,128)(2,1)S(1)}, bf16[128,768]{1,0:T(8,128)(2,1)S(1)}, u32[]{:S(2)}, u32[]{:S(2)}) collective-permute-start(bf16[128,768]{1,0:T(8,128)(2,1)S(1)} %fusion.2), channel_id=1, source_target_pairs={{0,16},{8,24},{16,0},{24,8},{1,17},{9,25},{17,1},{25,9},{2,18},{10... | collective-permute-start | bytes 589832 | tf_op jit(solution)/shard_map/ppermute | solution.py:29
  25.9 22.0 %collective-permute-start = (bf16[128,768]{1,0:T(8,128)(2,1)S(1)}, bf16[128,768]{1,0:T(8,128)(2,1)S(1)}, u32[]{:S(2)}, u32[]{:S(2)}) collective-permute-start(bf16[128,768]{1,0:T(8,128)(2,1)S(1)} %fusion.2), channel_id=1, source_target_pairs={{0,8},{8,16},{16,24},{24,0},{1,9},{9,17},{17,25},{25,1},{2,10},{10... | collective-permute-start | bytes 589832 | tf_op jit(solution)/shard_map/ppermute | solution.py:29
  47.9 13.9 %collective-permute-start.3 = (bf16[512,768]{1,0:T(8,128)(2,1)S(1)}, bf16[512,768]{1,0:T(8,128)(2,1)}, u32[]{:S(2)}, u32[]{:S(2)}) collective-permute-start(bf16[512,768]{1,0:T(8,128)(2,1)S(1)} %pad_maximum_fusion.own_ref), channel_id=1, source_target_pairs={{0,1},{1,0},{2,3},{3,2},{4,5},{5,4},{6,7},{7,6},{8,9},{9,8},{10,11... | collective-permute-start | bytes 2359304 | tf_op jit(solution)/shard_map/ppermute | solution.py:29
  49.8 16.8 %collective-permute-start.6 = (bf16[256,896]{1,0:T(8,128)(2,1)S(1)}, bf16[256,896]{1,0:T(8,128)(2,1)S(1)}, u32[]{:S(2)}, u32[]{:S(2)}) collective-permute-start(bf16[256,896]{1,0:T(8,128)(2,1)S(1)} %bitcast.10), channel_id=1, source_target_pairs={{0,4},{2,6},{4,0},{6,2},{1,5},{3,7},{5,1},{7,3},{8,12},{10,14},{12... | collective-permute-start | bytes 1376264 | tf_op jit(solution)/shard_map/ppermute | solution.py:29
  53.1 22.8 %collective-permute-start.5 = (bf16[256,896]{1,0:T(8,128)(2,1)S(1)}, bf16[256,896]{1,0:T(8,128)(2,1)S(1)}, u32[]{:S(2)}, u32[]{:S(2)}) collective-permute-start(bf16[256,896]{1,0:T(8,128)(2,1)S(1)} %bitcast.11), channel_id=1, source_target_pairs={{0,6},{2,0},{4,2},{6,4},{1,7},{3,1},{5,3},{7,5},{8,14},{10,8},{12,... | collective-permute-start | bytes 1376264 | tf_op jit(solution)/shard_map/ppermute | solution.py:29
  55.1 24.0 %collective-permute-start.4 = (bf16[256,896]{1,0:T(8,128)(2,1)S(1)}, bf16[256,896]{1,0:T(8,128)(2,1)S(1)}, u32[]{:S(2)}, u32[]{:S(2)}) collective-permute-start(bf16[256,896]{1,0:T(8,128)(2,1)S(1)} %bitcast.12), channel_id=1, source_target_pairs={{0,2},{2,4},{4,6},{6,0},{1,3},{3,5},{5,7},{7,1},{8,10},{10,12},{12... | collective-permute-start | bytes 1376264 | tf_op jit(solution)/shard_map/ppermute | solution.py:29
  84.2 37.7 %collective-permute-start.7 = (bf16[512,768]{1,0:T(8,128)(2,1)}, bf16[512,768]{1,0:T(8,128)(2,1)}, u32[]{:S(2)}, u32[]{:S(2)}) collective-permute-start(bf16[512,768]{1,0:T(8,128)(2,1)} %shard_map.73), channel_id=1, source_target_pairs={{0,1},{1,0},{2,3},{3,2},{4,5},{5,4},{6,7},{7,6},{8,9},{9,8},{10,11... | collective-permute-start | bytes 2359304 | tf_op jit(solution)/shard_map/ppermute | solution.py:29
  86.1 15.4 %collective-permute-start.13 = (bf16[256,768]{1,0:T(8,128)(2,1)S(1)}, bf16[256,768]{1,0:T(8,128)(2,1)S(1)}, u32[]{:S(2)}, u32[]{:S(2)}) collective-permute-start(bf16[256,768]{1,0:T(8,128)(2,1)S(1)} %get-tuple-element.17), channel_id=1, source_target_pairs={{0,4},{2,6},{4,0},{6,2},{1,5},{3,7},{5,1},{7,3},{8,12},{10,14},{12... | collective-permute-start | bytes 1179656 | tf_op jit(solution)/shard_map/ppermute | solution.py:29
  89.4 18.0 %collective-permute-start.12 = (bf16[256,768]{1,0:T(8,128)(2,1)S(1)}, bf16[256,768]{1,0:T(8,128)(2,1)S(1)}, u32[]{:S(2)}, u32[]{:S(2)}) collective-permute-start(bf16[256,768]{1,0:T(8,128)(2,1)S(1)} %get-tuple-element.16), channel_id=1, source_target_pairs={{0,2},{2,4},{4,6},{6,0},{1,3},{3,5},{5,7},{7,1},{8,10},{10,12},{12... | collective-permute-start | bytes 1179656 | tf_op jit(solution)/shard_map/ppermute | solution.py:29
  92.5 16.9 %collective-permute-start.11 = (bf16[256,768]{1,0:T(8,128)(2,1)S(1)}, bf16[256,768]{1,0:T(8,128)(2,1)S(1)}, u32[]{:S(2)}, u32[]{:S(2)}) collective-permute-start(bf16[256,768]{1,0:T(8,128)(2,1)S(1)} %get-tuple-element.15), channel_id=1, source_target_pairs={{0,6},{2,0},{4,2},{6,4},{1,7},{3,1},{5,3},{7,5},{8,14},{10,8},{12,... | collective-permute-start | bytes 1179656 | tf_op jit(solution)/shard_map/ppermute | solution.py:29
  110.3 38.4 %all-to-all-start.1 = ((bf16[16,16,768]{2,1,0:T(8,128)(2,1)}), bf16[16,16,768]{2,1,0:T(8,128)(2,1)S(1)}, u32[]{:S(2)}, u32[]{:S(2)}) async-start(bf16[16,16,768]{2,1,0:T(8,128)(2,1)} %bitcast.9), calls=%async_computation.1 | async-start | bytes 786432 | tf_op jit(solution)/shard_map/all_to_all | solution.py:154
  121.9 25.7 %copy-start.1 = (bf16[128,768]{1,0:T(8,128)(2,1)S(1)}, bf16[128,768]{1,0:T(8,128)(2,1)}, u32[]{:S(2)}) copy-start(bf16[128,768]{1,0:T(8,128)(2,1)} %param.5) | copy-start | bytes 589828
  123.3 25.5 %copy-start.2 = (bf16[16,768]{1,0:T(8,128)(2,1)S(1)}, bf16[16,768]{1,0:T(8,128)(2,1)}, u32[]{:S(2)}) copy-start(bf16[16,768]{1,0:T(8,128)(2,1)} %param.6) | copy-start | bytes 73732
  123.3 11.6 %collective-permute-start.8 = (bf16[128,768]{1,0:T(8,128)(2,1)S(1)}, bf16[128,768]{1,0:T(8,128)(2,1)S(1)}, u32[]{:S(2)}, u32[]{:S(2)}) collective-permute-start(bf16[128,768]{1,0:T(8,128)(2,1)S(1)} %get-tuple-element.20), channel_id=1, source_target_pairs={{0,24},{8,0},{16,8},{24,16},{1,25},{9,1},{17,9},{25,17},{2,26},{10... | collective-permute-start | bytes 589832 | tf_op jit(solution)/shard_map/ppermute | solution.py:29
  125.2 16.4 %collective-permute-start.10 = (bf16[128,768]{1,0:T(8,128)(2,1)S(1)}, bf16[128,768]{1,0:T(8,128)(2,1)S(1)}, u32[]{:S(2)}, u32[]{:S(2)}) collective-permute-start(bf16[128,768]{1,0:T(8,128)(2,1)S(1)} %get-tuple-element.21), channel_id=1, source_target_pairs={{0,8},{8,16},{16,24},{24,0},{1,9},{9,17},{17,25},{25,1},{2,10},{10... | collective-permute-start | bytes 589832 | tf_op jit(solution)/shard_map/ppermute | solution.py:29
  129.2 18.4 %collective-permute-start.9 = (bf16[128,768]{1,0:T(8,128)(2,1)S(1)}, bf16[128,768]{1,0:T(8,128)(2,1)S(1)}, u32[]{:S(2)}, u32[]{:S(2)}) collective-permute-start(bf16[128,768]{1,0:T(8,128)(2,1)S(1)} %get-tuple-element.22), channel_id=1, source_target_pairs={{0,16},{8,24},{16,0},{24,8},{1,17},{9,25},{17,1},{25,9},{2,18},{10... | collective-permute-start | bytes 589832 | tf_op jit(solution)/shard_map/ppermute | solution.py:29

commit v3 on v1

v3 whole, which is shorter than its diff:
```python
import math

import jax
import jax.numpy as jnp
from jax import lax
from jax.experimental import pallas as pl
from jax.experimental.pallas import tpu as pltpu
from jax.sharding import Mesh
from jax.sharding import PartitionSpec as P

AXES = ("z", "y", "x", "c")
SIZES = (8, 8, 4, 2)
LANES = 128
BLOCK = 256
VMEM = 40 * 1024 * 1024


def normalize(values):
    floats = values.astype(jnp.float32)
    inverse = lax.rsqrt(jnp.sum(floats * floats, axis=-1, keepdims=True) + 1e-06)
    return (floats * inverse, inverse)


def unit_backward(floats, inverse, grad):
    along = jnp.sum(floats * grad, axis=-1, keepdims=True)
    return ((grad - floats * along) * inverse).astype(jnp.bfloat16)


def image_rings():
    depth, length, width, cores = SIZES
    rings = []
    for z in range(depth):
        for x in range(width):
            for c in range(cores):
                ring = [((z * length + y) * width + x) * cores + c for y in range(length)]
                rings.append(ring if c == 0 else ring[::-1])
    return rings


def exchanged(array):
    return lax.ppermute(array, "c", [(0, 1), (1, 0)])


def spread(rows, axis):
    peers = lax.axis_size(axis)
    copies = jnp.broadcast_to(rows[None], (peers,) + rows.shape)
    return lax.all_to_all(copies, axis, split_axis=0, concat_axis=0, tiled=True).reshape(-1, rows.shape[1])


def summed(rows, axis):
    peers = lax.axis_size(axis)
    parts = rows.reshape(peers, -1, rows.shape[1])
    parts = lax.all_to_all(parts, axis, split_axis=0, concat_axis=0, tiled=True)
    return jnp.sum(parts.astype(jnp.float32), axis=0)


def weight_kernel(first_ref, scalars_ref, image_ref, own_ref, other_ref, weight_ref, grad_ref, pairs_ref):
    step = pl.program_id(0)
    width = image_ref.shape[1]
    count = own_ref.shape[0]
    halves = (own_ref, other_ref)

    @pl.when(step == 0)
    def _():
        for i, ref in enumerate(halves):
            digits = ref[:, width:].astype(jnp.float32).T
            pairs_ref[:, i * count : (i + 1) * count] = (digits[0:1] * 256.0 + digits[1:2]).astype(jnp.int32)

    scale = scalars_ref[0]
    slope = scalars_ref[1]
    shift = scalars_ref[2]
    images = image_ref[...]
    pieces = BLOCK // 128
    row = lax.broadcasted_iota(jnp.int32, (128, 1), 0)
    rows = jnp.concatenate([row + first_ref[step * pieces + p] for p in range(pieces)], axis=0)
    grad = None
    for i, ref in enumerate(halves):
        texts = ref[:, :width]
        dots = lax.dot_general(images, texts, (((1,), (1,)), ((), ())), preferred_element_type=jnp.float32)
        chance = 1.0 / (1.0 + jnp.exp2(dots * slope + shift))
        paired = pairs_ref[:, i * count : (i + 1) * count] == rows
        weight = (scale * jnp.where(paired, chance - 1.0, chance)).astype(jnp.bfloat16)
        weight_ref[:, i * count : (i + 1) * count] = weight
        term = jnp.dot(weight, texts, preferred_element_type=jnp.float32)
        grad = term if grad is None else grad + term
    grad_ref[...] = grad.astype(grad_ref.dtype)


def weights_and_image_terms(first, scalars, images, own, other):
    rows, width = images.shape
    count, wide = own.shape
    smem = pl.BlockSpec(memory_space=pltpu.SMEM)
    return pl.pallas_call(
        weight_kernel,
        grid=(rows // BLOCK,),
        in_specs=[
            smem,
            smem,
            pl.BlockSpec((BLOCK, width), lambda i: (i, 0)),
            pl.BlockSpec((count, wide), lambda i: (0, 0)),
            pl.BlockSpec((count, wide), lambda i: (0, 0)),
        ],
        out_specs=[
            pl.BlockSpec((BLOCK, 2 * count), lambda i: (i, 0)),
            pl.BlockSpec((BLOCK, width), lambda i: (i, 0)),
        ],
        out_shape=[
            jax.ShapeDtypeStruct((rows, 2 * count), jnp.bfloat16),
            jax.ShapeDtypeStruct((rows, width), jnp.bfloat16),
        ],
        scratch_shapes=[pltpu.VMEM((1, 2 * count), jnp.int32)],
        compiler_params=pltpu.CompilerParams(vmem_limit_bytes=VMEM),
        cost_estimate=pl.CostEstimate(
            flops=8 * rows * count * width,
            bytes_accessed=4 * rows * (width + count) + 4 * count * wide,
            transcendentals=4 * rows * count,
        ),
    )(first, scalars, images, own, other)


def text_kernel(weight_ref, image_ref, grad_ref, total_ref):
    step = pl.program_id(0)
    term = lax.dot_general(
        weight_ref[...], image_ref[...], (((0,), (0,)), ((), ())), preferred_element_type=jnp.float32
    )

    @pl.when(step == 0)
    def _():
        total_ref[...] = term

    @pl.when(step > 0)
    def _():
        total_ref[...] += term

    @pl.when(step == pl.num_programs(0) - 1)
    def _():
        grad_ref[...] = total_ref[...].astype(grad_ref.dtype)


def text_terms(weights, images, half, out_type):
    rows, width = images.shape
    count = weights.shape[1] // 2
    return pl.pallas_call(
        text_kernel,
        grid=(rows // BLOCK,),
        in_specs=[
            pl.BlockSpec((BLOCK, count), lambda i: (i, half)),
            pl.BlockSpec((BLOCK, width), lambda i: (i, 0)),
        ],
        out_specs=pl.BlockSpec((count, width), lambda i: (0, 0)),
        out_shape=jax.ShapeDtypeStruct((count, width), out_type),
        scratch_shapes=[pltpu.VMEM((count, width), jnp.float32)],
        compiler_params=pltpu.CompilerParams(vmem_limit_bytes=VMEM),
        cost_estimate=pl.CostEstimate(
            flops=2 * rows * count * width, bytes_accessed=2 * rows * (width + count) + 2 * count * width, transcendentals=0
        ),
    )(weights, images)


def on_device(image_embed, text_embed, log_scale, logit_bias, pair_index):
    own_images, width = image_embed.shape
    own_texts = text_embed.shape[0]
    rings = image_rings()
    image_float, image_inverse = normalize(image_embed)
    images = lax.all_gather(image_float.astype(jnp.bfloat16), AXES, axis=0, tiled=True, axis_index_groups=rings)

    text_float, text_inverse = normalize(text_embed)
    lane = lax.broadcasted_iota(jnp.int32, (own_texts, LANES), 1)
    digits = jnp.where(lane == 0, pair_index[:, None] // 256, jnp.where(lane == 1, pair_index[:, None] % 256, 0))
    packet = jnp.concatenate([text_float.astype(jnp.bfloat16), digits.astype(jnp.bfloat16)], axis=1)
    own = spread(spread(packet, "z"), "x")
    other = exchanged(own)

    scale = jnp.exp(log_scale)
    scalars = jnp.concatenate([scale, -math.log2(math.e) * scale, -math.log2(math.e) * logit_bias])
    z, x, c = lax.axis_index("z"), lax.axis_index("x"), lax.axis_index("c")
    place = jnp.arange(SIZES[1], dtype=jnp.int32)
    place = jnp.where(c == 0, place, SIZES[1] - 1 - place)
    first = (((z * SIZES[1] + place) * SIZES[2] + x) * SIZES[3] + c) * own_images

    weights, image_part = weights_and_image_terms(first.astype(jnp.int32), scalars, images, own, other)
    image_total = lax.psum_scatter(image_part, AXES, scatter_dimension=0, tiled=True, axis_index_groups=rings)

    other_part = exchanged(text_terms(weights, images, 1, jnp.bfloat16))
    text_part = text_terms(weights, images, 0, jnp.float32) + other_part.astype(jnp.float32)
    text_part = summed(text_part.astype(jnp.bfloat16), "x")
    text_total = summed(text_part.astype(jnp.bfloat16), "z")
    return (
        unit_backward(image_float, image_inverse, image_total.astype(jnp.float32)),
        unit_backward(text_float, text_inverse, text_total),
    )


def solution(mesh):
    split = Mesh(mesh.devices.reshape(SIZES), AXES)
    rows = P(AXES, None)
    return jax.shard_map(
        on_device,
        mesh=split,
        in_specs=(rows, rows, P(), P(), P(AXES)),
        out_specs=(rows, rows),
        check_vma=False,
    )
```

time: 147 us -> 121 us (0.82)
  waiting for transfers between devices: 84 us -> 4.9 us
  blocking collectives: 0 us -> 68.7 us
  starting transfers between devices: 24.4 us -> 3.91 us
  local copies, waits for them, and re-layouts: 2.91 us -> 6.16 us
  other arithmetic: 7.8 us -> 9.42 us
    all_to_all x2 -> x0, waiting for transfers between devices: 83.3 us -> none  [the longest x1 44.6 us: on_device(): lax.all_to_all(spread, TEXT_AXES, split_axis=0, concat_axis=0, tiled=True)]
    all_to_all x0 -> x4, blocking collectives: none -> 68.7 us  [the longest x2 35.8 us: spread(): lax.all_to_all(copies, axis, split_axis=0, concat_axis=0, tiled=True)]
    all_to_all x2 -> x0, starting transfers between devices: 24.3 us -> none  [the longest x1 16.7 us: on_device(): lax.all_to_all(spread, TEXT_AXES, split_axis=0, concat_axis=0, tiled=True)]
    unnamed x8 -> x14, local copies, waits for them, and re-layouts: 1.42 us -> 6.06 us
    all_gather x1, waiting for transfers between devices: 0.02 us -> 3.86 us  [on_device(): lax.all_gather(image_float.astype(jnp.bfloat16), AXES, axis=0, tiled=True...]
    ppermute x0 -> x2, starting transfers between devices: none -> 3.83 us  [exchanged(): return lax.ppermute(array, 'c', [(0, 1), (1, 0)])]
    pallas_call x1 -> x3, Pallas kernels: 9.4 us -> 10.6 us  [the longest x1 5.94 us: weights_and_image_terms(): pl.pallas_call(weight_kernel, grid=(rows // BLOCK,), in_specs=[smem, smem...]
  transfers between devices with their start and end apart: 4 -> 4, of which waited for: 2 -> 2; matrix products, arithmetic and copies ran while one was open for 2% -> 3% of each run, Pallas kernels for 0% -> 4%
where the time goes in v3:
time: 121 us; the launch traced here: 119 us
  blocking collectives  68.7 us (57%)
  between operations  15.5 us (13%)
  Pallas kernels  10.6 us (9%)
  other arithmetic  9.42 us (8%)
  local copies, waits for them, and re-layouts  6.16 us (5%)
  waiting for transfers between devices  4.9 us (4%)
  starting transfers between devices  3.91 us (3%)
    all_to_all x2, blocking collectives, spread(): lax.all_to_all(copies, axis, split_axis=0, concat_axis=0, tiled=True)  35.8 us
    all_to_all x2, blocking collectives, summed(): parts = lax.all_to_all(parts, axis, split_axis=0, concat_axis=0, tiled=True)  33 us
    unnamed x14, local copies, waits for them, and re-layouts  6.06 us
    pallas_call x1, Pallas kernels, weights_and_image_terms(): pl.pallas_call(weight_kernel, grid=(rows // BLOCK,), in_specs=[smem, smem...  5.94 us
    pallas_call x2, Pallas kernels, text_terms(): pl.pallas_call(text_kernel, grid=(rows // BLOCK,), in_specs=[pl.BlockSpec...  4.71 us
    all_gather x1, waiting for transfers between devices, on_device(): lax.all_gather(image_float.astype(jnp.bfloat16), AXES, axis=0, tiled=True...  3.86 us
    ppermute x2, starting transfers between devices, exchanged(): return lax.ppermute(array, 'c', [(0, 1), (1, 0)])  3.83 us
    convert_element_type x2, other arithmetic, unit_backward(): return ((grad - floats * along) * inverse).astype(jnp.bfloat16)  2.5 us
  transfers between devices with their start and end apart: 4, of which 2 were waited for; matrix products, arithmetic and copies ran while one was open for 3% of the time, Pallas kernels for 4%

profile of v3, /device:TPU:6, one launch (start us, length us, event | category | flops | bytes accessed | tf_op | source)
XLA Modules:
  0.0 119.3 jit_solution(1623375713394122645)
XLA Ops:
  7.2 0.0 all-gather.2.cloned.1.call-start
  7.2 1.0 fusion.2
  8.3 1.7 %fusion.1 = bf16[128,768]{1,0:T(8,128)(2,1)} fusion(bf16[128,768]{1,0:T(8,128)(2,1)} %param.5, f32[128]{0:T(128)S(1)} %add_rsqrt_fusion.1), kind=kLoop, calls=%fused_computation.6 | loop fusion | flops 294912 | bytes 393728 | tf_op jit(solution)/shard_map/convert_element_type | solution.py:165
  10.0 0.0 all-gather.2.cloned.1.call-update
  10.0 0.0 reduce-scatter.2.cloned.1.call-start
  10.1 0.9 fusion.13
  10.9 0.7 and_select_fusion.1
  11.6 0.1 select_convert_fusion
  11.7 0.8 fusion.8
  12.5 21.3 %all_to_all.20 = bf16[8,16,896]{2,1,0:T(8,128)(2,1)S(1)} all-to-all(bf16[8,16,896]{2,1,0:T(8,128)(2,1)S(1)} %broadcast_in_dim.26), channel_id=1, replica_groups=mesh['z'=8,'y'=8,'x'=4,'c'=2] {'z'}, dimensions={0} | all-to-all | bytes 458752 | tf_op jit(solution)/shard_map/all_to_all | solution.py:47
  33.8 0.1 broadcast_in_dim.41
  33.9 14.5 %all_to_all.21 = bf16[4,128,896]{2,1,0:T(8,128)(2,1)S(1)} all-to-all(bf16[4,128,896]{2,1,0:T(8,128)(2,1)S(1)} %broadcast_in_dim.41), channel_id=1, replica_groups=mesh['z'=8,'y'=8,'x'=4,'c'=2] {'x'}, dimensions={0} | all-to-all | bytes 1835008 | tf_op jit(solution)/shard_map/all_to_all | solution.py:47
  48.4 1.9 %collective-permute-start = (bf16[512,896]{1,0:T(8,128)(2,1)S(1)}, bf16[512,896]{1,0:T(8,128)(2,1)S(1)}, u32[]{:S(2)}, u32[]{:S(2)}) collective-permute-start(bf16[512,896]{1,0:T(8,128)(2,1)S(1)} %bitcast.4), channel_id=1, source_target_pairs={{0,1},{1,0},{2,3},{3,2},{4,5},{5,4},{6,7},{7,6},{8,9},{9,8},{10,11... | collective-permute-start | bytes 2752520 | tf_op jit(solution)/shard_map/ppermute | solution.py:41
  51.6 0.1 pad_maximum_fusion.1.scalars_ref
  51.7 1.0 collective-permute-done.other_ref
  52.7 0.0 copy-start.3
  52.7 0.9 copy-done.3
  53.7 3.9 %all-gather.2.cloned.1.call-done.image_ref = bf16[1024,768]{1,0:T(8,128)(2,1)} async-done(((bf16[128,768]{1,0:T(8,128)(2,1)}), bf16[1024,768]{1,0:T(8,128)(2,1)}) %all-gather.2.cloned.1.call-update) | async-done | bytes 1572880 | tf_op jit(solution)/shard_map/all_gather | solution.py:165
  57.5 0.0 copy-start
  57.5 1.4 %copy-done = bf16[1024,768]{1,0:T(8,128)(2,1)S(1)} copy-done((bf16[1024,768]{1,0:T(8,128)(2,1)S(1)}, bf16[1024,768]{1,0:T(8,128)(2,1)}, u32[]{:S(2)}) %copy-start) | copy-done | bytes 1572888
  58.9 0.0 copy-start.4
  58.9 1.2 copy-done.4
  60.1 5.9 %shard_map.68 = (bf16[1024,1024]{1,0:T(8,128)(2,1)S(1)}, bf16[1024,768]{1,0:T(8,128)(2,1)S(1)}) custom-call(s32[8]{0:T(128)S(1)} %add_multiply_fusion.first_ref, f32[3]{0:T(128)S(1)} %pad_maximum_fusion.1.scalars_ref, bf16[1024,768]{1,0:T(8,128)(2,1)S(1)} %copy-done, bf16[512,896]{1,0:T(8,128)(2,1)S(1)} %bitcast.5, bf16[512,896]{1,0:T(8,128)(2,1)S(1)} %copy-done.4), custom_call_target="tpu_custom_call" | custom-call | flops 3221225472 | bytes 7077888 | tf_op jit(solution)/shard_map/pallas_call | solution.py:93
  66.0 0.0 copy-start.2
  66.1 1.1 copy-done.2
  67.2 0.0 reduce-scatter.2.cloned.1.call-update
  67.2 0.0 copy-start.1
  67.2 1.4 %copy-done.1 = bf16[1024,768]{1,0:T(8,128)(2,1)S(1)} copy-done((bf16[1024,768]{1,0:T(8,128)(2,1)S(1)}, bf16[1024,768]{1,0:T(8,128)(2,1)}, u32[]{:S(2)}) %copy-start.1) | copy-done | bytes 1572888
  68.6 2.3 %shard_map.70 = bf16[512,768]{1,0:T(8,128)(2,1)S(1)} custom-call(bf16[1024,1024]{1,0:T(8,128)(2,1)S(1)} %get-tuple-element.5.weight_ref, bf16[1024,768]{1,0:T(8,128)(2,1)S(1)} %copy-done.1), custom_call_target="tpu_custom_call" | custom-call | flops 805306368 | bytes 3407872 | tf_op jit(solution)/shard_map/pallas_call | solution.py:143
  71.0 1.9 %collective-permute-start.1 = (bf16[512,768]{1,0:T(8,128)(2,1)S(1)}, bf16[512,768]{1,0:T(8,128)(2,1)S(1)}, u32[]{:S(2)}, u32[]{:S(2)}) collective-permute-start(bf16[512,768]{1,0:T(8,128)(2,1)S(1)} %shard_map.70), channel_id=1, source_target_pairs={{0,1},{1,0},{2,3},{3,2},{4,5},{5,4},{6,7},{7,6},{8,9},{9,8},{10,11... | collective-permute-start | bytes 2359304 | tf_op jit(solution)/shard_map/ppermute | solution.py:41
  72.9 2.4 %shard_map.69 = f32[512,768]{1,0:T(8,128)S(1)} custom-call(bf16[1024,1024]{1,0:T(8,128)(2,1)S(1)} %get-tuple-element.5.weight_ref, bf16[1024,768]{1,0:T(8,128)(2,1)S(1)} %copy-done.1), custom_call_target="tpu_custom_call" | custom-call | flops 805306368 | bytes 3407872 | tf_op jit(solution)/shard_map/pallas_call | solution.py:143
  75.3 0.0 collective-permute-done.1
  75.3 0.2 add_convert_fusion
  75.5 0.0 copy-start.6
  75.5 0.0 copy-start.5
  75.5 15.6 %all_to_all.22 = bf16[4,128,768]{2,1,0:T(8,128)(2,1)S(1)} all-to-all(bf16[4,128,768]{2,1,0:T(8,128)(2,1)S(1)} %bitcast.6), channel_id=1, replica_groups=mesh['z'=8,'y'=8,'x'=4,'c'=2] {'x'}, dimensions={0} | all-to-all | bytes 1572864 | tf_op jit(solution)/shard_map/all_to_all | solution.py:53
  91.1 0.1 reduce_sum.60
  91.2 17.4 %all_to_all.23 = bf16[8,16,768]{2,1,0:T(8,128)(2,1)S(1)} all-to-all(bf16[8,16,768]{2,1,0:T(8,128)(2,1)S(1)} %bitcast.8), channel_id=1, replica_groups=mesh['z'=8,'y'=8,'x'=4,'c'=2] {'z'}, dimensions={0} | all-to-all | bytes 393216 | tf_op jit(solution)/shard_map/all_to_all | solution.py:53
  108.6 0.0 copy-done.6
  108.6 0.2 fusion.9
  108.8 0.7 fusion.12
  109.5 0.0 reduce-scatter.2.cloned.1.call-done
  109.5 0.0 copy-done.5
  109.5 1.1 fusion.3
  110.6 1.8 %fusion.5 = bf16[128,768]{1,0:T(8,128)(2,1)} fusion(bf16[128,768]{1,0:T(8,128)(2,1)S(1)} %copy-done.5, bf16[128,768]{1,0:T(8,128)(2,1)} %reduce-scatter.2.cloned.1.call-done, f32[128]{0:T(128)S(1)} %fusion.3, f32[128]{0:T(128)S(1)} %add_rsqrt_fusion.1), kind=kLoop, calls=%fused_computation.10 | loop fusion | flops 688128 | bytes 590848 | tf_op jit(solution)/shard_map/convert_element_type | solution.py:26
  (7 shorter events, 0.1 us)
Async XLA Ops:
  7.2 50.4 %all-gather.2.cloned.1.call-start = ((), (), s32[]{:S(2)}) async-start(), calls=%async_computation.5 | async-start | bytes 1769472 | tf_op jit(solution)/shard_map/all_gather | solution.py:165
  10.0 99.5 %reduce-scatter.2.cloned.1.call-start = ((), (), s32[]{:S(2)}) async-start(), calls=%async_computation.6 | async-start | bytes 1769472 | tf_op jit(solution)/shard_map/reduce_scatter | solution.py:182
  48.4 4.4 %collective-permute-start = (bf16[512,896]{1,0:T(8,128)(2,1)S(1)}, bf16[512,896]{1,0:T(8,128)(2,1)S(1)}, u32[]{:S(2)}, u32[]{:S(2)}) collective-permute-start(bf16[512,896]{1,0:T(8,128)(2,1)S(1)} %bitcast.4), channel_id=1, source_target_pairs={{0,1},{1,0},{2,3},{3,2},{4,5},{5,4},{6,7},{7,6},{8,9},{9,8},{10,11... | collective-permute-start | bytes 2752520 | tf_op jit(solution)/shard_map/ppermute | solution.py:41
  52.7 0.9 copy-start.3
  57.5 1.4 %copy-start = (bf16[1024,768]{1,0:T(8,128)(2,1)S(1)}, bf16[1024,768]{1,0:T(8,128)(2,1)}, u32[]{:S(2)}) copy-start(bf16[1024,768]{1,0:T(8,128)(2,1)} %all-gather.2.cloned.1.call-done.image_ref) | copy-start | bytes 4718596
  58.9 1.2 copy-start.4
  66.0 1.1 copy-start.2
  67.2 1.4 %copy-start.1 = (bf16[1024,768]{1,0:T(8,128)(2,1)S(1)}, bf16[1024,768]{1,0:T(8,128)(2,1)}, u32[]{:S(2)}) copy-start(bf16[1024,768]{1,0:T(8,128)(2,1)} %all-gather.2.cloned.1.call-done.image_ref) | copy-start | bytes 4718596
  71.0 4.3 %collective-permute-start.1 = (bf16[512,768]{1,0:T(8,128)(2,1)S(1)}, bf16[512,768]{1,0:T(8,128)(2,1)S(1)}, u32[]{:S(2)}, u32[]{:S(2)}) collective-permute-start(bf16[512,768]{1,0:T(8,128)(2,1)S(1)} %shard_map.70), channel_id=1, source_target_pairs={{0,1},{1,0},{2,3},{3,2},{4,5},{5,4},{6,7},{7,6},{8,9},{9,8},{10,11... | collective-permute-start | bytes 2359304 | tf_op jit(solution)/shard_map/ppermute | solution.py:41
  75.5 33.1 %copy-start.6 = (bf16[16,768]{1,0:T(8,128)(2,1)S(1)}, bf16[16,768]{1,0:T(8,128)(2,1)}, u32[]{:S(2)}) copy-start(bf16[16,768]{1,0:T(8,128)(2,1)} %param.6) | copy-start | bytes 73732
  75.5 34.0 %copy-start.5 = (bf16[128,768]{1,0:T(8,128)(2,1)S(1)}, bf16[128,768]{1,0:T(8,128)(2,1)}, u32[]{:S(2)}) copy-start(bf16[128,768]{1,0:T(8,128)(2,1)} %param.5) | copy-start | bytes 589828
Sparse Core Ops, SparseCore 0:
  10.7 46.8 all-gather.1
  67.3 41.8 reduce-scatter.1

commit v4 on v1

v4 whole, which is shorter than its diff:
```python
import math

import jax
import jax.numpy as jnp
from jax import lax
from jax.experimental import pallas as pl
from jax.experimental.pallas import tpu as pltpu
from jax.sharding import Mesh
from jax.sharding import PartitionSpec as P

AXES = ("z", "yh", "ym", "yl", "x", "c")
SIZES = (8, 2, 2, 2, 4, 2)
FAR = ("z", "yh", "ym")
LANES = 128
BLOCK = 256
VMEM = 56 * 1024 * 1024
ROWS_BY_ROWS = (((1,), (1,)), ((), ()))
COLUMNS_BY_ROWS = (((0,), (0,)), ((), ()))

smem = pl.BlockSpec(memory_space=pltpu.SMEM)
vmem = pl.BlockSpec(memory_space=pltpu.VMEM)


def params():
    return pltpu.CompilerParams(vmem_limit_bytes=VMEM)


def shifted(array, axis, by):
    devices = lax.axis_size(axis)
    return lax.ppermute(array, axis, [(i, (i + by) % devices) for i in range(devices)])


def inverse_norm(floats):
    return lax.rsqrt(jnp.sum(floats * floats, axis=-1, keepdims=True) + 1e-06)


def image_unit_kernel(embed_ref, unit_ref):
    floats = embed_ref[...].astype(jnp.float32)
    unit_ref[...] = (floats * inverse_norm(floats)).astype(unit_ref.dtype)


def image_units(embed):
    return pl.pallas_call(
        image_unit_kernel,
        in_specs=[vmem],
        out_specs=vmem,
        out_shape=jax.ShapeDtypeStruct(embed.shape, jnp.bfloat16),
        compiler_params=params(),
    )(embed)


def packet_kernel(pair_ref, embed_ref, packet_ref):
    rows, width = embed_ref.shape
    floats = embed_ref[...].astype(jnp.float32)
    unit = (floats * inverse_norm(floats)).astype(packet_ref.dtype)
    row = lax.broadcasted_iota(jnp.int32, (rows, LANES), 0)
    lane = lax.broadcasted_iota(jnp.int32, (rows, LANES), 1)
    index = jnp.zeros((rows, LANES), jnp.int32)
    for i in range(rows):
        index = jnp.where(row == i, pair_ref[i], index)
    digits = jnp.where(lane == 0, index >> 8, jnp.where(lane == 1, index & 255, 0))
    digits = digits.astype(jnp.float32).astype(packet_ref.dtype)
    for peer in range(packet_ref.shape[0]):
        packet_ref[peer, :, :width] = unit
        packet_ref[peer, :, width:] = digits


def text_packets(pair_index, embed, peers):
    rows, width = embed.shape
    return pl.pallas_call(
        packet_kernel,
        in_specs=[smem, vmem],
        out_specs=vmem,
        out_shape=jax.ShapeDtypeStruct((peers, rows, width + LANES), jnp.bfloat16),
        compiler_params=params(),
    )(pair_index, embed)


def block_weights(first_ref, scalars_ref, images, texts, pairs):
    pieces = BLOCK // 128
    start = pl.program_id(0) * pieces
    row = lax.broadcasted_iota(jnp.int32, (128, 1), 0)
    rows = jnp.concatenate([row + first_ref[start + p] for p in range(pieces)], axis=0)
    dots = lax.dot_general(images, texts, ROWS_BY_ROWS, preferred_element_type=jnp.float32)
    chance = 1.0 / (1.0 + jnp.exp2(dots * scalars_ref[1] + scalars_ref[2]))
    return (scalars_ref[0] * jnp.where(pairs == rows, chance - 1.0, chance)).astype(jnp.bfloat16)


def weight_kernel(first_ref, scalars_ref, image_ref, packet_ref, weight_ref, *rest):
    pairs_ref = rest[-1]
    step = pl.program_id(0)
    width = image_ref.shape[1]

    @pl.when(step == 0)
    def _():
        digits = packet_ref[:, width:].astype(jnp.float32).T
        pairs_ref[...] = (digits[0:1] * 256.0 + digits[1:2]).astype(jnp.int32)

    images = image_ref[...]
    weight = block_weights(first_ref, scalars_ref, images, packet_ref[:, :width], pairs_ref[...])
    weight_ref[...] = weight
    if len(rest) > 1:
        grad_ref, total_ref = rest[:2]
        add_up(step, total_ref, lax.dot_general(weight, images, COLUMNS_BY_ROWS, preferred_element_type=jnp.float32))

        @pl.when(step == pl.num_programs(0) - 1)
        def _():
            grad_ref[...] = total_ref[...].astype(grad_ref.dtype)


def add_up(step, total_ref, term):
    @pl.when(step == 0)
    def _():
        total_ref[...] = term

    @pl.when(step > 0)
    def _():
        total_ref[...] += term


def pair_weights(first, scalars, images, packet, with_grad):
    rows, width = images.shape
    count, wide = packet.shape
    out_specs = [pl.BlockSpec((BLOCK, count), lambda i: (i, 0))]
    out_shape = [jax.ShapeDtypeStruct((rows, count), jnp.bfloat16)]
    scratch = [pltpu.VMEM((1, count), jnp.int32)]
    if with_grad:
        out_specs.append(pl.BlockSpec((count, width), lambda i: (0, 0)))
        out_shape.append(jax.ShapeDtypeStruct((count, width), jnp.bfloat16))
        scratch.insert(0, pltpu.VMEM((count, width), jnp.float32))
    return pl.pallas_call(
        weight_kernel,
        grid=(rows // BLOCK,),
        in_specs=[
            smem,
            smem,
            pl.BlockSpec((BLOCK, width), lambda i: (i, 0)),
            pl.BlockSpec((count, wide), lambda i: (0, 0)),
        ],
        out_specs=out_specs,
        out_shape=out_shape,
        scratch_shapes=scratch,
        compiler_params=params(),
        cost_estimate=pl.CostEstimate(
            flops=(4 if with_grad else 2) * rows * count * width,
            bytes_accessed=2 * rows * (width + count) + 2 * count * wide,
            transcendentals=2 * rows * count,
        ),
    )(first, scalars, images, packet)


def grad_kernel(own_weight_ref, other_weight_ref, image_ref, own_ref, other_ref, text_grad_ref, *rest):
    image_grad_refs, total_ref = rest[:-1], rest[-1]
    step = pl.program_id(0)
    width = image_ref.shape[1]
    weight = own_weight_ref[...]
    add_up(
        step, total_ref, lax.dot_general(weight, image_ref[...], COLUMNS_BY_ROWS, preferred_element_type=jnp.float32)
    )
    term = jnp.dot(weight, own_ref[:, :width], preferred_element_type=jnp.float32)
    term += jnp.dot(other_weight_ref[...], other_ref[:, :width], preferred_element_type=jnp.float32)
    for i, ref in enumerate(image_grad_refs):

        @pl.when(step == i)
        def _():
            ref[...] = term.astype(ref.dtype)

    @pl.when(step == pl.num_programs(0) - 1)
    def _():
        text_grad_ref[...] = total_ref[...]


def grad_terms(own_weight, other_weight, images, own, other):
    rows, width = images.shape
    count, wide = own.shape
    steps = rows // BLOCK
    rolling = pl.BlockSpec((BLOCK, count), lambda i: (i, 0))
    whole = pl.BlockSpec((count, wide), lambda i: (0, 0))
    return pl.pallas_call(
        grad_kernel,
        grid=(steps,),
        in_specs=[rolling, rolling, pl.BlockSpec((BLOCK, width), lambda i: (i, 0)), whole, whole],
        out_specs=[pl.BlockSpec((count, width), lambda i: (0, 0))]
        + [pl.BlockSpec((BLOCK, width), lambda i: (0, 0))] * steps,
        out_shape=[jax.ShapeDtypeStruct((count, width), jnp.float32)]
        + [jax.ShapeDtypeStruct((BLOCK, width), jnp.bfloat16)] * steps,
        scratch_shapes=[pltpu.VMEM((count, width), jnp.float32)],
        compiler_params=params(),
        cost_estimate=pl.CostEstimate(
            flops=6 * rows * count * width,
            bytes_accessed=4 * rows * (width + count) + 8 * count * wide,
            transcendentals=0,
        ),
    )(own_weight, other_weight, images, own, other)


def backward_kernel(embed_ref, *refs):
    floats = embed_ref[...].astype(jnp.float32)
    inverse = inverse_norm(floats)
    unit = floats * inverse
    parts_refs, out_ref = refs[:-1], refs[-1]
    grad = None
    for ref in parts_refs:
        parts = [ref[i] for i in range(ref.shape[0])] if len(ref.shape) == 3 else [ref[...]]
        for part in parts:
            part = part.astype(jnp.float32)
            grad = part if grad is None else grad + part
    along = jnp.sum(unit * grad, axis=-1, keepdims=True)
    out_ref[...] = ((grad - unit * along) * inverse).astype(out_ref.dtype)


def unit_backward(embed, *parts):
    return pl.pallas_call(
        backward_kernel,
        in_specs=[vmem] * (1 + len(parts)),
        out_specs=vmem,
        out_shape=jax.ShapeDtypeStruct(embed.shape, jnp.bfloat16),
        compiler_params=params(),
    )(embed, *parts)


def on_device(image_embed, text_embed, log_scale, logit_bias, pair_index):
    own_images, width = image_embed.shape
    own_texts = text_embed.shape[0]
    peers = lax.axis_size(FAR)
    ring = lax.axis_size("x")

    unit = image_units(image_embed)
    pair = jnp.concatenate([unit, shifted(unit, "yl", 1)], axis=0)
    packets = text_packets(pair_index, text_embed, peers)
    own = lax.all_to_all(packets, FAR, split_axis=0, concat_axis=0, tiled=True)
    own = own.reshape(peers * own_texts, width + LANES)
    other = shifted(own, "c", 1)
    images = jnp.concatenate([pair] + [shifted(pair, "x", s) for s in range(1, ring)], axis=0)

    scale = jnp.exp(log_scale)
    scalars = jnp.concatenate([scale, -math.log2(math.e) * scale, -math.log2(math.e) * logit_bias])
    far, yl, x, c = lax.axis_index(FAR), lax.axis_index("yl"), lax.axis_index("x"), lax.axis_index("c")
    first = jnp.stack(
        [
            (((far * 2 + place) * ring + (x - s) % ring) * 2 + c) * own_images
            for s in range(ring)
            for place in (yl, 1 - yl)
        ]
    ).astype(jnp.int32)

    (own_weight,) = pair_weights(first, scalars, images, own, False)
    other_weight, other_part = pair_weights(first, scalars, images, other, True)
    own_part, *image_parts = grad_terms(own_weight, other_weight, images, own, other)

    text_part = (own_part + shifted(other_part, "c", 1).astype(jnp.float32)).astype(jnp.bfloat16)
    text_parts = lax.all_to_all(
        text_part.reshape(peers, own_texts, width), FAR, split_axis=0, concat_axis=0, tiled=True
    )

    image_total = image_parts[0].astype(jnp.float32)
    for s in range(1, ring):
        image_total = image_total + shifted(image_parts[s], "x", -s).astype(jnp.float32)
    beside = shifted(image_total[own_images:].astype(jnp.bfloat16), "yl", 1)
    return (
        unit_backward(image_embed, image_total[:own_images], beside),
        unit_backward(text_embed, text_parts),
    )


def solution(mesh):
    split = Mesh(mesh.devices.reshape(SIZES), AXES)
    rows = P(AXES, None)
    return jax.shard_map(
        on_device,
        mesh=split,
        in_specs=(rows, rows, P(), P(), P(AXES)),
        out_specs=(rows, rows),
        check_vma=False,
    )
```

time: 147 us -> 152 us (1.034)
  the two profiles are of different devices: /device:TPU:6 before, /device:TPU:1 now
where the time goes in v4:
time: 152 us; the launch traced here: 151 us
  starting transfers between devices  54.5 us (36%)
  waiting for transfers between devices  54.4 us (36%)
  Pallas kernels  28.5 us (19%)
  local copies, waits for them, and re-layouts  7.23 us (5%)
  other arithmetic  4.2 us (3%)
  between operations  2.17 us (1%)
    ppermute x10, starting transfers between devices, shifted(): lax.ppermute(array, axis, [(i, (i + by) % devices) for i in range(devices)])  32.7 us
    ppermute x10, waiting for transfers between devices, shifted(): lax.ppermute(array, axis, [(i, (i + by) % devices) for i in range(devices)])  32 us
    all_to_all x1, waiting for transfers between devices, on_device(): own = lax.all_to_all(packets, FAR, split_axis=0, concat_axis=0, tiled=True)  22.4 us
    all_to_all x1, starting transfers between devices, on_device(): own = lax.all_to_all(packets, FAR, split_axis=0, concat_axis=0, tiled=True)  16.5 us
    pallas_call x2, Pallas kernels, pair_weights(): pl.pallas_call(weight_kernel, grid=(rows // BLOCK,), in_specs=[smem, smem...  11.6 us
    pallas_call x1, Pallas kernels, grad_terms(): pl.pallas_call(grad_kernel, grid=(steps,), in_specs=[rolling, rolling, pl...  9.35 us
    all_to_all x1, starting transfers between devices, on_device(): lax.all_to_all(text_part.reshape(peers, own_texts, width), FAR, split_axi...  5.33 us
    unnamed x20, local copies, waits for them, and re-layouts  4.72 us
  transfers between devices with their start and end apart: 12, of which 7 were waited for; matrix products, arithmetic and copies ran while one was open for 4% of the time, Pallas kernels for 12%

profile of v4, /device:TPU:1, one launch (start us, length us, event | category | flops | bytes accessed | tf_op | source)
XLA Modules:
  0.0 151.0 jit_solution(6565659245246499296)
XLA Ops:
  0.6 1.8 %shard_map.69 = bf16[32,16,896]{2,1,0:T(8,128)(2,1)} custom-call(s32[16]{0:T(128)} %pair_ref.1, bf16[16,768]{1,0:T(8,128)(2,1)} %embed_ref.7), custom_call_target="tpu_custom_call" | custom-call | tf_op jit(solution)/shard_map/pallas_call | solution.py:70
  2.5 16.5 %all-to-all-start = ((bf16[32,16,896]{2,1,0:T(8,128)(2,1)}), bf16[32,16,896]{2,1,0:T(8,128)(2,1)S(1)}, u32[]{:S(2)}, u32[]{:S(2)}) async-start(bf16[32,16,896]{2,1,0:T(8,128)(2,1)} %shard_map.69), calls=%async_computation | async-start | bytes 1835008 | tf_op jit(solution)/shard_map/all_to_all | solution.py:231
  19.0 1.7 %shard_map.68 = bf16[128,768]{1,0:T(8,128)(2,1)} custom-call(bf16[128,768]{1,0:T(8,128)(2,1)} %embed_ref.6), custom_call_target="tpu_custom_call" | custom-call | tf_op jit(solution)/shard_map/pallas_call | solution.py:43
  20.7 2.3 %collective-permute-start = (bf16[128,768]{1,0:T(8,128)(2,1)}, bf16[128,768]{1,0:T(8,128)(2,1)S(1)}, u32[]{:S(2)}, u32[]{:S(2)}) collective-permute-start(bf16[128,768]{1,0:T(8,128)(2,1)} %shard_map.68), channel_id=1, source_target_pairs={{0,8},{8,0},{1,9},{9,1},{2,10},{10,2},{3,11},{11,3},{4,12},{12,4},... | collective-permute-start | bytes 589832 | tf_op jit(solution)/shard_map/ppermute | solution.py:30
  23.0 22.4 %all-to-all-done = bf16[32,16,896]{2,1,0:T(8,128)(2,1)S(1)} async-done(((bf16[32,16,896]{2,1,0:T(8,128)(2,1)}), bf16[32,16,896]{2,1,0:T(8,128)(2,1)S(1)}, u32[]{:S(2)}, u32[]{:S(2)}) %all-to-all-start) | async-done | bytes 917536 | tf_op jit(solution)/shard_map/all_to_all | solution.py:231
  45.4 0.0 copy-start
  45.5 5.3 %collective-permute-start.4 = (bf16[512,896]{1,0:T(8,128)(2,1)S(1)}, bf16[512,896]{1,0:T(8,128)(2,1)}, u32[]{:S(2)}, u32[]{:S(2)}) collective-permute-start(bf16[512,896]{1,0:T(8,128)(2,1)S(1)} %bitcast.10), channel_id=1, source_target_pairs={{0,1},{1,0},{2,3},{3,2},{4,5},{5,4},{6,7},{7,6},{8,9},{9,8},{10,11... | collective-permute-start | bytes 2752520 | tf_op jit(solution)/shard_map/ppermute | solution.py:30
  50.7 0.0 collective-permute-done
  50.7 1.0 pad_maximum_fusion
  51.7 3.1 %collective-permute-start.1 = (bf16[256,768]{1,0:T(8,128)(2,1)S(1)}, bf16[256,768]{1,0:T(8,128)(2,1)}, u32[]{:S(2)}, u32[]{:S(2)}) collective-permute-start(bf16[256,768]{1,0:T(8,128)(2,1)S(1)} %pad_maximum_fusion), channel_id=1, source_target_pairs={{0,2},{2,4},{4,6},{6,0},{1,3},{3,5},{5,7},{7,1},{8,10},{10,12},{12... | collective-permute-start | bytes 1179656 | tf_op jit(solution)/shard_map/ppermute | solution.py:30
  54.8 4.4 %collective-permute-start.2 = (bf16[256,768]{1,0:T(8,128)(2,1)S(1)}, bf16[256,768]{1,0:T(8,128)(2,1)S(1)}, u32[]{:S(2)}, u32[]{:S(2)}) collective-permute-start(bf16[256,768]{1,0:T(8,128)(2,1)S(1)} %pad_maximum_fusion), channel_id=1, source_target_pairs={{0,4},{2,6},{4,0},{6,2},{1,5},{3,7},{5,1},{7,3},{8,12},{10,14},{12... | collective-permute-start | bytes 1179656 | tf_op jit(solution)/shard_map/ppermute | solution.py:30
  59.2 0.9 constant_dynamic-update-slice_fusion.4
  61.5 3.1 %collective-permute-start.3 = (bf16[256,768]{1,0:T(8,128)(2,1)S(1)}, bf16[256,768]{1,0:T(8,128)(2,1)}, u32[]{:S(2)}, u32[]{:S(2)}) collective-permute-start(bf16[256,768]{1,0:T(8,128)(2,1)S(1)} %pad_maximum_fusion), channel_id=1, source_target_pairs={{0,6},{2,0},{4,2},{6,4},{1,7},{3,1},{5,3},{7,5},{8,14},{10,8},{12,... | collective-permute-start | bytes 1179656 | tf_op jit(solution)/shard_map/ppermute | solution.py:30
  64.6 0.6 pad_maximum_fusion.1.scalars_ref
  65.2 0.7 stack.35.first_ref
  65.8 0.0 collective-permute-done.1
  65.9 1.0 constant_dynamic-update-slice_fusion.2
  66.9 8.1 %collective-permute-done.2 = bf16[256,768]{1,0:T(8,128)(2,1)S(1)} collective-permute-done((bf16[256,768]{1,0:T(8,128)(2,1)S(1)}, bf16[256,768]{1,0:T(8,128)(2,1)S(1)}, u32[]{:S(2)}, u32[]{:S(2)}) %collective-permute-start.2) | collective-permute-done | bytes 393248 | tf_op jit(solution)/shard_map/ppermute | solution.py:30
  75.0 0.0 copy-done
  75.0 1.3 collective-permute-done.3
  76.3 1.0 constant_dynamic-update-slice_fusion.image_ref
  77.3 0.0 copy-start.2
  77.3 0.0 collective-permute-done.4.packet_ref.other_ref
  77.3 1.1 copy-done.2
  78.5 6.7 %shard_map.71 = (bf16[1024,512]{1,0:T(8,128)(2,1)}, bf16[512,768]{1,0:T(8,128)(2,1)}) custom-call(s32[8]{0:T(128)} %stack.35.first_ref, f32[3]{0:T(128)} %pad_maximum_fusion.1.scalars_ref, bf16[1024,768]{1,0:T(8,128)(2,1)} %copy-done.2, bf16[512,896]{1,0:T(8,128)(2,1)} %collective-permute-done.4.packet_ref.other_ref), custom_call_target="tpu_custom_call" | custom-call | flops 1610612736 | bytes 3538944 | tf_op jit(solution)/shard_map/pallas_call | solution.py:131
  85.2 3.0 %collective-permute-start.9 = (bf16[512,768]{1,0:T(8,128)(2,1)}, bf16[512,768]{1,0:T(8,128)(2,1)S(1)}, u32[]{:S(2)}, u32[]{:S(2)}) collective-permute-start(bf16[512,768]{1,0:T(8,128)(2,1)} %get-tuple-element.15), channel_id=1, source_target_pairs={{0,1},{1,0},{2,3},{3,2},{4,5},{5,4},{6,7},{7,6},{8,9},{9,8},{10,11... | collective-permute-start | bytes 2359304 | tf_op jit(solution)/shard_map/ppermute | solution.py:30
  88.2 4.9 %shard_map.70.own_weight_ref = bf16[1024,512]{1,0:T(8,128)(2,1)} custom-call(s32[8]{0:T(128)} %stack.35.first_ref, f32[3]{0:T(128)} %pad_maximum_fusion.1.scalars_ref, bf16[1024,768]{1,0:T(8,128)(2,1)} %copy-done.2, bf16[512,896]{1,0:T(8,128)(2,1)} %bitcast.11), custom_call_target="tpu_custom_call" | custom-call | flops 805306368 | bytes 3538944 | tf_op jit(solution)/shard_map/pallas_call | solution.py:131
  93.1 9.3 %shard_map.72 = (f32[512,768]{1,0:T(8,128)}, bf16[256,768]{1,0:T(8,128)(2,1)}, bf16[256,768]{1,0:T(8,128)(2,1)}, bf16[256,768]{1,0:T(8,128)(2,1)}, bf16[256,768]{1,0:T(8,128)(2,1)}) custom-call(bf16[1024,512]{1,0:T(8,128)(2,1)} %shard_map.70.own_weight_ref, bf16[1024,512]{1,0:T(8,128)(2,1)} %get-tuple-element.9.other_weight_ref, ...), custom_call_target="tpu_custom_call" | custom-call | flops 2415919104 | bytes 8912896 | tf_op jit(solution)/shard_map/pallas_call | solution.py:179
  102.4 0.0 collective-permute-done.9
  102.4 2.4 %add_convert_fusion = bf16[512,768]{1,0:T(8,128)(2,1)} fusion(f32[512,768]{1,0:T(8,128)} %get-tuple-element.14, bf16[512,768]{1,0:T(8,128)(2,1)S(1)} %collective-permute-done.9), kind=kLoop, calls=%fused_computation | loop fusion | flops 1179648 | bytes 3145728 | tf_op jit(solution)/shard_map/convert_element_type | solution.py:251
  104.9 0.0 copy-start.7
  104.9 0.0 copy-start.6
  104.9 0.0 copy-start.5
  104.9 0.0 copy-start.3
  104.9 5.3 %all-to-all-start.1 = ((bf16[32,16,768]{2,1,0:T(8,128)(2,1)}), bf16[32,16,768]{2,1,0:T(8,128)(2,1)S(1)}, u32[]{:S(2)}, u32[]{:S(2)}) async-start(bf16[32,16,768]{2,1,0:T(8,128)(2,1)} %bitcast.9), calls=%async_computation.1 | async-start | bytes 1572864 | tf_op jit(solution)/shard_map/all_to_all | solution.py:252
  110.2 0.0 copy-done.7
  110.3 4.3 %collective-permute-start.5 = (bf16[256,768]{1,0:T(8,128)(2,1)S(1)}, bf16[256,768]{1,0:T(8,128)(2,1)S(1)}, u32[]{:S(2)}, u32[]{:S(2)}) collective-permute-start(bf16[256,768]{1,0:T(8,128)(2,1)S(1)} %copy-done.7), channel_id=1, source_target_pairs={{0,6},{2,0},{4,2},{6,4},{1,7},{3,1},{5,3},{7,5},{8,14},{10,8},{12,... | collective-permute-start | bytes 1179656 | tf_op jit(solution)/shard_map/ppermute | solution.py:30
  114.5 0.0 copy-done.6
  114.5 3.5 %collective-permute-start.6 = (bf16[256,768]{1,0:T(8,128)(2,1)S(1)}, bf16[256,768]{1,0:T(8,128)(2,1)S(1)}, u32[]{:S(2)}, u32[]{:S(2)}) collective-permute-start(bf16[256,768]{1,0:T(8,128)(2,1)S(1)} %copy-done.6), channel_id=1, source_target_pairs={{0,4},{2,6},{4,0},{6,2},{1,5},{3,7},{5,1},{7,3},{8,12},{10,14},{12... | collective-permute-start | bytes 1179656 | tf_op jit(solution)/shard_map/ppermute | solution.py:30
  118.0 0.0 copy-done.5
  118.0 1.9 %collective-permute-start.7 = (bf16[256,768]{1,0:T(8,128)(2,1)S(1)}, bf16[256,768]{1,0:T(8,128)(2,1)S(1)}, u32[]{:S(2)}, u32[]{:S(2)}) collective-permute-start(bf16[256,768]{1,0:T(8,128)(2,1)S(1)} %copy-done.5), channel_id=1, source_target_pairs={{0,2},{2,4},{4,6},{6,0},{1,3},{3,5},{5,7},{7,1},{8,10},{10,12},{12... | collective-permute-start | bytes 1179656 | tf_op jit(solution)/shard_map/ppermute | solution.py:30
  119.9 3.6 %collective-permute-done.5 = bf16[256,768]{1,0:T(8,128)(2,1)S(1)} collective-permute-done((bf16[256,768]{1,0:T(8,128)(2,1)S(1)}, bf16[256,768]{1,0:T(8,128)(2,1)S(1)}, u32[]{:S(2)}, u32[]{:S(2)}) %collective-permute-start.5) | collective-permute-done | bytes 393248 | tf_op jit(solution)/shard_map/ppermute | solution.py:30
  123.5 4.5 %collective-permute-done.6 = bf16[256,768]{1,0:T(8,128)(2,1)S(1)} collective-permute-done((bf16[256,768]{1,0:T(8,128)(2,1)S(1)}, bf16[256,768]{1,0:T(8,128)(2,1)S(1)}, u32[]{:S(2)}, u32[]{:S(2)}) %collective-permute-start.6) | collective-permute-done | bytes 393248 | tf_op jit(solution)/shard_map/ppermute | solution.py:30
  128.1 9.3 %collective-permute-done.7 = bf16[256,768]{1,0:T(8,128)(2,1)S(1)} collective-permute-done((bf16[256,768]{1,0:T(8,128)(2,1)S(1)}, bf16[256,768]{1,0:T(8,128)(2,1)S(1)}, u32[]{:S(2)}, u32[]{:S(2)}) %collective-permute-start.7) | collective-permute-done | bytes 393248 | tf_op jit(solution)/shard_map/ppermute | solution.py:30
  137.4 0.0 copy-done.3
  137.4 0.2 convert_add_fusion
  137.6 1.9 %collective-permute-start.8 = (bf16[128,768]{1,0:T(8,128)(2,1)S(1)}, bf16[128,768]{1,0:T(8,128)(2,1)S(1)}, u32[]{:S(2)}, u32[]{:S(2)}) collective-permute-start(bf16[128,768]{1,0:T(8,128)(2,1)S(1)} %slice.12), channel_id=1, source_target_pairs={{0,8},{8,0},{1,9},{9,1},{2,10},{10,2},{3,11},{11,3},{4,12},{12,4},... | collective-permute-start | bytes 589832 | tf_op jit(solution)/shard_map/ppermute | solution.py:30
  139.6 0.8 slice.9.refs_0_
  140.4 5.1 %collective-permute-done.8.refs_1_ = bf16[128,768]{1,0:T(8,128)(2,1)S(1)} collective-permute-done((bf16[128,768]{1,0:T(8,128)(2,1)S(1)}, bf16[128,768]{1,0:T(8,128)(2,1)S(1)}, u32[]{:S(2)}, u32[]{:S(2)}) %collective-permute-start.8) | collective-permute-done | bytes 196640 | tf_op jit(solution)/shard_map/ppermute | solution.py:30
  145.5 0.0 copy-start.4
  145.5 0.7 copy-done.4
  146.2 2.0 %shard_map.73 = bf16[128,768]{1,0:T(8,128)(2,1)} custom-call(bf16[128,768]{1,0:T(8,128)(2,1)} %embed_ref.6, f32[128,768]{1,0:T(8,128)} %slice.9.refs_0_, bf16[128,768]{1,0:T(8,128)(2,1)} %copy-done.4), custom_call_target="tpu_custom_call" | custom-call | tf_op jit(solution)/shard_map/pallas_call | solution.py:213
  148.2 0.0 all-to-all-done.1.refs_0_
  148.2 0.0 copy-start.1
  148.2 0.9 copy-done.1
  149.1 2.0 %shard_map.74 = bf16[16,768]{1,0:T(8,128)(2,1)} custom-call(bf16[16,768]{1,0:T(8,128)(2,1)} %embed_ref.7, bf16[32,16,768]{2,1,0:T(8,128)(2,1)} %copy-done.1), custom_call_target="tpu_custom_call" | custom-call | tf_op jit(solution)/shard_map/pallas_call | solution.py:213
  (3 shorter events, 0.1 us)
Async XLA Ops:
  2.5 43.0 %all-to-all-start = ((bf16[32,16,896]{2,1,0:T(8,128)(2,1)}), bf16[32,16,896]{2,1,0:T(8,128)(2,1)S(1)}, u32[]{:S(2)}, u32[]{:S(2)}) async-start(bf16[32,16,896]{2,1,0:T(8,128)(2,1)} %shard_map.69), calls=%async_computation | async-start | bytes 1835008 | tf_op jit(solution)/shard_map/all_to_all | solution.py:231
  20.7 30.0 %collective-permute-start = (bf16[128,768]{1,0:T(8,128)(2,1)}, bf16[128,768]{1,0:T(8,128)(2,1)S(1)}, u32[]{:S(2)}, u32[]{:S(2)}) collective-permute-start(bf16[128,768]{1,0:T(8,128)(2,1)} %shard_map.68), channel_id=1, source_target_pairs={{0,8},{8,0},{1,9},{9,1},{2,10},{10,2},{3,11},{11,3},{4,12},{12,4},... | collective-permute-start | bytes 589832 | tf_op jit(solution)/shard_map/ppermute | solution.py:30
  45.4 29.5 %copy-start = (bf16[32,16,896]{2,1,0:T(8,128)(2,1)}, bf16[32,16,896]{2,1,0:T(8,128)(2,1)S(1)}, u32[]{:S(2)}) copy-start(bf16[32,16,896]{2,1,0:T(8,128)(2,1)S(1)} %all-to-all-done) | copy-start | bytes 2752516
  45.5 31.9 %collective-permute-start.4 = (bf16[512,896]{1,0:T(8,128)(2,1)S(1)}, bf16[512,896]{1,0:T(8,128)(2,1)}, u32[]{:S(2)}, u32[]{:S(2)}) collective-permute-start(bf16[512,896]{1,0:T(8,128)(2,1)S(1)} %bitcast.10), channel_id=1, source_target_pairs={{0,1},{1,0},{2,3},{3,2},{4,5},{5,4},{6,7},{7,6},{8,9},{9,8},{10,11... | collective-permute-start | bytes 2752520 | tf_op jit(solution)/shard_map/ppermute | solution.py:30
  51.7 14.1 %collective-permute-start.1 = (bf16[256,768]{1,0:T(8,128)(2,1)S(1)}, bf16[256,768]{1,0:T(8,128)(2,1)}, u32[]{:S(2)}, u32[]{:S(2)}) collective-permute-start(bf16[256,768]{1,0:T(8,128)(2,1)S(1)} %pad_maximum_fusion), channel_id=1, source_target_pairs={{0,2},{2,4},{4,6},{6,0},{1,3},{3,5},{5,7},{7,1},{8,10},{10,12},{12... | collective-permute-start | bytes 1179656 | tf_op jit(solution)/shard_map/ppermute | solution.py:30
  54.8 20.1 %collective-permute-start.2 = (bf16[256,768]{1,0:T(8,128)(2,1)S(1)}, bf16[256,768]{1,0:T(8,128)(2,1)S(1)}, u32[]{:S(2)}, u32[]{:S(2)}) collective-permute-start(bf16[256,768]{1,0:T(8,128)(2,1)S(1)} %pad_maximum_fusion), channel_id=1, source_target_pairs={{0,4},{2,6},{4,0},{6,2},{1,5},{3,7},{5,1},{7,3},{8,12},{10,14},{12... | collective-permute-start | bytes 1179656 | tf_op jit(solution)/shard_map/ppermute | solution.py:30
  61.5 14.8 %collective-permute-start.3 = (bf16[256,768]{1,0:T(8,128)(2,1)S(1)}, bf16[256,768]{1,0:T(8,128)(2,1)}, u32[]{:S(2)}, u32[]{:S(2)}) collective-permute-start(bf16[256,768]{1,0:T(8,128)(2,1)S(1)} %pad_maximum_fusion), channel_id=1, source_target_pairs={{0,6},{2,0},{4,2},{6,4},{1,7},{3,1},{5,3},{7,5},{8,14},{10,8},{12,... | collective-permute-start | bytes 1179656 | tf_op jit(solution)/shard_map/ppermute | solution.py:30
  77.3 1.2 copy-start.2
  85.2 17.2 %collective-permute-start.9 = (bf16[512,768]{1,0:T(8,128)(2,1)}, bf16[512,768]{1,0:T(8,128)(2,1)S(1)}, u32[]{:S(2)}, u32[]{:S(2)}) collective-permute-start(bf16[512,768]{1,0:T(8,128)(2,1)} %get-tuple-element.15), channel_id=1, source_target_pairs={{0,1},{1,0},{2,3},{3,2},{4,5},{5,4},{6,7},{7,6},{8,9},{9,8},{10,11... | collective-permute-start | bytes 2359304 | tf_op jit(solution)/shard_map/ppermute | solution.py:30
  104.9 5.4 %copy-start.7 = (bf16[256,768]{1,0:T(8,128)(2,1)S(1)}, bf16[256,768]{1,0:T(8,128)(2,1)}, u32[]{:S(2)}) copy-start(bf16[256,768]{1,0:T(8,128)(2,1)} %get-tuple-element.11) | copy-start | bytes 1179652
  104.9 9.6 %copy-start.6 = (bf16[256,768]{1,0:T(8,128)(2,1)S(1)}, bf16[256,768]{1,0:T(8,128)(2,1)}, u32[]{:S(2)}) copy-start(bf16[256,768]{1,0:T(8,128)(2,1)} %get-tuple-element.12) | copy-start | bytes 1179652
  104.9 13.1 %copy-start.5 = (bf16[256,768]{1,0:T(8,128)(2,1)S(1)}, bf16[256,768]{1,0:T(8,128)(2,1)}, u32[]{:S(2)}) copy-start(bf16[256,768]{1,0:T(8,128)(2,1)} %get-tuple-element.13) | copy-start | bytes 1179652
  104.9 32.5 %copy-start.3 = (bf16[256,768]{1,0:T(8,128)(2,1)S(1)}, bf16[256,768]{1,0:T(8,128)(2,1)}, u32[]{:S(2)}) copy-start(bf16[256,768]{1,0:T(8,128)(2,1)} %get-tuple-element.10) | copy-start | bytes 1179652
  104.9 43.3 %all-to-all-start.1 = ((bf16[32,16,768]{2,1,0:T(8,128)(2,1)}), bf16[32,16,768]{2,1,0:T(8,128)(2,1)S(1)}, u32[]{:S(2)}, u32[]{:S(2)}) async-start(bf16[32,16,768]{2,1,0:T(8,128)(2,1)} %bitcast.9), calls=%async_computation.1 | async-start | bytes 1572864 | tf_op jit(solution)/shard_map/all_to_all | solution.py:252
  110.3 13.3 %collective-permute-start.5 = (bf16[256,768]{1,0:T(8,128)(2,1)S(1)}, bf16[256,768]{1,0:T(8,128)(2,1)S(1)}, u32[]{:S(2)}, u32[]{:S(2)}) collective-permute-start(bf16[256,768]{1,0:T(8,128)(2,1)S(1)} %copy-done.7), channel_id=1, source_target_pairs={{0,6},{2,0},{4,2},{6,4},{1,7},{3,1},{5,3},{7,5},{8,14},{10,8},{12,... | collective-permute-start | bytes 1179656 | tf_op jit(solution)/shard_map/ppermute | solution.py:30
  114.5 13.5 %collective-permute-start.6 = (bf16[256,768]{1,0:T(8,128)(2,1)S(1)}, bf16[256,768]{1,0:T(8,128)(2,1)S(1)}, u32[]{:S(2)}, u32[]{:S(2)}) collective-permute-start(bf16[256,768]{1,0:T(8,128)(2,1)S(1)} %copy-done.6), channel_id=1, source_target_pairs={{0,4},{2,6},{4,0},{6,2},{1,5},{3,7},{5,1},{7,3},{8,12},{10,14},{12... | collective-permute-start | bytes 1179656 | tf_op jit(solution)/shard_map/ppermute | solution.py:30
  118.0 19.4 %collective-permute-start.7 = (bf16[256,768]{1,0:T(8,128)(2,1)S(1)}, bf16[256,768]{1,0:T(8,128)(2,1)S(1)}, u32[]{:S(2)}, u32[]{:S(2)}) collective-permute-start(bf16[256,768]{1,0:T(8,128)(2,1)S(1)} %copy-done.5), channel_id=1, source_target_pairs={{0,2},{2,4},{4,6},{6,0},{1,3},{3,5},{5,7},{7,1},{8,10},{10,12},{12... | collective-permute-start | bytes 1179656 | tf_op jit(solution)/shard_map/ppermute | solution.py:30
  137.6 7.9 %collective-permute-start.8 = (bf16[128,768]{1,0:T(8,128)(2,1)S(1)}, bf16[128,768]{1,0:T(8,128)(2,1)S(1)}, u32[]{:S(2)}, u32[]{:S(2)}) collective-permute-start(bf16[128,768]{1,0:T(8,128)(2,1)S(1)} %slice.12), channel_id=1, source_target_pairs={{0,8},{8,0},{1,9},{9,1},{2,10},{10,2},{3,11},{11,3},{4,12},{12,4},... | collective-permute-start | bytes 589832 | tf_op jit(solution)/shard_map/ppermute | solution.py:30
  145.5 0.7 copy-start.4
  148.2 0.9 copy-start.1

commit v5 on v4

v5 whole, which is shorter than its diff:
```python
import math

import jax
import jax.numpy as jnp
from jax import lax
from jax.experimental import pallas as pl
from jax.experimental.pallas import tpu as pltpu
from jax.sharding import Mesh
from jax.sharding import PartitionSpec as P

AXES = ("z", "yh", "ym", "yl", "x", "c")
SIZES = (8, 2, 2, 2, 4, 2)
FAR = ("z", "yh", "ym")
MIDDLE = ("yh", "ym")
LANES = 128
VMEM = 56 * 1024 * 1024
ROWS_BY_ROWS = (((1,), (1,)), ((), ()))
COLUMNS_BY_ROWS = (((0,), (0,)), ((), ()))

smem = pl.BlockSpec(memory_space=pltpu.SMEM)
vmem = pl.BlockSpec(memory_space=pltpu.VMEM)


def params():
    return pltpu.CompilerParams(vmem_limit_bytes=VMEM)


def shifted(array, axis, by):
    devices = lax.axis_size(axis)
    return lax.ppermute(array, axis, [(i, (i + by) % devices) for i in range(devices)])


def inverse_norm(floats):
    return lax.rsqrt(jnp.sum(floats * floats, axis=-1, keepdims=True) + 1e-06)


def unit_kernel(pair_ref, image_ref, text_ref, unit_ref, packet_ref):
    floats = image_ref[...].astype(jnp.float32)
    unit_ref[...] = (floats * inverse_norm(floats)).astype(unit_ref.dtype)
    rows, width = text_ref.shape
    floats = text_ref[...].astype(jnp.float32)
    unit = (floats * inverse_norm(floats)).astype(packet_ref.dtype)
    row = lax.broadcasted_iota(jnp.int32, (rows, LANES), 0)
    lane = lax.broadcasted_iota(jnp.int32, (rows, LANES), 1)
    index = jnp.zeros((rows, LANES), jnp.int32)
    for i in range(rows):
        index = jnp.where(row == i, pair_ref[i], index)
    digits = jnp.where(lane == 0, index >> 8, jnp.where(lane == 1, index & 255, 0))
    digits = digits.astype(jnp.float32).astype(packet_ref.dtype)
    for peer in range(packet_ref.shape[0]):
        packet_ref[peer, :, :width] = unit
        packet_ref[peer, :, width:] = digits


def units_and_packets(pair_index, image_embed, text_embed, peers):
    rows, width = text_embed.shape
    return pl.pallas_call(
        unit_kernel,
        in_specs=[smem, vmem, vmem],
        out_specs=[vmem, vmem],
        out_shape=[
            jax.ShapeDtypeStruct(image_embed.shape, jnp.bfloat16),
            jax.ShapeDtypeStruct((peers, rows, width + LANES), jnp.bfloat16),
        ],
        compiler_params=params(),
    )(pair_index, image_embed, text_embed)


def pair_kernel(chunks, first_ref, scalars_ref, *refs):
    chunk_refs, packet_refs = refs[:chunks], refs[chunks : chunks + 2]
    text_grad_refs = refs[chunks + 2 : chunks + 4]
    image_grad_refs = refs[chunks + 4 : 2 * chunks + 4]
    image_ref, text_ref, sems = refs[2 * chunks + 4 :]
    block, width = chunk_refs[0].shape
    count = packet_refs[0].shape[0]
    copies = [
        pltpu.make_async_copy(ref, image_ref.at[pl.ds(i * block, block)], sems.at[i]) for i, ref in enumerate(chunk_refs)
    ]
    copies += [
        pltpu.make_async_copy(ref, text_ref.at[pl.ds(i * count, count)], sems.at[chunks + i])
        for i, ref in enumerate(packet_refs)
    ]
    for copy in copies:
        copy.start()
    for copy in copies:
        copy.wait()

    digits = text_ref[:, width:].astype(jnp.float32).T
    pairs = (digits[0:1] * 256.0 + digits[1:2]).astype(jnp.int32)
    row = lax.broadcasted_iota(jnp.int32, (128, 1), 0)
    rows = jnp.concatenate([row + first_ref[p] for p in range(chunks * block // 128)], axis=0)
    images = image_ref[...]
    texts = text_ref[:, :width]
    dots = lax.dot_general(images, texts, ROWS_BY_ROWS, preferred_element_type=jnp.float32)
    chance = 1.0 / (1.0 + jnp.exp2(dots * scalars_ref[1] + scalars_ref[2]))
    weight = (scalars_ref[0] * jnp.where(pairs == rows, chance - 1.0, chance)).astype(jnp.bfloat16)
    text_grad = lax.dot_general(weight, images, COLUMNS_BY_ROWS, preferred_element_type=jnp.float32)
    for i, ref in enumerate(text_grad_refs):
        ref[...] = text_grad[i * count : (i + 1) * count].astype(ref.dtype)
    image_grad = jnp.dot(weight, texts, preferred_element_type=jnp.float32)
    for i, ref in enumerate(image_grad_refs):
        ref[...] = image_grad[i * block : (i + 1) * block].astype(ref.dtype)


def pair_terms(first, scalars, chunks, packets):
    block, width = chunks[0].shape
    count, wide = packets[0].shape
    rows, texts = len(chunks) * block, 2 * count
    anywhere = pl.BlockSpec(memory_space=pl.ANY)
    return pl.pallas_call(
        lambda *refs: pair_kernel(len(chunks), *refs),
        in_specs=[smem, smem] + [anywhere] * (len(chunks) + 2),
        out_specs=[vmem] * (len(chunks) + 2),
        out_shape=[jax.ShapeDtypeStruct((count, width), jnp.bfloat16)] * 2
        + [jax.ShapeDtypeStruct((block, width), jnp.bfloat16)] * len(chunks),
        scratch_shapes=[
            pltpu.VMEM((rows, width), jnp.bfloat16),
            pltpu.VMEM((texts, wide), jnp.bfloat16),
            pltpu.SemaphoreType.DMA((len(chunks) + 2,)),
        ],
        compiler_params=params(),
        cost_estimate=pl.CostEstimate(
            flops=6 * rows * texts * width, bytes_accessed=4 * (rows + texts) * width, transcendentals=2 * rows * texts
        ),
    )(first, scalars, *chunks, *packets)


def backward_kernel(embed_ref, *refs):
    floats = embed_ref[...].astype(jnp.float32)
    inverse = inverse_norm(floats)
    unit = floats * inverse
    parts_refs, out_ref = refs[:-1], refs[-1]
    grad = None
    for ref in parts_refs:
        parts = [ref[i] for i in range(ref.shape[0])] if len(ref.shape) == 3 else [ref[...]]
        for part in parts:
            part = part.astype(jnp.float32)
            grad = part if grad is None else grad + part
    along = jnp.sum(unit * grad, axis=-1, keepdims=True)
    out_ref[...] = ((grad - unit * along) * inverse).astype(out_ref.dtype)


def unit_backward(embed, *parts):
    return pl.pallas_call(
        backward_kernel,
        in_specs=[vmem] * (1 + len(parts)),
        out_specs=vmem,
        out_shape=jax.ShapeDtypeStruct(embed.shape, jnp.bfloat16),
        compiler_params=params(),
    )(embed, *parts)


def spread(copies, axis):
    return lax.all_to_all(copies, axis, split_axis=0, concat_axis=0, tiled=True).reshape(-1, copies.shape[2])


def parted(rows, axis):
    parts = rows.reshape(lax.axis_size(axis), -1, rows.shape[1])
    return lax.all_to_all(parts, axis, split_axis=0, concat_axis=0, tiled=True)


def on_device(image_embed, text_embed, log_scale, logit_bias, pair_index):
    own_images = image_embed.shape[0]
    ring = lax.axis_size("x")
    together = lax.optimization_barrier

    unit, packets = units_and_packets(pair_index, image_embed, text_embed, lax.axis_size("z"))
    texts, beside = together((spread(packets, "z"), shifted(unit, "yl", 1)))
    pair = jnp.concatenate([unit, beside], axis=0)
    copies = jnp.broadcast_to(texts[None], (lax.axis_size(MIDDLE),) + texts.shape)
    copies, pair = together((copies, pair))
    own, *chunks = together((spread(copies, MIDDLE), *[shifted(pair, "x", s) for s in range(1, ring)]))
    other = shifted(own, "c", 1)

    scale = jnp.exp(log_scale)
    scalars = jnp.concatenate([scale, -math.log2(math.e) * scale, -math.log2(math.e) * logit_bias])
    far, yl, x, c = lax.axis_index(FAR), lax.axis_index("yl"), lax.axis_index("x"), lax.axis_index("c")
    first = jnp.stack(
        [
            (((far * 2 + place) * ring + (x - s) % ring) * 2 + c) * own_images
            for s in range(ring)
            for place in (yl, 1 - yl)
        ]
    ).astype(jnp.int32)
    own_part, other_part, *image_parts = pair_terms(first, scalars, [pair] + chunks, [own, other])

    text_part = own_part.astype(jnp.float32) + shifted(other_part, "c", 1).astype(jnp.float32)
    text_parts, *returned = together(
        (parted(text_part.astype(jnp.bfloat16), MIDDLE), *[shifted(image_parts[s], "x", -s) for s in range(1, ring)])
    )
    text_part = jnp.sum(text_parts.astype(jnp.float32), axis=0).astype(jnp.bfloat16)
    image_total = image_parts[0].astype(jnp.float32) + sum(part.astype(jnp.float32) for part in returned)
    image_own, image_beside = image_total[:own_images], image_total[own_images:].astype(jnp.bfloat16)
    text_part, image_beside = together((text_part, image_beside))
    text_parts, beside = together((parted(text_part, "z"), shifted(image_beside, "yl", 1)))
    return (
        unit_backward(image_embed, image_own, beside),
        unit_backward(text_embed, text_parts),
    )


def solution(mesh):
    split = Mesh(mesh.devices.reshape(SIZES), AXES)
    rows = P(AXES, None)
    return jax.shard_map(
        on_device,
        mesh=split,
        in_specs=(rows, rows, P(), P(), P(AXES)),
        out_specs=(rows, rows),
        check_vma=False,
    )
```

time: 152 us -> 133 us (0.88)
  the two profiles are of different devices: /device:TPU:1 before, /device:TPU:16 now
where the time goes in v5:
time: 133 us; the launch traced here: 132 us
  starting transfers between devices  58 us (44%)
  waiting for transfers between devices  48.6 us (37%)
  Pallas kernels  14.7 us (11%)
  other arithmetic  4.76 us (4%)
  local copies, waits for them, and re-layouts  4.14 us (3%)
  between operations  2.23 us (2%)
    ppermute x10, waiting for transfers between devices, shifted(): lax.ppermute(array, axis, [(i, (i + by) % devices) for i in range(devices)])  43.6 us
    ppermute x10, starting transfers between devices, shifted(): lax.ppermute(array, axis, [(i, (i + by) % devices) for i in range(devices)])  28.5 us
    all_to_all x2, starting transfers between devices, spread(): lax.all_to_all(copies, axis, split_axis=0, concat_axis=0, tiled=True)  17.7 us
    all_to_all x2, starting transfers between devices, parted(): return lax.all_to_all(parts, axis, split_axis=0, concat_axis=0, tiled=True)  11.8 us
    pallas_call x1, Pallas kernels, pair_terms(): pl.pallas_call(lambda *refs: pair_kernel(len(chunks), *refs), in_specs=[s...  9.13 us
    pallas_call x2, Pallas kernels, unit_backward(): pl.pallas_call(backward_kernel, in_specs=[vmem] * (1 + len(parts)), out_s...  3.77 us
    all_to_all x2, waiting for transfers between devices, spread(): lax.all_to_all(copies, axis, split_axis=0, concat_axis=0, tiled=True)  2.72 us
  transfers between devices with their start and end apart: 14, of which 11 were waited for; matrix products, arithmetic and copies ran while one was open for 2% of the time, Pallas kernels for 0%

profile of v5, /device:TPU:16, one launch (start us, length us, event | category | flops | bytes accessed | tf_op | source)
XLA Modules:
  0.0 132.4 jit_solution(8567728512212066938)
XLA Ops:
  0.6 1.8 %shard_map.68 = (bf16[128,768]{1,0:T(8,128)(2,1)}, bf16[8,16,896]{2,1,0:T(8,128)(2,1)}) custom-call(s32[16]{0:T(128)} %pair_ref.1, bf16[128,768]{1,0:T(8,128)(2,1)} %embed_ref.2, bf16[16,768]{1,0:T(8,128)(2,1)} %embed_ref.3), custom_call_target="tpu_custom_call" | custom-call | tf_op jit(solution)/shard_map/pallas_call | solution.py:57
  2.5 10.3 %all-to-all-start = ((bf16[8,16,896]{2,1,0:T(8,128)(2,1)}), bf16[8,16,896]{2,1,0:T(8,128)(2,1)S(1)}, u32[]{:S(2)}, u32[]{:S(2)}) async-start(bf16[8,16,896]{2,1,0:T(8,128)(2,1)} %get-tuple-element.26), calls=%async_computation | async-start | bytes 458752 | tf_op jit(solution)/shard_map/all_to_all | solution.py:154
  12.8 3.5 %collective-permute-start = (bf16[128,768]{1,0:T(8,128)(2,1)}, bf16[128,768]{1,0:T(8,128)(2,1)S(1)}, u32[]{:S(2)}, u32[]{:S(2)}) collective-permute-start(bf16[128,768]{1,0:T(8,128)(2,1)} %get-tuple-element.27), channel_id=1, source_target_pairs={{0,8},{8,0},{1,9},{9,1},{2,10},{10,2},{3,11},{11,3},{4,12},{12,4},... | collective-permute-start | bytes 589832 | tf_op jit(solution)/shard_map/ppermute | solution.py:30
  16.3 5.0 %collective-permute-done = bf16[128,768]{1,0:T(8,128)(2,1)S(1)} collective-permute-done((bf16[128,768]{1,0:T(8,128)(2,1)}, bf16[128,768]{1,0:T(8,128)(2,1)S(1)}, u32[]{:S(2)}, u32[]{:S(2)}) %collective-permute-start) | collective-permute-done | bytes 196640 | tf_op jit(solution)/shard_map/ppermute | solution.py:30
  21.2 2.7 %all-to-all-done = bf16[8,16,896]{2,1,0:T(8,128)(2,1)S(1)} async-done(((bf16[8,16,896]{2,1,0:T(8,128)(2,1)}), bf16[8,16,896]{2,1,0:T(8,128)(2,1)S(1)}, u32[]{:S(2)}, u32[]{:S(2)}) %all-to-all-start) | async-done | bytes 229408 | tf_op jit(solution)/shard_map/all_to_all | solution.py:154
  23.9 1.0 pad_maximum_fusion.refs_2_
  24.9 0.0 copy-start.3
  24.9 1.1 broadcast_in_dim.2
  26.0 7.4 %all-to-all-start.1 = ((bf16[4,128,896]{2,1,0:T(8,128)(2,1)}), bf16[4,128,896]{2,1,0:T(8,128)(2,1)S(1)}, u32[]{:S(2)}, u32[]{:S(2)}) async-start(bf16[4,128,896]{2,1,0:T(8,128)(2,1)} %broadcast_in_dim.2), calls=%async_computation.1 | async-start | bytes 1835008 | tf_op jit(solution)/shard_map/all_to_all | solution.py:154
  33.4 4.7 %collective-permute-start.3 = (bf16[256,768]{1,0:T(8,128)(2,1)S(1)}, bf16[256,768]{1,0:T(8,128)(2,1)S(1)}, u32[]{:S(2)}, u32[]{:S(2)}) collective-permute-start(bf16[256,768]{1,0:T(8,128)(2,1)S(1)} %pad_maximum_fusion.refs_2_), channel_id=1, source_target_pairs={{0,6},{2,0},{4,2},{6,4},{1,7},{3,1},{5,3},{7,5},{8,14},{10,8},{12,... | collective-permute-start | bytes 1179656 | tf_op jit(solution)/shard_map/ppermute | solution.py:30
  38.1 2.7 %collective-permute-start.2 = (bf16[256,768]{1,0:T(8,128)(2,1)S(1)}, bf16[256,768]{1,0:T(8,128)(2,1)S(1)}, u32[]{:S(2)}, u32[]{:S(2)}) collective-permute-start(bf16[256,768]{1,0:T(8,128)(2,1)S(1)} %pad_maximum_fusion.refs_2_), channel_id=1, source_target_pairs={{0,4},{2,6},{4,0},{6,2},{1,5},{3,7},{5,1},{7,3},{8,12},{10,14},{12... | collective-permute-start | bytes 1179656 | tf_op jit(solution)/shard_map/ppermute | solution.py:30
  40.8 0.0 copy-done.3
  40.8 2.8 %collective-permute-start.1 = (bf16[256,768]{1,0:T(8,128)(2,1)S(1)}, bf16[256,768]{1,0:T(8,128)(2,1)S(1)}, u32[]{:S(2)}, u32[]{:S(2)}) collective-permute-start(bf16[256,768]{1,0:T(8,128)(2,1)S(1)} %pad_maximum_fusion.refs_2_), channel_id=1, source_target_pairs={{0,2},{2,4},{4,6},{6,0},{1,3},{3,5},{5,7},{7,1},{8,10},{10,12},{12... | collective-permute-start | bytes 1179656 | tf_op jit(solution)/shard_map/ppermute | solution.py:30
  43.6 9.0 %collective-permute-done.3.refs_5_ = bf16[256,768]{1,0:T(8,128)(2,1)S(1)} collective-permute-done((bf16[256,768]{1,0:T(8,128)(2,1)S(1)}, bf16[256,768]{1,0:T(8,128)(2,1)S(1)}, u32[]{:S(2)}, u32[]{:S(2)}) %collective-permute-start.3) | collective-permute-done | bytes 393248 | tf_op jit(solution)/shard_map/ppermute | solution.py:30
  52.6 0.0 copy-start.6
  52.6 0.9 collective-permute-done.2.refs_4_
  53.6 0.0 copy-start.7
  53.6 4.6 %collective-permute-done.1.refs_3_ = bf16[256,768]{1,0:T(8,128)(2,1)S(1)} collective-permute-done((bf16[256,768]{1,0:T(8,128)(2,1)S(1)}, bf16[256,768]{1,0:T(8,128)(2,1)S(1)}, u32[]{:S(2)}, u32[]{:S(2)}) %collective-permute-start.1) | collective-permute-done | bytes 393248 | tf_op jit(solution)/shard_map/ppermute | solution.py:30
  58.2 0.0 copy-start.8
  58.2 0.0 all-to-all-done.1
  58.2 0.0 copy-start
  58.2 1.9 %collective-permute-start.4 = (bf16[512,896]{1,0:T(8,128)(2,1)S(1)}, bf16[512,896]{1,0:T(8,128)(2,1)S(1)}, u32[]{:S(2)}, u32[]{:S(2)}) collective-permute-start(bf16[512,896]{1,0:T(8,128)(2,1)S(1)} %bitcast.12), channel_id=1, source_target_pairs={{0,1},{1,0},{2,3},{3,2},{4,5},{5,4},{6,7},{7,6},{8,9},{9,8},{10,11... | collective-permute-start | bytes 2752520 | tf_op jit(solution)/shard_map/ppermute | solution.py:30
  61.6 0.6 stack.35.refs_0_
  62.2 0.6 pad_maximum_fusion.1.refs_1_
  62.8 0.0 collective-permute-done.4.refs_7_
  62.8 0.0 copy-done.6
  62.8 0.0 copy-done.7
  62.8 0.0 copy-done.8
  62.8 0.0 copy-done
  62.8 0.0 copy-start.5
  62.8 0.9 copy-done.5
  63.7 9.1 %shard_map.69 = (bf16[512,768]{1,0:T(8,128)(2,1)}, bf16[512,768]{1,0:T(8,128)(2,1)}, bf16[256,768]{1,0:T(8,128)(2,1)}, bf16[256,768]{1,0:T(8,128)(2,1)}, bf16[25...) custom-call(s32[8]{0:T(128)} %stack.35.refs_0_, f32[3]{0:T(128)} %pad_maximum_fusion.1.refs_1_, bf16[256,768]{1,0:T(8,128)(2,1)} %copy-done.3, ...), custom_call_target="tpu_custom_call" | custom-call | flops 4831838208 | bytes 6291456 | tf_op jit(solution)/shard_map/pallas_call | solution.py:110
  72.9 2.4 %collective-permute-start.5 = (bf16[512,768]{1,0:T(8,128)(2,1)}, bf16[512,768]{1,0:T(8,128)(2,1)S(1)}, u32[]{:S(2)}, u32[]{:S(2)}) collective-permute-start(bf16[512,768]{1,0:T(8,128)(2,1)} %get-tuple-element.38), channel_id=1, source_target_pairs={{0,1},{1,0},{2,3},{3,2},{4,5},{5,4},{6,7},{7,6},{8,9},{9,8},{10,11... | collective-permute-start | bytes 2359304 | tf_op jit(solution)/shard_map/ppermute | solution.py:30
  75.3 2.1 %collective-permute-done.5 = bf16[512,768]{1,0:T(8,128)(2,1)S(1)} collective-permute-done((bf16[512,768]{1,0:T(8,128)(2,1)}, bf16[512,768]{1,0:T(8,128)(2,1)S(1)}, u32[]{:S(2)}, u32[]{:S(2)}) %collective-permute-start.5) | collective-permute-done | bytes 786464 | tf_op jit(solution)/shard_map/ppermute | solution.py:30
  77.4 2.2 %add_convert_fusion = bf16[512,768]{1,0:T(8,128)(2,1)} fusion(bf16[512,768]{1,0:T(8,128)(2,1)S(1)} %collective-permute-done.5, bf16[512,768]{1,0:T(8,128)(2,1)} %get-tuple-element.37), kind=kLoop, calls=%fused_computation | loop fusion | flops 1572864 | bytes 2359296 | tf_op jit(solution)/shard_map/convert_element_type | solution.py:189
  79.6 0.0 copy-start.10
  79.6 0.0 copy-start.9
  79.6 0.0 copy-start.2
  79.6 7.3 %all-to-all-start.2 = ((bf16[4,128,768]{2,1,0:T(8,128)(2,1)}), bf16[4,128,768]{2,1,0:T(8,128)(2,1)S(1)}, u32[]{:S(2)}, u32[]{:S(2)}) async-start(bf16[4,128,768]{2,1,0:T(8,128)(2,1)} %bitcast.10), calls=%async_computation.2 | async-start | bytes 1572864 | tf_op jit(solution)/shard_map/all_to_all | solution.py:159
  87.0 2.5 %collective-permute-start.6 = (bf16[256,768]{1,0:T(8,128)(2,1)}, bf16[256,768]{1,0:T(8,128)(2,1)S(1)}, u32[]{:S(2)}, u32[]{:S(2)}) collective-permute-start(bf16[256,768]{1,0:T(8,128)(2,1)} %get-tuple-element.39), channel_id=1, source_target_pairs={{0,6},{2,0},{4,2},{6,4},{1,7},{3,1},{5,3},{7,5},{8,14},{10,8},{12,... | collective-permute-start | bytes 1179656 | tf_op jit(solution)/shard_map/ppermute | solution.py:30
  89.5 0.0 copy-done.10
  89.5 2.7 %collective-permute-start.7 = (bf16[256,768]{1,0:T(8,128)(2,1)S(1)}, bf16[256,768]{1,0:T(8,128)(2,1)S(1)}, u32[]{:S(2)}, u32[]{:S(2)}) collective-permute-start(bf16[256,768]{1,0:T(8,128)(2,1)S(1)} %copy-done.10), channel_id=1, source_target_pairs={{0,4},{2,6},{4,0},{6,2},{1,5},{3,7},{5,1},{7,3},{8,12},{10,14},{12... | collective-permute-start | bytes 1179656 | tf_op jit(solution)/shard_map/ppermute | solution.py:30
  92.2 0.0 copy-done.9
  92.2 2.7 %collective-permute-start.8 = (bf16[256,768]{1,0:T(8,128)(2,1)S(1)}, bf16[256,768]{1,0:T(8,128)(2,1)S(1)}, u32[]{:S(2)}, u32[]{:S(2)}) collective-permute-start(bf16[256,768]{1,0:T(8,128)(2,1)S(1)} %copy-done.9), channel_id=1, source_target_pairs={{0,2},{2,4},{4,6},{6,0},{1,3},{3,5},{5,7},{7,1},{8,10},{10,12},{12... | collective-permute-start | bytes 1179656 | tf_op jit(solution)/shard_map/ppermute | solution.py:30
  94.9 6.1 %collective-permute-done.6 = bf16[256,768]{1,0:T(8,128)(2,1)S(1)} collective-permute-done((bf16[256,768]{1,0:T(8,128)(2,1)}, bf16[256,768]{1,0:T(8,128)(2,1)S(1)}, u32[]{:S(2)}, u32[]{:S(2)}) %collective-permute-start.6) | collective-permute-done | bytes 393248 | tf_op jit(solution)/shard_map/ppermute | solution.py:30
  101.1 3.9 %collective-permute-done.7 = bf16[256,768]{1,0:T(8,128)(2,1)S(1)} collective-permute-done((bf16[256,768]{1,0:T(8,128)(2,1)S(1)}, bf16[256,768]{1,0:T(8,128)(2,1)S(1)}, u32[]{:S(2)}, u32[]{:S(2)}) %collective-permute-start.7) | collective-permute-done | bytes 393248 | tf_op jit(solution)/shard_map/ppermute | solution.py:30
  105.0 6.9 %collective-permute-done.8 = bf16[256,768]{1,0:T(8,128)(2,1)S(1)} collective-permute-done((bf16[256,768]{1,0:T(8,128)(2,1)S(1)}, bf16[256,768]{1,0:T(8,128)(2,1)S(1)}, u32[]{:S(2)}, u32[]{:S(2)}) %collective-permute-start.8) | collective-permute-done | bytes 393248 | tf_op jit(solution)/shard_map/ppermute | solution.py:30
  111.8 0.0 all-to-all-done.2
  111.8 0.0 copy-done.2
  111.8 0.2 add_add_fusion
  112.1 0.8 reduce_sum.12
  112.9 4.4 %all-to-all-start.3 = ((bf16[8,16,768]{2,1,0:T(8,128)(2,1)}), bf16[8,16,768]{2,1,0:T(8,128)(2,1)S(1)}, u32[]{:S(2)}, u32[]{:S(2)}) async-start(bf16[8,16,768]{2,1,0:T(8,128)(2,1)} %bitcast.11), calls=%async_computation.3 | async-start | bytes 393216 | tf_op jit(solution)/shard_map/all_to_all | solution.py:159
  117.3 2.6 %collective-permute-start.9 = (bf16[128,768]{1,0:T(8,128)(2,1)S(1)}, bf16[128,768]{1,0:T(8,128)(2,1)S(1)}, u32[]{:S(2)}, u32[]{:S(2)}) collective-permute-start(bf16[128,768]{1,0:T(8,128)(2,1)S(1)} %slice.12), channel_id=1, source_target_pairs={{0,8},{8,0},{1,9},{9,1},{2,10},{10,2},{3,11},{11,3},{4,12},{12,4},... | collective-permute-start | bytes 589832 | tf_op jit(solution)/shard_map/ppermute | solution.py:30
  119.9 0.8 slice.9.refs_0_
  120.7 5.1 %collective-permute-done.9.refs_1_ = bf16[128,768]{1,0:T(8,128)(2,1)S(1)} collective-permute-done((bf16[128,768]{1,0:T(8,128)(2,1)S(1)}, bf16[128,768]{1,0:T(8,128)(2,1)S(1)}, u32[]{:S(2)}, u32[]{:S(2)}) %collective-permute-start.9) | collective-permute-done | bytes 196640 | tf_op jit(solution)/shard_map/ppermute | solution.py:30
  125.7 0.0 copy-start.4
  125.7 2.2 %all-to-all-done.3.refs_0_ = bf16[8,16,768]{2,1,0:T(8,128)(2,1)S(1)} async-done(((bf16[8,16,768]{2,1,0:T(8,128)(2,1)}), bf16[8,16,768]{2,1,0:T(8,128)(2,1)S(1)}, u32[]{:S(2)}, u32[]{:S(2)}) %all-to-all-start.3) | async-done | bytes 196640 | tf_op jit(solution)/shard_map/all_to_all | solution.py:159
  128.0 0.0 copy-start.1
  128.0 0.7 copy-done.1
  128.6 1.7 %shard_map.71 = bf16[16,768]{1,0:T(8,128)(2,1)} custom-call(bf16[16,768]{1,0:T(8,128)(2,1)} %embed_ref.3, bf16[8,16,768]{2,1,0:T(8,128)(2,1)} %copy-done.1), custom_call_target="tpu_custom_call" | custom-call | tf_op jit(solution)/shard_map/pallas_call | solution.py:144
  130.4 0.0 copy-done.4
  130.4 2.0 %shard_map.70 = bf16[128,768]{1,0:T(8,128)(2,1)} custom-call(bf16[128,768]{1,0:T(8,128)(2,1)} %embed_ref.2, f32[128,768]{1,0:T(8,128)} %slice.9.refs_0_, bf16[128,768]{1,0:T(8,128)(2,1)} %copy-done.4), custom_call_target="tpu_custom_call" | custom-call | tf_op jit(solution)/shard_map/pallas_call | solution.py:144
  (1 shorter events, 0.0 us)
Async XLA Ops:
  2.5 21.5 %all-to-all-start = ((bf16[8,16,896]{2,1,0:T(8,128)(2,1)}), bf16[8,16,896]{2,1,0:T(8,128)(2,1)S(1)}, u32[]{:S(2)}, u32[]{:S(2)}) async-start(bf16[8,16,896]{2,1,0:T(8,128)(2,1)} %get-tuple-element.26), calls=%async_computation | async-start | bytes 458752 | tf_op jit(solution)/shard_map/all_to_all | solution.py:154
  12.8 8.5 %collective-permute-start = (bf16[128,768]{1,0:T(8,128)(2,1)}, bf16[128,768]{1,0:T(8,128)(2,1)S(1)}, u32[]{:S(2)}, u32[]{:S(2)}) collective-permute-start(bf16[128,768]{1,0:T(8,128)(2,1)} %get-tuple-element.27), channel_id=1, source_target_pairs={{0,8},{8,0},{1,9},{9,1},{2,10},{10,2},{3,11},{11,3},{4,12},{12,4},... | collective-permute-start | bytes 589832 | tf_op jit(solution)/shard_map/ppermute | solution.py:30
  24.9 15.9 %copy-start.3 = (bf16[256,768]{1,0:T(8,128)(2,1)}, bf16[256,768]{1,0:T(8,128)(2,1)S(1)}, u32[]{:S(2)}) copy-start(bf16[256,768]{1,0:T(8,128)(2,1)S(1)} %pad_maximum_fusion.refs_2_) | copy-start | bytes 1179652
  26.0 32.2 %all-to-all-start.1 = ((bf16[4,128,896]{2,1,0:T(8,128)(2,1)}), bf16[4,128,896]{2,1,0:T(8,128)(2,1)S(1)}, u32[]{:S(2)}, u32[]{:S(2)}) async-start(bf16[4,128,896]{2,1,0:T(8,128)(2,1)} %broadcast_in_dim.2), calls=%async_computation.1 | async-start | bytes 1835008 | tf_op jit(solution)/shard_map/all_to_all | solution.py:154
  33.4 19.2 %collective-permute-start.3 = (bf16[256,768]{1,0:T(8,128)(2,1)S(1)}, bf16[256,768]{1,0:T(8,128)(2,1)S(1)}, u32[]{:S(2)}, u32[]{:S(2)}) collective-permute-start(bf16[256,768]{1,0:T(8,128)(2,1)S(1)} %pad_maximum_fusion.refs_2_), channel_id=1, source_target_pairs={{0,6},{2,0},{4,2},{6,4},{1,7},{3,1},{5,3},{7,5},{8,14},{10,8},{12,... | collective-permute-start | bytes 1179656 | tf_op jit(solution)/shard_map/ppermute | solution.py:30
  38.1 15.5 %collective-permute-start.2 = (bf16[256,768]{1,0:T(8,128)(2,1)S(1)}, bf16[256,768]{1,0:T(8,128)(2,1)S(1)}, u32[]{:S(2)}, u32[]{:S(2)}) collective-permute-start(bf16[256,768]{1,0:T(8,128)(2,1)S(1)} %pad_maximum_fusion.refs_2_), channel_id=1, source_target_pairs={{0,4},{2,6},{4,0},{6,2},{1,5},{3,7},{5,1},{7,3},{8,12},{10,14},{12... | collective-permute-start | bytes 1179656 | tf_op jit(solution)/shard_map/ppermute | solution.py:30
  40.8 17.4 %collective-permute-start.1 = (bf16[256,768]{1,0:T(8,128)(2,1)S(1)}, bf16[256,768]{1,0:T(8,128)(2,1)S(1)}, u32[]{:S(2)}, u32[]{:S(2)}) collective-permute-start(bf16[256,768]{1,0:T(8,128)(2,1)S(1)} %pad_maximum_fusion.refs_2_), channel_id=1, source_target_pairs={{0,2},{2,4},{4,6},{6,0},{1,3},{3,5},{5,7},{7,1},{8,10},{10,12},{12... | collective-permute-start | bytes 1179656 | tf_op jit(solution)/shard_map/ppermute | solution.py:30
  52.6 10.2 %copy-start.6 = (bf16[256,768]{1,0:T(8,128)(2,1)}, bf16[256,768]{1,0:T(8,128)(2,1)S(1)}, u32[]{:S(2)}) copy-start(bf16[256,768]{1,0:T(8,128)(2,1)S(1)} %collective-permute-done.3.refs_5_) | copy-start | bytes 1179652
  53.6 9.2 %copy-start.7 = (bf16[256,768]{1,0:T(8,128)(2,1)}, bf16[256,768]{1,0:T(8,128)(2,1)S(1)}, u32[]{:S(2)}) copy-start(bf16[256,768]{1,0:T(8,128)(2,1)S(1)} %collective-permute-done.2.refs_4_) | copy-start | bytes 1179652
  58.2 4.6 %copy-start.8 = (bf16[256,768]{1,0:T(8,128)(2,1)}, bf16[256,768]{1,0:T(8,128)(2,1)S(1)}, u32[]{:S(2)}) copy-start(bf16[256,768]{1,0:T(8,128)(2,1)S(1)} %collective-permute-done.1.refs_3_) | copy-start | bytes 1179652
  58.2 4.6 %copy-start = (bf16[4,128,896]{2,1,0:T(8,128)(2,1)}, bf16[4,128,896]{2,1,0:T(8,128)(2,1)S(1)}, u32[]{:S(2)}) copy-start(bf16[4,128,896]{2,1,0:T(8,128)(2,1)S(1)} %all-to-all-done.1) | copy-start | bytes 2752516
  58.2 4.6 %collective-permute-start.4 = (bf16[512,896]{1,0:T(8,128)(2,1)S(1)}, bf16[512,896]{1,0:T(8,128)(2,1)S(1)}, u32[]{:S(2)}, u32[]{:S(2)}) collective-permute-start(bf16[512,896]{1,0:T(8,128)(2,1)S(1)} %bitcast.12), channel_id=1, source_target_pairs={{0,1},{1,0},{2,3},{3,2},{4,5},{5,4},{6,7},{7,6},{8,9},{9,8},{10,11... | collective-permute-start | bytes 2752520 | tf_op jit(solution)/shard_map/ppermute | solution.py:30
  62.8 0.9 copy-start.5
  72.9 4.5 %collective-permute-start.5 = (bf16[512,768]{1,0:T(8,128)(2,1)}, bf16[512,768]{1,0:T(8,128)(2,1)S(1)}, u32[]{:S(2)}, u32[]{:S(2)}) collective-permute-start(bf16[512,768]{1,0:T(8,128)(2,1)} %get-tuple-element.38), channel_id=1, source_target_pairs={{0,1},{1,0},{2,3},{3,2},{4,5},{5,4},{6,7},{7,6},{8,9},{9,8},{10,11... | collective-permute-start | bytes 2359304 | tf_op jit(solution)/shard_map/ppermute | solution.py:30
  79.6 9.9 %copy-start.10 = (bf16[256,768]{1,0:T(8,128)(2,1)S(1)}, bf16[256,768]{1,0:T(8,128)(2,1)}, u32[]{:S(2)}) copy-start(bf16[256,768]{1,0:T(8,128)(2,1)} %get-tuple-element.40) | copy-start | bytes 1179652
  79.6 12.6 %copy-start.9 = (bf16[256,768]{1,0:T(8,128)(2,1)S(1)}, bf16[256,768]{1,0:T(8,128)(2,1)}, u32[]{:S(2)}) copy-start(bf16[256,768]{1,0:T(8,128)(2,1)} %get-tuple-element.41) | copy-start | bytes 1179652
  79.6 32.2 %copy-start.2 = (bf16[256,768]{1,0:T(8,128)(2,1)S(1)}, bf16[256,768]{1,0:T(8,128)(2,1)}, u32[]{:S(2)}) copy-start(bf16[256,768]{1,0:T(8,128)(2,1)} %get-tuple-element.36) | copy-start | bytes 1179652
  79.6 32.2 %all-to-all-start.2 = ((bf16[4,128,768]{2,1,0:T(8,128)(2,1)}), bf16[4,128,768]{2,1,0:T(8,128)(2,1)S(1)}, u32[]{:S(2)}, u32[]{:S(2)}) async-start(bf16[4,128,768]{2,1,0:T(8,128)(2,1)} %bitcast.10), calls=%async_computation.2 | async-start | bytes 1572864 | tf_op jit(solution)/shard_map/all_to_all | solution.py:159
  87.0 14.1 %collective-permute-start.6 = (bf16[256,768]{1,0:T(8,128)(2,1)}, bf16[256,768]{1,0:T(8,128)(2,1)S(1)}, u32[]{:S(2)}, u32[]{:S(2)}) collective-permute-start(bf16[256,768]{1,0:T(8,128)(2,1)} %get-tuple-element.39), channel_id=1, source_target_pairs={{0,6},{2,0},{4,2},{6,4},{1,7},{3,1},{5,3},{7,5},{8,14},{10,8},{12,... | collective-permute-start | bytes 1179656 | tf_op jit(solution)/shard_map/ppermute | solution.py:30
  89.5 15.5 %collective-permute-start.7 = (bf16[256,768]{1,0:T(8,128)(2,1)S(1)}, bf16[256,768]{1,0:T(8,128)(2,1)S(1)}, u32[]{:S(2)}, u32[]{:S(2)}) collective-permute-start(bf16[256,768]{1,0:T(8,128)(2,1)S(1)} %copy-done.10), channel_id=1, source_target_pairs={{0,4},{2,6},{4,0},{6,2},{1,5},{3,7},{5,1},{7,3},{8,12},{10,14},{12... | collective-permute-start | bytes 1179656 | tf_op jit(solution)/shard_map/ppermute | solution.py:30
  92.2 19.6 %collective-permute-start.8 = (bf16[256,768]{1,0:T(8,128)(2,1)S(1)}, bf16[256,768]{1,0:T(8,128)(2,1)S(1)}, u32[]{:S(2)}, u32[]{:S(2)}) collective-permute-start(bf16[256,768]{1,0:T(8,128)(2,1)S(1)} %copy-done.9), channel_id=1, source_target_pairs={{0,2},{2,4},{4,6},{6,0},{1,3},{3,5},{5,7},{7,1},{8,10},{10,12},{12... | collective-permute-start | bytes 1179656 | tf_op jit(solution)/shard_map/ppermute | solution.py:30
  112.9 15.1 %all-to-all-start.3 = ((bf16[8,16,768]{2,1,0:T(8,128)(2,1)}), bf16[8,16,768]{2,1,0:T(8,128)(2,1)S(1)}, u32[]{:S(2)}, u32[]{:S(2)}) async-start(bf16[8,16,768]{2,1,0:T(8,128)(2,1)} %bitcast.11), calls=%async_computation.3 | async-start | bytes 393216 | tf_op jit(solution)/shard_map/all_to_all | solution.py:159
  117.3 8.4 %collective-permute-start.9 = (bf16[128,768]{1,0:T(8,128)(2,1)S(1)}, bf16[128,768]{1,0:T(8,128)(2,1)S(1)}, u32[]{:S(2)}, u32[]{:S(2)}) collective-permute-start(bf16[128,768]{1,0:T(8,128)(2,1)S(1)} %slice.12), channel_id=1, source_target_pairs={{0,8},{8,0},{1,9},{9,1},{2,10},{10,2},{3,11},{11,3},{4,12},{12,4},... | collective-permute-start | bytes 589832 | tf_op jit(solution)/shard_map/ppermute | solution.py:30
  125.7 4.6 %copy-start.4 = (bf16[128,768]{1,0:T(8,128)(2,1)}, bf16[128,768]{1,0:T(8,128)(2,1)S(1)}, u32[]{:S(2)}) copy-start(bf16[128,768]{1,0:T(8,128)(2,1)S(1)} %collective-permute-done.9.refs_1_) | copy-start | bytes 589828
  128.0 0.7 copy-start.1

commit v6 on v5

--- a/solution.py
+++ b/solution.py
@@ -11,9 +11,8 @@
 AXES = ("z", "yh", "ym", "yl", "x", "c")
 SIZES = (8, 2, 2, 2, 4, 2)
 FAR = ("z", "yh", "ym")
-MIDDLE = ("yh", "ym")
 LANES = 128
-VMEM = 56 * 1024 * 1024
+VMEM = 40 * 1024 * 1024
 ROWS_BY_ROWS = (((1,), (1,)), ((), ()))
 COLUMNS_BY_ROWS = (((0,), (0,)), ((), ()))
 
@@ -69,21 +68,14 @@
 def pair_kernel(chunks, first_ref, scalars_ref, *refs):
     chunk_refs, packet_refs = refs[:chunks], refs[chunks : chunks + 2]
     text_grad_refs = refs[chunks + 2 : chunks + 4]
-    image_grad_refs = refs[chunks + 4 : 2 * chunks + 4]
-    image_ref, text_ref, sems = refs[2 * chunks + 4 :]
+    image_grad_refs = refs[chunks + 4 : -2]
+    image_ref, text_ref = refs[-2:]
     block, width = chunk_refs[0].shape
     count = packet_refs[0].shape[0]
-    copies = [
-        pltpu.make_async_copy(ref, image_ref.at[pl.ds(i * block, block)], sems.at[i]) for i, ref in enumerate(chunk_refs)
-    ]
-    copies += [
-        pltpu.make_async_copy(ref, text_ref.at[pl.ds(i * count, count)], sems.at[chunks + i])
-        for i, ref in enumerate(packet_refs)
-    ]
-    for copy in copies:
-        copy.start()
-    for copy in copies:
-        copy.wait()
+    for i, ref in enumerate(chunk_refs):
+        image_ref[i * block : (i + 1) * block, :] = ref[...]
+    for i, ref in enumerate(packet_refs):
+        text_ref[i * count : (i + 1) * count, :] = ref[...]
 
     digits = text_ref[:, width:].astype(jnp.float32).T
     pairs = (digits[0:1] * 256.0 + digits[1:2]).astype(jnp.int32)
@@ -99,24 +91,22 @@
         ref[...] = text_grad[i * count : (i + 1) * count].astype(ref.dtype)
     image_grad = jnp.dot(weight, texts, preferred_element_type=jnp.float32)
     for i, ref in enumerate(image_grad_refs):
-        ref[...] = image_grad[i * block : (i + 1) * block].astype(ref.dtype)
-
-
-def pair_terms(first, scalars, chunks, packets):
+        ref[...] = image_grad[i * ref.shape[0] : (i + 1) * ref.shape[0]].astype(ref.dtype)
+
+
+def pair_terms(first, scalars, chunks, packets, shares):
     block, width = chunks[0].shape
     count, wide = packets[0].shape
     rows, texts = len(chunks) * block, 2 * count
-    anywhere = pl.BlockSpec(memory_space=pl.ANY)
     return pl.pallas_call(
         lambda *refs: pair_kernel(len(chunks), *refs),
-        in_specs=[smem, smem] + [anywhere] * (len(chunks) + 2),
-        out_specs=[vmem] * (len(chunks) + 2),
+        in_specs=[smem, smem] + [vmem] * (len(chunks) + 2),
+        out_specs=[vmem] * (shares + 2),
         out_shape=[jax.ShapeDtypeStruct((count, width), jnp.bfloat16)] * 2
-        + [jax.ShapeDtypeStruct((block, width), jnp.bfloat16)] * len(chunks),
+        + [jax.ShapeDtypeStruct((rows // shares, width), jnp.bfloat16)] * shares,
         scratch_shapes=[
             pltpu.VMEM((rows, width), jnp.bfloat16),
             pltpu.VMEM((texts, wide), jnp.bfloat16),
-            pltpu.SemaphoreType.DMA((len(chunks) + 2,)),
         ],
         compiler_params=params(),
         cost_estimate=pl.CostEstimate(
@@ -159,17 +149,22 @@
     return lax.all_to_all(parts, axis, split_axis=0, concat_axis=0, tiled=True)
 
 
+def gathered(rows, by, across):
+    pairs, ring = lax.axis_size("yl"), lax.axis_size("x")
+    moves = [
+        (p * ring + i, (p + across) % pairs * ring + (i + by) % ring) for p in range(pairs) for i in range(ring)
+    ]
+    return lax.ppermute(rows, ("yl", "x"), moves)
+
+
 def on_device(image_embed, text_embed, log_scale, logit_bias, pair_index):
     own_images = image_embed.shape[0]
     ring = lax.axis_size("x")
     together = lax.optimization_barrier
 
-    unit, packets = units_and_packets(pair_index, image_embed, text_embed, lax.axis_size("z"))
-    texts, beside = together((spread(packets, "z"), shifted(unit, "yl", 1)))
-    pair = jnp.concatenate([unit, beside], axis=0)
-    copies = jnp.broadcast_to(texts[None], (lax.axis_size(MIDDLE),) + texts.shape)
-    copies, pair = together((copies, pair))
-    own, *chunks = together((spread(copies, MIDDLE), *[shifted(pair, "x", s) for s in range(1, ring)]))
+    unit, packets = units_and_packets(pair_index, image_embed, text_embed, lax.axis_size(FAR))
+    places = [(s, p) for s in range(ring) for p in range(2)]
+    own, *chunks = together((spread(packets, FAR), *[gathered(unit, s, p) for s, p in places[1:]]))
     other = shifted(own, "c", 1)
 
     scale = jnp.exp(log_scale)
@@ -182,17 +177,16 @@
             for place in (yl, 1 - yl)
         ]
     ).astype(jnp.int32)
-    own_part, other_part, *image_parts = pair_terms(first, scalars, [pair] + chunks, [own, other])
+    own_part, other_part, *image_parts = pair_terms(
+        first, scalars, [unit] + chunks, [own, other], ring
+    )
 
     text_part = own_part.astype(jnp.float32) + shifted(other_part, "c", 1).astype(jnp.float32)
-    text_parts, *returned = together(
-        (parted(text_part.astype(jnp.bfloat16), MIDDLE), *[shifted(image_parts[s], "x", -s) for s in range(1, ring)])
-    )
-    text_part = jnp.sum(text_parts.astype(jnp.float32), axis=0).astype(jnp.bfloat16)
+    text_parts = parted(text_part.astype(jnp.bfloat16), FAR)
+    returned = [shifted(image_parts[s], "x", -s) for s in range(1, ring)]
     image_total = image_parts[0].astype(jnp.float32) + sum(part.astype(jnp.float32) for part in returned)
     image_own, image_beside = image_total[:own_images], image_total[own_images:].astype(jnp.bfloat16)
-    text_part, image_beside = together((text_part, image_beside))
-    text_parts, beside = together((parted(text_part, "z"), shifted(image_beside, "yl", 1)))
+    beside = shifted(image_beside, "yl", 1)
     return (
         unit_backward(image_embed, image_own, beside),
         unit_backward(text_embed, text_parts),

time: 133 us -> 134 us (level)
  the two profiles are of different devices: /device:TPU:16 before, /device:TPU:1 now
where the time goes in v6:
time: 134 us; the launch traced here: 133 us
  starting transfers between devices  65.9 us (49%)
  waiting for transfers between devices  39.4 us (29%)
  local copies, waits for them, and re-layouts  14.6 us (11%)
  Pallas kernels  9.51 us (7%)
  between operations  2.28 us (2%)
  other arithmetic  1.36 us (1%)
    ppermute x6, waiting for transfers between devices, shifted(): lax.ppermute(array, axis, [(i, (i + by) % devices) for i in range(devices)])  25.8 us
    ppermute x7, starting transfers between devices, gathered(): return lax.ppermute(rows, ('yl', 'x'), moves)  23.4 us
    all_to_all x1, starting transfers between devices, spread(): lax.all_to_all(copies, axis, split_axis=0, concat_axis=0, tiled=True)  16.5 us
    unnamed x42, local copies, waits for them, and re-layouts  14.4 us
    ppermute x6, starting transfers between devices, shifted(): lax.ppermute(array, axis, [(i, (i + by) % devices) for i in range(devices)])  14.3 us
    ppermute x7, waiting for transfers between devices, gathered(): return lax.ppermute(rows, ('yl', 'x'), moves)  13.6 us
    all_to_all x1, starting transfers between devices, parted(): return lax.all_to_all(parts, axis, split_axis=0, concat_axis=0, tiled=True)  11.6 us
    pallas_call x1, Pallas kernels, pair_terms(): pl.pallas_call(lambda *refs: pair_kernel(len(chunks), *refs), in_specs=[s...  6.19 us
  transfers between devices with their start and end apart: 15, of which 9 were waited for; matrix products, arithmetic and copies ran while one was open for 0% of the time, Pallas kernels for 1%

profile of v6, /device:TPU:1, one launch (start us, length us, event | category | flops | bytes accessed | tf_op | source)
XLA Modules:
  0.0 133.0 jit_solution(6605558132808163738)
XLA Ops:
  0.6 0.0 copy-start
  0.6 0.9 copy-done
  1.6 0.7 copy-done.2
  2.3 0.7 copy-done.4
  3.0 1.6 %shard_map.68 = (bf16[128,768]{1,0:T(8,128)(2,1)S(1)}, bf16[32,16,896]{2,1,0:T(8,128)(2,1)}) custom-call(s32[16]{0:T(128)S(1)} %copy-done.4, bf16[128,768]{1,0:T(8,128)(2,1)S(1)} %copy-done, bf16[16,768]{1,0:T(8,128)(2,1)S(1)} %copy-done.2), custom_call_target="tpu_custom_call" | custom-call | tf_op jit(solution)/shard_map/pallas_call | solution.py:56
  4.6 16.5 %all-to-all-start = ((bf16[32,16,896]{2,1,0:T(8,128)(2,1)}), bf16[32,16,896]{2,1,0:T(8,128)(2,1)S(1)}, u32[]{:S(2)}, u32[]{:S(2)}) async-start(bf16[32,16,896]{2,1,0:T(8,128)(2,1)} %get-tuple-element.19), calls=%async_computation | async-start | bytes 1835008 | tf_op jit(solution)/shard_map/all_to_all | solution.py:144
  21.1 4.5 %collective-permute-start.6 = (bf16[128,768]{1,0:T(8,128)(2,1)S(1)}, bf16[128,768]{1,0:T(8,128)(2,1)S(1)}, u32[]{:S(2)}, u32[]{:S(2)}) collective-permute-start(bf16[128,768]{1,0:T(8,128)(2,1)S(1)} %get-tuple-element.18.refs_2_), channel_id=1, source_target_pairs={{0,14},{2,8},{4,10},{6,12},{8,6},{10,0},{12,2},{14,4},{1,15},{3,9}... | collective-permute-start | bytes 589832 | tf_op jit(solution)/shard_map/ppermute | solution.py:157
  25.6 2.5 %collective-permute-start.5 = (bf16[128,768]{1,0:T(8,128)(2,1)S(1)}, bf16[128,768]{1,0:T(8,128)(2,1)S(1)}, u32[]{:S(2)}, u32[]{:S(2)}) collective-permute-start(bf16[128,768]{1,0:T(8,128)(2,1)S(1)} %get-tuple-element.18.refs_2_), channel_id=1, source_target_pairs={{0,6},{2,0},{4,2},{6,4},{8,14},{10,8},{12,10},{14,12},{1,7},{3,1},... | collective-permute-start | bytes 589832 | tf_op jit(solution)/shard_map/ppermute | solution.py:157
  28.1 2.9 %collective-permute-start.4 = (bf16[128,768]{1,0:T(8,128)(2,1)S(1)}, bf16[128,768]{1,0:T(8,128)(2,1)S(1)}, u32[]{:S(2)}, u32[]{:S(2)}) collective-permute-start(bf16[128,768]{1,0:T(8,128)(2,1)S(1)} %get-tuple-element.18.refs_2_), channel_id=1, source_target_pairs={{0,12},{2,14},{4,8},{6,10},{8,4},{10,6},{12,0},{14,2},{1,13},{3,15... | collective-permute-start | bytes 589832 | tf_op jit(solution)/shard_map/ppermute | solution.py:157
  31.0 4.7 %collective-permute-start.3 = (bf16[128,768]{1,0:T(8,128)(2,1)S(1)}, bf16[128,768]{1,0:T(8,128)(2,1)S(1)}, u32[]{:S(2)}, u32[]{:S(2)}) collective-permute-start(bf16[128,768]{1,0:T(8,128)(2,1)S(1)} %get-tuple-element.18.refs_2_), channel_id=1, source_target_pairs={{0,4},{2,6},{4,0},{6,2},{8,12},{10,14},{12,8},{14,10},{1,5},{3,7},... | collective-permute-start | bytes 589832 | tf_op jit(solution)/shard_map/ppermute | solution.py:157
  35.7 2.9 %collective-permute-start.2 = (bf16[128,768]{1,0:T(8,128)(2,1)S(1)}, bf16[128,768]{1,0:T(8,128)(2,1)S(1)}, u32[]{:S(2)}, u32[]{:S(2)}) collective-permute-start(bf16[128,768]{1,0:T(8,128)(2,1)S(1)} %get-tuple-element.18.refs_2_), channel_id=1, source_target_pairs={{0,10},{2,12},{4,14},{6,8},{8,2},{10,4},{12,6},{14,0},{1,11},{3,13... | collective-permute-start | bytes 589832 | tf_op jit(solution)/shard_map/ppermute | solution.py:157
  38.6 7.8 %collective-permute-done.6.refs_9_ = bf16[128,768]{1,0:T(8,128)(2,1)S(1)} collective-permute-done((bf16[128,768]{1,0:T(8,128)(2,1)S(1)}, bf16[128,768]{1,0:T(8,128)(2,1)S(1)}, u32[]{:S(2)}, u32[]{:S(2)}) %collective-permute-start.6) | collective-permute-done | bytes 196640 | tf_op jit(solution)/shard_map/ppermute | solution.py:157
  46.5 0.7 copy-done.7
  47.1 3.1 %collective-permute-start.1 = (bf16[128,768]{1,0:T(8,128)(2,1)S(1)}, bf16[128,768]{1,0:T(8,128)(2,1)S(1)}, u32[]{:S(2)}, u32[]{:S(2)}) collective-permute-start(bf16[128,768]{1,0:T(8,128)(2,1)S(1)} %get-tuple-element.18.refs_2_), channel_id=1, source_target_pairs={{0,2},{2,4},{4,6},{6,0},{8,10},{10,12},{12,14},{14,8},{1,3},{3,5},... | collective-permute-start | bytes 589832 | tf_op jit(solution)/shard_map/ppermute | solution.py:157
  50.3 0.0 collective-permute-done.5.refs_8_
  50.3 0.0 copy-done.5
  50.3 0.0 copy-start.9
  50.3 0.7 copy-done.9
  50.9 2.9 %collective-permute-start = (bf16[128,768]{1,0:T(8,128)(2,1)S(1)}, bf16[128,768]{1,0:T(8,128)(2,1)S(1)}, u32[]{:S(2)}, u32[]{:S(2)}) collective-permute-start(bf16[128,768]{1,0:T(8,128)(2,1)S(1)} %get-tuple-element.18.refs_2_), channel_id=1, source_target_pairs={{0,8},{2,10},{4,12},{6,14},{8,0},{10,2},{12,4},{14,6},{1,9},{3,11}... | collective-permute-start | bytes 589832 | tf_op jit(solution)/shard_map/ppermute | solution.py:157
  53.8 0.0 collective-permute-done.4.refs_7_
  53.8 0.0 copy-start.11
  53.8 0.7 copy-done.11
  54.5 0.0 collective-permute-done.3.refs_6_
  54.5 0.7 copy-done.13
  55.2 1.3 collective-permute-done.2.refs_5_
  56.5 0.7 copy-done.15
  57.1 4.5 %collective-permute-done.1.refs_4_ = bf16[128,768]{1,0:T(8,128)(2,1)S(1)} collective-permute-done((bf16[128,768]{1,0:T(8,128)(2,1)S(1)}, bf16[128,768]{1,0:T(8,128)(2,1)S(1)}, u32[]{:S(2)}, u32[]{:S(2)}) %collective-permute-start.1) | collective-permute-done | bytes 196640 | tf_op jit(solution)/shard_map/ppermute | solution.py:157
  61.6 0.7 copy-done.17
  62.3 0.0 collective-permute-done.refs_3_
  62.3 0.7 copy-done.19
  63.0 0.0 all-to-all-done
  63.0 2.4 %collective-permute-start.7 = (bf16[512,896]{1,0:T(8,128)(2,1)S(1)}, bf16[512,896]{1,0:T(8,128)(2,1)S(1)}, u32[]{:S(2)}, u32[]{:S(2)}) collective-permute-start(bf16[512,896]{1,0:T(8,128)(2,1)S(1)} %bitcast.10), channel_id=1, source_target_pairs={{0,1},{1,0},{2,3},{3,2},{4,5},{5,4},{6,7},{7,6},{8,9},{9,8},{10,11... | collective-permute-start | bytes 2752520 | tf_op jit(solution)/shard_map/ppermute | solution.py:29
  66.8 0.1 stack.35.refs_0_
  66.9 0.1 pad_maximum_fusion.refs_1_
  67.0 0.5 collective-permute-done.7.refs_11_
  67.5 0.9 copy-done.6
  68.4 0.9 copy-done.8
  69.3 0.9 copy-done.10
  70.2 0.9 copy-done.12
  71.2 0.9 copy-done.14
  72.1 0.9 copy-done.16
  73.0 0.9 copy-done.18
  74.0 0.9 copy-done.20
  74.9 6.2 %shard_map.69 = (bf16[512,768]{1,0:T(8,128)(2,1)S(1)}, bf16[512,768]{1,0:T(8,128)(2,1)S(1)}, bf16[256,768]{1,0:T(8,128)(2,1)S(1)}, bf16[256,768]{1,0:T(8,128)(2,...) custom-call(s32[8]{0:T(128)S(1)} %stack.35.refs_0_, f32[3]{0:T(128)S(1)} %pad_maximum_fusion.refs_1_, ...), custom_call_target="tpu_custom_call" | custom-call | flops 4831838208 | bytes 6291456 | tf_op jit(solution)/shard_map/pallas_call | solution.py:101
  81.1 2.3 %collective-permute-start.12 = (bf16[512,768]{1,0:T(8,128)(2,1)S(1)}, bf16[512,768]{1,0:T(8,128)(2,1)S(1)}, u32[]{:S(2)}, u32[]{:S(2)}) collective-permute-start(bf16[512,768]{1,0:T(8,128)(2,1)S(1)} %get-tuple-element.33), channel_id=1, source_target_pairs={{0,1},{1,0},{2,3},{3,2},{4,5},{5,4},{6,7},{7,6},{8,9},{9,8},{10,11... | collective-permute-start | bytes 2359304 | tf_op jit(solution)/shard_map/ppermute | solution.py:29
  83.4 1.9 %collective-permute-done.12 = bf16[512,768]{1,0:T(8,128)(2,1)S(1)} collective-permute-done((bf16[512,768]{1,0:T(8,128)(2,1)S(1)}, bf16[512,768]{1,0:T(8,128)(2,1)S(1)}, u32[]{:S(2)}, u32[]{:S(2)}) %collective-permute-start.12) | collective-permute-done | bytes 786464 | tf_op jit(solution)/shard_map/ppermute | solution.py:29
  85.3 1.1 add_convert_fusion
  86.4 11.6 %all-to-all-start.1 = ((bf16[32,16,768]{2,1,0:T(8,128)(2,1)}), bf16[32,16,768]{2,1,0:T(8,128)(2,1)S(1)}, u32[]{:S(2)}, u32[]{:S(2)}) async-start(bf16[32,16,768]{2,1,0:T(8,128)(2,1)} %bitcast.9), calls=%async_computation.1 | async-start | bytes 1572864 | tf_op jit(solution)/shard_map/all_to_all | solution.py:149
  97.9 2.2 %collective-permute-start.8 = (bf16[256,768]{1,0:T(8,128)(2,1)S(1)}, bf16[256,768]{1,0:T(8,128)(2,1)S(1)}, u32[]{:S(2)}, u32[]{:S(2)}) collective-permute-start(bf16[256,768]{1,0:T(8,128)(2,1)S(1)} %get-tuple-element.29), channel_id=1, source_target_pairs={{0,6},{2,0},{4,2},{6,4},{1,7},{3,1},{5,3},{7,5},{8,14},{10,8},{12,... | collective-permute-start | bytes 1179656 | tf_op jit(solution)/shard_map/ppermute | solution.py:29
  100.1 2.9 %collective-permute-start.9 = (bf16[256,768]{1,0:T(8,128)(2,1)S(1)}, bf16[256,768]{1,0:T(8,128)(2,1)S(1)}, u32[]{:S(2)}, u32[]{:S(2)}) collective-permute-start(bf16[256,768]{1,0:T(8,128)(2,1)S(1)} %get-tuple-element.30), channel_id=1, source_target_pairs={{0,4},{2,6},{4,0},{6,2},{1,5},{3,7},{5,1},{7,3},{8,12},{10,14},{12... | collective-permute-start | bytes 1179656 | tf_op jit(solution)/shard_map/ppermute | solution.py:29
  103.0 2.1 %collective-permute-start.10 = (bf16[256,768]{1,0:T(8,128)(2,1)S(1)}, bf16[256,768]{1,0:T(8,128)(2,1)S(1)}, u32[]{:S(2)}, u32[]{:S(2)}) collective-permute-start(bf16[256,768]{1,0:T(8,128)(2,1)S(1)} %get-tuple-element.31), channel_id=1, source_target_pairs={{0,2},{2,4},{4,6},{6,0},{1,3},{3,5},{5,7},{7,1},{8,10},{10,12},{12... | collective-permute-start | bytes 1179656 | tf_op jit(solution)/shard_map/ppermute | solution.py:29
  105.2 4.7 %collective-permute-done.8 = bf16[256,768]{1,0:T(8,128)(2,1)S(1)} collective-permute-done((bf16[256,768]{1,0:T(8,128)(2,1)S(1)}, bf16[256,768]{1,0:T(8,128)(2,1)S(1)}, u32[]{:S(2)}, u32[]{:S(2)}) %collective-permute-start.8) | collective-permute-done | bytes 393248 | tf_op jit(solution)/shard_map/ppermute | solution.py:29
  109.8 3.4 %collective-permute-done.9 = bf16[256,768]{1,0:T(8,128)(2,1)S(1)} collective-permute-done((bf16[256,768]{1,0:T(8,128)(2,1)S(1)}, bf16[256,768]{1,0:T(8,128)(2,1)S(1)}, u32[]{:S(2)}, u32[]{:S(2)}) %collective-permute-start.9) | collective-permute-done | bytes 393248 | tf_op jit(solution)/shard_map/ppermute | solution.py:29
  113.3 9.7 %collective-permute-done.10 = bf16[256,768]{1,0:T(8,128)(2,1)S(1)} collective-permute-done((bf16[256,768]{1,0:T(8,128)(2,1)S(1)}, bf16[256,768]{1,0:T(8,128)(2,1)S(1)}, u32[]{:S(2)}, u32[]{:S(2)}) %collective-permute-start.10) | collective-permute-done | bytes 393248 | tf_op jit(solution)/shard_map/ppermute | solution.py:29
  123.0 0.2 add_add_fusion
  123.2 0.0 copy-start.1
  123.2 0.0 copy-start.3
  123.2 2.4 %collective-permute-start.11 = (bf16[128,768]{1,0:T(8,128)(2,1)S(1)}, bf16[128,768]{1,0:T(8,128)(2,1)S(1)}, u32[]{:S(2)}, u32[]{:S(2)}) collective-permute-start(bf16[128,768]{1,0:T(8,128)(2,1)S(1)} %slice.12), channel_id=1, source_target_pairs={{0,8},{8,0},{1,9},{9,1},{2,10},{10,2},{3,11},{11,3},{4,12},{12,4},... | collective-permute-start | bytes 589832 | tf_op jit(solution)/shard_map/ppermute | solution.py:29
  125.7 5.5 %collective-permute-done.11.refs_1_ = bf16[128,768]{1,0:T(8,128)(2,1)S(1)} collective-permute-done((bf16[128,768]{1,0:T(8,128)(2,1)S(1)}, bf16[128,768]{1,0:T(8,128)(2,1)S(1)}, u32[]{:S(2)}, u32[]{:S(2)}) %collective-permute-start.11) | collective-permute-done | bytes 196640 | tf_op jit(solution)/shard_map/ppermute | solution.py:29
  131.3 0.0 copy-done.1
  131.3 0.9 shard_map.70
  132.2 0.0 all-to-all-done.1.refs_0_
  132.2 0.0 copy-done.3
  132.2 0.8 shard_map.71
  (18 shorter events, 0.1 us)
Async XLA Ops:
  0.6 0.9 copy-start
  1.6 0.7 copy-start.2
  2.3 0.7 copy-start.4
  4.6 45.7 %copy-start.5 = (bf16[128,768]{1,0:T(8,128)(2,1)}, bf16[128,768]{1,0:T(8,128)(2,1)S(1)}, u32[]{:S(2)}) copy-start(bf16[128,768]{1,0:T(8,128)(2,1)S(1)} %get-tuple-element.18.refs_2_) | copy-start | bytes 589828
  4.6 58.4 %all-to-all-start = ((bf16[32,16,896]{2,1,0:T(8,128)(2,1)}), bf16[32,16,896]{2,1,0:T(8,128)(2,1)S(1)}, u32[]{:S(2)}, u32[]{:S(2)}) async-start(bf16[32,16,896]{2,1,0:T(8,128)(2,1)} %get-tuple-element.19), calls=%async_computation | async-start | bytes 1835008 | tf_op jit(solution)/shard_map/all_to_all | solution.py:144
  21.1 25.4 %collective-permute-start.6 = (bf16[128,768]{1,0:T(8,128)(2,1)S(1)}, bf16[128,768]{1,0:T(8,128)(2,1)S(1)}, u32[]{:S(2)}, u32[]{:S(2)}) collective-permute-start(bf16[128,768]{1,0:T(8,128)(2,1)S(1)} %get-tuple-element.18.refs_2_), channel_id=1, source_target_pairs={{0,14},{2,8},{4,10},{6,12},{8,6},{10,0},{12,2},{14,4},{1,15},{3,9}... | collective-permute-start | bytes 589832 | tf_op jit(solution)/shard_map/ppermute | solution.py:157
  25.6 24.6 %collective-permute-start.5 = (bf16[128,768]{1,0:T(8,128)(2,1)S(1)}, bf16[128,768]{1,0:T(8,128)(2,1)S(1)}, u32[]{:S(2)}, u32[]{:S(2)}) collective-permute-start(bf16[128,768]{1,0:T(8,128)(2,1)S(1)} %get-tuple-element.18.refs_2_), channel_id=1, source_target_pairs={{0,6},{2,0},{4,2},{6,4},{8,14},{10,8},{12,10},{14,12},{1,7},{3,1},... | collective-permute-start | bytes 589832 | tf_op jit(solution)/shard_map/ppermute | solution.py:157
  28.1 25.7 %collective-permute-start.4 = (bf16[128,768]{1,0:T(8,128)(2,1)S(1)}, bf16[128,768]{1,0:T(8,128)(2,1)S(1)}, u32[]{:S(2)}, u32[]{:S(2)}) collective-permute-start(bf16[128,768]{1,0:T(8,128)(2,1)S(1)} %get-tuple-element.18.refs_2_), channel_id=1, source_target_pairs={{0,12},{2,14},{4,8},{6,10},{8,4},{10,6},{12,0},{14,2},{1,13},{3,15... | collective-permute-start | bytes 589832 | tf_op jit(solution)/shard_map/ppermute | solution.py:157
  31.0 23.5 %collective-permute-start.3 = (bf16[128,768]{1,0:T(8,128)(2,1)S(1)}, bf16[128,768]{1,0:T(8,128)(2,1)S(1)}, u32[]{:S(2)}, u32[]{:S(2)}) collective-permute-start(bf16[128,768]{1,0:T(8,128)(2,1)S(1)} %get-tuple-element.18.refs_2_), channel_id=1, source_target_pairs={{0,4},{2,6},{4,0},{6,2},{8,12},{10,14},{12,8},{14,10},{1,5},{3,7},... | collective-permute-start | bytes 589832 | tf_op jit(solution)/shard_map/ppermute | solution.py:157
  35.7 20.8 %collective-permute-start.2 = (bf16[128,768]{1,0:T(8,128)(2,1)S(1)}, bf16[128,768]{1,0:T(8,128)(2,1)S(1)}, u32[]{:S(2)}, u32[]{:S(2)}) collective-permute-start(bf16[128,768]{1,0:T(8,128)(2,1)S(1)} %get-tuple-element.18.refs_2_), channel_id=1, source_target_pairs={{0,10},{2,12},{4,14},{6,8},{8,2},{10,4},{12,6},{14,0},{1,11},{3,13... | collective-permute-start | bytes 589832 | tf_op jit(solution)/shard_map/ppermute | solution.py:157
  46.5 0.7 copy-start.7
  47.1 14.5 %collective-permute-start.1 = (bf16[128,768]{1,0:T(8,128)(2,1)S(1)}, bf16[128,768]{1,0:T(8,128)(2,1)S(1)}, u32[]{:S(2)}, u32[]{:S(2)}) collective-permute-start(bf16[128,768]{1,0:T(8,128)(2,1)S(1)} %get-tuple-element.18.refs_2_), channel_id=1, source_target_pairs={{0,2},{2,4},{4,6},{6,0},{8,10},{10,12},{12,14},{14,8},{1,3},{3,5},... | collective-permute-start | bytes 589832 | tf_op jit(solution)/shard_map/ppermute | solution.py:157
  50.3 0.7 copy-start.9
  50.9 11.4 %collective-permute-start = (bf16[128,768]{1,0:T(8,128)(2,1)S(1)}, bf16[128,768]{1,0:T(8,128)(2,1)S(1)}, u32[]{:S(2)}, u32[]{:S(2)}) collective-permute-start(bf16[128,768]{1,0:T(8,128)(2,1)S(1)} %get-tuple-element.18.refs_2_), channel_id=1, source_target_pairs={{0,8},{2,10},{4,12},{6,14},{8,0},{10,2},{12,4},{14,6},{1,9},{3,11}... | collective-permute-start | bytes 589832 | tf_op jit(solution)/shard_map/ppermute | solution.py:157
  53.8 0.7 copy-start.11
  54.5 0.7 copy-start.13
  56.5 0.7 copy-start.15
  61.6 0.7 copy-start.17
  62.3 0.7 copy-start.19
  63.0 4.5 %collective-permute-start.7 = (bf16[512,896]{1,0:T(8,128)(2,1)S(1)}, bf16[512,896]{1,0:T(8,128)(2,1)S(1)}, u32[]{:S(2)}, u32[]{:S(2)}) collective-permute-start(bf16[512,896]{1,0:T(8,128)(2,1)S(1)} %bitcast.10), channel_id=1, source_target_pairs={{0,1},{1,0},{2,3},{3,2},{4,5},{5,4},{6,7},{7,6},{8,9},{9,8},{10,11... | collective-permute-start | bytes 2752520 | tf_op jit(solution)/shard_map/ppermute | solution.py:29
  67.5 0.9 copy-start.6
  68.4 0.9 copy-start.8
  69.3 0.9 copy-start.10
  70.2 0.9 copy-start.12
  71.2 0.9 copy-start.14
  72.1 0.9 copy-start.16
  73.0 0.9 copy-start.18
  74.0 0.9 copy-start.20
  81.1 4.2 %collective-permute-start.12 = (bf16[512,768]{1,0:T(8,128)(2,1)S(1)}, bf16[512,768]{1,0:T(8,128)(2,1)S(1)}, u32[]{:S(2)}, u32[]{:S(2)}) collective-permute-start(bf16[512,768]{1,0:T(8,128)(2,1)S(1)} %get-tuple-element.33), channel_id=1, source_target_pairs={{0,1},{1,0},{2,3},{3,2},{4,5},{5,4},{6,7},{7,6},{8,9},{9,8},{10,11... | collective-permute-start | bytes 2359304 | tf_op jit(solution)/shard_map/ppermute | solution.py:29
  86.4 45.8 %all-to-all-start.1 = ((bf16[32,16,768]{2,1,0:T(8,128)(2,1)}), bf16[32,16,768]{2,1,0:T(8,128)(2,1)S(1)}, u32[]{:S(2)}, u32[]{:S(2)}) async-start(bf16[32,16,768]{2,1,0:T(8,128)(2,1)} %bitcast.9), calls=%async_computation.1 | async-start | bytes 1572864 | tf_op jit(solution)/shard_map/all_to_all | solution.py:149
  97.9 11.9 %collective-permute-start.8 = (bf16[256,768]{1,0:T(8,128)(2,1)S(1)}, bf16[256,768]{1,0:T(8,128)(2,1)S(1)}, u32[]{:S(2)}, u32[]{:S(2)}) collective-permute-start(bf16[256,768]{1,0:T(8,128)(2,1)S(1)} %get-tuple-element.29), channel_id=1, source_target_pairs={{0,6},{2,0},{4,2},{6,4},{1,7},{3,1},{5,3},{7,5},{8,14},{10,8},{12,... | collective-permute-start | bytes 1179656 | tf_op jit(solution)/shard_map/ppermute | solution.py:29
  100.1 13.1 %collective-permute-start.9 = (bf16[256,768]{1,0:T(8,128)(2,1)S(1)}, bf16[256,768]{1,0:T(8,128)(2,1)S(1)}, u32[]{:S(2)}, u32[]{:S(2)}) collective-permute-start(bf16[256,768]{1,0:T(8,128)(2,1)S(1)} %get-tuple-element.30), channel_id=1, source_target_pairs={{0,4},{2,6},{4,0},{6,2},{1,5},{3,7},{5,1},{7,3},{8,12},{10,14},{12... | collective-permute-start | bytes 1179656 | tf_op jit(solution)/shard_map/ppermute | solution.py:29
  103.0 20.0 %collective-permute-start.10 = (bf16[256,768]{1,0:T(8,128)(2,1)S(1)}, bf16[256,768]{1,0:T(8,128)(2,1)S(1)}, u32[]{:S(2)}, u32[]{:S(2)}) collective-permute-start(bf16[256,768]{1,0:T(8,128)(2,1)S(1)} %get-tuple-element.31), channel_id=1, source_target_pairs={{0,2},{2,4},{4,6},{6,0},{1,3},{3,5},{5,7},{7,1},{8,10},{10,12},{12... | collective-permute-start | bytes 1179656 | tf_op jit(solution)/shard_map/ppermute | solution.py:29
  123.2 8.1 %copy-start.1 = (bf16[128,768]{1,0:T(8,128)(2,1)S(1)}, bf16[128,768]{1,0:T(8,128)(2,1)}, u32[]{:S(2)}) copy-start(bf16[128,768]{1,0:T(8,128)(2,1)} %embed_ref.2) | copy-start | bytes 589828
  123.2 8.9 %copy-start.3 = (bf16[16,768]{1,0:T(8,128)(2,1)S(1)}, bf16[16,768]{1,0:T(8,128)(2,1)}, u32[]{:S(2)}) copy-start(bf16[16,768]{1,0:T(8,128)(2,1)} %embed_ref.3) | copy-start | bytes 73732
  123.2 8.0 %collective-permute-start.11 = (bf16[128,768]{1,0:T(8,128)(2,1)S(1)}, bf16[128,768]{1,0:T(8,128)(2,1)S(1)}, u32[]{:S(2)}, u32[]{:S(2)}) collective-permute-start(bf16[128,768]{1,0:T(8,128)(2,1)S(1)} %slice.12), channel_id=1, source_target_pairs={{0,8},{8,0},{1,9},{9,1},{2,10},{10,2},{3,11},{11,3},{4,12},{12,4},... | collective-permute-start | bytes 589832 | tf_op jit(solution)/shard_map/ppermute | solution.py:29

commit v7 on v6

v7 whole, which is shorter than its diff:
```python
import math

import jax
import jax.numpy as jnp
from jax import lax
from jax.experimental import pallas as pl
from jax.experimental.pallas import tpu as pltpu
from jax.sharding import Mesh
from jax.sharding import PartitionSpec as P

AXES = ("z", "y", "x", "c")
SIZES = (8, 8, 4, 2)
LANES = 128
MIB = 1024 * 1024
ROWS_BY_ROWS = (((1,), (1,)), ((), ()))
COLUMNS_BY_ROWS = (((0,), (0,)), ((), ()))

smem = pl.BlockSpec(memory_space=pltpu.SMEM)
vmem = pl.BlockSpec(memory_space=pltpu.VMEM)


def params(mib):
    return pltpu.CompilerParams(vmem_limit_bytes=mib * MIB)


def inverse_norm(floats):
    return lax.rsqrt(jnp.sum(floats * floats, axis=-1, keepdims=True) + 1e-06)


def unit_kernel(embed_ref, unit_ref):
    floats = embed_ref[...].astype(jnp.float32)
    unit_ref[...] = (floats * inverse_norm(floats)).astype(unit_ref.dtype)


def units(embed):
    return pl.pallas_call(
        unit_kernel,
        in_specs=[vmem],
        out_specs=vmem,
        out_shape=jax.ShapeDtypeStruct(embed.shape, jnp.bfloat16),
        compiler_params=params(56),
    )(embed)


def packet_kernel(pair_ref, text_ref, packet_ref):
    rows, width = text_ref.shape
    floats = text_ref[...].astype(jnp.float32)
    unit = (floats * inverse_norm(floats)).astype(packet_ref.dtype)
    row = lax.broadcasted_iota(jnp.int32, (rows, LANES), 0)
    lane = lax.broadcasted_iota(jnp.int32, (rows, LANES), 1)
    index = jnp.zeros((rows, LANES), jnp.int32)
    for i in range(rows):
        index = jnp.where(row == i, pair_ref[i], index)
    digits = jnp.where(lane == 0, index >> 8, jnp.where(lane == 1, index & 255, 0))
    digits = digits.astype(jnp.float32).astype(packet_ref.dtype)
    for peer in range(packet_ref.shape[0]):
        packet_ref[peer, :, :width] = unit
        packet_ref[peer, :, width:] = digits


def text_packets(pair_index, embed, peers):
    rows, width = embed.shape
    return pl.pallas_call(
        packet_kernel,
        in_specs=[smem, vmem],
        out_specs=vmem,
        out_shape=jax.ShapeDtypeStruct((peers, rows, width + LANES), jnp.bfloat16),
        compiler_params=params(56),
    )(pair_index, embed)


def pair_kernel(first_ref, scalars_ref, images_ref, own_ref, other_ref, *refs):
    image_grad_ref, own_grad_ref, other_grad_ref, image_ref, text_ref, sem = refs
    copy = pltpu.make_async_copy(images_ref, image_ref, sem)
    copy.start()
    width = image_ref.shape[1]
    count = own_ref.shape[0]
    text_ref[:count, :] = own_ref[...]
    text_ref[count:, :] = other_ref[...]
    digits = text_ref[:, width:].astype(jnp.float32).T
    pairs = (digits[0:1] * 256.0 + digits[1:2]).astype(jnp.int32)
    row = lax.broadcasted_iota(jnp.int32, (128, 1), 0)
    rows = jnp.concatenate([row + first_ref[p] for p in range(image_ref.shape[0] // 128)], axis=0)
    texts = text_ref[:, :width]
    copy.wait()
    images = image_ref[...]
    dots = lax.dot_general(images, texts, ROWS_BY_ROWS, preferred_element_type=jnp.float32)
    chance = 1.0 / (1.0 + jnp.exp2(dots * scalars_ref[1] + scalars_ref[2]))
    weight = (scalars_ref[0] * jnp.where(pairs == rows, chance - 1.0, chance)).astype(jnp.bfloat16)
    image_grad_ref[...] = jnp.dot(weight, texts, preferred_element_type=jnp.float32).astype(image_grad_ref.dtype)
    text_grad = lax.dot_general(weight, images, COLUMNS_BY_ROWS, preferred_element_type=jnp.float32)
    own_grad_ref[...] = text_grad[:count].astype(own_grad_ref.dtype)
    other_grad_ref[...] = text_grad[count:].astype(other_grad_ref.dtype)


def pair_terms(first, scalars, images, own, other):
    rows, width = images.shape
    count, wide = own.shape
    texts = 2 * count
    return pl.pallas_call(
        pair_kernel,
        in_specs=[smem, smem, pl.BlockSpec(memory_space=pl.ANY), vmem, vmem],
        out_specs=[vmem] * 3,
        out_shape=[
            jax.ShapeDtypeStruct((rows, width), jnp.bfloat16),
            jax.ShapeDtypeStruct((count, width), jnp.bfloat16),
            jax.ShapeDtypeStruct((count, width), jnp.bfloat16),
        ],
        scratch_shapes=[
            pltpu.VMEM((rows, width), jnp.bfloat16),
            pltpu.VMEM((texts, wide), jnp.bfloat16),
            pltpu.SemaphoreType.DMA,
        ],
        compiler_params=params(32),
        cost_estimate=pl.CostEstimate(
            flops=6 * rows * texts * width, bytes_accessed=4 * (rows + texts) * width, transcendentals=2 * rows * texts
        ),
    )(first, scalars, images, own, other)


def project(embed_ref, grad, out_ref):
    floats = embed_ref[...].astype(jnp.float32)
    inverse = inverse_norm(floats)
    unit = floats * inverse
    along = jnp.sum(unit * grad, axis=-1, keepdims=True)
    out_ref[...] = ((grad - unit * along) * inverse).astype(out_ref.dtype)


def backward_kernel(image_ref, text_ref, image_grad_ref, text_grads_ref, image_out_ref, text_out_ref):
    project(image_ref, image_grad_ref[...].astype(jnp.float32), image_out_ref)
    text_grad = text_grads_ref[0].astype(jnp.float32)
    for part in range(1, text_grads_ref.shape[0]):
        text_grad += text_grads_ref[part].astype(jnp.float32)
    project(text_ref, text_grad, text_out_ref)


def unit_backward(image_embed, text_embed, image_grad, text_grads):
    return pl.pallas_call(
        backward_kernel,
        in_specs=[vmem] * 4,
        out_specs=[vmem] * 2,
        out_shape=[
            jax.ShapeDtypeStruct(image_embed.shape, jnp.bfloat16),
            jax.ShapeDtypeStruct(text_embed.shape, jnp.bfloat16),
        ],
        compiler_params=params(8),
    )(image_embed, text_embed, image_grad, text_grads)


def image_rings():
    depth, length, width, cores = SIZES
    rings = []
    for z in range(depth):
        for x in range(width):
            for c in range(cores):
                ring = [((z * length + y) * width + x) * cores + c for y in range(length)]
                rings.append(ring if c == 0 else ring[::-1])
    return rings


def exchanged(array):
    return lax.ppermute(array, "c", [(0, 1), (1, 0)])


def spread(copies, axis):
    return lax.all_to_all(copies, axis, split_axis=0, concat_axis=0, tiled=True).reshape(-1, copies.shape[2])


def parted(rows, axis):
    parts = rows.reshape(lax.axis_size(axis), -1, rows.shape[1])
    return lax.all_to_all(parts, axis, split_axis=0, concat_axis=0, tiled=True)


def on_device(image_embed, text_embed, log_scale, logit_bias, pair_index):
    own_images = image_embed.shape[0]
    rings = image_rings()
    images = lax.all_gather(units(image_embed), AXES, axis=0, tiled=True, axis_index_groups=rings)

    texts = spread(text_packets(pair_index, text_embed, lax.axis_size("z")), "z")
    own = spread(jnp.broadcast_to(texts[None], (lax.axis_size("x"),) + texts.shape), "x")
    other = exchanged(own)

    scale = jnp.exp(log_scale)
    scalars = jnp.concatenate([scale, -math.log2(math.e) * scale, -math.log2(math.e) * logit_bias])
    z, x, c = lax.axis_index("z"), lax.axis_index("x"), lax.axis_index("c")
    place = jnp.arange(SIZES[1], dtype=jnp.int32)
    place = jnp.where(c == 0, place, SIZES[1] - 1 - place)
    first = (((z * SIZES[1] + place) * SIZES[2] + x) * SIZES[3] + c) * own_images

    image_part, own_part, other_part = pair_terms(first.astype(jnp.int32), scalars, images, own, other)
    image_grad = lax.psum_scatter(image_part, AXES, scatter_dimension=0, tiled=True, axis_index_groups=rings)

    text_part = own_part.astype(jnp.float32) + exchanged(other_part).astype(jnp.float32)
    text_part = jnp.sum(parted(text_part.astype(jnp.bfloat16), "x").astype(jnp.float32), axis=0)
    text_grads = parted(text_part.astype(jnp.bfloat16), "z")
    return unit_backward(image_embed, text_embed, image_grad, text_grads)


def solution(mesh):
    split = Mesh(mesh.devices.reshape(SIZES), AXES)
    rows = P(AXES, None)
    return jax.shard_map(
        on_device,
        mesh=split,
        in_specs=(rows, rows, P(), P(), P(AXES)),
        out_specs=(rows, rows),
        check_vma=False,
    )
```

time: 134 us -> 117 us (0.87)
  the two profiles are of different devices: /device:TPU:1 before, /device:TPU:6 now
where the time goes in v7:
time: 117 us; the launch traced here: 116 us
  blocking collectives  68.3 us (58%)
  between operations  15.4 us (13%)
  waiting for transfers between devices  14.9 us (13%)
  Pallas kernels  10.4 us (9%)
  starting transfers between devices  3.91 us (3%)
  local copies, waits for them, and re-layouts  2.42 us (2%)
    all_to_all x2, blocking collectives, spread(): lax.all_to_all(copies, axis, split_axis=0, concat_axis=0, tiled=True)  36 us
    all_to_all x2, blocking collectives, parted(): return lax.all_to_all(parts, axis, split_axis=0, concat_axis=0, tiled=True)  32.4 us
    all_gather x1, waiting for transfers between devices, on_device(): lax.all_gather(units(image_embed), AXES, axis=0, tiled=True, axis_index_g...  6.54 us
    pallas_call x1, Pallas kernels, pair_terms(): pl.pallas_call(pair_kernel, in_specs=[smem, smem, pl.BlockSpec(memory_spa...  6.27 us
    reduce_scatter x1, waiting for transfers between devices, on_device(): lax.psum_scatter(image_part, AXES, scatter_dimension=0, tiled=True, axis_...  5.07 us
    ppermute x2, starting transfers between devices, exchanged(): return lax.ppermute(array, 'c', [(0, 1), (1, 0)])  3.83 us
    ppermute x2, waiting for transfers between devices, exchanged(): return lax.ppermute(array, 'c', [(0, 1), (1, 0)])  3.25 us
    unnamed x8, local copies, waits for them, and re-layouts  2.35 us
  transfers between devices with their start and end apart: 4, of which 4 were waited for; matrix products, arithmetic and copies ran while one was open for 0% of the time, Pallas kernels for 1%

profile of v7, /device:TPU:6, one launch (start us, length us, event | category | flops | bytes accessed | tf_op | source)
XLA Modules:
  0.0 115.9 jit_solution(13725702947826108710)
XLA Ops:
  7.2 0.0 all-gather.2.cloned.1.call-start
  7.2 1.7 %shard_map.68 = bf16[128,768]{1,0:T(8,128)(2,1)} custom-call(bf16[128,768]{1,0:T(8,128)(2,1)} %image_ref.1), custom_call_target="tpu_custom_call" | custom-call | tf_op jit(solution)/shard_map/pallas_call | solution.py:36
  8.9 0.0 all-gather.2.cloned.1.call-update
  9.0 0.0 reduce-scatter.2.cloned.1.call-start
  9.0 1.5 %shard_map.69 = bf16[8,16,896]{2,1,0:T(8,128)(2,1)} custom-call(s32[16]{0:T(128)} %pair_ref.1, bf16[16,768]{1,0:T(8,128)(2,1)} %text_ref.3), custom_call_target="tpu_custom_call" | custom-call | tf_op jit(solution)/shard_map/pallas_call | solution.py:63
  10.6 21.5 %all_to_all.20 = bf16[8,16,896]{2,1,0:T(8,128)(2,1)S(1)} all-to-all(bf16[8,16,896]{2,1,0:T(8,128)(2,1)} %shard_map.69), channel_id=1, replica_groups=mesh['z'=8,'y'=8,'x'=4,'c'=2] {'z'}, dimensions={0} | all-to-all | bytes 458752 | tf_op jit(solution)/shard_map/all_to_all | solution.py:166
  32.0 0.1 broadcast_in_dim.8
  32.1 14.5 %all_to_all.21 = bf16[4,128,896]{2,1,0:T(8,128)(2,1)S(1)} all-to-all(bf16[4,128,896]{2,1,0:T(8,128)(2,1)S(1)} %broadcast_in_dim.8), channel_id=1, replica_groups=mesh['z'=8,'y'=8,'x'=4,'c'=2] {'x'}, dimensions={0} | all-to-all | bytes 1835008 | tf_op jit(solution)/shard_map/all_to_all | solution.py:166
  46.6 1.9 %collective-permute-start = (bf16[512,896]{1,0:T(8,128)(2,1)S(1)}, bf16[512,896]{1,0:T(8,128)(2,1)S(1)}, u32[]{:S(2)}, u32[]{:S(2)}) collective-permute-start(bf16[512,896]{1,0:T(8,128)(2,1)S(1)} %bitcast.4), channel_id=1, source_target_pairs={{0,1},{1,0},{2,3},{3,2},{4,5},{5,4},{6,7},{7,6},{8,9},{9,8},{10,11... | collective-permute-start | bytes 2752520 | tf_op jit(solution)/shard_map/ppermute | solution.py:162
  49.9 0.1 pad_maximum_fusion.scalars_ref
  50.0 1.0 collective-permute-done.other_ref
  51.0 6.5 %all-gather.2.cloned.1.call-done.images_ref = bf16[1024,768]{1,0:T(8,128)(2,1)} async-done(((bf16[128,768]{1,0:T(8,128)(2,1)}), bf16[1024,768]{1,0:T(8,128)(2,1)}) %all-gather.2.cloned.1.call-update) | async-done | bytes 1572880 | tf_op jit(solution)/shard_map/all_gather | solution.py:177
  57.5 0.0 copy-start.3
  57.5 1.4 %copy-done.3 = bf16[1024,768]{1,0:T(8,128)(2,1)S(1)} copy-done((bf16[1024,768]{1,0:T(8,128)(2,1)S(1)}, bf16[1024,768]{1,0:T(8,128)(2,1)}, u32[]{:S(2)}) %copy-start.3) | copy-done | bytes 1572888
  58.9 6.3 %shard_map.70 = (bf16[1024,768]{1,0:T(8,128)(2,1)}, bf16[512,768]{1,0:T(8,128)(2,1)S(1)}, bf16[512,768]{1,0:T(8,128)(2,1)S(1)}) custom-call(s32[8]{0:T(128)S(1)} %add_multiply_fusion.first_ref, f32[3]{0:T(128)S(1)} %pad_maximum_fusion.scalars_ref, bf16[1024,768]{1,0:T(8,128)(2,1)S(1)} %copy-done.3, bf16[512,896]{1,0:T(8,128)(2,1)S(1)} %bitcast.5, ...), custom_call_target="tpu_custom_call" | custom-call | flops 4831838208 | bytes 6291456 | tf_op jit(solution)/shard_map/pallas_call | solution.py:100
  65.2 0.0 reduce-scatter.2.cloned.1.call-update
  65.2 1.9 %collective-permute-start.1 = (bf16[512,768]{1,0:T(8,128)(2,1)S(1)}, bf16[512,768]{1,0:T(8,128)(2,1)S(1)}, u32[]{:S(2)}, u32[]{:S(2)}) collective-permute-start(bf16[512,768]{1,0:T(8,128)(2,1)S(1)} %get-tuple-element.7), channel_id=1, source_target_pairs={{0,1},{1,0},{2,3},{3,2},{4,5},{5,4},{6,7},{7,6},{8,9},{9,8},{10,11... | collective-permute-start | bytes 2359304 | tf_op jit(solution)/shard_map/ppermute | solution.py:162
  67.1 2.3 %collective-permute-done.1 = bf16[512,768]{1,0:T(8,128)(2,1)S(1)} collective-permute-done((bf16[512,768]{1,0:T(8,128)(2,1)S(1)}, bf16[512,768]{1,0:T(8,128)(2,1)S(1)}, u32[]{:S(2)}, u32[]{:S(2)}) %collective-permute-start.1) | collective-permute-done | bytes 786464 | tf_op jit(solution)/shard_map/ppermute | solution.py:162
  69.4 0.2 add_convert_fusion
  69.6 0.0 copy-start
  69.6 0.0 copy-start.2
  69.6 15.3 %all_to_all.22 = bf16[4,128,768]{2,1,0:T(8,128)(2,1)S(1)} all-to-all(bf16[4,128,768]{2,1,0:T(8,128)(2,1)S(1)} %bitcast.6), channel_id=1, replica_groups=mesh['z'=8,'y'=8,'x'=4,'c'=2] {'x'}, dimensions={0} | all-to-all | bytes 1572864 | tf_op jit(solution)/shard_map/all_to_all | solution.py:171
  84.9 0.1 reduce_sum.12
  85.0 17.1 %all_to_all.23.text_grads_ref = bf16[8,16,768]{2,1,0:T(8,128)(2,1)S(1)} all-to-all(bf16[8,16,768]{2,1,0:T(8,128)(2,1)S(1)} %bitcast.8), channel_id=1, replica_groups=mesh['z'=8,'y'=8,'x'=4,'c'=2] {'z'}, dimensions={0} | all-to-all | bytes 393216 | tf_op jit(solution)/shard_map/all_to_all | solution.py:171
  102.1 5.1 %reduce-scatter.2.cloned.1.call-done.image_grad_ref = bf16[128,768]{1,0:T(8,128)(2,1)} async-done(((bf16[1024,768]{1,0:T(8,128)(2,1)}), bf16[128,768]{1,0:T(8,128)(2,1)}) %reduce-scatter.2.cloned.1.call-update) | async-done | bytes 196624 | tf_op jit(solution)/shard_map/reduce_scatter | solution.py:191
  107.2 0.0 copy-done
  107.2 0.0 copy-done.2
  107.2 0.0 copy-start.1
  107.2 0.9 copy-done.1
  108.1 0.9 shard_map.71
  (1 shorter events, 0.0 us)
Async XLA Ops:
  7.2 50.3 %all-gather.2.cloned.1.call-start = ((), (), s32[]{:S(2)}) async-start(), calls=%async_computation.5 | async-start | bytes 1769472 | tf_op jit(solution)/shard_map/all_gather | solution.py:177
  9.0 98.2 %reduce-scatter.2.cloned.1.call-start = ((), (), s32[]{:S(2)}) async-start(), calls=%async_computation.6 | async-start | bytes 1769472 | tf_op jit(solution)/shard_map/reduce_scatter | solution.py:191
  46.6 4.4 %collective-permute-start = (bf16[512,896]{1,0:T(8,128)(2,1)S(1)}, bf16[512,896]{1,0:T(8,128)(2,1)S(1)}, u32[]{:S(2)}, u32[]{:S(2)}) collective-permute-start(bf16[512,896]{1,0:T(8,128)(2,1)S(1)} %bitcast.4), channel_id=1, source_target_pairs={{0,1},{1,0},{2,3},{3,2},{4,5},{5,4},{6,7},{7,6},{8,9},{9,8},{10,11... | collective-permute-start | bytes 2752520 | tf_op jit(solution)/shard_map/ppermute | solution.py:162
  57.5 1.4 %copy-start.3 = (bf16[1024,768]{1,0:T(8,128)(2,1)S(1)}, bf16[1024,768]{1,0:T(8,128)(2,1)}, u32[]{:S(2)}) copy-start(bf16[1024,768]{1,0:T(8,128)(2,1)} %all-gather.2.cloned.1.call-done.images_ref) | copy-start | bytes 4718596
  65.2 4.2 %collective-permute-start.1 = (bf16[512,768]{1,0:T(8,128)(2,1)S(1)}, bf16[512,768]{1,0:T(8,128)(2,1)S(1)}, u32[]{:S(2)}, u32[]{:S(2)}) collective-permute-start(bf16[512,768]{1,0:T(8,128)(2,1)S(1)} %get-tuple-element.7), channel_id=1, source_target_pairs={{0,1},{1,0},{2,3},{3,2},{4,5},{5,4},{6,7},{7,6},{8,9},{9,8},{10,11... | collective-permute-start | bytes 2359304 | tf_op jit(solution)/shard_map/ppermute | solution.py:162
  69.6 37.6 %copy-start = (bf16[128,768]{1,0:T(8,128)(2,1)S(1)}, bf16[128,768]{1,0:T(8,128)(2,1)}, u32[]{:S(2)}) copy-start(bf16[128,768]{1,0:T(8,128)(2,1)} %image_ref.1) | copy-start | bytes 589828
  69.6 37.6 %copy-start.2 = (bf16[16,768]{1,0:T(8,128)(2,1)S(1)}, bf16[16,768]{1,0:T(8,128)(2,1)}, u32[]{:S(2)}) copy-start(bf16[16,768]{1,0:T(8,128)(2,1)} %text_ref.3) | copy-start | bytes 73732
  107.2 0.9 copy-start.1
Sparse Core Ops, SparseCore 0:
  10.7 46.8 all-gather.1
  65.3 41.8 reduce-scatter.1

commit v8 on v7

v8 whole, which is shorter than its diff:
```python
import math

import jax
import jax.numpy as jnp
from jax import lax
from jax.experimental import pallas as pl
from jax.experimental.pallas import tpu as pltpu
from jax.sharding import Mesh
from jax.sharding import PartitionSpec as P

AXES = ("z", "yh", "ym", "yl", "x", "c")
SIZES = (8, 2, 2, 2, 4, 2)
MIDDLE = ("yh", "ym")
LANES = 128
MIB = 1024 * 1024
ROWS_BY_ROWS = (((1,), (1,)), ((), ()))
COLUMNS_BY_ROWS = (((0,), (0,)), ((), ()))

smem = pl.BlockSpec(memory_space=pltpu.SMEM)
vmem = pl.BlockSpec(memory_space=pltpu.VMEM)


def params(mib):
    return pltpu.CompilerParams(vmem_limit_bytes=mib * MIB)


def inverse_norm(floats):
    return lax.rsqrt(jnp.sum(floats * floats, axis=-1, keepdims=True) + 1e-06)


def unit_kernel(pair_ref, image_ref, text_ref, unit_ref, packet_ref):
    floats = image_ref[...].astype(jnp.float32)
    unit_ref[...] = (floats * inverse_norm(floats)).astype(unit_ref.dtype)
    rows, width = text_ref.shape
    floats = text_ref[...].astype(jnp.float32)
    unit = (floats * inverse_norm(floats)).astype(packet_ref.dtype)
    row = lax.broadcasted_iota(jnp.int32, (rows, LANES), 0)
    lane = lax.broadcasted_iota(jnp.int32, (rows, LANES), 1)
    index = jnp.zeros((rows, LANES), jnp.int32)
    for i in range(rows):
        index = jnp.where(row == i, pair_ref[i], index)
    digits = jnp.where(lane == 0, index >> 8, jnp.where(lane == 1, index & 255, 0))
    digits = digits.astype(jnp.float32).astype(packet_ref.dtype)
    for peer in range(packet_ref.shape[0]):
        packet_ref[peer, :, :width] = unit
        packet_ref[peer, :, width:] = digits


def units_and_packets(pair_index, image_embed, text_embed, peers):
    rows, width = text_embed.shape
    return pl.pallas_call(
        unit_kernel,
        in_specs=[smem, vmem, vmem],
        out_specs=[vmem, vmem],
        out_shape=[
            jax.ShapeDtypeStruct(image_embed.shape, jnp.bfloat16),
            jax.ShapeDtypeStruct((peers, rows, width + LANES), jnp.bfloat16),
        ],
        compiler_params=params(56),
    )(pair_index, image_embed, text_embed)


def pair_kernel(chunks, first_ref, scalars_ref, image_ref, *refs):
    chunk_refs, other_ref = refs[:chunks], refs[chunks]
    image_grad_ref, other_grad_ref, text_ref = refs[chunks + 1], refs[chunks + 2], refs[-1]
    own_grad_refs = refs[chunks + 3 : -1]
    rows, width = image_ref.shape
    size = chunk_refs[0].shape[0]
    count = chunks * size
    for i, ref in enumerate(chunk_refs):
        text_ref[i * size : (i + 1) * size, :] = ref[...]
    text_ref[count:, :] = other_ref[...]
    digits = text_ref[:, width:].astype(jnp.float32).T
    pairs = (digits[0:1] * 256.0 + digits[1:2]).astype(jnp.int32)
    row = lax.broadcasted_iota(jnp.int32, (128, 1), 0)
    places = jnp.concatenate([row + first_ref[p] for p in range(rows // 128)], axis=0)
    images = image_ref[...]
    texts = text_ref[:, :width]
    dots = lax.dot_general(images, texts, ROWS_BY_ROWS, preferred_element_type=jnp.float32)
    chance = 1.0 / (1.0 + jnp.exp2(dots * scalars_ref[1] + scalars_ref[2]))
    weight = (scalars_ref[0] * jnp.where(pairs == places, chance - 1.0, chance)).astype(jnp.bfloat16)
    image_grad_ref[...] = jnp.dot(weight, texts, preferred_element_type=jnp.float32).astype(image_grad_ref.dtype)
    text_grad = lax.dot_general(weight, images, COLUMNS_BY_ROWS, preferred_element_type=jnp.float32)
    for i, ref in enumerate(own_grad_refs):
        ref[...] = text_grad[i * size : (i + 1) * size].astype(ref.dtype)
    other_grad_ref[...] = text_grad[count:].astype(other_grad_ref.dtype)


def pair_terms(first, scalars, images, chunks, other):
    rows, width = images.shape
    size, wide = chunks[0].shape
    count = other.shape[0]
    texts = 2 * count
    return pl.pallas_call(
        lambda *refs: pair_kernel(len(chunks), *refs),
        in_specs=[smem, smem] + [vmem] * (len(chunks) + 2),
        out_specs=[vmem] * (len(chunks) + 2),
        out_shape=[
            jax.ShapeDtypeStruct((rows, width), jnp.bfloat16),
            jax.ShapeDtypeStruct((count, width), jnp.bfloat16),
        ]
        + [jax.ShapeDtypeStruct((size, width), jnp.bfloat16)] * len(chunks),
        scratch_shapes=[pltpu.VMEM((texts, wide), jnp.bfloat16)],
        compiler_params=params(32),
        cost_estimate=pl.CostEstimate(
            flops=6 * rows * texts * width, bytes_accessed=4 * (rows + texts) * width, transcendentals=2 * rows * texts
        ),
    )(first, scalars, images, *chunks, other)


def project(embed_ref, grad, out_ref):
    floats = embed_ref[...].astype(jnp.float32)
    inverse = inverse_norm(floats)
    unit = floats * inverse
    along = jnp.sum(unit * grad, axis=-1, keepdims=True)
    out_ref[...] = ((grad - unit * along) * inverse).astype(out_ref.dtype)


def backward_kernel(image_ref, text_ref, image_grad_ref, beside_ref, text_grads_ref, image_out_ref, text_out_ref):
    project(image_ref, image_grad_ref[...] + beside_ref[...].astype(jnp.float32), image_out_ref)
    text_grad = text_grads_ref[0].astype(jnp.float32)
    for part in range(1, text_grads_ref.shape[0]):
        text_grad += text_grads_ref[part].astype(jnp.float32)
    project(text_ref, text_grad, text_out_ref)


def unit_backward(image_embed, text_embed, image_grad, beside, text_grads):
    return pl.pallas_call(
        backward_kernel,
        in_specs=[vmem] * 5,
        out_specs=[vmem] * 2,
        out_shape=[
            jax.ShapeDtypeStruct(image_embed.shape, jnp.bfloat16),
            jax.ShapeDtypeStruct(text_embed.shape, jnp.bfloat16),
        ],
        compiler_params=params(8),
    )(image_embed, text_embed, image_grad, beside, text_grads)


def shifted(array, axis, by):
    devices = lax.axis_size(axis)
    return lax.ppermute(array, axis, [(i, (i + by) % devices) for i in range(devices)])


def spread(copies, axis):
    return lax.all_to_all(copies, axis, split_axis=0, concat_axis=0, tiled=True).reshape(-1, copies.shape[2])


def parted(rows, axis):
    parts = rows.reshape(lax.axis_size(axis), -1, rows.shape[1])
    return lax.all_to_all(parts, axis, split_axis=0, concat_axis=0, tiled=True)


def total(parts):
    return sum(part.astype(jnp.float32) for part in parts)


def on_device(image_embed, text_embed, log_scale, logit_bias, pair_index):
    own_images = image_embed.shape[0]
    own_texts = text_embed.shape[0] * lax.axis_size("z")
    ring, middle = lax.axis_size("x"), lax.axis_size(MIDDLE)
    together = lax.optimization_barrier

    unit, packets = units_and_packets(pair_index, image_embed, text_embed, lax.axis_size("z"))
    texts, beside = together((spread(packets, "z"), shifted(unit, "yl", 1)))
    pair = jnp.concatenate([unit, beside], axis=0)
    copies = jnp.broadcast_to(pair[None], (ring,) + pair.shape)
    images, *chunks = together((spread(copies, "x"), *[shifted(texts, MIDDLE, s) for s in range(1, middle)]))
    chunks = [texts] + chunks
    other = shifted(jnp.concatenate(chunks, axis=0), "c", 1)

    scale = jnp.exp(log_scale)
    scalars = jnp.concatenate([scale, -math.log2(math.e) * scale, -math.log2(math.e) * logit_bias])
    far, yl, c = lax.axis_index(("z",) + MIDDLE), lax.axis_index("yl"), lax.axis_index("c")
    first = jnp.stack(
        [(((far * 2 + place) * ring + x) * 2 + c) * own_images for x in range(ring) for place in (yl, 1 - yl)]
    ).astype(jnp.int32)
    image_part, other_part, *own_parts = pair_terms(first, scalars, images, chunks, other)

    back = shifted(other_part, "c", 1)
    sums = [
        total([part, back[s * own_texts : (s + 1) * own_texts]]).astype(jnp.bfloat16) for s, part in enumerate(own_parts)
    ]
    image_parts, *returned = together(
        (parted(image_part, "x"), *[shifted(sums[s], MIDDLE, -s) for s in range(1, middle)])
    )
    text_part = total([sums[0]] + returned).astype(jnp.bfloat16)
    image_total = jnp.sum(image_parts.astype(jnp.float32), axis=0)
    image_own, image_beside = image_total[:own_images], image_total[own_images:].astype(jnp.bfloat16)
    text_part, image_beside = together((text_part, image_beside))
    text_grads, beside = together((parted(text_part, "z"), shifted(image_beside, "yl", 1)))
    return unit_backward(image_embed, text_embed, image_own, beside, text_grads)


def solution(mesh):
    split = Mesh(mesh.devices.reshape(SIZES), AXES)
    rows = P(AXES, None)
    return jax.shard_map(
        on_device,
        mesh=split,
        in_specs=(rows, rows, P(), P(), P(AXES)),
        out_specs=(rows, rows),
        check_vma=False,
    )
```

time: 117 us -> 128 us (1.094)
  blocking collectives: 68.3 us -> 0 us
  starting transfers between devices: 3.91 us -> 67.1 us
  waiting for transfers between devices: 14.9 us -> 40.6 us
  between operations: 15.4 us -> 2.16 us
  other arithmetic: 0.43 us -> 4.23 us
    all_to_all x4 -> x0, blocking collectives: 68.3 us -> none  [the longest x2 36 us: spread(): lax.all_to_all(copies, axis, split_axis=0, concat_axis=0, tiled=True)]
    ppermute x2 -> x10, starting transfers between devices: 3.83 us -> 43 us  [shifted(): lax.ppermute(array, axis, [(i, (i + by) % devices) for i in range(devices)])]
    ppermute x2 -> x10, waiting for transfers between devices: 3.25 us -> 35.6 us  [shifted(): lax.ppermute(array, axis, [(i, (i + by) % devices) for i in range(devices)])]
    all_to_all x0 -> x4, starting transfers between devices: none -> 24.1 us  [the longest x2 15.1 us: spread(): lax.all_to_all(copies, axis, split_axis=0, concat_axis=0, tiled=True)]
    all_gather x1 -> x0, waiting for transfers between devices: 6.54 us -> none  [on_device(): lax.all_gather(units(image_embed), AXES, axis=0, tiled=True, axis_index_g...]
    reduce_scatter x1 -> x0, waiting for transfers between devices: 5.07 us -> none  [on_device(): lax.psum_scatter(image_part, AXES, scatter_dimension=0, tiled=True, axis_...]
    all_to_all x0 -> x4, waiting for transfers between devices: none -> 4.95 us  [the longest x2 2.72 us: spread(): lax.all_to_all(copies, axis, split_axis=0, concat_axis=0, tiled=True)]
    concatenate x0 -> x2, other arithmetic: none -> 1.97 us  [the longest x1 1.02 us: on_device(): other = shifted(jnp.concatenate(chunks, axis=0), 'c', 1)]
  transfers between devices with their start and end apart: 4 -> 14, of which waited for: 4 -> 9; matrix products, arithmetic and copies ran while one was open for 0% -> 0% of each run, Pallas kernels for 1% -> 0%
where the time goes in v8:
time: 128 us; the launch traced here: 127 us
  starting transfers between devices  67.1 us (52%)
  waiting for transfers between devices  40.6 us (32%)
  Pallas kernels  10.5 us (8%)
  other arithmetic  4.23 us (3%)
  local copies, waits for them, and re-layouts  2.86 us (2%)
  between operations  2.16 us (2%)
    ppermute x10, starting transfers between devices, shifted(): lax.ppermute(array, axis, [(i, (i + by) % devices) for i in range(devices)])  43 us
    ppermute x10, waiting for transfers between devices, shifted(): lax.ppermute(array, axis, [(i, (i + by) % devices) for i in range(devices)])  35.6 us
    all_to_all x2, starting transfers between devices, spread(): lax.all_to_all(copies, axis, split_axis=0, concat_axis=0, tiled=True)  15.1 us
    all_to_all x2, starting transfers between devices, parted(): return lax.all_to_all(parts, axis, split_axis=0, concat_axis=0, tiled=True)  9.06 us
    pallas_call x1, Pallas kernels, pair_terms(): pl.pallas_call(lambda *refs: pair_kernel(len(chunks), *refs), in_specs=[s...  7.79 us
    all_to_all x2, waiting for transfers between devices, spread(): lax.all_to_all(copies, axis, split_axis=0, concat_axis=0, tiled=True)  2.72 us
  transfers between devices with their start and end apart: 14, of which 9 were waited for; matrix products, arithmetic and copies ran while one was open for 0% of the time, Pallas kernels for 0%

profile of v8, /device:TPU:6, one launch (start us, length us, event | category | flops | bytes accessed | tf_op | source)
XLA Modules:
  0.0 127.5 jit_solution(1863408429628594896)
XLA Ops:
  0.6 1.8 %shard_map.68 = (bf16[128,768]{1,0:T(8,128)(2,1)}, bf16[8,16,896]{2,1,0:T(8,128)(2,1)}) custom-call(s32[16]{0:T(128)} %pair_ref.1, bf16[128,768]{1,0:T(8,128)(2,1)} %image_ref.3, bf16[16,768]{1,0:T(8,128)(2,1)} %text_ref.3), custom_call_target="tpu_custom_call" | custom-call | tf_op jit(solution)/shard_map/pallas_call | solution.py:51
  2.4 10.3 %all-to-all-start = ((bf16[8,16,896]{2,1,0:T(8,128)(2,1)}), bf16[8,16,896]{2,1,0:T(8,128)(2,1)S(1)}, u32[]{:S(2)}, u32[]{:S(2)}) async-start(bf16[8,16,896]{2,1,0:T(8,128)(2,1)} %get-tuple-element.25), calls=%async_computation | async-start | bytes 458752 | tf_op jit(solution)/shard_map/all_to_all | solution.py:146
  12.8 3.5 %collective-permute-start = (bf16[128,768]{1,0:T(8,128)(2,1)}, bf16[128,768]{1,0:T(8,128)(2,1)S(1)}, u32[]{:S(2)}, u32[]{:S(2)}) collective-permute-start(bf16[128,768]{1,0:T(8,128)(2,1)} %get-tuple-element.24), channel_id=1, source_target_pairs={{0,8},{8,0},{1,9},{9,1},{2,10},{10,2},{3,11},{11,3},{4,12},{12,4},... | collective-permute-start | bytes 589832 | tf_op jit(solution)/shard_map/ppermute | solution.py:142
  16.2 5.0 %collective-permute-done = bf16[128,768]{1,0:T(8,128)(2,1)S(1)} collective-permute-done((bf16[128,768]{1,0:T(8,128)(2,1)}, bf16[128,768]{1,0:T(8,128)(2,1)S(1)}, u32[]{:S(2)}, u32[]{:S(2)}) %collective-permute-start) | collective-permute-done | bytes 196640 | tf_op jit(solution)/shard_map/ppermute | solution.py:142
  21.2 2.7 %all-to-all-done = bf16[8,16,896]{2,1,0:T(8,128)(2,1)S(1)} async-done(((bf16[8,16,896]{2,1,0:T(8,128)(2,1)}), bf16[8,16,896]{2,1,0:T(8,128)(2,1)S(1)}, u32[]{:S(2)}, u32[]{:S(2)}) %all-to-all-start) | async-done | bytes 229408 | tf_op jit(solution)/shard_map/all_to_all | solution.py:146
  23.9 1.0 pad_maximum_fusion.1
  24.9 1.3 broadcast_in_dim.2
  26.2 4.8 %all-to-all-start.1 = ((bf16[4,256,768]{2,1,0:T(8,128)(2,1)}), bf16[4,256,768]{2,1,0:T(8,128)(2,1)S(1)}, u32[]{:S(2)}, u32[]{:S(2)}) async-start(bf16[4,256,768]{2,1,0:T(8,128)(2,1)} %broadcast_in_dim.2), calls=%async_computation.1 | async-start | bytes 3145728 | tf_op jit(solution)/shard_map/all_to_all | solution.py:146
  30.9 6.2 %collective-permute-start.3 = (bf16[128,896]{1,0:T(8,128)(2,1)S(1)}, bf16[128,896]{1,0:T(8,128)(2,1)S(1)}, u32[]{:S(2)}, u32[]{:S(2)}) collective-permute-start(bf16[128,896]{1,0:T(8,128)(2,1)S(1)} %bitcast.13), channel_id=1, source_target_pairs={{0,48},{16,0},{32,16},{48,32},{1,49},{17,1},{33,17},{49,33},{2,50}... | collective-permute-start | bytes 688136 | tf_op jit(solution)/shard_map/ppermute | solution.py:142
  37.1 3.8 %collective-permute-start.2 = (bf16[128,896]{1,0:T(8,128)(2,1)S(1)}, bf16[128,896]{1,0:T(8,128)(2,1)S(1)}, u32[]{:S(2)}, u32[]{:S(2)}) collective-permute-start(bf16[128,896]{1,0:T(8,128)(2,1)S(1)} %bitcast.14), channel_id=1, source_target_pairs={{0,32},{16,48},{32,0},{48,16},{1,33},{17,49},{33,1},{49,17},{2,34}... | collective-permute-start | bytes 688136 | tf_op jit(solution)/shard_map/ppermute | solution.py:142
  40.9 4.5 %collective-permute-start.1 = (bf16[128,896]{1,0:T(8,128)(2,1)S(1)}, bf16[128,896]{1,0:T(8,128)(2,1)S(1)}, u32[]{:S(2)}, u32[]{:S(2)}) collective-permute-start(bf16[128,896]{1,0:T(8,128)(2,1)S(1)} %bitcast.15), channel_id=1, source_target_pairs={{0,16},{16,32},{32,48},{48,0},{1,17},{17,33},{33,49},{49,1},{2,18}... | collective-permute-start | bytes 688136 | tf_op jit(solution)/shard_map/ppermute | solution.py:142
  45.4 9.0 %collective-permute-done.3.refs_6_ = bf16[128,896]{1,0:T(8,128)(2,1)S(1)} collective-permute-done((bf16[128,896]{1,0:T(8,128)(2,1)S(1)}, bf16[128,896]{1,0:T(8,128)(2,1)S(1)}, u32[]{:S(2)}, u32[]{:S(2)}) %collective-permute-start.3) | collective-permute-done | bytes 229408 | tf_op jit(solution)/shard_map/ppermute | solution.py:142
  54.4 0.0 collective-permute-done.2.refs_5_
  54.4 0.8 collective-permute-done.1.refs_4_
  55.2 0.0 all-to-all-done.1
  55.2 1.0 pad_maximum_fusion
  56.2 1.9 %collective-permute-start.4 = (bf16[512,896]{1,0:T(8,128)(2,1)}, bf16[512,896]{1,0:T(8,128)(2,1)}, u32[]{:S(2)}, u32[]{:S(2)}) collective-permute-start(bf16[512,896]{1,0:T(8,128)(2,1)} %pad_maximum_fusion), channel_id=1, source_target_pairs={{0,1},{1,0},{2,3},{3,2},{4,5},{5,4},{6,7},{7,6},{8,9},{9,8},{10,11... | collective-permute-start | bytes 2752520 | tf_op jit(solution)/shard_map/ppermute | solution.py:142
  59.5 0.1 stack.35.refs_0_
  59.6 0.1 pad_maximum_fusion.2.refs_1_
  59.7 1.3 collective-permute-done.4.refs_7_
  60.9 7.8 %shard_map.69 = (bf16[1024,768]{1,0:T(8,128)(2,1)}, bf16[512,768]{1,0:T(8,128)(2,1)}, bf16[128,768]{1,0:T(8,128)(2,1)S(1)}, bf16[128,768]{1,0:T(8,128)(2,1)S(1)}...) custom-call(s32[8]{0:T(128)S(1)} %stack.35.refs_0_, f32[3]{0:T(128)S(1)} %pad_maximum_fusion.2.refs_1_, ...), custom_call_target="tpu_custom_call" | custom-call | flops 4831838208 | bytes 6291456 | tf_op jit(solution)/shard_map/pallas_call | solution.py:94
  68.7 2.0 %collective-permute-start.5 = (bf16[512,768]{1,0:T(8,128)(2,1)}, bf16[512,768]{1,0:T(8,128)(2,1)S(1)}, u32[]{:S(2)}, u32[]{:S(2)}) collective-permute-start(bf16[512,768]{1,0:T(8,128)(2,1)} %get-tuple-element.34), channel_id=1, source_target_pairs={{0,1},{1,0},{2,3},{3,2},{4,5},{5,4},{6,7},{7,6},{8,9},{9,8},{10,11... | collective-permute-start | bytes 2359304 | tf_op jit(solution)/shard_map/ppermute | solution.py:142
  70.8 4.8 %all-to-all-start.2 = ((bf16[4,256,768]{2,1,0:T(8,128)(2,1)}), bf16[4,256,768]{2,1,0:T(8,128)(2,1)S(1)}, u32[]{:S(2)}, u32[]{:S(2)}) async-start(bf16[4,256,768]{2,1,0:T(8,128)(2,1)} %bitcast.10), calls=%async_computation.2 | async-start | bytes 3145728 | tf_op jit(solution)/shard_map/all_to_all | solution.py:151
  75.6 0.0 collective-permute-done.5
  75.6 0.0 copy-start.2
  75.6 0.1 add_convert_fusion.2
  75.7 6.4 %collective-permute-start.8 = (bf16[128,768]{1,0:T(8,128)(2,1)S(1)}, bf16[128,768]{1,0:T(8,128)(2,1)S(1)}, u32[]{:S(2)}, u32[]{:S(2)}) collective-permute-start(bf16[128,768]{1,0:T(8,128)(2,1)S(1)} %get-tuple-element.46), channel_id=1, source_target_pairs={{0,16},{16,32},{32,48},{48,0},{1,17},{17,33},{33,49},{49,1},{2,18}... | collective-permute-start | bytes 589832 | tf_op jit(solution)/shard_map/ppermute | solution.py:142
  82.1 6.8 %collective-permute-start.7 = (bf16[128,768]{1,0:T(8,128)(2,1)S(1)}, bf16[128,768]{1,0:T(8,128)(2,1)S(1)}, u32[]{:S(2)}, u32[]{:S(2)}) collective-permute-start(bf16[128,768]{1,0:T(8,128)(2,1)S(1)} %get-tuple-element.47), channel_id=1, source_target_pairs={{0,32},{16,48},{32,0},{48,16},{1,33},{17,49},{33,1},{49,17},{2,34}... | collective-permute-start | bytes 589832 | tf_op jit(solution)/shard_map/ppermute | solution.py:142
  88.9 6.0 %collective-permute-start.6 = (bf16[128,768]{1,0:T(8,128)(2,1)S(1)}, bf16[128,768]{1,0:T(8,128)(2,1)}, u32[]{:S(2)}, u32[]{:S(2)}) collective-permute-start(bf16[128,768]{1,0:T(8,128)(2,1)S(1)} %get-tuple-element.48), channel_id=1, source_target_pairs={{0,48},{16,0},{32,16},{48,32},{1,49},{17,1},{33,17},{49,33},{2,50}... | collective-permute-start | bytes 589832 | tf_op jit(solution)/shard_map/ppermute | solution.py:142
  95.0 0.0 collective-permute-done.8
  95.0 0.0 copy-start.3
  95.0 5.3 %collective-permute-done.7 = bf16[128,768]{1,0:T(8,128)(2,1)S(1)} collective-permute-done((bf16[128,768]{1,0:T(8,128)(2,1)S(1)}, bf16[128,768]{1,0:T(8,128)(2,1)S(1)}, u32[]{:S(2)}, u32[]{:S(2)}) %collective-permute-start.7) | collective-permute-done | bytes 196640 | tf_op jit(solution)/shard_map/ppermute | solution.py:142
  100.3 0.0 copy-done.3
  100.3 0.0 copy-start.5
  100.3 0.7 copy-done.5
  101.0 7.8 %collective-permute-done.6 = bf16[128,768]{1,0:T(8,128)(2,1)} collective-permute-done((bf16[128,768]{1,0:T(8,128)(2,1)S(1)}, bf16[128,768]{1,0:T(8,128)(2,1)}, u32[]{:S(2)}, u32[]{:S(2)}) %collective-permute-start.6) | collective-permute-done | bytes 196640 | tf_op jit(solution)/shard_map/ppermute | solution.py:142
  108.8 0.0 copy-done.2
  108.8 0.0 all-to-all-done.2
  108.8 0.0 copy-start.4
  108.8 0.0 copy-start.6
  108.8 0.2 convert_reduce_fusion
  109.1 0.0 copy-start
  109.1 0.0 copy-start.1
  109.1 0.6 copy-done.4
  109.7 0.1 copy-done.6
  109.8 1.8 %add_convert_fusion = bf16[128,768]{1,0:T(8,128)(2,1)} fusion(bf16[128,768]{1,0:T(8,128)(2,1)S(1)} %copy-done.4, bf16[128,768]{1,0:T(8,128)(2,1)S(1)} %copy-done.6, bf16[128,768]{1,0:T(8,128)(2,1)} %collective-permute-done.6, bf16[128,768]{1,0:T(8,128)(2,1)S(1)} %get-tuple-element.38, bf16[512,768]{1,0:T(8,128)(2,1)} %copy-done.2), kind=kLoop, calls=%fused_computation.4 | loop fusion | flops 1179648 | bytes 1179648 | tf_op jit(solution)/shard_map/convert_element_type | solution.py:187
  111.7 4.2 %all-to-all-start.3 = ((bf16[8,16,768]{2,1,0:T(8,128)(2,1)}), bf16[8,16,768]{2,1,0:T(8,128)(2,1)S(1)}, u32[]{:S(2)}, u32[]{:S(2)}) async-start(bf16[8,16,768]{2,1,0:T(8,128)(2,1)} %bitcast.11), calls=%async_computation.3 | async-start | bytes 393216 | tf_op jit(solution)/shard_map/all_to_all | solution.py:151
  115.9 1.9 %collective-permute-start.9 = (bf16[128,768]{1,0:T(8,128)(2,1)S(1)}, bf16[128,768]{1,0:T(8,128)(2,1)S(1)}, u32[]{:S(2)}, u32[]{:S(2)}) collective-permute-start(bf16[128,768]{1,0:T(8,128)(2,1)S(1)} %slice.36), channel_id=1, source_target_pairs={{0,8},{8,0},{1,9},{9,1},{2,10},{10,2},{3,11},{11,3},{4,12},{12,4},... | collective-permute-start | bytes 589832 | tf_op jit(solution)/shard_map/ppermute | solution.py:142
  117.9 6.5 %collective-permute-done.9.beside_ref = bf16[128,768]{1,0:T(8,128)(2,1)S(1)} collective-permute-done((bf16[128,768]{1,0:T(8,128)(2,1)S(1)}, bf16[128,768]{1,0:T(8,128)(2,1)S(1)}, u32[]{:S(2)}, u32[]{:S(2)}) %collective-permute-start.9) | collective-permute-done | bytes 196640 | tf_op jit(solution)/shard_map/ppermute | solution.py:142
  124.4 2.2 %all-to-all-done.3.text_grads_ref = bf16[8,16,768]{2,1,0:T(8,128)(2,1)S(1)} async-done(((bf16[8,16,768]{2,1,0:T(8,128)(2,1)}), bf16[8,16,768]{2,1,0:T(8,128)(2,1)S(1)}, u32[]{:S(2)}, u32[]{:S(2)}) %all-to-all-start.3) | async-done | bytes 196640 | tf_op jit(solution)/shard_map/all_to_all | solution.py:151
  126.6 0.0 copy-done
  126.6 0.0 copy-done.1
  126.6 0.9 shard_map.70
  (2 shorter events, 0.1 us)
Async XLA Ops:
  2.4 21.5 %all-to-all-start = ((bf16[8,16,896]{2,1,0:T(8,128)(2,1)}), bf16[8,16,896]{2,1,0:T(8,128)(2,1)S(1)}, u32[]{:S(2)}, u32[]{:S(2)}) async-start(bf16[8,16,896]{2,1,0:T(8,128)(2,1)} %get-tuple-element.25), calls=%async_computation | async-start | bytes 458752 | tf_op jit(solution)/shard_map/all_to_all | solution.py:146
  12.8 8.5 %collective-permute-start = (bf16[128,768]{1,0:T(8,128)(2,1)}, bf16[128,768]{1,0:T(8,128)(2,1)S(1)}, u32[]{:S(2)}, u32[]{:S(2)}) collective-permute-start(bf16[128,768]{1,0:T(8,128)(2,1)} %get-tuple-element.24), channel_id=1, source_target_pairs={{0,8},{8,0},{1,9},{9,1},{2,10},{10,2},{3,11},{11,3},{4,12},{12,4},... | collective-permute-start | bytes 589832 | tf_op jit(solution)/shard_map/ppermute | solution.py:142
  26.2 29.1 %all-to-all-start.1 = ((bf16[4,256,768]{2,1,0:T(8,128)(2,1)}), bf16[4,256,768]{2,1,0:T(8,128)(2,1)S(1)}, u32[]{:S(2)}, u32[]{:S(2)}) async-start(bf16[4,256,768]{2,1,0:T(8,128)(2,1)} %broadcast_in_dim.2), calls=%async_computation.1 | async-start | bytes 3145728 | tf_op jit(solution)/shard_map/all_to_all | solution.py:146
  30.9 23.5 %collective-permute-start.3 = (bf16[128,896]{1,0:T(8,128)(2,1)S(1)}, bf16[128,896]{1,0:T(8,128)(2,1)S(1)}, u32[]{:S(2)}, u32[]{:S(2)}) collective-permute-start(bf16[128,896]{1,0:T(8,128)(2,1)S(1)} %bitcast.13), channel_id=1, source_target_pairs={{0,48},{16,0},{32,16},{48,32},{1,49},{17,1},{33,17},{49,33},{2,50}... | collective-permute-start | bytes 688136 | tf_op jit(solution)/shard_map/ppermute | solution.py:142
  37.1 17.4 %collective-permute-start.2 = (bf16[128,896]{1,0:T(8,128)(2,1)S(1)}, bf16[128,896]{1,0:T(8,128)(2,1)S(1)}, u32[]{:S(2)}, u32[]{:S(2)}) collective-permute-start(bf16[128,896]{1,0:T(8,128)(2,1)S(1)} %bitcast.14), channel_id=1, source_target_pairs={{0,32},{16,48},{32,0},{48,16},{1,33},{17,49},{33,1},{49,17},{2,34}... | collective-permute-start | bytes 688136 | tf_op jit(solution)/shard_map/ppermute | solution.py:142
  40.9 14.3 %collective-permute-start.1 = (bf16[128,896]{1,0:T(8,128)(2,1)S(1)}, bf16[128,896]{1,0:T(8,128)(2,1)S(1)}, u32[]{:S(2)}, u32[]{:S(2)}) collective-permute-start(bf16[128,896]{1,0:T(8,128)(2,1)S(1)} %bitcast.15), channel_id=1, source_target_pairs={{0,16},{16,32},{32,48},{48,0},{1,17},{17,33},{33,49},{49,1},{2,18}... | collective-permute-start | bytes 688136 | tf_op jit(solution)/shard_map/ppermute | solution.py:142
  56.2 4.7 %collective-permute-start.4 = (bf16[512,896]{1,0:T(8,128)(2,1)}, bf16[512,896]{1,0:T(8,128)(2,1)}, u32[]{:S(2)}, u32[]{:S(2)}) collective-permute-start(bf16[512,896]{1,0:T(8,128)(2,1)} %pad_maximum_fusion), channel_id=1, source_target_pairs={{0,1},{1,0},{2,3},{3,2},{4,5},{5,4},{6,7},{7,6},{8,9},{9,8},{10,11... | collective-permute-start | bytes 2752520 | tf_op jit(solution)/shard_map/ppermute | solution.py:142
  68.7 6.9 %collective-permute-start.5 = (bf16[512,768]{1,0:T(8,128)(2,1)}, bf16[512,768]{1,0:T(8,128)(2,1)S(1)}, u32[]{:S(2)}, u32[]{:S(2)}) collective-permute-start(bf16[512,768]{1,0:T(8,128)(2,1)} %get-tuple-element.34), channel_id=1, source_target_pairs={{0,1},{1,0},{2,3},{3,2},{4,5},{5,4},{6,7},{7,6},{8,9},{9,8},{10,11... | collective-permute-start | bytes 2359304 | tf_op jit(solution)/shard_map/ppermute | solution.py:142
  70.8 38.0 %all-to-all-start.2 = ((bf16[4,256,768]{2,1,0:T(8,128)(2,1)}), bf16[4,256,768]{2,1,0:T(8,128)(2,1)S(1)}, u32[]{:S(2)}, u32[]{:S(2)}) async-start(bf16[4,256,768]{2,1,0:T(8,128)(2,1)} %bitcast.10), calls=%async_computation.2 | async-start | bytes 3145728 | tf_op jit(solution)/shard_map/all_to_all | solution.py:151
  75.6 33.2 %copy-start.2 = (bf16[512,768]{1,0:T(8,128)(2,1)}, bf16[512,768]{1,0:T(8,128)(2,1)S(1)}, u32[]{:S(2)}) copy-start(bf16[512,768]{1,0:T(8,128)(2,1)S(1)} %collective-permute-done.5) | copy-start | bytes 2359300
  75.7 19.2 %collective-permute-start.8 = (bf16[128,768]{1,0:T(8,128)(2,1)S(1)}, bf16[128,768]{1,0:T(8,128)(2,1)S(1)}, u32[]{:S(2)}, u32[]{:S(2)}) collective-permute-start(bf16[128,768]{1,0:T(8,128)(2,1)S(1)} %get-tuple-element.46), channel_id=1, source_target_pairs={{0,16},{16,32},{32,48},{48,0},{1,17},{17,33},{33,49},{49,1},{2,18}... | collective-permute-start | bytes 589832 | tf_op jit(solution)/shard_map/ppermute | solution.py:142
  82.1 18.2 %collective-permute-start.7 = (bf16[128,768]{1,0:T(8,128)(2,1)S(1)}, bf16[128,768]{1,0:T(8,128)(2,1)S(1)}, u32[]{:S(2)}, u32[]{:S(2)}) collective-permute-start(bf16[128,768]{1,0:T(8,128)(2,1)S(1)} %get-tuple-element.47), channel_id=1, source_target_pairs={{0,32},{16,48},{32,0},{48,16},{1,33},{17,49},{33,1},{49,17},{2,34}... | collective-permute-start | bytes 589832 | tf_op jit(solution)/shard_map/ppermute | solution.py:142
  88.9 19.9 %collective-permute-start.6 = (bf16[128,768]{1,0:T(8,128)(2,1)S(1)}, bf16[128,768]{1,0:T(8,128)(2,1)}, u32[]{:S(2)}, u32[]{:S(2)}) collective-permute-start(bf16[128,768]{1,0:T(8,128)(2,1)S(1)} %get-tuple-element.48), channel_id=1, source_target_pairs={{0,48},{16,0},{32,16},{48,32},{1,49},{17,1},{33,17},{49,33},{2,50}... | collective-permute-start | bytes 589832 | tf_op jit(solution)/shard_map/ppermute | solution.py:142
  95.0 5.3 %copy-start.3 = (bf16[128,768]{1,0:T(8,128)(2,1)}, bf16[128,768]{1,0:T(8,128)(2,1)S(1)}, u32[]{:S(2)}) copy-start(bf16[128,768]{1,0:T(8,128)(2,1)S(1)} %collective-permute-done.8) | copy-start | bytes 589828
  100.3 0.7 copy-start.5
  108.8 0.9 copy-start.4
  108.8 1.0 copy-start.6
  109.1 17.5 %copy-start = (bf16[128,768]{1,0:T(8,128)(2,1)S(1)}, bf16[128,768]{1,0:T(8,128)(2,1)}, u32[]{:S(2)}) copy-start(bf16[128,768]{1,0:T(8,128)(2,1)} %image_ref.3) | copy-start | bytes 589828
  109.1 17.5 %copy-start.1 = (bf16[16,768]{1,0:T(8,128)(2,1)S(1)}, bf16[16,768]{1,0:T(8,128)(2,1)}, u32[]{:S(2)}) copy-start(bf16[16,768]{1,0:T(8,128)(2,1)} %text_ref.3) | copy-start | bytes 73732
  111.7 14.9 %all-to-all-start.3 = ((bf16[8,16,768]{2,1,0:T(8,128)(2,1)}), bf16[8,16,768]{2,1,0:T(8,128)(2,1)S(1)}, u32[]{:S(2)}, u32[]{:S(2)}) async-start(bf16[8,16,768]{2,1,0:T(8,128)(2,1)} %bitcast.11), calls=%async_computation.3 | async-start | bytes 393216 | tf_op jit(solution)/shard_map/all_to_all | solution.py:151
  115.9 8.4 %collective-permute-start.9 = (bf16[128,768]{1,0:T(8,128)(2,1)S(1)}, bf16[128,768]{1,0:T(8,128)(2,1)S(1)}, u32[]{:S(2)}, u32[]{:S(2)}) collective-permute-start(bf16[128,768]{1,0:T(8,128)(2,1)S(1)} %slice.36), channel_id=1, source_target_pairs={{0,8},{8,0},{1,9},{9,1},{2,10},{10,2},{3,11},{11,3},{4,12},{12,4},... | collective-permute-start | bytes 589832 | tf_op jit(solution)/shard_map/ppermute | solution.py:142

commit v9 on v7

--- a/solution.py
+++ b/solution.py
@@ -25,21 +25,6 @@
 
 def inverse_norm(floats):
     return lax.rsqrt(jnp.sum(floats * floats, axis=-1, keepdims=True) + 1e-06)
-
-
-def unit_kernel(embed_ref, unit_ref):
-    floats = embed_ref[...].astype(jnp.float32)
-    unit_ref[...] = (floats * inverse_norm(floats)).astype(unit_ref.dtype)
-
-
-def units(embed):
-    return pl.pallas_call(
-        unit_kernel,
-        in_specs=[vmem],
-        out_specs=vmem,
-        out_shape=jax.ShapeDtypeStruct(embed.shape, jnp.bfloat16),
-        compiler_params=params(56),
-    )(embed)
 
 
 def packet_kernel(pair_ref, text_ref, packet_ref):
@@ -69,10 +54,8 @@
     )(pair_index, embed)
 
 
-def pair_kernel(first_ref, scalars_ref, images_ref, own_ref, other_ref, *refs):
-    image_grad_ref, own_grad_ref, other_grad_ref, image_ref, text_ref, sem = refs
-    copy = pltpu.make_async_copy(images_ref, image_ref, sem)
-    copy.start()
+def weight_kernel(first_ref, scalars_ref, image_ref, own_ref, other_ref, *refs):
+    image_grad_ref, weight_ref, unit_ref, text_ref = refs
     width = image_ref.shape[1]
     count = own_ref.shape[0]
     text_ref[:count, :] = own_ref[...]
@@ -82,40 +65,57 @@
     row = lax.broadcasted_iota(jnp.int32, (128, 1), 0)
     rows = jnp.concatenate([row + first_ref[p] for p in range(image_ref.shape[0] // 128)], axis=0)
     texts = text_ref[:, :width]
-    copy.wait()
-    images = image_ref[...]
+    floats = image_ref[...].astype(jnp.float32)
+    images = (floats * inverse_norm(floats)).astype(unit_ref.dtype)
+    unit_ref[...] = images
     dots = lax.dot_general(images, texts, ROWS_BY_ROWS, preferred_element_type=jnp.float32)
     chance = 1.0 / (1.0 + jnp.exp2(dots * scalars_ref[1] + scalars_ref[2]))
     weight = (scalars_ref[0] * jnp.where(pairs == rows, chance - 1.0, chance)).astype(jnp.bfloat16)
+    weight_ref[...] = weight
     image_grad_ref[...] = jnp.dot(weight, texts, preferred_element_type=jnp.float32).astype(image_grad_ref.dtype)
-    text_grad = lax.dot_general(weight, images, COLUMNS_BY_ROWS, preferred_element_type=jnp.float32)
-    own_grad_ref[...] = text_grad[:count].astype(own_grad_ref.dtype)
-    other_grad_ref[...] = text_grad[count:].astype(other_grad_ref.dtype)
-
-
-def pair_terms(first, scalars, images, own, other):
+
+
+def weights_and_image_terms(first, scalars, images, own, other):
     rows, width = images.shape
     count, wide = own.shape
     texts = 2 * count
     return pl.pallas_call(
-        pair_kernel,
-        in_specs=[smem, smem, pl.BlockSpec(memory_space=pl.ANY), vmem, vmem],
+        weight_kernel,
+        in_specs=[smem, smem, vmem, vmem, vmem],
         out_specs=[vmem] * 3,
         out_shape=[
             jax.ShapeDtypeStruct((rows, width), jnp.bfloat16),
-            jax.ShapeDtypeStruct((count, width), jnp.bfloat16),
-            jax.ShapeDtypeStruct((count, width), jnp.bfloat16),
+            jax.ShapeDtypeStruct((rows, texts), jnp.bfloat16),
+            jax.ShapeDtypeStruct((rows, width), jnp.bfloat16),
         ],
-        scratch_shapes=[
-            pltpu.VMEM((rows, width), jnp.bfloat16),
-            pltpu.VMEM((texts, wide), jnp.bfloat16),
-            pltpu.SemaphoreType.DMA,
-        ],
+        scratch_shapes=[pltpu.VMEM((texts, wide), jnp.bfloat16)],
         compiler_params=params(32),
         cost_estimate=pl.CostEstimate(
-            flops=6 * rows * texts * width, bytes_accessed=4 * (rows + texts) * width, transcendentals=2 * rows * texts
+            flops=4 * rows * texts * width, bytes_accessed=4 * (rows + texts) * width, transcendentals=2 * rows * texts
         ),
     )(first, scalars, images, own, other)
+
+
+def text_kernel(weight_ref, unit_ref, own_grad_ref, other_grad_ref):
+    count = own_grad_ref.shape[0]
+    grad = lax.dot_general(weight_ref[...], unit_ref[...], COLUMNS_BY_ROWS, preferred_element_type=jnp.float32)
+    own_grad_ref[...] = grad[:count].astype(own_grad_ref.dtype)
+    other_grad_ref[...] = grad[count:].astype(other_grad_ref.dtype)
+
+
+def text_terms(weights, units):
+    rows, texts = weights.shape
+    width = units.shape[1]
+    return pl.pallas_call(
+        text_kernel,
+        in_specs=[vmem] * 2,
+        out_specs=[vmem] * 2,
+        out_shape=[jax.ShapeDtypeStruct((texts // 2, width), jnp.bfloat16)] * 2,
+        compiler_params=params(24),
+        cost_estimate=pl.CostEstimate(
+            flops=2 * rows * texts * width, bytes_accessed=2 * (rows + texts) * width, transcendentals=0
+        ),
+    )(weights, units)
 
 
 def project(embed_ref, grad, out_ref):
@@ -174,7 +174,7 @@
 def on_device(image_embed, text_embed, log_scale, logit_bias, pair_index):
     own_images = image_embed.shape[0]
     rings = image_rings()
-    images = lax.all_gather(units(image_embed), AXES, axis=0, tiled=True, axis_index_groups=rings)
+    images = lax.all_gather(image_embed, AXES, axis=0, tiled=True, axis_index_groups=rings)
 
     texts = spread(text_packets(pair_index, text_embed, lax.axis_size("z")), "z")
     own = spread(jnp.broadcast_to(texts[None], (lax.axis_size("x"),) + texts.shape), "x")
@@ -187,9 +187,10 @@
     place = jnp.where(c == 0, place, SIZES[1] - 1 - place)
     first = (((z * SIZES[1] + place) * SIZES[2] + x) * SIZES[3] + c) * own_images
 
-    image_part, own_part, other_part = pair_terms(first.astype(jnp.int32), scalars, images, own, other)
+    image_part, weights, units = weights_and_image_terms(first.astype(jnp.int32), scalars, images, own, other)
     image_grad = lax.psum_scatter(image_part, AXES, scatter_dimension=0, tiled=True, axis_index_groups=rings)
 
+    own_part, other_part = text_terms(weights, units)
     text_part = own_part.astype(jnp.float32) + exchanged(other_part).astype(jnp.float32)
     text_part = jnp.sum(parted(text_part.astype(jnp.bfloat16), "x").astype(jnp.float32), axis=0)
     text_grads = parted(text_part.astype(jnp.bfloat16), "z")

time: 117 us -> 117 us (level)
  local copies, waits for them, and re-layouts: 2.42 us -> 5.33 us
  waiting for transfers between devices: 14.9 us -> 12.8 us
    reduce_scatter x1, waiting for transfers between devices: 5.07 us -> 1.68 us  [on_device(): lax.psum_scatter(image_part, AXES, scatter_dimension=0, tiled=True, axis_...]
    unnamed x8 -> x12, local copies, waits for them, and re-layouts: 2.35 us -> 5.26 us
  transfers between devices with their start and end apart: 4 -> 4, of which waited for: 4 -> 4; matrix products, arithmetic and copies ran while one was open for 0% -> 0% of each run, Pallas kernels for 1% -> 3%
where the time goes in v9:
time: 117 us; the launch traced here: 116 us
  blocking collectives  68.2 us (58%)
  between operations  15.5 us (13%)
  waiting for transfers between devices  12.8 us (11%)
  Pallas kernels  10 us (9%)
  local copies, waits for them, and re-layouts  5.33 us (5%)
  starting transfers between devices  3.9 us (3%)
    all_to_all x2, blocking collectives, spread(): lax.all_to_all(copies, axis, split_axis=0, concat_axis=0, tiled=True)  36 us
    all_to_all x2, blocking collectives, parted(): return lax.all_to_all(parts, axis, split_axis=0, concat_axis=0, tiled=True)  32.2 us
    all_gather x1, waiting for transfers between devices, on_device(): lax.all_gather(image_embed, AXES, axis=0, tiled=True, axis_index_groups=r...  7.19 us
    pallas_call x1, Pallas kernels, weights_and_image_terms(): pl.pallas_call(weight_kernel, in_specs=[smem, smem, vmem, vmem, vmem], ou...  5.69 us
    unnamed x12, local copies, waits for them, and re-layouts  5.26 us
    ppermute x2, starting transfers between devices, exchanged(): return lax.ppermute(array, 'c', [(0, 1), (1, 0)])  3.83 us
    ppermute x2, waiting for transfers between devices, exchanged(): return lax.ppermute(array, 'c', [(0, 1), (1, 0)])  3.25 us
  transfers between devices with their start and end apart: 4, of which 4 were waited for; matrix products, arithmetic and copies ran while one was open for 0% of the time, Pallas kernels for 3%

profile of v9, /device:TPU:6, one launch (start us, length us, event | category | flops | bytes accessed | tf_op | source)
XLA Modules:
  0.0 116.1 jit_solution(12678437161359585644)
XLA Ops:
  7.2 0.0 all-gather.2.cloned.1.call-start
  7.2 0.7 all-gather.2.cloned.1.call-update
  7.9 0.0 reduce-scatter.2.cloned.1.call-start
  7.9 1.5 %shard_map.68 = bf16[8,16,896]{2,1,0:T(8,128)(2,1)} custom-call(s32[16]{0:T(128)} %pair_ref.1, bf16[16,768]{1,0:T(8,128)(2,1)} %text_ref.3), custom_call_target="tpu_custom_call" | custom-call | tf_op jit(solution)/shard_map/pallas_call | solution.py:48
  9.5 21.5 %all_to_all.20 = bf16[8,16,896]{2,1,0:T(8,128)(2,1)S(1)} all-to-all(bf16[8,16,896]{2,1,0:T(8,128)(2,1)} %shard_map.68), channel_id=1, replica_groups=mesh['z'=8,'y'=8,'x'=4,'c'=2] {'z'}, dimensions={0} | all-to-all | bytes 458752 | tf_op jit(solution)/shard_map/all_to_all | solution.py:166
  31.0 0.1 broadcast_in_dim.8
  31.0 14.5 %all_to_all.21 = bf16[4,128,896]{2,1,0:T(8,128)(2,1)S(1)} all-to-all(bf16[4,128,896]{2,1,0:T(8,128)(2,1)S(1)} %broadcast_in_dim.8), channel_id=1, replica_groups=mesh['z'=8,'y'=8,'x'=4,'c'=2] {'x'}, dimensions={0} | all-to-all | bytes 1835008 | tf_op jit(solution)/shard_map/all_to_all | solution.py:166
  45.5 1.9 %collective-permute-start = (bf16[512,896]{1,0:T(8,128)(2,1)S(1)}, bf16[512,896]{1,0:T(8,128)(2,1)S(1)}, u32[]{:S(2)}, u32[]{:S(2)}) collective-permute-start(bf16[512,896]{1,0:T(8,128)(2,1)S(1)} %bitcast.4), channel_id=1, source_target_pairs={{0,1},{1,0},{2,3},{3,2},{4,5},{5,4},{6,7},{7,6},{8,9},{9,8},{10,11... | collective-permute-start | bytes 2752520 | tf_op jit(solution)/shard_map/ppermute | solution.py:162
  48.8 0.1 pad_maximum_fusion.scalars_ref
  48.9 1.0 collective-permute-done.other_ref
  49.9 7.2 %all-gather.2.cloned.1.call-done.image_ref = bf16[1024,768]{1,0:T(8,128)(2,1)} async-done(((bf16[128,768]{1,0:T(8,128)(2,1)}), bf16[1024,768]{1,0:T(8,128)(2,1)}) %all-gather.2.cloned.1.call-update) | async-done | bytes 1572880 | tf_op jit(solution)/shard_map/all_gather | solution.py:177
  57.1 0.0 copy-start.3
  57.1 1.4 %copy-done.3 = bf16[1024,768]{1,0:T(8,128)(2,1)S(1)} copy-done((bf16[1024,768]{1,0:T(8,128)(2,1)S(1)}, bf16[1024,768]{1,0:T(8,128)(2,1)}, u32[]{:S(2)}) %copy-start.3) | copy-done | bytes 1572888
  58.5 5.7 %shard_map.69 = (bf16[1024,768]{1,0:T(8,128)(2,1)}, bf16[1024,1024]{1,0:T(8,128)(2,1)S(1)}, bf16[1024,768]{1,0:T(8,128)(2,1)S(1)}) custom-call(s32[8]{0:T(128)S(1)} %add_multiply_fusion.first_ref, f32[3]{0:T(128)S(1)} %pad_maximum_fusion.scalars_ref, bf16[1024,768]{1,0:T(8,128)(2,1)S(1)} %copy-done.3, bf16[512,896]{1,0:T(8,128)(2,1)S(1)} %bitcast.5, ...), custom_call_target="tpu_custom_call" | custom-call | flops 3221225472 | bytes 6291456 | tf_op jit(solution)/shard_map/pallas_call | solution.py:82
  64.2 0.0 copy-start.4
  64.2 1.3 %copy-done.4 = bf16[1024,1024]{1,0:T(8,128)(2,1)} copy-done((bf16[1024,1024]{1,0:T(8,128)(2,1)}, bf16[1024,1024]{1,0:T(8,128)(2,1)S(1)}, u32[]{:S(2)}) %copy-start.4) | copy-done | bytes 2097176
  65.5 0.0 reduce-scatter.2.cloned.1.call-update
  65.5 0.0 copy-start.5
  65.5 1.6 %copy-done.5 = bf16[1024,1024]{1,0:T(8,128)(2,1)S(1)} copy-done((bf16[1024,1024]{1,0:T(8,128)(2,1)S(1)}, bf16[1024,1024]{1,0:T(8,128)(2,1)}, u32[]{:S(2)}) %copy-start.5) | copy-done | bytes 2097176
  67.1 1.9 %shard_map.70 = (bf16[512,768]{1,0:T(8,128)(2,1)S(1)}, bf16[512,768]{1,0:T(8,128)(2,1)S(1)}) custom-call(bf16[1024,1024]{1,0:T(8,128)(2,1)S(1)} %copy-done.5, bf16[1024,768]{1,0:T(8,128)(2,1)S(1)} %get-tuple-element.9.unit_ref), custom_call_target="tpu_custom_call" | custom-call | flops 1610612736 | bytes 3145728 | tf_op jit(solution)/shard_map/pallas_call | solution.py:109
  69.0 1.9 %collective-permute-start.1 = (bf16[512,768]{1,0:T(8,128)(2,1)S(1)}, bf16[512,768]{1,0:T(8,128)(2,1)S(1)}, u32[]{:S(2)}, u32[]{:S(2)}) collective-permute-start(bf16[512,768]{1,0:T(8,128)(2,1)S(1)} %get-tuple-element.11), channel_id=1, source_target_pairs={{0,1},{1,0},{2,3},{3,2},{4,5},{5,4},{6,7},{7,6},{8,9},{9,8},{10,11... | collective-permute-start | bytes 2359304 | tf_op jit(solution)/shard_map/ppermute | solution.py:162
  70.9 2.3 %collective-permute-done.1 = bf16[512,768]{1,0:T(8,128)(2,1)S(1)} collective-permute-done((bf16[512,768]{1,0:T(8,128)(2,1)S(1)}, bf16[512,768]{1,0:T(8,128)(2,1)S(1)}, u32[]{:S(2)}, u32[]{:S(2)}) %collective-permute-start.1) | collective-permute-done | bytes 786464 | tf_op jit(solution)/shard_map/ppermute | solution.py:162
  73.2 0.2 add_convert_fusion
  73.4 0.0 copy-start
  73.4 0.0 copy-start.2
  73.4 15.1 %all_to_all.22 = bf16[4,128,768]{2,1,0:T(8,128)(2,1)S(1)} all-to-all(bf16[4,128,768]{2,1,0:T(8,128)(2,1)S(1)} %bitcast.6), channel_id=1, replica_groups=mesh['z'=8,'y'=8,'x'=4,'c'=2] {'x'}, dimensions={0} | all-to-all | bytes 1572864 | tf_op jit(solution)/shard_map/all_to_all | solution.py:171
  88.5 0.1 reduce_sum.12
  88.6 17.1 %all_to_all.23.text_grads_ref = bf16[8,16,768]{2,1,0:T(8,128)(2,1)S(1)} all-to-all(bf16[8,16,768]{2,1,0:T(8,128)(2,1)S(1)} %bitcast.8), channel_id=1, replica_groups=mesh['z'=8,'y'=8,'x'=4,'c'=2] {'z'}, dimensions={0} | all-to-all | bytes 393216 | tf_op jit(solution)/shard_map/all_to_all | solution.py:171
  105.7 1.7 %reduce-scatter.2.cloned.1.call-done.image_grad_ref = bf16[128,768]{1,0:T(8,128)(2,1)} async-done(((bf16[1024,768]{1,0:T(8,128)(2,1)}), bf16[128,768]{1,0:T(8,128)(2,1)}) %reduce-scatter.2.cloned.1.call-update) | async-done | bytes 196624 | tf_op jit(solution)/shard_map/reduce_scatter | solution.py:191
  107.4 0.0 copy-done
  107.4 0.0 copy-done.2
  107.4 0.0 copy-start.1
  107.4 0.9 copy-done.1
  108.3 0.9 shard_map.71
  (1 shorter events, 0.0 us)
Async XLA Ops:
  7.2 49.9 %all-gather.2.cloned.1.call-start = ((), (), s32[]{:S(2)}) async-start(), calls=%async_computation.5 | async-start | bytes 1769472 | tf_op jit(solution)/shard_map/all_gather | solution.py:177
  7.9 99.5 %reduce-scatter.2.cloned.1.call-start = ((), (), s32[]{:S(2)}) async-start(), calls=%async_computation.6 | async-start | bytes 1769472 | tf_op jit(solution)/shard_map/reduce_scatter | solution.py:191
  45.5 4.4 %collective-permute-start = (bf16[512,896]{1,0:T(8,128)(2,1)S(1)}, bf16[512,896]{1,0:T(8,128)(2,1)S(1)}, u32[]{:S(2)}, u32[]{:S(2)}) collective-permute-start(bf16[512,896]{1,0:T(8,128)(2,1)S(1)} %bitcast.4), channel_id=1, source_target_pairs={{0,1},{1,0},{2,3},{3,2},{4,5},{5,4},{6,7},{7,6},{8,9},{9,8},{10,11... | collective-permute-start | bytes 2752520 | tf_op jit(solution)/shard_map/ppermute | solution.py:162
  57.1 1.4 %copy-start.3 = (bf16[1024,768]{1,0:T(8,128)(2,1)S(1)}, bf16[1024,768]{1,0:T(8,128)(2,1)}, u32[]{:S(2)}) copy-start(bf16[1024,768]{1,0:T(8,128)(2,1)} %all-gather.2.cloned.1.call-done.image_ref) | copy-start | bytes 4718596
  64.2 1.3 %copy-start.4 = (bf16[1024,1024]{1,0:T(8,128)(2,1)}, bf16[1024,1024]{1,0:T(8,128)(2,1)S(1)}, u32[]{:S(2)}) copy-start(bf16[1024,1024]{1,0:T(8,128)(2,1)S(1)} %get-tuple-element.8.weight_ref) | copy-start | bytes 6291460
  65.5 1.6 %copy-start.5 = (bf16[1024,1024]{1,0:T(8,128)(2,1)S(1)}, bf16[1024,1024]{1,0:T(8,128)(2,1)}, u32[]{:S(2)}) copy-start(bf16[1024,1024]{1,0:T(8,128)(2,1)} %copy-done.4) | copy-start | bytes 6291460
  69.0 4.2 %collective-permute-start.1 = (bf16[512,768]{1,0:T(8,128)(2,1)S(1)}, bf16[512,768]{1,0:T(8,128)(2,1)S(1)}, u32[]{:S(2)}, u32[]{:S(2)}) collective-permute-start(bf16[512,768]{1,0:T(8,128)(2,1)S(1)} %get-tuple-element.11), channel_id=1, source_target_pairs={{0,1},{1,0},{2,3},{3,2},{4,5},{5,4},{6,7},{7,6},{8,9},{9,8},{10,11... | collective-permute-start | bytes 2359304 | tf_op jit(solution)/shard_map/ppermute | solution.py:162
  73.4 34.0 %copy-start = (bf16[128,768]{1,0:T(8,128)(2,1)S(1)}, bf16[128,768]{1,0:T(8,128)(2,1)}, u32[]{:S(2)}) copy-start(bf16[128,768]{1,0:T(8,128)(2,1)} %image_ref.1) | copy-start | bytes 589828
  73.4 34.0 %copy-start.2 = (bf16[16,768]{1,0:T(8,128)(2,1)S(1)}, bf16[16,768]{1,0:T(8,128)(2,1)}, u32[]{:S(2)}) copy-start(bf16[16,768]{1,0:T(8,128)(2,1)} %text_ref.3) | copy-start | bytes 73732
  107.4 0.9 copy-start.1
Sparse Core Ops, SparseCore 0:
  10.1 46.9 all-gather.1
  65.7 41.7 reduce-scatter.1

commit v10 on v9

--- a/solution.py
+++ b/solution.py
@@ -17,6 +17,7 @@
 
 smem = pl.BlockSpec(memory_space=pltpu.SMEM)
 vmem = pl.BlockSpec(memory_space=pltpu.VMEM)
+hbm = pl.BlockSpec(memory_space=pltpu.HBM)
 
 
 def params(mib):
@@ -27,7 +28,9 @@
     return lax.rsqrt(jnp.sum(floats * floats, axis=-1, keepdims=True) + 1e-06)
 
 
-def packet_kernel(pair_ref, text_ref, packet_ref):
+def unit_kernel(pair_ref, image_ref, text_ref, unit_ref, packet_ref):
+    floats = image_ref[...].astype(jnp.float32)
+    unit_ref[...] = (floats * inverse_norm(floats)).astype(unit_ref.dtype)
     rows, width = text_ref.shape
     floats = text_ref[...].astype(jnp.float32)
     unit = (floats * inverse_norm(floats)).astype(packet_ref.dtype)
@@ -43,36 +46,49 @@
         packet_ref[peer, :, width:] = digits
 
 
-def text_packets(pair_index, embed, peers):
-    rows, width = embed.shape
-    return pl.pallas_call(
-        packet_kernel,
-        in_specs=[smem, vmem],
-        out_specs=vmem,
-        out_shape=jax.ShapeDtypeStruct((peers, rows, width + LANES), jnp.bfloat16),
+def units_and_packets(pair_index, image_embed, text_embed, peers):
+    rows, width = text_embed.shape
+    return pl.pallas_call(
+        unit_kernel,
+        in_specs=[smem, vmem, vmem],
+        out_specs=[vmem, vmem],
+        out_shape=[
+            jax.ShapeDtypeStruct(image_embed.shape, jnp.bfloat16),
+            jax.ShapeDtypeStruct((peers, rows, width + LANES), jnp.bfloat16),
+        ],
         compiler_params=params(56),
-    )(pair_index, embed)
-
-
-def weight_kernel(first_ref, scalars_ref, image_ref, own_ref, other_ref, *refs):
-    image_grad_ref, weight_ref, unit_ref, text_ref = refs
-    width = image_ref.shape[1]
+    )(pair_index, image_embed, text_embed)
+
+
+def weight_kernel(first_ref, scalars_ref, images_ref, own_ref, other_ref, *refs):
+    image_grad_ref, weights_ref, image_ref, text_ref, weight_ref, grad_ref, sems = refs
+    arrival = pltpu.make_async_copy(images_ref, image_ref, sems.at[0])
+    arrival.start()
+    rows, width = image_ref.shape
     count = own_ref.shape[0]
     text_ref[:count, :] = own_ref[...]
     text_ref[count:, :] = other_ref[...]
     digits = text_ref[:, width:].astype(jnp.float32).T
     pairs = (digits[0:1] * 256.0 + digits[1:2]).astype(jnp.int32)
     row = lax.broadcasted_iota(jnp.int32, (128, 1), 0)
-    rows = jnp.concatenate([row + first_ref[p] for p in range(image_ref.shape[0] // 128)], axis=0)
+    places = jnp.concatenate([row + first_ref[p] for p in range(rows // 128)], axis=0)
     texts = text_ref[:, :width]
-    floats = image_ref[...].astype(jnp.float32)
-    images = (floats * inverse_norm(floats)).astype(unit_ref.dtype)
-    unit_ref[...] = images
-    dots = lax.dot_general(images, texts, ROWS_BY_ROWS, preferred_element_type=jnp.float32)
+    arrival.wait()
+    dots = lax.dot_general(image_ref[...], texts, ROWS_BY_ROWS, preferred_element_type=jnp.float32)
     chance = 1.0 / (1.0 + jnp.exp2(dots * scalars_ref[1] + scalars_ref[2]))
-    weight = (scalars_ref[0] * jnp.where(pairs == rows, chance - 1.0, chance)).astype(jnp.bfloat16)
+    weight = (scalars_ref[0] * jnp.where(pairs == places, chance - 1.0, chance)).astype(jnp.bfloat16)
     weight_ref[...] = weight
-    image_grad_ref[...] = jnp.dot(weight, texts, preferred_element_type=jnp.float32).astype(image_grad_ref.dtype)
+    leaving = [pltpu.make_async_copy(weight_ref, weights_ref, sems.at[1])]
+    leaving[0].start()
+    half = rows // 2
+    for i in range(2):
+        part = pl.ds(i * half, half)
+        grad = jnp.dot(weight[i * half : (i + 1) * half], texts, preferred_element_type=jnp.float32)
+        grad_ref[part, :] = grad.astype(grad_ref.dtype)
+        leaving.append(pltpu.make_async_copy(grad_ref.at[part], image_grad_ref.at[part], sems.at[2 + i]))
+        leaving[-1].start()
+    for copy in leaving:
+        copy.wait()
 
 
 def weights_and_image_terms(first, scalars, images, own, other):
@@ -81,14 +97,19 @@
     texts = 2 * count
     return pl.pallas_call(
         weight_kernel,
-        in_specs=[smem, smem, vmem, vmem, vmem],
-        out_specs=[vmem] * 3,
+        in_specs=[smem, smem, hbm, vmem, vmem],
+        out_specs=[hbm] * 2,
         out_shape=[
             jax.ShapeDtypeStruct((rows, width), jnp.bfloat16),
             jax.ShapeDtypeStruct((rows, texts), jnp.bfloat16),
-            jax.ShapeDtypeStruct((rows, width), jnp.bfloat16),
-        ],
-        scratch_shapes=[pltpu.VMEM((texts, wide), jnp.bfloat16)],
+        ],
+        scratch_shapes=[
+            pltpu.VMEM((rows, width), jnp.bfloat16),
+            pltpu.VMEM((texts, wide), jnp.bfloat16),
+            pltpu.VMEM((rows, texts), jnp.bfloat16),
+            pltpu.VMEM((rows, width), jnp.bfloat16),
+            pltpu.SemaphoreType.DMA((4,)),
+        ],
         compiler_params=params(32),
         cost_estimate=pl.CostEstimate(
             flops=4 * rows * texts * width, bytes_accessed=4 * (rows + texts) * width, transcendentals=2 * rows * texts
@@ -96,26 +117,39 @@
     )(first, scalars, images, own, other)
 
 
-def text_kernel(weight_ref, unit_ref, own_grad_ref, other_grad_ref):
+def text_kernel(weights_ref, images_ref, own_grad_ref, other_grad_ref, weight_ref, image_ref, sems):
+    copies = [
+        pltpu.make_async_copy(weights_ref, weight_ref, sems.at[0]),
+        pltpu.make_async_copy(images_ref, image_ref, sems.at[1]),
+    ]
+    for copy in copies:
+        copy.start()
+    for copy in copies:
+        copy.wait()
     count = own_grad_ref.shape[0]
-    grad = lax.dot_general(weight_ref[...], unit_ref[...], COLUMNS_BY_ROWS, preferred_element_type=jnp.float32)
+    grad = lax.dot_general(weight_ref[...], image_ref[...], COLUMNS_BY_ROWS, preferred_element_type=jnp.float32)
     own_grad_ref[...] = grad[:count].astype(own_grad_ref.dtype)
     other_grad_ref[...] = grad[count:].astype(other_grad_ref.dtype)
 
 
-def text_terms(weights, units):
+def text_terms(weights, images):
     rows, texts = weights.shape
-    width = units.shape[1]
+    width = images.shape[1]
     return pl.pallas_call(
         text_kernel,
-        in_specs=[vmem] * 2,
+        in_specs=[hbm] * 2,
         out_specs=[vmem] * 2,
         out_shape=[jax.ShapeDtypeStruct((texts // 2, width), jnp.bfloat16)] * 2,
+        scratch_shapes=[
+            pltpu.VMEM(weights.shape, jnp.bfloat16),
+            pltpu.VMEM(images.shape, jnp.bfloat16),
+            pltpu.SemaphoreType.DMA((2,)),
+        ],
         compiler_params=params(24),
         cost_estimate=pl.CostEstimate(
             flops=2 * rows * texts * width, bytes_accessed=2 * (rows + texts) * width, transcendentals=0
         ),
-    )(weights, units)
+    )(weights, images)
 
 
 def project(embed_ref, grad, out_ref):
@@ -126,23 +160,27 @@
     out_ref[...] = ((grad - unit * along) * inverse).astype(out_ref.dtype)
 
 
-def backward_kernel(image_ref, text_ref, image_grad_ref, text_grads_ref, image_out_ref, text_out_ref):
-    project(image_ref, image_grad_ref[...].astype(jnp.float32), image_out_ref)
+def backward_kernel(image_ref, text_ref, image_grads_ref, text_grads_ref, image_out_ref, text_out_ref, image_grad_ref, sem):
+    copy = pltpu.make_async_copy(image_grads_ref, image_grad_ref, sem)
+    copy.start()
     text_grad = text_grads_ref[0].astype(jnp.float32)
     for part in range(1, text_grads_ref.shape[0]):
         text_grad += text_grads_ref[part].astype(jnp.float32)
     project(text_ref, text_grad, text_out_ref)
+    copy.wait()
+    project(image_ref, image_grad_ref[...].astype(jnp.float32), image_out_ref)
 
 
 def unit_backward(image_embed, text_embed, image_grad, text_grads):
     return pl.pallas_call(
         backward_kernel,
-        in_specs=[vmem] * 4,
+        in_specs=[vmem, vmem, hbm, vmem],
         out_specs=[vmem] * 2,
         out_shape=[
             jax.ShapeDtypeStruct(image_embed.shape, jnp.bfloat16),
             jax.ShapeDtypeStruct(text_embed.shape, jnp.bfloat16),
         ],
+        scratch_shapes=[pltpu.VMEM(image_grad.shape, image_grad.dtype), pltpu.SemaphoreType.DMA],
         compiler_params=params(8),
     )(image_embed, text_embed, image_grad, text_grads)
 
@@ -174,9 +212,10 @@
 def on_device(image_embed, text_embed, log_scale, logit_bias, pair_index):
     own_images = image_embed.shape[0]
     rings = image_rings()
-    images = lax.all_gather(image_embed, AXES, axis=0, tiled=True, axis_index_groups=rings)
-
-    texts = spread(text_packets(pair_index, text_embed, lax.axis_size("z")), "z")
+    unit, packets = units_and_packets(pair_index, image_embed, text_embed, lax.axis_size("z"))
+    images = lax.all_gather(unit, AXES, axis=0, tiled=True, axis_index_groups=rings)
+
+    texts = spread(packets, "z")
     own = spread(jnp.broadcast_to(texts[None], (lax.axis_size("x"),) + texts.shape), "x")
     other = exchanged(own)
 
@@ -187,10 +226,10 @@
     place = jnp.where(c == 0, place, SIZES[1] - 1 - place)
     first = (((z * SIZES[1] + place) * SIZES[2] + x) * SIZES[3] + c) * own_images
 
-    image_part, weights, units = weights_and_image_terms(first.astype(jnp.int32), scalars, images, own, other)
+    image_part, weights = weights_and_image_terms(first.astype(jnp.int32), scalars, images, own, other)
     image_grad = lax.psum_scatter(image_part, AXES, scatter_dimension=0, tiled=True, axis_index_groups=rings)
 
-    own_part, other_part = text_terms(weights, units)
+    own_part, other_part = text_terms(weights, images)
     text_part = own_part.astype(jnp.float32) + exchanged(other_part).astype(jnp.float32)
     text_part = jnp.sum(parted(text_part.astype(jnp.bfloat16), "x").astype(jnp.float32), axis=0)
     text_grads = parted(text_part.astype(jnp.bfloat16), "z")

time: 117 us -> 120 us (1.026); the launches traced: 116 us -> 118 us
  Pallas kernels: 10 us -> 11.7 us
  local copies, waits for them, and re-layouts: 5.33 us -> 6.71 us
  waiting for transfers between devices: 12.8 us -> 11.5 us
    pallas_call x4, Pallas kernels: 10 us -> 11.7 us  [the longest x1 6.44 us: weights_and_image_terms(): pl.pallas_call(weight_kernel, in_specs=[smem, smem, hbm, vmem, vmem], out...]
    reduce_scatter x1, waiting for transfers between devices: 1.68 us -> 0.06 us  [on_device(): lax.psum_scatter(image_part, AXES, scatter_dimension=0, tiled=True, axis_...]
    unnamed x12 -> x14, local copies, waits for them, and re-layouts: 5.26 us -> 6.64 us
  transfers between devices with their start and end apart: 4 -> 4, of which waited for: 4 -> 4; matrix products, arithmetic and copies ran while one was open for 0% -> 0% of each run, Pallas kernels for 3% -> 2%
where the time goes in v10:
time: 120 us; the launch traced here: 118 us
  blocking collectives  68.2 us (57%)
  between operations  15.5 us (13%)
  Pallas kernels  11.7 us (10%)
  waiting for transfers between devices  11.5 us (10%)
  local copies, waits for them, and re-layouts  6.71 us (6%)
  starting transfers between devices  3.91 us (3%)
    all_to_all x2, blocking collectives, spread(): lax.all_to_all(copies, axis, split_axis=0, concat_axis=0, tiled=True)  36 us
    all_to_all x2, blocking collectives, parted(): return lax.all_to_all(parts, axis, split_axis=0, concat_axis=0, tiled=True)  32.2 us
    all_gather x1, waiting for transfers between devices, on_device(): lax.all_gather(unit, AXES, axis=0, tiled=True, axis_index_groups=rings)  8.12 us
    unnamed x14, local copies, waits for them, and re-layouts  6.64 us
    pallas_call x1, Pallas kernels, weights_and_image_terms(): pl.pallas_call(weight_kernel, in_specs=[smem, smem, hbm, vmem, vmem], out...  6.44 us
    ppermute x2, starting transfers between devices, exchanged(): return lax.ppermute(array, 'c', [(0, 1), (1, 0)])  3.83 us
    ppermute x2, waiting for transfers between devices, exchanged(): return lax.ppermute(array, 'c', [(0, 1), (1, 0)])  3.25 us
  transfers between devices with their start and end apart: 4, of which 4 were waited for; matrix products, arithmetic and copies ran while one was open for 0% of the time, Pallas kernels for 2%

profile of v10, /device:TPU:6, one launch (start us, length us, event | category | flops | bytes accessed | tf_op | source)
XLA Modules:
  0.0 117.9 jit_solution(8898639993055341341)
XLA Ops:
  7.2 0.0 all-gather.2.cloned.1.call-start
  7.2 1.8 %shard_map.68 = (bf16[128,768]{1,0:T(8,128)(2,1)}, bf16[8,16,896]{2,1,0:T(8,128)(2,1)}) custom-call(s32[16]{0:T(128)} %pair_ref.1, bf16[128,768]{1,0:T(8,128)(2,1)} %image_ref.3, bf16[16,768]{1,0:T(8,128)(2,1)} %text_ref.3), custom_call_target="tpu_custom_call" | custom-call | tf_op jit(solution)/shard_map/pallas_call | solution.py:51
  9.0 0.0 all-gather.2.cloned.1.call-update
  9.1 0.0 reduce-scatter.2.cloned.1.call-start
  9.1 21.5 %all_to_all.20 = bf16[8,16,896]{2,1,0:T(8,128)(2,1)S(1)} all-to-all(bf16[8,16,896]{2,1,0:T(8,128)(2,1)} %get-tuple-element.9), channel_id=1, replica_groups=mesh['z'=8,'y'=8,'x'=4,'c'=2] {'z'}, dimensions={0} | all-to-all | bytes 458752 | tf_op jit(solution)/shard_map/all_to_all | solution.py:204
  30.6 0.1 broadcast_in_dim.8
  30.7 14.5 %all_to_all.21 = bf16[4,128,896]{2,1,0:T(8,128)(2,1)S(1)} all-to-all(bf16[4,128,896]{2,1,0:T(8,128)(2,1)S(1)} %broadcast_in_dim.8), channel_id=1, replica_groups=mesh['z'=8,'y'=8,'x'=4,'c'=2] {'x'}, dimensions={0} | all-to-all | bytes 1835008 | tf_op jit(solution)/shard_map/all_to_all | solution.py:204
  45.2 1.9 %collective-permute-start = (bf16[512,896]{1,0:T(8,128)(2,1)S(1)}, bf16[512,896]{1,0:T(8,128)(2,1)S(1)}, u32[]{:S(2)}, u32[]{:S(2)}) collective-permute-start(bf16[512,896]{1,0:T(8,128)(2,1)S(1)} %bitcast.4), channel_id=1, source_target_pairs={{0,1},{1,0},{2,3},{3,2},{4,5},{5,4},{6,7},{7,6},{8,9},{9,8},{10,11... | collective-permute-start | bytes 2752520 | tf_op jit(solution)/shard_map/ppermute | solution.py:200
  48.5 0.1 pad_maximum_fusion.scalars_ref
  48.5 1.0 collective-permute-done.other_ref
  49.5 8.1 %all-gather.2.cloned.1.call-done.images_ref = bf16[1024,768]{1,0:T(8,128)(2,1)} async-done(((bf16[128,768]{1,0:T(8,128)(2,1)}), bf16[1024,768]{1,0:T(8,128)(2,1)}) %all-gather.2.cloned.1.call-update) | async-done | bytes 1572880 | tf_op jit(solution)/shard_map/all_gather | solution.py:216
  57.7 0.0 copy-start.3
  57.7 1.4 %copy-done.3 = bf16[1024,768]{1,0:T(8,128)(2,1)S(1)} copy-done((bf16[1024,768]{1,0:T(8,128)(2,1)S(1)}, bf16[1024,768]{1,0:T(8,128)(2,1)}, u32[]{:S(2)}) %copy-start.3) | copy-done | bytes 1572888
  59.1 6.4 %shard_map.69 = (bf16[1024,768]{1,0:T(8,128)(2,1)}, bf16[1024,1024]{1,0:T(8,128)(2,1)S(1)}) custom-call(s32[8]{0:T(128)S(1)} %add_multiply_fusion.first_ref, f32[3]{0:T(128)S(1)} %pad_maximum_fusion.scalars_ref, bf16[1024,768]{1,0:T(8,128)(2,1)S(1)} %copy-done.3, bf16[512,896]{1,0:T(8,128)(2,1)S(1)} %bitcast.5, ...), custom_call_target="tpu_custom_call" | custom-call | flops 3221225472 | bytes 6291456 | tf_op jit(solution)/shard_map/pallas_call | solution.py:98
  65.5 0.0 copy-start.5
  65.5 1.3 %copy-done.5 = bf16[1024,1024]{1,0:T(8,128)(2,1)} copy-done((bf16[1024,1024]{1,0:T(8,128)(2,1)}, bf16[1024,1024]{1,0:T(8,128)(2,1)S(1)}, u32[]{:S(2)}) %copy-start.5) | copy-done | bytes 2097176
  66.8 0.0 copy-start.4
  66.8 0.0 reduce-scatter.2.cloned.1.call-update
  66.9 1.4 %copy-done.4 = bf16[1024,768]{1,0:T(8,128)(2,1)S(1)} copy-done((bf16[1024,768]{1,0:T(8,128)(2,1)S(1)}, bf16[1024,768]{1,0:T(8,128)(2,1)}, u32[]{:S(2)}) %copy-start.4) | copy-done | bytes 1572888
  68.3 0.0 copy-start.6
  68.3 1.6 %copy-done.6 = bf16[1024,1024]{1,0:T(8,128)(2,1)S(1)} copy-done((bf16[1024,1024]{1,0:T(8,128)(2,1)S(1)}, bf16[1024,1024]{1,0:T(8,128)(2,1)}, u32[]{:S(2)}) %copy-start.6) | copy-done | bytes 2097176
  69.8 2.1 %shard_map.70 = (bf16[512,768]{1,0:T(8,128)(2,1)S(1)}, bf16[512,768]{1,0:T(8,128)(2,1)S(1)}) custom-call(bf16[1024,1024]{1,0:T(8,128)(2,1)S(1)} %copy-done.6, bf16[1024,768]{1,0:T(8,128)(2,1)S(1)} %copy-done.4), custom_call_target="tpu_custom_call" | custom-call | flops 1610612736 | bytes 3145728 | tf_op jit(solution)/shard_map/pallas_call | solution.py:138
  72.0 1.9 %collective-permute-start.1 = (bf16[512,768]{1,0:T(8,128)(2,1)S(1)}, bf16[512,768]{1,0:T(8,128)(2,1)S(1)}, u32[]{:S(2)}, u32[]{:S(2)}) collective-permute-start(bf16[512,768]{1,0:T(8,128)(2,1)S(1)} %get-tuple-element.13), channel_id=1, source_target_pairs={{0,1},{1,0},{2,3},{3,2},{4,5},{5,4},{6,7},{7,6},{8,9},{9,8},{10,11... | collective-permute-start | bytes 2359304 | tf_op jit(solution)/shard_map/ppermute | solution.py:200
  73.9 2.3 %collective-permute-done.1 = bf16[512,768]{1,0:T(8,128)(2,1)S(1)} collective-permute-done((bf16[512,768]{1,0:T(8,128)(2,1)S(1)}, bf16[512,768]{1,0:T(8,128)(2,1)S(1)}, u32[]{:S(2)}, u32[]{:S(2)}) %collective-permute-start.1) | collective-permute-done | bytes 786464 | tf_op jit(solution)/shard_map/ppermute | solution.py:200
  76.2 0.2 add_convert_fusion
  76.3 0.0 copy-start
  76.4 0.0 copy-start.2
  76.4 15.2 %all_to_all.22 = bf16[4,128,768]{2,1,0:T(8,128)(2,1)S(1)} all-to-all(bf16[4,128,768]{2,1,0:T(8,128)(2,1)S(1)} %bitcast.6), channel_id=1, replica_groups=mesh['z'=8,'y'=8,'x'=4,'c'=2] {'x'}, dimensions={0} | all-to-all | bytes 1572864 | tf_op jit(solution)/shard_map/all_to_all | solution.py:209
  91.6 0.1 reduce_sum.12
  91.7 17.0 %all_to_all.23.text_grads_ref = bf16[8,16,768]{2,1,0:T(8,128)(2,1)S(1)} all-to-all(bf16[8,16,768]{2,1,0:T(8,128)(2,1)S(1)} %bitcast.8), channel_id=1, replica_groups=mesh['z'=8,'y'=8,'x'=4,'c'=2] {'z'}, dimensions={0} | all-to-all | bytes 393216 | tf_op jit(solution)/shard_map/all_to_all | solution.py:209
  108.7 0.1 reduce-scatter.2.cloned.1.call-done.image_grads_ref
  108.8 0.0 copy-done
  108.8 0.0 copy-done.2
  108.8 0.0 copy-start.1
  108.8 0.9 copy-done.1
  109.7 1.3 %shard_map.71 = (bf16[128,768]{1,0:T(8,128)(2,1)}, bf16[16,768]{1,0:T(8,128)(2,1)}) custom-call(bf16[128,768]{1,0:T(8,128)(2,1)S(1)} %copy-done, bf16[16,768]{1,0:T(8,128)(2,1)S(1)} %copy-done.2, bf16[128,768]{1,0:T(8,128)(2,1)S(1)} %copy-done.1, bf16[8,16,768]{2,1,0:T(8,128)(2,1)S(1)} %all_to_all.23.text_grads_ref), custom_call_target="tpu_custom_call" | custom-call | tf_op jit(solution)/shard_map/pallas_call | solution.py:175
  (1 shorter events, 0.0 us)
Async XLA Ops:
  7.2 50.5 %all-gather.2.cloned.1.call-start = ((), (), s32[]{:S(2)}) async-start(), calls=%async_computation.5 | async-start | bytes 1769472 | tf_op jit(solution)/shard_map/all_gather | solution.py:216
  9.1 99.7 %reduce-scatter.2.cloned.1.call-start = ((), (), s32[]{:S(2)}) async-start(), calls=%async_computation.6 | async-start | bytes 1769472 | tf_op jit(solution)/shard_map/reduce_scatter | solution.py:230
  45.2 4.4 %collective-permute-start = (bf16[512,896]{1,0:T(8,128)(2,1)S(1)}, bf16[512,896]{1,0:T(8,128)(2,1)S(1)}, u32[]{:S(2)}, u32[]{:S(2)}) collective-permute-start(bf16[512,896]{1,0:T(8,128)(2,1)S(1)} %bitcast.4), channel_id=1, source_target_pairs={{0,1},{1,0},{2,3},{3,2},{4,5},{5,4},{6,7},{7,6},{8,9},{9,8},{10,11... | collective-permute-start | bytes 2752520 | tf_op jit(solution)/shard_map/ppermute | solution.py:200
  57.7 1.4 %copy-start.3 = (bf16[1024,768]{1,0:T(8,128)(2,1)S(1)}, bf16[1024,768]{1,0:T(8,128)(2,1)}, u32[]{:S(2)}) copy-start(bf16[1024,768]{1,0:T(8,128)(2,1)} %all-gather.2.cloned.1.call-done.images_ref) | copy-start | bytes 4718596
  65.5 1.3 %copy-start.5 = (bf16[1024,1024]{1,0:T(8,128)(2,1)}, bf16[1024,1024]{1,0:T(8,128)(2,1)S(1)}, u32[]{:S(2)}) copy-start(bf16[1024,1024]{1,0:T(8,128)(2,1)S(1)} %get-tuple-element.11.weights_ref) | copy-start | bytes 6291460
  66.8 1.4 %copy-start.4 = (bf16[1024,768]{1,0:T(8,128)(2,1)S(1)}, bf16[1024,768]{1,0:T(8,128)(2,1)}, u32[]{:S(2)}) copy-start(bf16[1024,768]{1,0:T(8,128)(2,1)} %all-gather.2.cloned.1.call-done.images_ref) | copy-start | bytes 4718596
  68.3 1.6 %copy-start.6 = (bf16[1024,1024]{1,0:T(8,128)(2,1)S(1)}, bf16[1024,1024]{1,0:T(8,128)(2,1)}, u32[]{:S(2)}) copy-start(bf16[1024,1024]{1,0:T(8,128)(2,1)} %copy-done.5) | copy-start | bytes 6291460
  72.0 4.2 %collective-permute-start.1 = (bf16[512,768]{1,0:T(8,128)(2,1)S(1)}, bf16[512,768]{1,0:T(8,128)(2,1)S(1)}, u32[]{:S(2)}, u32[]{:S(2)}) collective-permute-start(bf16[512,768]{1,0:T(8,128)(2,1)S(1)} %get-tuple-element.13), channel_id=1, source_target_pairs={{0,1},{1,0},{2,3},{3,2},{4,5},{5,4},{6,7},{7,6},{8,9},{9,8},{10,11... | collective-permute-start | bytes 2359304 | tf_op jit(solution)/shard_map/ppermute | solution.py:200
  76.3 32.4 %copy-start = (bf16[128,768]{1,0:T(8,128)(2,1)S(1)}, bf16[128,768]{1,0:T(8,128)(2,1)}, u32[]{:S(2)}) copy-start(bf16[128,768]{1,0:T(8,128)(2,1)} %image_ref.3) | copy-start | bytes 589828
  76.4 32.4 %copy-start.2 = (bf16[16,768]{1,0:T(8,128)(2,1)S(1)}, bf16[16,768]{1,0:T(8,128)(2,1)}, u32[]{:S(2)}) copy-start(bf16[16,768]{1,0:T(8,128)(2,1)} %text_ref.3) | copy-start | bytes 73732
  108.8 0.9 copy-start.1
Sparse Core Ops, SparseCore 0:
  10.7 46.9 all-gather.1
  67.0 41.7 reduce-scatter.1

commit v11 on v10

--- a/solution.py
+++ b/solution.py
@@ -110,7 +110,7 @@
             pltpu.VMEM((rows, width), jnp.bfloat16),
             pltpu.SemaphoreType.DMA((4,)),
         ],
-        compiler_params=params(32),
+        compiler_params=params(58),
         cost_estimate=pl.CostEstimate(
             flops=4 * rows * texts * width, bytes_accessed=4 * (rows + texts) * width, transcendentals=2 * rows * texts
         ),
@@ -145,7 +145,7 @@
             pltpu.VMEM(images.shape, jnp.bfloat16),
             pltpu.SemaphoreType.DMA((2,)),
         ],
-        compiler_params=params(24),
+        compiler_params=params(58),
         cost_estimate=pl.CostEstimate(
             flops=2 * rows * texts * width, bytes_accessed=2 * (rows + texts) * width, transcendentals=0
         ),

time: 120 us -> 119 us (level)
  local copies, waits for them, and re-layouts: 6.71 us -> 1.01 us
  Pallas kernels: 11.7 us -> 15.6 us
  other arithmetic: 0.39 us -> 2.56 us
    unnamed x14 -> x10, local copies, waits for them, and re-layouts: 6.64 us -> 0.94 us
    pallas_call x1, Pallas kernels: 2.13 us -> 4.98 us  [text_terms(): pl.pallas_call(text_kernel, in_specs=[hbm] * 2, out_specs=[vmem] * 2, out...]
  transfers between devices with their start and end apart: 4 -> 4, of which waited for: 4 -> 2; matrix products, arithmetic and copies ran while one was open for 0% -> 2% of each run, Pallas kernels for 2% -> 4%
where the time goes in v11:
time: 119 us; the launch traced here: 117 us
  blocking collectives  68.2 us (57%)
  Pallas kernels  15.6 us (13%)
  between operations  15.5 us (13%)
  waiting for transfers between devices  10.6 us (9%)
  starting transfers between devices  3.91 us (3%)
  other arithmetic  2.56 us (2%)
    all_to_all x2, blocking collectives, spread(): lax.all_to_all(copies, axis, split_axis=0, concat_axis=0, tiled=True)  36 us
    all_to_all x2, blocking collectives, parted(): return lax.all_to_all(parts, axis, split_axis=0, concat_axis=0, tiled=True)  32.2 us
    all_gather x1, waiting for transfers between devices, on_device(): lax.all_gather(unit, AXES, axis=0, tiled=True, axis_index_groups=rings)  8.11 us
    pallas_call x1, Pallas kernels, weights_and_image_terms(): pl.pallas_call(weight_kernel, in_specs=[smem, smem, hbm, vmem, vmem], out...  7.52 us
    pallas_call x1, Pallas kernels, text_terms(): pl.pallas_call(text_kernel, in_specs=[hbm] * 2, out_specs=[vmem] * 2, out...  4.98 us
    ppermute x2, starting transfers between devices, exchanged(): return lax.ppermute(array, 'c', [(0, 1), (1, 0)])  3.83 us
    ppermute x2, waiting for transfers between devices, exchanged(): return lax.ppermute(array, 'c', [(0, 1), (1, 0)])  2.46 us
  transfers between devices with their start and end apart: 4, of which 2 were waited for; matrix products, arithmetic and copies ran while one was open for 2% of the time, Pallas kernels for 4%

profile of v11, /device:TPU:6, one launch (start us, length us, event | category | flops | bytes accessed | tf_op | source)
XLA Modules:
  0.0 117.4 jit_solution(18417307276409844887)
XLA Ops:
  7.2 0.0 all-gather.2.cloned.1.call-start
  7.2 1.8 %shard_map.68 = (bf16[128,768]{1,0:T(8,128)(2,1)}, bf16[8,16,896]{2,1,0:T(8,128)(2,1)}) custom-call(s32[16]{0:T(128)} %pair_ref.1, bf16[128,768]{1,0:T(8,128)(2,1)} %image_ref.3, bf16[16,768]{1,0:T(8,128)(2,1)} %text_ref.3), custom_call_target="tpu_custom_call" | custom-call | tf_op jit(solution)/shard_map/pallas_call | solution.py:51
  9.0 0.0 all-gather.2.cloned.1.call-update
  9.0 0.0 reduce-scatter.2.cloned.1.call-start
  9.1 21.5 %all_to_all.20 = bf16[8,16,896]{2,1,0:T(8,128)(2,1)S(1)} all-to-all(bf16[8,16,896]{2,1,0:T(8,128)(2,1)} %get-tuple-element.9), channel_id=1, replica_groups=mesh['z'=8,'y'=8,'x'=4,'c'=2] {'z'}, dimensions={0} | all-to-all | bytes 458752 | tf_op jit(solution)/shard_map/all_to_all | solution.py:204
  30.6 0.1 broadcast_in_dim.8
  30.7 14.5 %all_to_all.21 = bf16[4,128,896]{2,1,0:T(8,128)(2,1)S(1)} all-to-all(bf16[4,128,896]{2,1,0:T(8,128)(2,1)S(1)} %broadcast_in_dim.8), channel_id=1, replica_groups=mesh['z'=8,'y'=8,'x'=4,'c'=2] {'x'}, dimensions={0} | all-to-all | bytes 1835008 | tf_op jit(solution)/shard_map/all_to_all | solution.py:204
  45.2 0.0 copy-start.3
  45.2 1.9 %collective-permute-start = (bf16[512,896]{1,0:T(8,128)(2,1)S(1)}, bf16[512,896]{1,0:T(8,128)(2,1)S(1)}, u32[]{:S(2)}, u32[]{:S(2)}) collective-permute-start(bf16[512,896]{1,0:T(8,128)(2,1)S(1)} %bitcast.5), channel_id=1, source_target_pairs={{0,1},{1,0},{2,3},{3,2},{4,5},{5,4},{6,7},{7,6},{8,9},{9,8},{10,11... | collective-permute-start | bytes 2752520 | tf_op jit(solution)/shard_map/ppermute | solution.py:200
  48.4 0.6 pad_maximum_fusion.scalars_ref
  49.0 0.5 add_multiply_fusion.first_ref
  49.6 0.0 collective-permute-done.other_ref
  49.6 0.0 copy-start.4
  49.6 8.1 %all-gather.2.cloned.1.call-done.images_ref = bf16[1024,768]{1,0:T(8,128)(2,1)} async-done(((bf16[128,768]{1,0:T(8,128)(2,1)}), bf16[1024,768]{1,0:T(8,128)(2,1)}) %all-gather.2.cloned.1.call-update) | async-done | bytes 1572880 | tf_op jit(solution)/shard_map/all_gather | solution.py:216
  57.7 0.0 copy-done.3
  57.7 0.0 copy-done.4
  57.7 7.5 %shard_map.69 = (bf16[1024,768]{1,0:T(8,128)(2,1)}, bf16[1024,1024]{1,0:T(8,128)(2,1)}) custom-call(s32[8]{0:T(128)} %add_multiply_fusion.first_ref, f32[3]{0:T(128)} %pad_maximum_fusion.scalars_ref, bf16[1024,768]{1,0:T(8,128)(2,1)} %all-gather.2.cloned.1.call-done.images_ref, bf16[512,896]{1,0:T(8,128)(2,1)} %bitcast.6, bf16[512,896]{1,0:T(8,128)(2,1)} %copy-done.4), custom_call_target="tpu_custom_call" | custom-call | flops 3221225472 | bytes 6291456 | tf_op jit(solution)/shard_map/pallas_call | solution.py:98
  65.2 0.0 reduce-scatter.2.cloned.1.call-update
  65.2 5.0 %shard_map.70 = (bf16[512,768]{1,0:T(8,128)(2,1)}, bf16[512,768]{1,0:T(8,128)(2,1)}) custom-call(bf16[1024,1024]{1,0:T(8,128)(2,1)} %get-tuple-element.11.weights_ref, bf16[1024,768]{1,0:T(8,128)(2,1)} %all-gather.2.cloned.1.call-done.images_ref), custom_call_target="tpu_custom_call" | custom-call | flops 1610612736 | bytes 3145728 | tf_op jit(solution)/shard_map/pallas_call | solution.py:138
  70.2 1.9 %collective-permute-start.1 = (bf16[512,768]{1,0:T(8,128)(2,1)}, bf16[512,768]{1,0:T(8,128)(2,1)S(1)}, u32[]{:S(2)}, u32[]{:S(2)}) collective-permute-start(bf16[512,768]{1,0:T(8,128)(2,1)} %get-tuple-element.13), channel_id=1, source_target_pairs={{0,1},{1,0},{2,3},{3,2},{4,5},{5,4},{6,7},{7,6},{8,9},{9,8},{10,11... | collective-permute-start | bytes 2359304 | tf_op jit(solution)/shard_map/ppermute | solution.py:200
  72.1 2.5 %collective-permute-done.1 = bf16[512,768]{1,0:T(8,128)(2,1)S(1)} collective-permute-done((bf16[512,768]{1,0:T(8,128)(2,1)}, bf16[512,768]{1,0:T(8,128)(2,1)S(1)}, u32[]{:S(2)}, u32[]{:S(2)}) %collective-permute-start.1) | collective-permute-done | bytes 786464 | tf_op jit(solution)/shard_map/ppermute | solution.py:200
  74.6 1.3 %add_convert_fusion = bf16[512,768]{1,0:T(8,128)(2,1)S(1)} fusion(bf16[512,768]{1,0:T(8,128)(2,1)S(1)} %collective-permute-done.1, bf16[512,768]{1,0:T(8,128)(2,1)} %get-tuple-element.12), kind=kLoop, calls=%fused_computation | loop fusion | flops 1572864 | bytes 2359296 | tf_op jit(solution)/shard_map/convert_element_type | solution.py:234
  75.9 0.0 copy-start
  75.9 0.0 copy-start.2
  75.9 15.2 %all_to_all.22 = bf16[4,128,768]{2,1,0:T(8,128)(2,1)S(1)} all-to-all(bf16[4,128,768]{2,1,0:T(8,128)(2,1)S(1)} %bitcast.4), channel_id=1, replica_groups=mesh['z'=8,'y'=8,'x'=4,'c'=2] {'x'}, dimensions={0} | all-to-all | bytes 1572864 | tf_op jit(solution)/shard_map/all_to_all | solution.py:209
  91.1 0.1 reduce_sum.12
  91.3 17.0 %all_to_all.23.text_grads_ref = bf16[8,16,768]{2,1,0:T(8,128)(2,1)S(1)} all-to-all(bf16[8,16,768]{2,1,0:T(8,128)(2,1)S(1)} %bitcast.8), channel_id=1, replica_groups=mesh['z'=8,'y'=8,'x'=4,'c'=2] {'z'}, dimensions={0} | all-to-all | bytes 393216 | tf_op jit(solution)/shard_map/all_to_all | solution.py:209
  108.3 0.0 reduce-scatter.2.cloned.1.call-done.image_grads_ref
  108.3 0.0 copy-done
  108.3 0.0 copy-done.2
  108.3 0.0 copy-start.1
  108.3 0.9 copy-done.1
  109.2 1.3 %shard_map.71 = (bf16[128,768]{1,0:T(8,128)(2,1)}, bf16[16,768]{1,0:T(8,128)(2,1)}) custom-call(bf16[128,768]{1,0:T(8,128)(2,1)S(1)} %copy-done, bf16[16,768]{1,0:T(8,128)(2,1)S(1)} %copy-done.2, bf16[128,768]{1,0:T(8,128)(2,1)S(1)} %copy-done.1, bf16[8,16,768]{2,1,0:T(8,128)(2,1)S(1)} %all_to_all.23.text_grads_ref), custom_call_target="tpu_custom_call" | custom-call | tf_op jit(solution)/shard_map/pallas_call | solution.py:175
Async XLA Ops:
  7.2 50.5 %all-gather.2.cloned.1.call-start = ((), (), s32[]{:S(2)}) async-start(), calls=%async_computation.5 | async-start | bytes 1769472 | tf_op jit(solution)/shard_map/all_gather | solution.py:216
  9.0 99.2 %reduce-scatter.2.cloned.1.call-start = ((), (), s32[]{:S(2)}) async-start(), calls=%async_computation.6 | async-start | bytes 1769472 | tf_op jit(solution)/shard_map/reduce_scatter | solution.py:230
  45.2 12.5 %copy-start.3 = (bf16[4,128,896]{2,1,0:T(8,128)(2,1)}, bf16[4,128,896]{2,1,0:T(8,128)(2,1)S(1)}, u32[]{:S(2)}) copy-start(bf16[4,128,896]{2,1,0:T(8,128)(2,1)S(1)} %all_to_all.21) | copy-start | bytes 2752516
  45.2 4.4 %collective-permute-start = (bf16[512,896]{1,0:T(8,128)(2,1)S(1)}, bf16[512,896]{1,0:T(8,128)(2,1)S(1)}, u32[]{:S(2)}, u32[]{:S(2)}) collective-permute-start(bf16[512,896]{1,0:T(8,128)(2,1)S(1)} %bitcast.5), channel_id=1, source_target_pairs={{0,1},{1,0},{2,3},{3,2},{4,5},{5,4},{6,7},{7,6},{8,9},{9,8},{10,11... | collective-permute-start | bytes 2752520 | tf_op jit(solution)/shard_map/ppermute | solution.py:200
  49.6 8.1 %copy-start.4 = (bf16[512,896]{1,0:T(8,128)(2,1)}, bf16[512,896]{1,0:T(8,128)(2,1)S(1)}, u32[]{:S(2)}) copy-start(bf16[512,896]{1,0:T(8,128)(2,1)S(1)} %collective-permute-done.other_ref) | copy-start | bytes 2752516
  70.2 4.4 %collective-permute-start.1 = (bf16[512,768]{1,0:T(8,128)(2,1)}, bf16[512,768]{1,0:T(8,128)(2,1)S(1)}, u32[]{:S(2)}, u32[]{:S(2)}) collective-permute-start(bf16[512,768]{1,0:T(8,128)(2,1)} %get-tuple-element.13), channel_id=1, source_target_pairs={{0,1},{1,0},{2,3},{3,2},{4,5},{5,4},{6,7},{7,6},{8,9},{9,8},{10,11... | collective-permute-start | bytes 2359304 | tf_op jit(solution)/shard_map/ppermute | solution.py:200
  75.9 32.3 %copy-start = (bf16[128,768]{1,0:T(8,128)(2,1)S(1)}, bf16[128,768]{1,0:T(8,128)(2,1)}, u32[]{:S(2)}) copy-start(bf16[128,768]{1,0:T(8,128)(2,1)} %image_ref.3) | copy-start | bytes 589828
  75.9 32.3 %copy-start.2 = (bf16[16,768]{1,0:T(8,128)(2,1)S(1)}, bf16[16,768]{1,0:T(8,128)(2,1)}, u32[]{:S(2)}) copy-start(bf16[16,768]{1,0:T(8,128)(2,1)} %text_ref.3) | copy-start | bytes 73732
  108.3 0.9 copy-start.1
Sparse Core Ops, SparseCore 0:
  10.7 46.9 all-gather.1
  65.3 41.5 reduce-scatter.1

commit v12 on v7

--- a/solution.py
+++ b/solution.py
@@ -11,12 +11,14 @@
 AXES = ("z", "y", "x", "c")
 SIZES = (8, 8, 4, 2)
 LANES = 128
+PIECES = 4
 MIB = 1024 * 1024
 ROWS_BY_ROWS = (((1,), (1,)), ((), ()))
 COLUMNS_BY_ROWS = (((0,), (0,)), ((), ()))
 
 smem = pl.BlockSpec(memory_space=pltpu.SMEM)
 vmem = pl.BlockSpec(memory_space=pltpu.VMEM)
+hbm = pl.BlockSpec(memory_space=pltpu.HBM)
 
 
 def params(mib):
@@ -70,10 +72,13 @@
 
 
 def pair_kernel(first_ref, scalars_ref, images_ref, own_ref, other_ref, *refs):
-    image_grad_ref, own_grad_ref, other_grad_ref, image_ref, text_ref, sem = refs
-    copy = pltpu.make_async_copy(images_ref, image_ref, sem)
-    copy.start()
-    width = image_ref.shape[1]
+    image_grads_ref, own_grad_ref, other_grad_ref, image_ref, text_ref, grad_ref, sems = refs
+    height, width = image_ref.shape
+    size = height // PIECES
+    pieces = [pl.ds(i * size, size) for i in range(PIECES)]
+    arriving = [pltpu.make_async_copy(images_ref.at[p], image_ref.at[p], sems.at[i]) for i, p in enumerate(pieces)]
+    for copy in arriving:
+        copy.start()
     count = own_ref.shape[0]
     text_ref[:count, :] = own_ref[...]
     text_ref[count:, :] = other_ref[...]
@@ -82,15 +87,21 @@
     row = lax.broadcasted_iota(jnp.int32, (128, 1), 0)
     rows = jnp.concatenate([row + first_ref[p] for p in range(image_ref.shape[0] // 128)], axis=0)
     texts = text_ref[:, :width]
-    copy.wait()
+    for copy in arriving:
+        copy.wait()
     images = image_ref[...]
     dots = lax.dot_general(images, texts, ROWS_BY_ROWS, preferred_element_type=jnp.float32)
     chance = 1.0 / (1.0 + jnp.exp2(dots * scalars_ref[1] + scalars_ref[2]))
     weight = (scalars_ref[0] * jnp.where(pairs == rows, chance - 1.0, chance)).astype(jnp.bfloat16)
-    image_grad_ref[...] = jnp.dot(weight, texts, preferred_element_type=jnp.float32).astype(image_grad_ref.dtype)
+    grad_ref[...] = jnp.dot(weight, texts, preferred_element_type=jnp.float32).astype(grad_ref.dtype)
+    leaving = [pltpu.make_async_copy(grad_ref.at[p], image_grads_ref.at[p], sems.at[i]) for i, p in enumerate(pieces)]
+    for copy in leaving:
+        copy.start()
     text_grad = lax.dot_general(weight, images, COLUMNS_BY_ROWS, preferred_element_type=jnp.float32)
     own_grad_ref[...] = text_grad[:count].astype(own_grad_ref.dtype)
     other_grad_ref[...] = text_grad[count:].astype(other_grad_ref.dtype)
+    for copy in leaving:
+        copy.wait()
 
 
 def pair_terms(first, scalars, images, own, other):
@@ -99,8 +110,8 @@
     texts = 2 * count
     return pl.pallas_call(
         pair_kernel,
-        in_specs=[smem, smem, pl.BlockSpec(memory_space=pl.ANY), vmem, vmem],
-        out_specs=[vmem] * 3,
+        in_specs=[smem, smem, hbm, vmem, vmem],
+        out_specs=[hbm, vmem, vmem],
         out_shape=[
             jax.ShapeDtypeStruct((rows, width), jnp.bfloat16),
             jax.ShapeDtypeStruct((count, width), jnp.bfloat16),
@@ -109,9 +120,10 @@
         scratch_shapes=[
             pltpu.VMEM((rows, width), jnp.bfloat16),
             pltpu.VMEM((texts, wide), jnp.bfloat16),
-            pltpu.SemaphoreType.DMA,
+            pltpu.VMEM((rows, width), jnp.bfloat16),
+            pltpu.SemaphoreType.DMA((PIECES,)),
         ],
-        compiler_params=params(32),
+        compiler_params=params(48),
         cost_estimate=pl.CostEstimate(
             flops=6 * rows * texts * width, bytes_accessed=4 * (rows + texts) * width, transcendentals=2 * rows * texts
         ),

time: 117 us -> 117 us (level)
  Pallas kernels: 10.4 us -> 12.2 us
  local copies, waits for them, and re-layouts: 2.42 us -> 1.01 us
    pallas_call x1, Pallas kernels: 6.27 us -> 8.01 us  [pair_terms(): pl.pallas_call(pair_kernel, in_specs=[smem, smem, hbm, vmem, vmem], out_s...]
    unnamed x8 -> x6, local copies, waits for them, and re-layouts: 2.35 us -> 0.94 us
where the time goes in v12:
time: 117 us; the launch traced here: 116 us
  blocking collectives  68.3 us (58%)
  between operations  15.4 us (13%)
  waiting for transfers between devices  14.9 us (13%)
  Pallas kernels  12.2 us (10%)
  starting transfers between devices  3.91 us (3%)
    all_to_all x2, blocking collectives, spread(): lax.all_to_all(copies, axis, split_axis=0, concat_axis=0, tiled=True)  36 us
    all_to_all x2, blocking collectives, parted(): return lax.all_to_all(parts, axis, split_axis=0, concat_axis=0, tiled=True)  32.4 us
    pallas_call x1, Pallas kernels, pair_terms(): pl.pallas_call(pair_kernel, in_specs=[smem, smem, hbm, vmem, vmem], out_s...  8.01 us
    all_gather x1, waiting for transfers between devices, on_device(): lax.all_gather(units(image_embed), AXES, axis=0, tiled=True, axis_index_g...  6.53 us
    reduce_scatter x1, waiting for transfers between devices, on_device(): lax.psum_scatter(image_part, AXES, scatter_dimension=0, tiled=True, axis_...  5.1 us
    ppermute x2, starting transfers between devices, exchanged(): return lax.ppermute(array, 'c', [(0, 1), (1, 0)])  3.83 us
    ppermute x2, waiting for transfers between devices, exchanged(): return lax.ppermute(array, 'c', [(0, 1), (1, 0)])  3.25 us
  transfers between devices with their start and end apart: 4, of which 4 were waited for; matrix products, arithmetic and copies ran while one was open for 0% of the time, Pallas kernels for 1%

profile of v12, /device:TPU:6, one launch (start us, length us, event | category | flops | bytes accessed | tf_op | source)
XLA Modules:
  0.0 116.2 jit_solution(16859672378311382402)
XLA Ops:
  7.2 0.0 all-gather.2.cloned.1.call-start
  7.2 1.7 %shard_map.68 = bf16[128,768]{1,0:T(8,128)(2,1)} custom-call(bf16[128,768]{1,0:T(8,128)(2,1)} %image_ref.1), custom_call_target="tpu_custom_call" | custom-call | tf_op jit(solution)/shard_map/pallas_call | solution.py:38
  8.9 0.0 all-gather.2.cloned.1.call-update
  9.0 0.0 reduce-scatter.2.cloned.1.call-start
  9.0 1.5 %shard_map.69 = bf16[8,16,896]{2,1,0:T(8,128)(2,1)} custom-call(s32[16]{0:T(128)} %pair_ref.1, bf16[16,768]{1,0:T(8,128)(2,1)} %text_ref.3), custom_call_target="tpu_custom_call" | custom-call | tf_op jit(solution)/shard_map/pallas_call | solution.py:65
  10.6 21.5 %all_to_all.20 = bf16[8,16,896]{2,1,0:T(8,128)(2,1)S(1)} all-to-all(bf16[8,16,896]{2,1,0:T(8,128)(2,1)} %shard_map.69), channel_id=1, replica_groups=mesh['z'=8,'y'=8,'x'=4,'c'=2] {'z'}, dimensions={0} | all-to-all | bytes 458752 | tf_op jit(solution)/shard_map/all_to_all | solution.py:178
  32.0 0.1 broadcast_in_dim.8
  32.1 14.5 %all_to_all.21 = bf16[4,128,896]{2,1,0:T(8,128)(2,1)S(1)} all-to-all(bf16[4,128,896]{2,1,0:T(8,128)(2,1)S(1)} %broadcast_in_dim.8), channel_id=1, replica_groups=mesh['z'=8,'y'=8,'x'=4,'c'=2] {'x'}, dimensions={0} | all-to-all | bytes 1835008 | tf_op jit(solution)/shard_map/all_to_all | solution.py:178
  46.6 1.9 %collective-permute-start = (bf16[512,896]{1,0:T(8,128)(2,1)S(1)}, bf16[512,896]{1,0:T(8,128)(2,1)S(1)}, u32[]{:S(2)}, u32[]{:S(2)}) collective-permute-start(bf16[512,896]{1,0:T(8,128)(2,1)S(1)} %bitcast.4), channel_id=1, source_target_pairs={{0,1},{1,0},{2,3},{3,2},{4,5},{5,4},{6,7},{7,6},{8,9},{9,8},{10,11... | collective-permute-start | bytes 2752520 | tf_op jit(solution)/shard_map/ppermute | solution.py:174
  49.9 0.1 pad_maximum_fusion.scalars_ref
  50.0 1.0 collective-permute-done.other_ref
  51.0 6.5 %all-gather.2.cloned.1.call-done.images_ref = bf16[1024,768]{1,0:T(8,128)(2,1)} async-done(((bf16[128,768]{1,0:T(8,128)(2,1)}), bf16[1024,768]{1,0:T(8,128)(2,1)}) %all-gather.2.cloned.1.call-update) | async-done | bytes 1572880 | tf_op jit(solution)/shard_map/all_gather | solution.py:189
  57.5 8.0 %shard_map.70 = (bf16[1024,768]{1,0:T(8,128)(2,1)}, bf16[512,768]{1,0:T(8,128)(2,1)S(1)}, bf16[512,768]{1,0:T(8,128)(2,1)S(1)}) custom-call(s32[8]{0:T(128)S(1)} %add_multiply_fusion.first_ref, f32[3]{0:T(128)S(1)} %pad_maximum_fusion.scalars_ref, bf16[1024,768]{1,0:T(8,128)(2,1)} %all-gather.2.cloned.1.call-done.images_ref, bf16[512,896]{1,0:T(8,128)(2,1)S(1)} %bitcast.5, ...), custom_call_target="tpu_custom_call" | custom-call | flops 4831838208 | bytes 6291456 | tf_op jit(solution)/shard_map/pallas_call | solution.py:111
  65.5 0.0 reduce-scatter.2.cloned.1.call-update
  65.5 1.9 %collective-permute-start.1 = (bf16[512,768]{1,0:T(8,128)(2,1)S(1)}, bf16[512,768]{1,0:T(8,128)(2,1)S(1)}, u32[]{:S(2)}, u32[]{:S(2)}) collective-permute-start(bf16[512,768]{1,0:T(8,128)(2,1)S(1)} %get-tuple-element.7), channel_id=1, source_target_pairs={{0,1},{1,0},{2,3},{3,2},{4,5},{5,4},{6,7},{7,6},{8,9},{9,8},{10,11... | collective-permute-start | bytes 2359304 | tf_op jit(solution)/shard_map/ppermute | solution.py:174
  67.5 2.3 %collective-permute-done.1 = bf16[512,768]{1,0:T(8,128)(2,1)S(1)} collective-permute-done((bf16[512,768]{1,0:T(8,128)(2,1)S(1)}, bf16[512,768]{1,0:T(8,128)(2,1)S(1)}, u32[]{:S(2)}, u32[]{:S(2)}) %collective-permute-start.1) | collective-permute-done | bytes 786464 | tf_op jit(solution)/shard_map/ppermute | solution.py:174
  69.7 0.2 add_convert_fusion
  69.9 0.0 copy-start
  70.0 0.0 copy-start.2
  70.0 15.2 %all_to_all.22 = bf16[4,128,768]{2,1,0:T(8,128)(2,1)S(1)} all-to-all(bf16[4,128,768]{2,1,0:T(8,128)(2,1)S(1)} %bitcast.6), channel_id=1, replica_groups=mesh['z'=8,'y'=8,'x'=4,'c'=2] {'x'}, dimensions={0} | all-to-all | bytes 1572864 | tf_op jit(solution)/shard_map/all_to_all | solution.py:183
  85.2 0.1 reduce_sum.12
  85.3 17.1 %all_to_all.23.text_grads_ref = bf16[8,16,768]{2,1,0:T(8,128)(2,1)S(1)} all-to-all(bf16[8,16,768]{2,1,0:T(8,128)(2,1)S(1)} %bitcast.8), channel_id=1, replica_groups=mesh['z'=8,'y'=8,'x'=4,'c'=2] {'z'}, dimensions={0} | all-to-all | bytes 393216 | tf_op jit(solution)/shard_map/all_to_all | solution.py:183
  102.5 5.1 %reduce-scatter.2.cloned.1.call-done.image_grad_ref = bf16[128,768]{1,0:T(8,128)(2,1)} async-done(((bf16[1024,768]{1,0:T(8,128)(2,1)}), bf16[128,768]{1,0:T(8,128)(2,1)}) %reduce-scatter.2.cloned.1.call-update) | async-done | bytes 196624 | tf_op jit(solution)/shard_map/reduce_scatter | solution.py:203
  107.6 0.0 copy-done
  107.6 0.0 copy-done.2
  107.6 0.0 copy-start.1
  107.6 0.9 copy-done.1
  108.5 0.9 shard_map.71
  (1 shorter events, 0.0 us)
Async XLA Ops:
  7.2 50.3 %all-gather.2.cloned.1.call-start = ((), (), s32[]{:S(2)}) async-start(), calls=%async_computation.5 | async-start | bytes 1769472 | tf_op jit(solution)/shard_map/all_gather | solution.py:189
  9.0 98.6 %reduce-scatter.2.cloned.1.call-start = ((), (), s32[]{:S(2)}) async-start(), calls=%async_computation.6 | async-start | bytes 1769472 | tf_op jit(solution)/shard_map/reduce_scatter | solution.py:203
  46.6 4.4 %collective-permute-start = (bf16[512,896]{1,0:T(8,128)(2,1)S(1)}, bf16[512,896]{1,0:T(8,128)(2,1)S(1)}, u32[]{:S(2)}, u32[]{:S(2)}) collective-permute-start(bf16[512,896]{1,0:T(8,128)(2,1)S(1)} %bitcast.4), channel_id=1, source_target_pairs={{0,1},{1,0},{2,3},{3,2},{4,5},{5,4},{6,7},{7,6},{8,9},{9,8},{10,11... | collective-permute-start | bytes 2752520 | tf_op jit(solution)/shard_map/ppermute | solution.py:174
  65.5 4.2 %collective-permute-start.1 = (bf16[512,768]{1,0:T(8,128)(2,1)S(1)}, bf16[512,768]{1,0:T(8,128)(2,1)S(1)}, u32[]{:S(2)}, u32[]{:S(2)}) collective-permute-start(bf16[512,768]{1,0:T(8,128)(2,1)S(1)} %get-tuple-element.7), channel_id=1, source_target_pairs={{0,1},{1,0},{2,3},{3,2},{4,5},{5,4},{6,7},{7,6},{8,9},{9,8},{10,11... | collective-permute-start | bytes 2359304 | tf_op jit(solution)/shard_map/ppermute | solution.py:174
  69.9 37.6 %copy-start = (bf16[128,768]{1,0:T(8,128)(2,1)S(1)}, bf16[128,768]{1,0:T(8,128)(2,1)}, u32[]{:S(2)}) copy-start(bf16[128,768]{1,0:T(8,128)(2,1)} %image_ref.1) | copy-start | bytes 589828
  70.0 37.6 %copy-start.2 = (bf16[16,768]{1,0:T(8,128)(2,1)S(1)}, bf16[16,768]{1,0:T(8,128)(2,1)}, u32[]{:S(2)}) copy-start(bf16[16,768]{1,0:T(8,128)(2,1)} %text_ref.3) | copy-start | bytes 73732
  107.6 0.9 copy-start.1
Sparse Core Ops, SparseCore 0:
  10.7 46.8 all-gather.1
  65.7 41.8 reduce-scatter.1

commit v13 on v6

v13 whole, which is shorter than its diff:
```python
import math

import jax
import jax.numpy as jnp
from jax import lax
from jax.experimental import pallas as pl
from jax.experimental.pallas import tpu as pltpu
from jax.sharding import Mesh
from jax.sharding import PartitionSpec as P

AXES = ("z", "y", "x", "c")
SIZES = (8, 8, 4, 2)
FAR = ("z", "y")
MIB = 1024 * 1024
ROWS_BY_ROWS = (((1,), (1,)), ((), ()))
COLUMNS_BY_ROWS = (((0,), (0,)), ((), ()))

smem = pl.BlockSpec(memory_space=pltpu.SMEM)
vmem = pl.BlockSpec(memory_space=pltpu.VMEM)


def params(mib):
    return pltpu.CompilerParams(vmem_limit_bytes=mib * MIB)


def inverse_norm(floats):
    return lax.rsqrt(jnp.sum(floats * floats, axis=-1, keepdims=True) + 1e-06)


def unit_kernel(image_ref, text_ref, unit_ref, copies_ref):
    floats = image_ref[...].astype(jnp.float32)
    unit_ref[...] = (floats * inverse_norm(floats)).astype(unit_ref.dtype)
    floats = text_ref[...].astype(jnp.float32)
    unit = (floats * inverse_norm(floats)).astype(copies_ref.dtype)
    for peer in range(copies_ref.shape[0]):
        copies_ref[peer] = unit


def units_and_copies(image_embed, text_embed, peers):
    return pl.pallas_call(
        unit_kernel,
        in_specs=[vmem] * 2,
        out_specs=[vmem] * 2,
        out_shape=[
            jax.ShapeDtypeStruct(image_embed.shape, jnp.bfloat16),
            jax.ShapeDtypeStruct((peers,) + text_embed.shape, jnp.bfloat16),
        ],
        compiler_params=params(56),
    )(image_embed, text_embed)


def weight_kernel(first_ref, scalars_ref, own_ref, other_ref, text_ref, pair_ref, weight_ref, grad_ref, image_ref):
    half = own_ref.shape[0]
    image_ref[:half, :] = own_ref[...]
    image_ref[half:, :] = other_ref[...]
    row = lax.broadcasted_iota(jnp.int32, (128, 1), 0)
    places = jnp.concatenate([row + first_ref[p] for p in range(2 * half // 128)], axis=0)
    images = image_ref[...]
    dots = lax.dot_general(images, text_ref[...], ROWS_BY_ROWS, preferred_element_type=jnp.float32)
    chance = 1.0 / (1.0 + jnp.exp2(dots * scalars_ref[1] + scalars_ref[2]))
    weight = (scalars_ref[0] * jnp.where(pair_ref[...] == places, chance - 1.0, chance)).astype(jnp.bfloat16)
    weight_ref[...] = weight
    grad = lax.dot_general(weight, images, COLUMNS_BY_ROWS, preferred_element_type=jnp.float32)
    grad_ref[...] = grad.astype(grad_ref.dtype)


def weights_and_text_terms(first, scalars, own, other, texts, pairs):
    half, width = own.shape
    count = texts.shape[0]
    return pl.pallas_call(
        weight_kernel,
        in_specs=[smem, smem] + [vmem] * 4,
        out_specs=[vmem] * 2,
        out_shape=[
            jax.ShapeDtypeStruct((2 * half, count), jnp.bfloat16),
            jax.ShapeDtypeStruct((count, width), jnp.bfloat16),
        ],
        scratch_shapes=[pltpu.VMEM((2 * half, width), jnp.bfloat16)],
        compiler_params=params(32),
        cost_estimate=pl.CostEstimate(
            flops=8 * half * count * width,
            bytes_accessed=4 * (half + count) * width + 4 * half * count,
            transcendentals=4 * half * count,
        ),
    )(first, scalars, own, other, texts, pairs)


def image_kernel(weight_ref, text_ref, own_ref, other_ref):
    grad = jnp.dot(weight_ref[...], text_ref[...], preferred_element_type=jnp.float32)
    half = own_ref.shape[0]
    own_ref[...] = grad[:half].astype(own_ref.dtype)
    other_ref[...] = grad[half:].astype(other_ref.dtype)


def image_terms(weights, texts):
    rows, count = weights.shape
    width = texts.shape[1]
    return pl.pallas_call(
        image_kernel,
        in_specs=[vmem] * 2,
        out_specs=[vmem] * 2,
        out_shape=[jax.ShapeDtypeStruct((rows // 2, width), jnp.bfloat16)] * 2,
        compiler_params=params(24),
        cost_estimate=pl.CostEstimate(
            flops=2 * rows * count * width, bytes_accessed=2 * (rows + count) * width + 2 * rows * count, transcendentals=0
        ),
    )(weights, texts)


def backward_kernel(embed_ref, *refs):
    floats = embed_ref[...].astype(jnp.float32)
    inverse = inverse_norm(floats)
    unit = floats * inverse
    parts_refs, out_ref = refs[:-1], refs[-1]
    grad = None
    for ref in parts_refs:
        for part in [ref[...]] if len(ref.shape) == 2 else [ref[i] for i in range(ref.shape[0])]:
            part = part.astype(jnp.float32)
            grad = part if grad is None else grad + part
    along = jnp.sum(unit * grad, axis=-1, keepdims=True)
    out_ref[...] = ((grad - unit * along) * inverse).astype(out_ref.dtype)


def unit_backward(embed, *parts):
    return pl.pallas_call(
        backward_kernel,
        in_specs=[vmem] * (1 + len(parts)),
        out_specs=vmem,
        out_shape=jax.ShapeDtypeStruct(embed.shape, jnp.bfloat16),
        compiler_params=params(8),
    )(embed, *parts)


def shifted(array, axis, by):
    devices = lax.axis_size(axis)
    return lax.ppermute(array, axis, [(i, (i + by) % devices) for i in range(devices)])


def on_device(image_embed, text_embed, log_scale, logit_bias, pair_index):
    own_images, width = image_embed.shape
    own_texts = text_embed.shape[0]
    peers, ring = lax.axis_size(FAR), lax.axis_size("x")

    unit, copies = units_and_copies(image_embed, text_embed, peers)
    texts = lax.all_to_all(copies, FAR, split_axis=0, concat_axis=0, tiled=True).reshape(-1, width)
    pairs = lax.all_gather(pair_index, FAR, axis=0, tiled=True)
    own = lax.all_gather(unit, "x", axis=0, tiled=True)
    other = shifted(own, "c", 1)

    scale = jnp.exp(log_scale)
    scalars = jnp.concatenate([scale, -math.log2(math.e) * scale, -math.log2(math.e) * logit_bias])
    far, x, c = lax.axis_index(FAR), lax.axis_index("x"), lax.axis_index("c")
    first = jnp.stack(
        [((far * ring + place) * 2 + core) * own_images for core in (c, 1 - c) for place in range(ring)]
    ).astype(jnp.int32)
    weights, text_part = weights_and_text_terms(first, scalars, own, other, texts, pairs[None, :])
    text_parts = lax.all_to_all(
        text_part.reshape(peers, own_texts, width), FAR, split_axis=0, concat_axis=0, tiled=True
    )

    own_part, other_part = image_terms(weights, texts)
    part = own_part.astype(jnp.float32) + shifted(other_part, "c", 1).astype(jnp.float32)
    part = part.astype(jnp.bfloat16).reshape(ring, own_images, width)
    parts = [lax.dynamic_index_in_dim(part, (x + s) % ring, 0, keepdims=False) for s in range(ring)]
    parts = parts[:1] + [shifted(parts[s], "x", s) for s in range(1, ring)]
    return unit_backward(image_embed, *parts), unit_backward(text_embed, text_parts)


def solution(mesh):
    split = Mesh(mesh.devices.reshape(SIZES), AXES)
    rows = P(AXES, None)
    return jax.shard_map(
        on_device,
        mesh=split,
        in_specs=(rows, rows, P(), P(), P(AXES)),
        out_specs=(rows, rows),
        check_vma=False,
    )
```

time: 134 us -> 128 us (0.955)
  the two profiles are of different devices: /device:TPU:1 before, /device:TPU:6 now
where the time goes in v13:
time: 128 us
  blocking collectives  49.3 us (39%)
  starting transfers between devices  37.5 us (29%)
  waiting for transfers between devices  17.3 us (14%)
  Pallas kernels  13.7 us (11%)
  local copies, waits for them, and re-layouts  5.55 us (4%)
  between operations  2.81 us (2%)
  other arithmetic  1.43 us (1%)
    unnamed x1, blocking collectives  35.2 us
    all_to_all x1, starting transfers between devices, on_device(): lax.all_to_all(copies, FAR, split_axis=0, concat_axis=0, tiled=True)  16.7 us
    all_gather x1, blocking collectives, on_device(): own = lax.all_gather(unit, 'x', axis=0, tiled=True)  14.1 us
    ppermute x5, starting transfers between devices, shifted(): lax.ppermute(array, axis, [(i, (i + by) % devices) for i in range(devices)])  12.4 us
    ppermute x5, waiting for transfers between devices, shifted(): lax.ppermute(array, axis, [(i, (i + by) % devices) for i in range(devices)])  10.4 us
    all_to_all x1, starting transfers between devices, on_device(): lax.all_to_all(text_part.reshape(peers, own_texts, width), FAR, split_axi...  8.34 us
    all_to_all x1, waiting for transfers between devices, on_device(): lax.all_to_all(text_part.reshape(peers, own_texts, width), FAR, split_axi...  6.87 us
    pallas_call x1, Pallas kernels, weights_and_text_terms(): pl.pallas_call(weight_kernel, in_specs=[smem, smem] + [vmem] * 4, out_spe...  6.84 us
  transfers between devices with their start and end apart: 7, of which 5 were waited for; matrix products, arithmetic and copies ran while one was open for 2% of the time, Pallas kernels for 3%

profile of v13, /device:TPU:6, one launch (start us, length us, event | category | flops | bytes accessed | tf_op | source)
XLA Modules:
  0.0 127.6 jit_solution(10613986659434311725)
XLA Ops:
  0.6 2.3 %shard_map.68 = (bf16[128,768]{1,0:T(8,128)(2,1)}, bf16[64,16,768]{2,1,0:T(8,128)(2,1)}) custom-call(bf16[128,768]{1,0:T(8,128)(2,1)} %embed_ref.2, bf16[16,768]{1,0:T(8,128)(2,1)} %embed_ref.3), custom_call_target="tpu_custom_call" | custom-call | tf_op jit(solution)/shard_map/pallas_call | solution.py:40
  3.0 0.0 copy-start.5
  3.0 0.0 copy-start.6
  3.0 16.7 %all-to-all-start = ((bf16[64,16,768]{2,1,0:T(8,128)(2,1)}), bf16[64,16,768]{2,1,0:T(8,128)(2,1)S(1)}, u32[]{:S(2)}, u32[]{:S(2)}) async-start(bf16[64,16,768]{2,1,0:T(8,128)(2,1)} %get-tuple-element.9), calls=%async_computation | async-start | bytes 3145728 | tf_op jit(solution)/shard_map/all_to_all | solution.py:145
  19.7 0.0 copy-done.5
  19.7 14.1 %all_gather.6.own_ref = bf16[512,768]{1,0:T(8,128)(2,1)S(1)} all-gather(bf16[128,768]{1,0:T(8,128)(2,1)S(1)} %copy-done.5), channel_id=1, replica_groups=mesh['z'=8,'y'=8,'x'=4,'c'=2] {'x'}, dimensions={0}, use_global_device_ids=true | all-gather | bytes 983040 | tf_op jit(solution)/shard_map/all_gather | solution.py:147
  33.8 1.9 %collective-permute-start = (bf16[512,768]{1,0:T(8,128)(2,1)S(1)}, bf16[512,768]{1,0:T(8,128)(2,1)}, u32[]{:S(2)}, u32[]{:S(2)}) collective-permute-start(bf16[512,768]{1,0:T(8,128)(2,1)S(1)} %all_gather.6.own_ref), channel_id=1, source_target_pairs={{0,1},{1,0},{2,3},{3,2},{4,5},{5,4},{6,7},{7,6},{8,9},{9,8},{10,11... | collective-permute-start | bytes 2359304 | tf_op jit(solution)/shard_map/ppermute | solution.py:136
  37.1 1.3 %dynamic-slice = u32[1]{0:T(128)} dynamic-slice(u32[512]{0:T(512)} %constant.68, u32[]{:T(128)S(6)} %add.101), dynamic_slice_sizes={1} | dynamic-slice | bytes 12
  39.0 0.0 copy-done.6
  39.0 0.2 dynamic-update-slice
  39.3 0.1 stack.35.first_ref
  39.4 35.2 %all-reduce = s32[1024]{0:T(1024)S(1)} all-reduce(s32[1024]{0:T(1024)S(1)} %dynamic-update-slice), channel_id=1, replica_groups=mesh['z'=8,'y'=8,'x'=4,'c'=2] {'z','y'}, use_global_device_ids=true, to_apply=%add | all-reduce | flops 1024 | bytes 8192
  74.6 0.1 pad_maximum_fusion.scalars_ref
  74.7 0.0 collective-permute-done.other_ref
  74.7 0.0 all-to-all-done
  74.7 6.8 %shard_map.69 = (bf16[1024,1024]{1,0:T(8,128)(2,1)S(1)}, bf16[1024,768]{1,0:T(8,128)(2,1)}) custom-call(s32[8]{0:T(128)S(1)} %stack.35.first_ref, f32[3]{0:T(128)S(1)} %pad_maximum_fusion.scalars_ref, bf16[512,768]{1,0:T(8,128)(2,1)S(1)} %all_gather.6.own_ref, bf16[512,768]{1,0:T(8,128)(2,1)} %collective-permute-done.other_ref, ...), custom_call_target="tpu_custom_call" | custom-call | flops 3221225472 | bytes 6815744 | tf_op jit(solution)/shard_map/pallas_call | solution.py:70
  81.5 0.0 copy-start.3
  81.5 1.3 %copy-done.3 = bf16[1024,1024]{1,0:T(8,128)(2,1)} copy-done((bf16[1024,1024]{1,0:T(8,128)(2,1)}, bf16[1024,1024]{1,0:T(8,128)(2,1)S(1)}, u32[]{:S(2)}) %copy-start.3) | copy-done | bytes 2097176
  82.9 8.3 %all-to-all-start.1 = ((bf16[64,16,768]{2,1,0:T(8,128)(2,1)}), bf16[64,16,768]{2,1,0:T(8,128)(2,1)S(1)}, u32[]{:S(2)}, u32[]{:S(2)}) async-start(bf16[64,16,768]{2,1,0:T(8,128)(2,1)} %bitcast.16), calls=%async_computation.1 | async-start | bytes 3145728 | tf_op jit(solution)/shard_map/all_to_all | solution.py:157
  91.2 0.0 copy-start.4
  91.2 1.6 %copy-done.4 = bf16[1024,1024]{1,0:T(8,128)(2,1)S(1)} copy-done((bf16[1024,1024]{1,0:T(8,128)(2,1)S(1)}, bf16[1024,1024]{1,0:T(8,128)(2,1)}, u32[]{:S(2)}) %copy-start.4) | copy-done | bytes 2097176
  92.8 2.7 %shard_map.70 = (bf16[512,768]{1,0:T(8,128)(2,1)S(1)}, bf16[512,768]{1,0:T(8,128)(2,1)}) custom-call(bf16[1024,1024]{1,0:T(8,128)(2,1)S(1)} %copy-done.4, bf16[1024,768]{1,0:T(8,128)(2,1)S(1)} %bitcast.22), custom_call_target="tpu_custom_call" | custom-call | flops 1610612736 | bytes 5242880 | tf_op jit(solution)/shard_map/pallas_call | solution.py:98
  95.5 0.0 copy-start.1
  95.5 0.9 copy-done.1
  96.4 1.9 %collective-permute-start.1 = (bf16[512,768]{1,0:T(8,128)(2,1)}, bf16[512,768]{1,0:T(8,128)(2,1)S(1)}, u32[]{:S(2)}, u32[]{:S(2)}) collective-permute-start(bf16[512,768]{1,0:T(8,128)(2,1)} %get-tuple-element.12), channel_id=1, source_target_pairs={{0,1},{1,0},{2,3},{3,2},{4,5},{5,4},{6,7},{7,6},{8,9},{9,8},{10,11... | collective-permute-start | bytes 2359304 | tf_op jit(solution)/shard_map/ppermute | solution.py:136
  98.4 2.4 %collective-permute-done.1 = bf16[512,768]{1,0:T(8,128)(2,1)S(1)} collective-permute-done((bf16[512,768]{1,0:T(8,128)(2,1)}, bf16[512,768]{1,0:T(8,128)(2,1)S(1)}, u32[]{:S(2)}, u32[]{:S(2)}) %collective-permute-start.1) | collective-permute-done | bytes 786464 | tf_op jit(solution)/shard_map/ppermute | solution.py:136
  100.8 0.0 copy-start
  100.8 1.4 %add_convert_fusion = bf16[512,768]{1,0:T(8,128)(2,1)S(1)} fusion(bf16[512,768]{1,0:T(8,128)(2,1)S(1)} %collective-permute-done.1, bf16[512,768]{1,0:T(8,128)(2,1)} %copy-done.1), kind=kLoop, calls=%fused_computation | loop fusion | flops 1572864 | bytes 2359296 | tf_op jit(solution)/shard_map/convert_element_type | solution.py:163
  102.2 0.0 copy-start.2
  102.2 0.1 dynamic-slice_bitcast_fusion
  102.2 2.4 %collective-permute-start.2 = (bf16[128,768]{1,0:T(8,128)(2,1)S(1)}, bf16[128,768]{1,0:T(8,128)(2,1)S(1)}, u32[]{:S(2)}, u32[]{:S(2)}) collective-permute-start(bf16[128,768]{1,0:T(8,128)(2,1)S(1)} %get-tuple-element.16), channel_id=1, source_target_pairs={{0,2},{2,4},{4,6},{6,0},{1,3},{3,5},{5,7},{7,1},{8,10},{10,12},{12... | collective-permute-start | bytes 589832 | tf_op jit(solution)/shard_map/ppermute | solution.py:136
  104.6 4.3 %collective-permute-start.3 = (bf16[128,768]{1,0:T(8,128)(2,1)S(1)}, bf16[128,768]{1,0:T(8,128)(2,1)S(1)}, u32[]{:S(2)}, u32[]{:S(2)}) collective-permute-start(bf16[128,768]{1,0:T(8,128)(2,1)S(1)} %get-tuple-element.15), channel_id=1, source_target_pairs={{0,4},{2,6},{4,0},{6,2},{1,5},{3,7},{5,1},{7,3},{8,12},{10,14},{12... | collective-permute-start | bytes 589832 | tf_op jit(solution)/shard_map/ppermute | solution.py:136
  109.0 1.9 %collective-permute-start.4 = (bf16[128,768]{1,0:T(8,128)(2,1)S(1)}, bf16[128,768]{1,0:T(8,128)(2,1)S(1)}, u32[]{:S(2)}, u32[]{:S(2)}) collective-permute-start(bf16[128,768]{1,0:T(8,128)(2,1)S(1)} %get-tuple-element.14), channel_id=1, source_target_pairs={{0,6},{2,0},{4,2},{6,4},{1,7},{3,1},{5,3},{7,5},{8,14},{10,8},{12,... | collective-permute-start | bytes 589832 | tf_op jit(solution)/shard_map/ppermute | solution.py:136
  110.9 1.0 collective-permute-done.2.refs_1_
  111.9 3.2 %collective-permute-done.3.refs_2_ = bf16[128,768]{1,0:T(8,128)(2,1)S(1)} collective-permute-done((bf16[128,768]{1,0:T(8,128)(2,1)S(1)}, bf16[128,768]{1,0:T(8,128)(2,1)S(1)}, u32[]{:S(2)}, u32[]{:S(2)}) %collective-permute-start.3) | collective-permute-done | bytes 196640 | tf_op jit(solution)/shard_map/ppermute | solution.py:136
  115.1 3.9 %collective-permute-done.4.refs_3_ = bf16[128,768]{1,0:T(8,128)(2,1)S(1)} collective-permute-done((bf16[128,768]{1,0:T(8,128)(2,1)S(1)}, bf16[128,768]{1,0:T(8,128)(2,1)S(1)}, u32[]{:S(2)}, u32[]{:S(2)}) %collective-permute-start.4) | collective-permute-done | bytes 196640 | tf_op jit(solution)/shard_map/ppermute | solution.py:136
  118.9 0.0 copy-done
  118.9 0.9 shard_map.71
  119.8 6.9 %all-to-all-done.1.refs_0_ = bf16[64,16,768]{2,1,0:T(8,128)(2,1)S(1)} async-done(((bf16[64,16,768]{2,1,0:T(8,128)(2,1)}), bf16[64,16,768]{2,1,0:T(8,128)(2,1)S(1)}, u32[]{:S(2)}, u32[]{:S(2)}) %all-to-all-start.1) | async-done | bytes 1572896 | tf_op jit(solution)/shard_map/all_to_all | solution.py:157
  126.7 0.0 copy-done.2
  126.7 0.9 shard_map.72
  (1 shorter events, 0.0 us)
Async XLA Ops:
  3.0 16.7 %copy-start.5 = (bf16[128,768]{1,0:T(8,128)(2,1)S(1)}, bf16[128,768]{1,0:T(8,128)(2,1)}, u32[]{:S(2)}) copy-start(bf16[128,768]{1,0:T(8,128)(2,1)} %get-tuple-element.8) | copy-start | bytes 589828
  3.0 36.1 %copy-start.6 = (s32[16]{0:T(128)S(1)}, s32[16]{0:T(128)}, u32[]{:S(2)}) copy-start(s32[16]{0:T(128)} %param.9) | copy-start | bytes 196
  3.0 71.7 %all-to-all-start = ((bf16[64,16,768]{2,1,0:T(8,128)(2,1)}), bf16[64,16,768]{2,1,0:T(8,128)(2,1)S(1)}, u32[]{:S(2)}, u32[]{:S(2)}) async-start(bf16[64,16,768]{2,1,0:T(8,128)(2,1)} %get-tuple-element.9), calls=%async_computation | async-start | bytes 3145728 | tf_op jit(solution)/shard_map/all_to_all | solution.py:145
  33.8 40.9 %collective-permute-start = (bf16[512,768]{1,0:T(8,128)(2,1)S(1)}, bf16[512,768]{1,0:T(8,128)(2,1)}, u32[]{:S(2)}, u32[]{:S(2)}) collective-permute-start(bf16[512,768]{1,0:T(8,128)(2,1)S(1)} %all_gather.6.own_ref), channel_id=1, source_target_pairs={{0,1},{1,0},{2,3},{3,2},{4,5},{5,4},{6,7},{7,6},{8,9},{9,8},{10,11... | collective-permute-start | bytes 2359304 | tf_op jit(solution)/shard_map/ppermute | solution.py:136
  81.5 1.3 %copy-start.3 = (bf16[1024,1024]{1,0:T(8,128)(2,1)}, bf16[1024,1024]{1,0:T(8,128)(2,1)S(1)}, u32[]{:S(2)}) copy-start(bf16[1024,1024]{1,0:T(8,128)(2,1)S(1)} %get-tuple-element.10.weight_ref) | copy-start | bytes 6291460
  82.9 43.8 %all-to-all-start.1 = ((bf16[64,16,768]{2,1,0:T(8,128)(2,1)}), bf16[64,16,768]{2,1,0:T(8,128)(2,1)S(1)}, u32[]{:S(2)}, u32[]{:S(2)}) async-start(bf16[64,16,768]{2,1,0:T(8,128)(2,1)} %bitcast.16), calls=%async_computation.1 | async-start | bytes 3145728 | tf_op jit(solution)/shard_map/all_to_all | solution.py:157
  91.2 1.6 %copy-start.4 = (bf16[1024,1024]{1,0:T(8,128)(2,1)S(1)}, bf16[1024,1024]{1,0:T(8,128)(2,1)}, u32[]{:S(2)}) copy-start(bf16[1024,1024]{1,0:T(8,128)(2,1)} %copy-done.3) | copy-start | bytes 6291460
  95.5 0.9 copy-start.1
  96.4 4.4 %collective-permute-start.1 = (bf16[512,768]{1,0:T(8,128)(2,1)}, bf16[512,768]{1,0:T(8,128)(2,1)S(1)}, u32[]{:S(2)}, u32[]{:S(2)}) collective-permute-start(bf16[512,768]{1,0:T(8,128)(2,1)} %get-tuple-element.12), channel_id=1, source_target_pairs={{0,1},{1,0},{2,3},{3,2},{4,5},{5,4},{6,7},{7,6},{8,9},{9,8},{10,11... | collective-permute-start | bytes 2359304 | tf_op jit(solution)/shard_map/ppermute | solution.py:136
  100.8 18.1 %copy-start = (bf16[128,768]{1,0:T(8,128)(2,1)S(1)}, bf16[128,768]{1,0:T(8,128)(2,1)}, u32[]{:S(2)}) copy-start(bf16[128,768]{1,0:T(8,128)(2,1)} %embed_ref.2) | copy-start | bytes 589828
  102.2 24.6 %copy-start.2 = (bf16[16,768]{1,0:T(8,128)(2,1)S(1)}, bf16[16,768]{1,0:T(8,128)(2,1)}, u32[]{:S(2)}) copy-start(bf16[16,768]{1,0:T(8,128)(2,1)} %embed_ref.3) | copy-start | bytes 73732
  102.2 9.6 %collective-permute-start.2 = (bf16[128,768]{1,0:T(8,128)(2,1)S(1)}, bf16[128,768]{1,0:T(8,128)(2,1)S(1)}, u32[]{:S(2)}, u32[]{:S(2)}) collective-permute-start(bf16[128,768]{1,0:T(8,128)(2,1)S(1)} %get-tuple-element.16), channel_id=1, source_target_pairs={{0,2},{2,4},{4,6},{6,0},{1,3},{3,5},{5,7},{7,1},{8,10},{10,12},{12... | collective-permute-start | bytes 589832 | tf_op jit(solution)/shard_map/ppermute | solution.py:136
  104.6 10.4 %collective-permute-start.3 = (bf16[128,768]{1,0:T(8,128)(2,1)S(1)}, bf16[128,768]{1,0:T(8,128)(2,1)S(1)}, u32[]{:S(2)}, u32[]{:S(2)}) collective-permute-start(bf16[128,768]{1,0:T(8,128)(2,1)S(1)} %get-tuple-element.15), channel_id=1, source_target_pairs={{0,4},{2,6},{4,0},{6,2},{1,5},{3,7},{5,1},{7,3},{8,12},{10,14},{12... | collective-permute-start | bytes 589832 | tf_op jit(solution)/shard_map/ppermute | solution.py:136
  109.0 9.9 %collective-permute-start.4 = (bf16[128,768]{1,0:T(8,128)(2,1)S(1)}, bf16[128,768]{1,0:T(8,128)(2,1)S(1)}, u32[]{:S(2)}, u32[]{:S(2)}) collective-permute-start(bf16[128,768]{1,0:T(8,128)(2,1)S(1)} %get-tuple-element.14), channel_id=1, source_target_pairs={{0,6},{2,0},{4,2},{6,4},{1,7},{3,1},{5,3},{7,5},{8,14},{10,8},{12,... | collective-permute-start | bytes 589832 | tf_op jit(solution)/shard_map/ppermute | solution.py:136

commit v14 on v13

--- a/solution.py
+++ b/solution.py
@@ -11,12 +11,15 @@
 AXES = ("z", "y", "x", "c")
 SIZES = (8, 8, 4, 2)
 FAR = ("z", "y")
+LANES = 128
+SUBLANES = 8
 MIB = 1024 * 1024
 ROWS_BY_ROWS = (((1,), (1,)), ((), ()))
 COLUMNS_BY_ROWS = (((0,), (0,)), ((), ()))
 
 smem = pl.BlockSpec(memory_space=pltpu.SMEM)
 vmem = pl.BlockSpec(memory_space=pltpu.VMEM)
+hbm = pl.BlockSpec(memory_space=pltpu.HBM)
 
 
 def params(mib):
@@ -27,84 +30,130 @@
     return lax.rsqrt(jnp.sum(floats * floats, axis=-1, keepdims=True) + 1e-06)
 
 
-def unit_kernel(image_ref, text_ref, unit_ref, copies_ref):
+def unit_kernel(pair_ref, image_ref, text_ref, unit_ref, packet_ref):
     floats = image_ref[...].astype(jnp.float32)
     unit_ref[...] = (floats * inverse_norm(floats)).astype(unit_ref.dtype)
+    rows, width = text_ref.shape
     floats = text_ref[...].astype(jnp.float32)
-    unit = (floats * inverse_norm(floats)).astype(copies_ref.dtype)
-    for peer in range(copies_ref.shape[0]):
-        copies_ref[peer] = unit
-
-
-def units_and_copies(image_embed, text_embed, peers):
+    unit = (floats * inverse_norm(floats)).astype(packet_ref.dtype)
+    lane = lax.broadcasted_iota(jnp.int32, (SUBLANES, LANES), 1)
+    digits = jnp.zeros((SUBLANES, LANES), jnp.int32)
+    for i in range(rows):
+        digits = jnp.where(lane == i, pair_ref[i] >> 8, digits)
+        digits = jnp.where(lane == rows + i, pair_ref[i] & 255, digits)
+    digits = digits.astype(jnp.float32).astype(packet_ref.dtype)
+    blocks = width // LANES
+    for peer in range(packet_ref.shape[0]):
+        for k in range(blocks):
+            packet_ref[peer, k * rows : (k + 1) * rows, :] = unit[:, k * LANES : (k + 1) * LANES]
+        packet_ref[peer, blocks * rows :, :] = digits
+
+
+def units_and_packets(pair_index, image_embed, text_embed, peers):
+    rows, width = text_embed.shape
     return pl.pallas_call(
         unit_kernel,
-        in_specs=[vmem] * 2,
+        in_specs=[smem, vmem, vmem],
         out_specs=[vmem] * 2,
         out_shape=[
             jax.ShapeDtypeStruct(image_embed.shape, jnp.bfloat16),
-            jax.ShapeDtypeStruct((peers,) + text_embed.shape, jnp.bfloat16),
+            jax.ShapeDtypeStruct((peers, width // LANES * rows + SUBLANES, LANES), jnp.bfloat16),
         ],
         compiler_params=params(56),
-    )(image_embed, text_embed)
-
-
-def weight_kernel(first_ref, scalars_ref, own_ref, other_ref, text_ref, pair_ref, weight_ref, grad_ref, image_ref):
+    )(pair_index, image_embed, text_embed)
+
+
+def pairs_of(digits, rows):
+    count = digits.shape[0] // SUBLANES * rows
+    lane = lax.broadcasted_iota(jnp.int32, (LANES, count), 0)
+    text = lax.broadcasted_iota(jnp.int32, (LANES, count), 1) % rows
+    place = jnp.where(lane == text, 256.0, jnp.where(lane == rows + text, 1.0, 0.0)).astype(jnp.bfloat16)
+    spread = jnp.dot(digits, place, preferred_element_type=jnp.float32)
+    tile = lax.broadcasted_iota(jnp.int32, spread.shape, 0)
+    peer = lax.broadcasted_iota(jnp.int32, spread.shape, 1) // rows
+    return jnp.sum(jnp.where(tile == peer * SUBLANES, spread, 0.0), axis=0, keepdims=True).astype(jnp.int32)
+
+
+def put_texts(packet_ref, text_ref):
+    blocks = text_ref.shape[1] // LANES
+    rows = text_ref.shape[0] // packet_ref.shape[0]
+    for k in range(blocks):
+        block = packet_ref[:, k * rows : (k + 1) * rows, :]
+        text_ref[:, k * LANES : (k + 1) * LANES] = block.reshape(text_ref.shape[0], LANES)
+    return packet_ref[:, blocks * rows :, :].reshape(-1, LANES), rows
+
+
+def weight_kernel(first_ref, scalars_ref, own_ref, other_ref, packet_ref, *refs):
+    weights_ref, grads_ref, image_ref, text_ref, weight_ref, grad_ref, sems = refs
     half = own_ref.shape[0]
     image_ref[:half, :] = own_ref[...]
     image_ref[half:, :] = other_ref[...]
+    pairs = pairs_of(*put_texts(packet_ref, text_ref))
     row = lax.broadcasted_iota(jnp.int32, (128, 1), 0)
     places = jnp.concatenate([row + first_ref[p] for p in range(2 * half // 128)], axis=0)
     images = image_ref[...]
     dots = lax.dot_general(images, text_ref[...], ROWS_BY_ROWS, preferred_element_type=jnp.float32)
     chance = 1.0 / (1.0 + jnp.exp2(dots * scalars_ref[1] + scalars_ref[2]))
-    weight = (scalars_ref[0] * jnp.where(pair_ref[...] == places, chance - 1.0, chance)).astype(jnp.bfloat16)
+    weight = (scalars_ref[0] * jnp.where(pairs == places, chance - 1.0, chance)).astype(jnp.bfloat16)
     weight_ref[...] = weight
+    leaving = [pltpu.make_async_copy(weight_ref, weights_ref, sems.at[0])]
+    leaving[0].start()
     grad = lax.dot_general(weight, images, COLUMNS_BY_ROWS, preferred_element_type=jnp.float32)
     grad_ref[...] = grad.astype(grad_ref.dtype)
-
-
-def weights_and_text_terms(first, scalars, own, other, texts, pairs):
+    leaving.append(pltpu.make_async_copy(grad_ref, grads_ref, sems.at[1]))
+    leaving[1].start()
+    for copy in leaving:
+        copy.wait()
+
+
+def weights_and_text_terms(first, scalars, own, other, packets, rows):
     half, width = own.shape
-    count = texts.shape[0]
+    count = packets.shape[0] * rows
     return pl.pallas_call(
         weight_kernel,
-        in_specs=[smem, smem] + [vmem] * 4,
-        out_specs=[vmem] * 2,
+        in_specs=[smem, smem] + [vmem] * 3,
+        out_specs=[hbm, hbm],
         out_shape=[
             jax.ShapeDtypeStruct((2 * half, count), jnp.bfloat16),
             jax.ShapeDtypeStruct((count, width), jnp.bfloat16),
         ],
-        scratch_shapes=[pltpu.VMEM((2 * half, width), jnp.bfloat16)],
-        compiler_params=params(32),
+        scratch_shapes=[
+            pltpu.VMEM((2 * half, width), jnp.bfloat16),
+            pltpu.VMEM((count, width), jnp.bfloat16),
+            pltpu.VMEM((2 * half, count), jnp.bfloat16),
+            pltpu.VMEM((count, width), jnp.bfloat16),
+            pltpu.SemaphoreType.DMA((2,)),
+        ],
+        compiler_params=params(48),
         cost_estimate=pl.CostEstimate(
             flops=8 * half * count * width,
             bytes_accessed=4 * (half + count) * width + 4 * half * count,
             transcendentals=4 * half * count,
         ),
-    )(first, scalars, own, other, texts, pairs)
-
-
-def image_kernel(weight_ref, text_ref, own_ref, other_ref):
+    )(first, scalars, own, other, packets)
+
+
+def image_kernel(weight_ref, packet_ref, own_ref, other_ref, text_ref):
+    put_texts(packet_ref, text_ref)
     grad = jnp.dot(weight_ref[...], text_ref[...], preferred_element_type=jnp.float32)
     half = own_ref.shape[0]
     own_ref[...] = grad[:half].astype(own_ref.dtype)
     other_ref[...] = grad[half:].astype(other_ref.dtype)
 
 
-def image_terms(weights, texts):
+def image_terms(weights, packets, width):
     rows, count = weights.shape
-    width = texts.shape[1]
     return pl.pallas_call(
         image_kernel,
         in_specs=[vmem] * 2,
         out_specs=[vmem] * 2,
         out_shape=[jax.ShapeDtypeStruct((rows // 2, width), jnp.bfloat16)] * 2,
+        scratch_shapes=[pltpu.VMEM((count, width), jnp.bfloat16)],
         compiler_params=params(24),
         cost_estimate=pl.CostEstimate(
             flops=2 * rows * count * width, bytes_accessed=2 * (rows + count) * width + 2 * rows * count, transcendentals=0
         ),
-    )(weights, texts)
+    )(weights, packets)
 
 
 def backward_kernel(embed_ref, *refs):
@@ -141,9 +190,8 @@
     own_texts = text_embed.shape[0]
     peers, ring = lax.axis_size(FAR), lax.axis_size("x")
 
-    unit, copies = units_and_copies(image_embed, text_embed, peers)
-    texts = lax.all_to_all(copies, FAR, split_axis=0, concat_axis=0, tiled=True).reshape(-1, width)
-    pairs = lax.all_gather(pair_index, FAR, axis=0, tiled=True)
+    unit, packets = units_and_packets(pair_index, image_embed, text_embed, peers)
+    packets = lax.all_to_all(packets, FAR, split_axis=0, concat_axis=0, tiled=True)
     own = lax.all_gather(unit, "x", axis=0, tiled=True)
     other = shifted(own, "c", 1)
 
@@ -153,12 +201,12 @@
     first = jnp.stack(
         [((far * ring + place) * 2 + core) * own_images for core in (c, 1 - c) for place in range(ring)]
     ).astype(jnp.int32)
-    weights, text_part = weights_and_text_terms(first, scalars, own, other, texts, pairs[None, :])
+    weights, text_part = weights_and_text_terms(first, scalars, own, other, packets, own_texts)
     text_parts = lax.all_to_all(
         text_part.reshape(peers, own_texts, width), FAR, split_axis=0, concat_axis=0, tiled=True
     )
 
-    own_part, other_part = image_terms(weights, texts)
+    own_part, other_part = image_terms(weights, packets, width)
     part = own_part.astype(jnp.float32) + shifted(other_part, "c", 1).astype(jnp.float32)
     part = part.astype(jnp.bfloat16).reshape(ring, own_images, width)
     parts = [lax.dynamic_index_in_dim(part, (x + s) % ring, 0, keepdims=False) for s in range(ring)]

time: 128 us -> 120 us (0.938)
  blocking collectives: 49.3 us -> 14.1 us
  waiting for transfers between devices: 17.3 us -> 48.1 us
  local copies, waits for them, and re-layouts: 5.55 us -> 3.8 us
    unnamed x1 -> x0, blocking collectives: 35.2 us -> none
    all_to_all x1, waiting for transfers between devices: 0.01 us -> 25.8 us  [on_device(): lax.all_to_all(packets, FAR, split_axis=0, concat_axis=0, tiled=True)]
    all_to_all x1, waiting for transfers between devices: 6.87 us -> 11 us  [on_device(): lax.all_to_all(text_part.reshape(peers, own_texts, width), FAR, split_axi...]
    unnamed x17 -> x12, local copies, waits for them, and re-layouts: 5.4 us -> 3.65 us
  transfers between devices with their start and end apart: 7 -> 7, of which waited for: 5 -> 7; matrix products, arithmetic and copies ran while one was open for 2% -> 1% of each run, Pallas kernels for 3% -> 3%
where the time goes in v14:
time: 120 us; the launch traced here: 119 us
  waiting for transfers between devices  48.1 us (40%)
  starting transfers between devices  36.4 us (30%)
  blocking collectives  14.1 us (12%)
  Pallas kernels  13.3 us (11%)
  local copies, waits for them, and re-layouts  3.8 us (3%)
  between operations  2.16 us (2%)
  other arithmetic  1.43 us (1%)
    all_to_all x1, waiting for transfers between devices, on_device(): lax.all_to_all(packets, FAR, split_axis=0, concat_axis=0, tiled=True)  25.8 us
    all_to_all x1, starting transfers between devices, on_device(): lax.all_to_all(packets, FAR, split_axis=0, concat_axis=0, tiled=True)  16.7 us
    all_gather x1, blocking collectives, on_device(): own = lax.all_gather(unit, 'x', axis=0, tiled=True)  14.1 us
    ppermute x5, starting transfers between devices, shifted(): lax.ppermute(array, axis, [(i, (i + by) % devices) for i in range(devices)])  12.5 us
    ppermute x5, waiting for transfers between devices, shifted(): lax.ppermute(array, axis, [(i, (i + by) % devices) for i in range(devices)])  11.3 us
    all_to_all x1, waiting for transfers between devices, on_device(): lax.all_to_all(text_part.reshape(peers, own_texts, width), FAR, split_axi...  11 us
    all_to_all x1, starting transfers between devices, on_device(): lax.all_to_all(text_part.reshape(peers, own_texts, width), FAR, split_axi...  7.23 us
    pallas_call x1, Pallas kernels, weights_and_text_terms(): pl.pallas_call(weight_kernel, in_specs=[smem, smem] + [vmem] * 3, out_spe...  6.18 us
  transfers between devices with their start and end apart: 7, of which 7 were waited for; matrix products, arithmetic and copies ran while one was open for 1% of the time, Pallas kernels for 3%

profile of v14, /device:TPU:6, one launch (start us, length us, event | category | flops | bytes accessed | tf_op | source)
XLA Modules:
  0.0 119.3 jit_solution(2646027848782958779)
XLA Ops:
  0.6 2.4 %shard_map.68 = (bf16[128,768]{1,0:T(8,128)(2,1)}, bf16[64,104,128]{2,1,0:T(8,128)(2,1)}) custom-call(s32[16]{0:T(128)} %pair_ref.1, bf16[128,768]{1,0:T(8,128)(2,1)} %embed_ref.2, bf16[16,768]{1,0:T(8,128)(2,1)} %embed_ref.3), custom_call_target="tpu_custom_call" | custom-call | tf_op jit(solution)/shard_map/pallas_call | solution.py:54
  3.0 0.0 copy-start.5
  3.0 16.7 %all-to-all-start = ((bf16[64,104,128]{2,1,0:T(8,128)(2,1)}), bf16[64,104,128]{2,1,0:T(8,128)(2,1)S(1)}, u32[]{:S(2)}, u32[]{:S(2)}) async-start(bf16[64,104,128]{2,1,0:T(8,128)(2,1)} %get-tuple-element.9), calls=%async_computation | async-start | bytes 3407872 | tf_op jit(solution)/shard_map/all_to_all | solution.py:194
  19.8 0.0 copy-done.5
  19.8 14.1 %all_gather.3.own_ref = bf16[512,768]{1,0:T(8,128)(2,1)S(1)} all-gather(bf16[128,768]{1,0:T(8,128)(2,1)S(1)} %copy-done.5), channel_id=1, replica_groups=mesh['z'=8,'y'=8,'x'=4,'c'=2] {'x'}, dimensions={0}, use_global_device_ids=true | all-gather | bytes 983040 | tf_op jit(solution)/shard_map/all_gather | solution.py:195
  33.9 1.9 %collective-permute-start = (bf16[512,768]{1,0:T(8,128)(2,1)S(1)}, bf16[512,768]{1,0:T(8,128)(2,1)}, u32[]{:S(2)}, u32[]{:S(2)}) collective-permute-start(bf16[512,768]{1,0:T(8,128)(2,1)S(1)} %all_gather.3.own_ref), channel_id=1, source_target_pairs={{0,1},{1,0},{2,3},{3,2},{4,5},{5,4},{6,7},{7,6},{8,9},{9,8},{10,11... | collective-permute-start | bytes 2359304 | tf_op jit(solution)/shard_map/ppermute | solution.py:185
  37.1 0.1 stack.35.first_ref
  37.2 0.1 pad_maximum_fusion.scalars_ref
  37.3 0.9 collective-permute-done.other_ref
  38.2 25.8 %all-to-all-done.packet_ref = bf16[64,104,128]{2,1,0:T(8,128)(2,1)S(1)} async-done(((bf16[64,104,128]{2,1,0:T(8,128)(2,1)}), bf16[64,104,128]{2,1,0:T(8,128)(2,1)S(1)}, u32[]{:S(2)}, u32[]{:S(2)}) %all-to-all-start) | async-done | bytes 1703968 | tf_op jit(solution)/shard_map/all_to_all | solution.py:194
  64.0 6.2 %shard_map.69 = (bf16[1024,1024]{1,0:T(8,128)(2,1)}, bf16[1024,768]{1,0:T(8,128)(2,1)S(1)}) custom-call(s32[8]{0:T(128)S(1)} %stack.35.first_ref, f32[3]{0:T(128)S(1)} %pad_maximum_fusion.scalars_ref, bf16[512,768]{1,0:T(8,128)(2,1)S(1)} %all_gather.3.own_ref, bf16[512,768]{1,0:T(8,128)(2,1)} %collective-permute-done.other_ref, ...), custom_call_target="tpu_custom_call" | custom-call | flops 3221225472 | bytes 6815744 | tf_op jit(solution)/shard_map/pallas_call | solution.py:112
  70.2 0.0 copy-start
  70.2 1.1 copy-done
  71.3 7.2 %all-to-all-start.1 = ((bf16[64,16,768]{2,1,0:T(8,128)(2,1)}), bf16[64,16,768]{2,1,0:T(8,128)(2,1)S(1)}, u32[]{:S(2)}, u32[]{:S(2)}) async-start(bf16[64,16,768]{2,1,0:T(8,128)(2,1)} %bitcast.18), calls=%async_computation.1 | async-start | bytes 3145728 | tf_op jit(solution)/shard_map/all_to_all | solution.py:205
  78.6 0.0 copy-start.4
  78.6 1.6 %copy-done.4 = bf16[1024,1024]{1,0:T(8,128)(2,1)S(1)} copy-done((bf16[1024,1024]{1,0:T(8,128)(2,1)S(1)}, bf16[1024,1024]{1,0:T(8,128)(2,1)}, u32[]{:S(2)}) %copy-start.4) | copy-done | bytes 2097176
  80.2 2.9 %shard_map.70 = (bf16[512,768]{1,0:T(8,128)(2,1)S(1)}, bf16[512,768]{1,0:T(8,128)(2,1)}) custom-call(bf16[1024,1024]{1,0:T(8,128)(2,1)S(1)} %copy-done.4, bf16[64,104,128]{2,1,0:T(8,128)(2,1)S(1)} %all-to-all-done.packet_ref), custom_call_target="tpu_custom_call" | custom-call | flops 1610612736 | bytes 5242880 | tf_op jit(solution)/shard_map/pallas_call | solution.py:146
  83.0 0.0 copy-start.2
  83.0 0.9 copy-done.2
  83.9 1.9 %collective-permute-start.1 = (bf16[512,768]{1,0:T(8,128)(2,1)}, bf16[512,768]{1,0:T(8,128)(2,1)S(1)}, u32[]{:S(2)}, u32[]{:S(2)}) collective-permute-start(bf16[512,768]{1,0:T(8,128)(2,1)} %get-tuple-element.12), channel_id=1, source_target_pairs={{0,1},{1,0},{2,3},{3,2},{4,5},{5,4},{6,7},{7,6},{8,9},{9,8},{10,11... | collective-permute-start | bytes 2359304 | tf_op jit(solution)/shard_map/ppermute | solution.py:185
  85.9 2.4 %collective-permute-done.1 = bf16[512,768]{1,0:T(8,128)(2,1)S(1)} collective-permute-done((bf16[512,768]{1,0:T(8,128)(2,1)}, bf16[512,768]{1,0:T(8,128)(2,1)S(1)}, u32[]{:S(2)}, u32[]{:S(2)}) %collective-permute-start.1) | collective-permute-done | bytes 786464 | tf_op jit(solution)/shard_map/ppermute | solution.py:185
  88.3 0.0 copy-start.1
  88.3 1.4 %add_convert_fusion = bf16[512,768]{1,0:T(8,128)(2,1)S(1)} fusion(bf16[512,768]{1,0:T(8,128)(2,1)S(1)} %collective-permute-done.1, bf16[512,768]{1,0:T(8,128)(2,1)} %copy-done.2), kind=kLoop, calls=%fused_computation | loop fusion | flops 1572864 | bytes 2359296 | tf_op jit(solution)/shard_map/convert_element_type | solution.py:211
  89.7 0.0 copy-start.3
  89.7 0.1 dynamic-slice_bitcast_fusion
  89.8 2.4 %collective-permute-start.2 = (bf16[128,768]{1,0:T(8,128)(2,1)S(1)}, bf16[128,768]{1,0:T(8,128)(2,1)S(1)}, u32[]{:S(2)}, u32[]{:S(2)}) collective-permute-start(bf16[128,768]{1,0:T(8,128)(2,1)S(1)} %get-tuple-element.16), channel_id=1, source_target_pairs={{0,2},{2,4},{4,6},{6,0},{1,3},{3,5},{5,7},{7,1},{8,10},{10,12},{12... | collective-permute-start | bytes 589832 | tf_op jit(solution)/shard_map/ppermute | solution.py:185
  92.2 4.3 %collective-permute-start.3 = (bf16[128,768]{1,0:T(8,128)(2,1)S(1)}, bf16[128,768]{1,0:T(8,128)(2,1)S(1)}, u32[]{:S(2)}, u32[]{:S(2)}) collective-permute-start(bf16[128,768]{1,0:T(8,128)(2,1)S(1)} %get-tuple-element.15), channel_id=1, source_target_pairs={{0,4},{2,6},{4,0},{6,2},{1,5},{3,7},{5,1},{7,3},{8,12},{10,14},{12... | collective-permute-start | bytes 589832 | tf_op jit(solution)/shard_map/ppermute | solution.py:185
  96.5 1.9 %collective-permute-start.4 = (bf16[128,768]{1,0:T(8,128)(2,1)S(1)}, bf16[128,768]{1,0:T(8,128)(2,1)S(1)}, u32[]{:S(2)}, u32[]{:S(2)}) collective-permute-start(bf16[128,768]{1,0:T(8,128)(2,1)S(1)} %get-tuple-element.14), channel_id=1, source_target_pairs={{0,6},{2,0},{4,2},{6,4},{1,7},{3,1},{5,3},{7,5},{8,14},{10,8},{12,... | collective-permute-start | bytes 589832 | tf_op jit(solution)/shard_map/ppermute | solution.py:185
  98.4 1.0 collective-permute-done.2.refs_1_
  99.4 3.2 %collective-permute-done.3.refs_2_ = bf16[128,768]{1,0:T(8,128)(2,1)S(1)} collective-permute-done((bf16[128,768]{1,0:T(8,128)(2,1)S(1)}, bf16[128,768]{1,0:T(8,128)(2,1)S(1)}, u32[]{:S(2)}, u32[]{:S(2)}) %collective-permute-start.3) | collective-permute-done | bytes 196640 | tf_op jit(solution)/shard_map/ppermute | solution.py:185
  102.6 3.9 %collective-permute-done.4.refs_3_ = bf16[128,768]{1,0:T(8,128)(2,1)S(1)} collective-permute-done((bf16[128,768]{1,0:T(8,128)(2,1)S(1)}, bf16[128,768]{1,0:T(8,128)(2,1)S(1)}, u32[]{:S(2)}, u32[]{:S(2)}) %collective-permute-start.4) | collective-permute-done | bytes 196640 | tf_op jit(solution)/shard_map/ppermute | solution.py:185
  106.4 0.0 copy-done.1
  106.4 0.9 shard_map.71
  107.4 11.0 %all-to-all-done.1.refs_0_ = bf16[64,16,768]{2,1,0:T(8,128)(2,1)S(1)} async-done(((bf16[64,16,768]{2,1,0:T(8,128)(2,1)}), bf16[64,16,768]{2,1,0:T(8,128)(2,1)S(1)}, u32[]{:S(2)}, u32[]{:S(2)}) %all-to-all-start.1) | async-done | bytes 1572896 | tf_op jit(solution)/shard_map/all_to_all | solution.py:205
  118.4 0.0 copy-done.3
  118.4 0.9 shard_map.72
Async XLA Ops:
  3.0 16.7 %copy-start.5 = (bf16[128,768]{1,0:T(8,128)(2,1)S(1)}, bf16[128,768]{1,0:T(8,128)(2,1)}, u32[]{:S(2)}) copy-start(bf16[128,768]{1,0:T(8,128)(2,1)} %get-tuple-element.8) | copy-start | bytes 589828
  3.0 61.0 %all-to-all-start = ((bf16[64,104,128]{2,1,0:T(8,128)(2,1)}), bf16[64,104,128]{2,1,0:T(8,128)(2,1)S(1)}, u32[]{:S(2)}, u32[]{:S(2)}) async-start(bf16[64,104,128]{2,1,0:T(8,128)(2,1)} %get-tuple-element.9), calls=%async_computation | async-start | bytes 3407872 | tf_op jit(solution)/shard_map/all_to_all | solution.py:194
  33.9 4.3 %collective-permute-start = (bf16[512,768]{1,0:T(8,128)(2,1)S(1)}, bf16[512,768]{1,0:T(8,128)(2,1)}, u32[]{:S(2)}, u32[]{:S(2)}) collective-permute-start(bf16[512,768]{1,0:T(8,128)(2,1)S(1)} %all_gather.3.own_ref), channel_id=1, source_target_pairs={{0,1},{1,0},{2,3},{3,2},{4,5},{5,4},{6,7},{7,6},{8,9},{9,8},{10,11... | collective-permute-start | bytes 2359304 | tf_op jit(solution)/shard_map/ppermute | solution.py:185
  70.2 1.1 copy-start
  71.3 47.0 %all-to-all-start.1 = ((bf16[64,16,768]{2,1,0:T(8,128)(2,1)}), bf16[64,16,768]{2,1,0:T(8,128)(2,1)S(1)}, u32[]{:S(2)}, u32[]{:S(2)}) async-start(bf16[64,16,768]{2,1,0:T(8,128)(2,1)} %bitcast.18), calls=%async_computation.1 | async-start | bytes 3145728 | tf_op jit(solution)/shard_map/all_to_all | solution.py:205
  78.6 1.6 %copy-start.4 = (bf16[1024,1024]{1,0:T(8,128)(2,1)S(1)}, bf16[1024,1024]{1,0:T(8,128)(2,1)}, u32[]{:S(2)}) copy-start(bf16[1024,1024]{1,0:T(8,128)(2,1)} %get-tuple-element.10.weight_ref) | copy-start | bytes 6291460
  83.0 0.9 copy-start.2
  83.9 4.4 %collective-permute-start.1 = (bf16[512,768]{1,0:T(8,128)(2,1)}, bf16[512,768]{1,0:T(8,128)(2,1)S(1)}, u32[]{:S(2)}, u32[]{:S(2)}) collective-permute-start(bf16[512,768]{1,0:T(8,128)(2,1)} %get-tuple-element.12), channel_id=1, source_target_pairs={{0,1},{1,0},{2,3},{3,2},{4,5},{5,4},{6,7},{7,6},{8,9},{9,8},{10,11... | collective-permute-start | bytes 2359304 | tf_op jit(solution)/shard_map/ppermute | solution.py:185
  88.3 18.1 %copy-start.1 = (bf16[128,768]{1,0:T(8,128)(2,1)S(1)}, bf16[128,768]{1,0:T(8,128)(2,1)}, u32[]{:S(2)}) copy-start(bf16[128,768]{1,0:T(8,128)(2,1)} %embed_ref.2) | copy-start | bytes 589828
  89.7 28.7 %copy-start.3 = (bf16[16,768]{1,0:T(8,128)(2,1)S(1)}, bf16[16,768]{1,0:T(8,128)(2,1)}, u32[]{:S(2)}) copy-start(bf16[16,768]{1,0:T(8,128)(2,1)} %embed_ref.3) | copy-start | bytes 73732
  89.8 9.6 %collective-permute-start.2 = (bf16[128,768]{1,0:T(8,128)(2,1)S(1)}, bf16[128,768]{1,0:T(8,128)(2,1)S(1)}, u32[]{:S(2)}, u32[]{:S(2)}) collective-permute-start(bf16[128,768]{1,0:T(8,128)(2,1)S(1)} %get-tuple-element.16), channel_id=1, source_target_pairs={{0,2},{2,4},{4,6},{6,0},{1,3},{3,5},{5,7},{7,1},{8,10},{10,12},{12... | collective-permute-start | bytes 589832 | tf_op jit(solution)/shard_map/ppermute | solution.py:185
  92.2 10.4 %collective-permute-start.3 = (bf16[128,768]{1,0:T(8,128)(2,1)S(1)}, bf16[128,768]{1,0:T(8,128)(2,1)S(1)}, u32[]{:S(2)}, u32[]{:S(2)}) collective-permute-start(bf16[128,768]{1,0:T(8,128)(2,1)S(1)} %get-tuple-element.15), channel_id=1, source_target_pairs={{0,4},{2,6},{4,0},{6,2},{1,5},{3,7},{5,1},{7,3},{8,12},{10,14},{12... | collective-permute-start | bytes 589832 | tf_op jit(solution)/shard_map/ppermute | solution.py:185
  96.5 9.9 %collective-permute-start.4 = (bf16[128,768]{1,0:T(8,128)(2,1)S(1)}, bf16[128,768]{1,0:T(8,128)(2,1)S(1)}, u32[]{:S(2)}, u32[]{:S(2)}) collective-permute-start(bf16[128,768]{1,0:T(8,128)(2,1)S(1)} %get-tuple-element.14), channel_id=1, source_target_pairs={{0,6},{2,0},{4,2},{6,4},{1,7},{3,1},{5,3},{7,5},{8,14},{10,8},{12,... | collective-permute-start | bytes 589832 | tf_op jit(solution)/shard_map/ppermute | solution.py:185

commit v15 on v14

--- a/solution.py
+++ b/solution.py
@@ -8,9 +8,9 @@
 from jax.sharding import Mesh
 from jax.sharding import PartitionSpec as P
 
-AXES = ("z", "y", "x", "c")
-SIZES = (8, 8, 4, 2)
-FAR = ("z", "y")
+AXES = ("z", "yh", "ym", "yl", "x", "c")
+SIZES = (8, 2, 2, 2, 4, 2)
+FAR = ("z", "yh", "ym")
 LANES = 128
 SUBLANES = 8
 MIB = 1024 * 1024
@@ -74,21 +74,25 @@
     return jnp.sum(jnp.where(tile == peer * SUBLANES, spread, 0.0), axis=0, keepdims=True).astype(jnp.int32)
 
 
-def put_texts(packet_ref, text_ref):
+def put_texts(packet_refs, text_ref):
     blocks = text_ref.shape[1] // LANES
-    rows = text_ref.shape[0] // packet_ref.shape[0]
-    for k in range(blocks):
-        block = packet_ref[:, k * rows : (k + 1) * rows, :]
-        text_ref[:, k * LANES : (k + 1) * LANES] = block.reshape(text_ref.shape[0], LANES)
-    return packet_ref[:, blocks * rows :, :].reshape(-1, LANES), rows
-
-
-def weight_kernel(first_ref, scalars_ref, own_ref, other_ref, packet_ref, *refs):
-    weights_ref, grads_ref, image_ref, text_ref, weight_ref, grad_ref, sems = refs
+    count = text_ref.shape[0] // len(packet_refs)
+    pairs = []
+    for i, ref in enumerate(packet_refs):
+        rows = count // ref.shape[0]
+        for k in range(blocks):
+            block = ref[:, k * rows : (k + 1) * rows, :].reshape(count, LANES)
+            text_ref[i * count : (i + 1) * count, k * LANES : (k + 1) * LANES] = block
+        pairs.append(pairs_of(ref[:, blocks * rows :, :].reshape(-1, LANES), rows))
+    return jnp.concatenate(pairs, axis=1)
+
+
+def weight_kernel(first_ref, scalars_ref, own_ref, beside_ref, own_packet_ref, other_packet_ref, *refs):
+    weights_ref, own_grad_ref, other_grad_ref, image_ref, text_ref, weight_ref, sem = refs
     half = own_ref.shape[0]
     image_ref[:half, :] = own_ref[...]
-    image_ref[half:, :] = other_ref[...]
-    pairs = pairs_of(*put_texts(packet_ref, text_ref))
+    image_ref[half:, :] = beside_ref[...]
+    pairs = put_texts((own_packet_ref, other_packet_ref), text_ref)
     row = lax.broadcasted_iota(jnp.int32, (128, 1), 0)
     places = jnp.concatenate([row + first_ref[p] for p in range(2 * half // 128)], axis=0)
     images = image_ref[...]
@@ -96,56 +100,55 @@
     chance = 1.0 / (1.0 + jnp.exp2(dots * scalars_ref[1] + scalars_ref[2]))
     weight = (scalars_ref[0] * jnp.where(pairs == places, chance - 1.0, chance)).astype(jnp.bfloat16)
     weight_ref[...] = weight
-    leaving = [pltpu.make_async_copy(weight_ref, weights_ref, sems.at[0])]
-    leaving[0].start()
+    leaving = pltpu.make_async_copy(weight_ref, weights_ref, sem)
+    leaving.start()
     grad = lax.dot_general(weight, images, COLUMNS_BY_ROWS, preferred_element_type=jnp.float32)
-    grad_ref[...] = grad.astype(grad_ref.dtype)
-    leaving.append(pltpu.make_async_copy(grad_ref, grads_ref, sems.at[1]))
-    leaving[1].start()
-    for copy in leaving:
-        copy.wait()
-
-
-def weights_and_text_terms(first, scalars, own, other, packets, rows):
+    count = own_grad_ref.shape[0]
+    own_grad_ref[...] = grad[:count].astype(own_grad_ref.dtype)
+    other_grad_ref[...] = grad[count:].astype(other_grad_ref.dtype)
+    leaving.wait()
+
+
+def weights_and_text_terms(first, scalars, own, beside, packets, other_packets, rows):
     half, width = own.shape
     count = packets.shape[0] * rows
     return pl.pallas_call(
         weight_kernel,
-        in_specs=[smem, smem] + [vmem] * 3,
-        out_specs=[hbm, hbm],
+        in_specs=[smem, smem] + [vmem] * 4,
+        out_specs=[hbm, vmem, vmem],
         out_shape=[
-            jax.ShapeDtypeStruct((2 * half, count), jnp.bfloat16),
+            jax.ShapeDtypeStruct((2 * half, 2 * count), jnp.bfloat16),
+            jax.ShapeDtypeStruct((count, width), jnp.bfloat16),
             jax.ShapeDtypeStruct((count, width), jnp.bfloat16),
         ],
         scratch_shapes=[
             pltpu.VMEM((2 * half, width), jnp.bfloat16),
-            pltpu.VMEM((count, width), jnp.bfloat16),
-            pltpu.VMEM((2 * half, count), jnp.bfloat16),
-            pltpu.VMEM((count, width), jnp.bfloat16),
-            pltpu.SemaphoreType.DMA((2,)),
+            pltpu.VMEM((2 * count, width), jnp.bfloat16),
+            pltpu.VMEM((2 * half, 2 * count), jnp.bfloat16),
+            pltpu.SemaphoreType.DMA,
         ],
         compiler_params=params(48),
         cost_estimate=pl.CostEstimate(
-            flops=8 * half * count * width,
-            bytes_accessed=4 * (half + count) * width + 4 * half * count,
-            transcendentals=4 * half * count,
+            flops=16 * half * count * width,
+            bytes_accessed=4 * (half + count) * width + 8 * half * count,
+            transcendentals=8 * half * count,
         ),
-    )(first, scalars, own, other, packets)
-
-
-def image_kernel(weight_ref, packet_ref, own_ref, other_ref, text_ref):
-    put_texts(packet_ref, text_ref)
+    )(first, scalars, own, beside, packets, other_packets)
+
+
+def image_kernel(weight_ref, own_packet_ref, other_packet_ref, own_ref, beside_ref, text_ref):
+    put_texts((own_packet_ref, other_packet_ref), text_ref)
     grad = jnp.dot(weight_ref[...], text_ref[...], preferred_element_type=jnp.float32)
     half = own_ref.shape[0]
     own_ref[...] = grad[:half].astype(own_ref.dtype)
-    other_ref[...] = grad[half:].astype(other_ref.dtype)
-
-
-def image_terms(weights, packets, width):
+    beside_ref[...] = grad[half:].astype(beside_ref.dtype)
+
+
+def image_terms(weights, packets, other_packets, width):
     rows, count = weights.shape
     return pl.pallas_call(
         image_kernel,
-        in_specs=[vmem] * 2,
+        in_specs=[vmem] * 3,
         out_specs=[vmem] * 2,
         out_shape=[jax.ShapeDtypeStruct((rows // 2, width), jnp.bfloat16)] * 2,
         scratch_shapes=[pltpu.VMEM((count, width), jnp.bfloat16)],
@@ -153,7 +156,7 @@
         cost_estimate=pl.CostEstimate(
             flops=2 * rows * count * width, bytes_accessed=2 * (rows + count) * width + 2 * rows * count, transcendentals=0
         ),
-    )(weights, packets)
+    )(weights, packets, other_packets)
 
 
 def backward_kernel(embed_ref, *refs):
@@ -193,21 +196,26 @@
     unit, packets = units_and_packets(pair_index, image_embed, text_embed, peers)
     packets = lax.all_to_all(packets, FAR, split_axis=0, concat_axis=0, tiled=True)
     own = lax.all_gather(unit, "x", axis=0, tiled=True)
-    other = shifted(own, "c", 1)
+    beside = shifted(own, "yl", 1)
+    packets, beside = lax.optimization_barrier((packets, beside))
+    other_packets = shifted(packets, "c", 1)
 
     scale = jnp.exp(log_scale)
     scalars = jnp.concatenate([scale, -math.log2(math.e) * scale, -math.log2(math.e) * logit_bias])
-    far, x, c = lax.axis_index(FAR), lax.axis_index("x"), lax.axis_index("c")
+    far, yl, x, c = lax.axis_index(FAR), lax.axis_index("yl"), lax.axis_index("x"), lax.axis_index("c")
     first = jnp.stack(
-        [((far * ring + place) * 2 + core) * own_images for core in (c, 1 - c) for place in range(ring)]
+        [(((far * 2 + half) * ring + place) * 2 + c) * own_images for half in (yl, 1 - yl) for place in range(ring)]
     ).astype(jnp.int32)
-    weights, text_part = weights_and_text_terms(first, scalars, own, other, packets, own_texts)
+    weights, own_part, other_part = weights_and_text_terms(
+        first, scalars, own, beside, packets, other_packets, own_texts
+    )
+    text_part = own_part.astype(jnp.float32) + shifted(other_part, "c", 1).astype(jnp.float32)
     text_parts = lax.all_to_all(
-        text_part.reshape(peers, own_texts, width), FAR, split_axis=0, concat_axis=0, tiled=True
+        text_part.astype(jnp.bfloat16).reshape(peers, own_texts, width), FAR, split_axis=0, concat_axis=0, tiled=True
     )
 
-    own_part, other_part = image_terms(weights, packets, width)
-    part = own_part.astype(jnp.float32) + shifted(other_part, "c", 1).astype(jnp.float32)
+    own_part, beside_part = image_terms(weights, packets, other_packets, width)
+    part = own_part.astype(jnp.float32) + shifted(beside_part, "yl", 1).astype(jnp.float32)
     part = part.astype(jnp.bfloat16).reshape(ring, own_images, width)
     parts = [lax.dynamic_index_in_dim(part, (x + s) % ring, 0, keepdims=False) for s in range(ring)]
     parts = parts[:1] + [shifted(parts[s], "x", s) for s in range(1, ring)]

time: 120 us -> 140 us (1.17)
  waiting for transfers between devices: 48.1 us -> 57.5 us
  starting transfers between devices: 36.4 us -> 45.7 us
  Pallas kernels: 13.3 us -> 11.9 us
    ppermute x5 -> x7, waiting for transfers between devices: 11.3 us -> 57.5 us  [shifted(): lax.ppermute(array, axis, [(i, (i + by) % devices) for i in range(devices)])]
    all_to_all x1, waiting for transfers between devices: 25.8 us -> 0.01 us  [on_device(): lax.all_to_all(packets, FAR, split_axis=0, concat_axis=0, tiled=True)]
    all_to_all x1, waiting for transfers between devices: 11 us -> 0.01 us  [on_device(): lax.all_to_all(text_part.astype(jnp.bfloat16).reshape(peers, own_texts, w...]
    ppermute x5 -> x7, starting transfers between devices: 12.5 us -> 17.7 us  [shifted(): lax.ppermute(array, axis, [(i, (i + by) % devices) for i in range(devices)])]
    all_to_all x1, starting transfers between devices: 7.23 us -> 11.9 us  [on_device(): lax.all_to_all(text_part.astype(jnp.bfloat16).reshape(peers, own_texts, w...]
    unnamed x12 -> x14, local copies, waits for them, and re-layouts: 3.65 us -> 4.54 us
  transfers between devices with their start and end apart: 7 -> 9, of which waited for: 7 -> 7; matrix products, arithmetic and copies ran while one was open for 1% -> 1% of each run, Pallas kernels for 3% -> 3%
where the time goes in v15:
time: 140 us; the launch traced here: 139 us
  waiting for transfers between devices  57.5 us (41%)
  starting transfers between devices  45.7 us (33%)
  blocking collectives  14.3 us (10%)
  Pallas kernels  11.9 us (8%)
  local copies, waits for them, and re-layouts  4.69 us (3%)
  other arithmetic  2.5 us (2%)
  between operations  2.18 us (2%)
    ppermute x7, waiting for transfers between devices, shifted(): lax.ppermute(array, axis, [(i, (i + by) % devices) for i in range(devices)])  57.5 us
    ppermute x7, starting transfers between devices, shifted(): lax.ppermute(array, axis, [(i, (i + by) % devices) for i in range(devices)])  17.7 us
    all_to_all x1, starting transfers between devices, on_device(): lax.all_to_all(packets, FAR, split_axis=0, concat_axis=0, tiled=True)  16.1 us
    all_gather x1, blocking collectives, on_device(): own = lax.all_gather(unit, 'x', axis=0, tiled=True)  14.3 us
    all_to_all x1, starting transfers between devices, on_device(): lax.all_to_all(text_part.astype(jnp.bfloat16).reshape(peers, own_texts, w...  11.9 us
    pallas_call x1, Pallas kernels, weights_and_text_terms(): pl.pallas_call(weight_kernel, in_specs=[smem, smem] + [vmem] * 4, out_spe...  5.31 us
    unnamed x14, local copies, waits for them, and re-layouts  4.54 us
    pallas_call x1, Pallas kernels, image_terms(): pl.pallas_call(image_kernel, in_specs=[vmem] * 3, out_specs=[vmem] * 2, o...  2.84 us
  transfers between devices with their start and end apart: 9, of which 7 were waited for; matrix products, arithmetic and copies ran while one was open for 1% of the time, Pallas kernels for 3%

profile of v15, /device:TPU:6, one launch (start us, length us, event | category | flops | bytes accessed | tf_op | source)
XLA Modules:
  0.0 138.8 jit_solution(13247089854729881213)
XLA Ops:
  0.6 2.0 %shard_map.68 = (bf16[128,768]{1,0:T(8,128)(2,1)}, bf16[32,104,128]{2,1,0:T(8,128)(2,1)}) custom-call(s32[16]{0:T(128)} %pair_ref.1, bf16[128,768]{1,0:T(8,128)(2,1)} %embed_ref.2, bf16[16,768]{1,0:T(8,128)(2,1)} %embed_ref.3), custom_call_target="tpu_custom_call" | custom-call | tf_op jit(solution)/shard_map/pallas_call | solution.py:54
  2.7 0.0 copy-start.6
  2.7 16.1 %all-to-all-start = ((bf16[32,104,128]{2,1,0:T(8,128)(2,1)}), bf16[32,104,128]{2,1,0:T(8,128)(2,1)S(1)}, u32[]{:S(2)}, u32[]{:S(2)}) async-start(bf16[32,104,128]{2,1,0:T(8,128)(2,1)} %get-tuple-element.12), calls=%async_computation | async-start | bytes 1703936 | tf_op jit(solution)/shard_map/all_to_all | solution.py:197
  18.8 0.0 copy-done.6
  18.8 14.3 %all_gather.3.own_ref = bf16[512,768]{1,0:T(8,128)(2,1)S(1)} all-gather(bf16[128,768]{1,0:T(8,128)(2,1)S(1)} %copy-done.6), channel_id=1, replica_groups=mesh['z'=8,'yh'=2,'ym'=2,'yl'=2,'x'=4,'c'=2] {'x'}, dimensions={0}, use_global_device_ids=true | all-gather | bytes 983040 | tf_op jit(solution)/shard_map/all_gather | solution.py:198
  33.1 2.6 %collective-permute-start = (bf16[512,768]{1,0:T(8,128)(2,1)S(1)}, bf16[512,768]{1,0:T(8,128)(2,1)S(1)}, u32[]{:S(2)}, u32[]{:S(2)}) collective-permute-start(bf16[512,768]{1,0:T(8,128)(2,1)S(1)} %all_gather.3.own_ref), channel_id=1, source_target_pairs={{0,8},{8,0},{1,9},{9,1},{2,10},{10,2},{3,11},{11,3},{4,12},{12,4},... | collective-permute-start | bytes 2359304 | tf_op jit(solution)/shard_map/ppermute | solution.py:188
  35.7 19.3 %collective-permute-done.beside_ref = bf16[512,768]{1,0:T(8,128)(2,1)S(1)} collective-permute-done((bf16[512,768]{1,0:T(8,128)(2,1)S(1)}, bf16[512,768]{1,0:T(8,128)(2,1)S(1)}, u32[]{:S(2)}, u32[]{:S(2)}) %collective-permute-start) | collective-permute-done | bytes 786464 | tf_op jit(solution)/shard_map/ppermute | solution.py:188
  55.0 0.0 copy-start.2
  55.0 0.9 copy-done.2
  55.9 0.0 all-to-all-done.own_packet_ref
  55.9 1.9 %collective-permute-start.1 = (bf16[32,104,128]{2,1,0:T(8,128)(2,1)S(1)}, bf16[32,104,128]{2,1,0:T(8,128)(2,1)S(1)}, u32[]{:S(2)}, u32[]{:S(2)}) collective-permute-start(bf16[32,104,128]{2,1,0:T(8,128)(2,1)S(1)} %all-to-all-done.own_packet_ref), channel_id=1, source_target_pairs={{0,1},{1,0},{2,3},{3,2},{4,5},{5,4},{6,7},{7,6},{8,9},{9,8},{10,11... | collective-permute-start | bytes 2555912 | tf_op jit(solution)/shard_map/ppermute | solution.py:188
  59.2 0.1 stack.35.first_ref
  59.3 0.1 pad_maximum_fusion.scalars_ref
  59.4 0.8 collective-permute-done.1.other_packet_ref
  60.2 0.0 copy-start.3
  60.2 1.1 copy-done.3
  61.3 5.3 %shard_map.69 = (bf16[1024,1024]{1,0:T(8,128)(2,1)}, bf16[512,768]{1,0:T(8,128)(2,1)S(1)}, bf16[512,768]{1,0:T(8,128)(2,1)S(1)}) custom-call(s32[8]{0:T(128)S(1)} %stack.35.first_ref, f32[3]{0:T(128)S(1)} %pad_maximum_fusion.scalars_ref, bf16[512,768]{1,0:T(8,128)(2,1)S(1)} %all_gather.3.own_ref, bf16[512,768]{1,0:T(8,128)(2,1)S(1)} %copy-done.3, ...), custom_call_target="tpu_custom_call" | custom-call | flops 3221225472 | bytes 5242880 | tf_op jit(solution)/shard_map/pallas_call | solution.py:115
  66.6 2.0 %collective-permute-start.6 = (bf16[512,768]{1,0:T(8,128)(2,1)S(1)}, bf16[512,768]{1,0:T(8,128)(2,1)S(1)}, u32[]{:S(2)}, u32[]{:S(2)}) collective-permute-start(bf16[512,768]{1,0:T(8,128)(2,1)S(1)} %get-tuple-element.19), channel_id=1, source_target_pairs={{0,1},{1,0},{2,3},{3,2},{4,5},{5,4},{6,7},{7,6},{8,9},{9,8},{10,11... | collective-permute-start | bytes 2359304 | tf_op jit(solution)/shard_map/ppermute | solution.py:188
  68.7 2.1 %collective-permute-done.6 = bf16[512,768]{1,0:T(8,128)(2,1)S(1)} collective-permute-done((bf16[512,768]{1,0:T(8,128)(2,1)S(1)}, bf16[512,768]{1,0:T(8,128)(2,1)S(1)}, u32[]{:S(2)}, u32[]{:S(2)}) %collective-permute-start.6) | collective-permute-done | bytes 786464 | tf_op jit(solution)/shard_map/ppermute | solution.py:188
  70.8 1.1 add_convert_fusion
  71.9 11.9 %all-to-all-start.1 = ((bf16[32,16,768]{2,1,0:T(8,128)(2,1)}), bf16[32,16,768]{2,1,0:T(8,128)(2,1)S(1)}, u32[]{:S(2)}, u32[]{:S(2)}) async-start(bf16[32,16,768]{2,1,0:T(8,128)(2,1)} %bitcast.13), calls=%async_computation.1 | async-start | bytes 1572864 | tf_op jit(solution)/shard_map/all_to_all | solution.py:213
  83.7 0.0 copy-start.4
  83.8 1.6 %copy-done.4 = bf16[1024,1024]{1,0:T(8,128)(2,1)S(1)} copy-done((bf16[1024,1024]{1,0:T(8,128)(2,1)S(1)}, bf16[1024,1024]{1,0:T(8,128)(2,1)}, u32[]{:S(2)}) %copy-start.4) | copy-done | bytes 2097176
  85.3 2.8 %shard_map.70 = (bf16[512,768]{1,0:T(8,128)(2,1)S(1)}, bf16[512,768]{1,0:T(8,128)(2,1)}) custom-call(bf16[1024,1024]{1,0:T(8,128)(2,1)S(1)} %copy-done.4, bf16[32,104,128]{2,1,0:T(8,128)(2,1)S(1)} %all-to-all-done.own_packet_ref, bf16[32,104,128]{2,1,0:T(8,128)(2,1)S(1)} %collective-permute-done.1.other_packet_ref), custom_call_target="tpu_custom_call" | custom-call | flops 1610612736 | bytes 5242880 | tf_op jit(solution)/shard_map/pallas_call | solution.py:149
  88.2 2.6 %collective-permute-start.2 = (bf16[512,768]{1,0:T(8,128)(2,1)}, bf16[512,768]{1,0:T(8,128)(2,1)S(1)}, u32[]{:S(2)}, u32[]{:S(2)}) collective-permute-start(bf16[512,768]{1,0:T(8,128)(2,1)} %get-tuple-element.17), channel_id=1, source_target_pairs={{0,8},{8,0},{1,9},{9,1},{2,10},{10,2},{3,11},{11,3},{4,12},{12,4},... | collective-permute-start | bytes 2359304 | tf_op jit(solution)/shard_map/ppermute | solution.py:188
  90.8 28.0 %collective-permute-done.2 = bf16[512,768]{1,0:T(8,128)(2,1)S(1)} collective-permute-done((bf16[512,768]{1,0:T(8,128)(2,1)}, bf16[512,768]{1,0:T(8,128)(2,1)S(1)}, u32[]{:S(2)}, u32[]{:S(2)}) %collective-permute-start.2) | collective-permute-done | bytes 786464 | tf_op jit(solution)/shard_map/ppermute | solution.py:188
  118.8 0.0 copy-start.5
  118.9 0.9 copy-done.5
  119.7 0.0 copy-start
  119.7 1.4 add_convert_fusion.1
  121.1 0.0 copy-start.1
  121.1 0.1 dynamic-slice_bitcast_fusion
  121.2 2.4 %collective-permute-start.3 = (bf16[128,768]{1,0:T(8,128)(2,1)S(1)}, bf16[128,768]{1,0:T(8,128)(2,1)S(1)}, u32[]{:S(2)}, u32[]{:S(2)}) collective-permute-start(bf16[128,768]{1,0:T(8,128)(2,1)S(1)} %get-tuple-element.22), channel_id=1, source_target_pairs={{0,2},{2,4},{4,6},{6,0},{1,3},{3,5},{5,7},{7,1},{8,10},{10,12},{12... | collective-permute-start | bytes 589832 | tf_op jit(solution)/shard_map/ppermute | solution.py:188
  123.6 4.3 %collective-permute-start.4 = (bf16[128,768]{1,0:T(8,128)(2,1)S(1)}, bf16[128,768]{1,0:T(8,128)(2,1)S(1)}, u32[]{:S(2)}, u32[]{:S(2)}) collective-permute-start(bf16[128,768]{1,0:T(8,128)(2,1)S(1)} %get-tuple-element.21), channel_id=1, source_target_pairs={{0,4},{2,6},{4,0},{6,2},{1,5},{3,7},{5,1},{7,3},{8,12},{10,14},{12... | collective-permute-start | bytes 589832 | tf_op jit(solution)/shard_map/ppermute | solution.py:188
  127.9 1.9 %collective-permute-start.5 = (bf16[128,768]{1,0:T(8,128)(2,1)S(1)}, bf16[128,768]{1,0:T(8,128)(2,1)S(1)}, u32[]{:S(2)}, u32[]{:S(2)}) collective-permute-start(bf16[128,768]{1,0:T(8,128)(2,1)S(1)} %get-tuple-element.20), channel_id=1, source_target_pairs={{0,6},{2,0},{4,2},{6,4},{1,7},{3,1},{5,3},{7,5},{8,14},{10,8},{12,... | collective-permute-start | bytes 589832 | tf_op jit(solution)/shard_map/ppermute | solution.py:188
  129.8 1.1 collective-permute-done.3.refs_1_
  130.9 2.3 %collective-permute-done.4.refs_2_ = bf16[128,768]{1,0:T(8,128)(2,1)S(1)} collective-permute-done((bf16[128,768]{1,0:T(8,128)(2,1)S(1)}, bf16[128,768]{1,0:T(8,128)(2,1)S(1)}, u32[]{:S(2)}, u32[]{:S(2)}) %collective-permute-start.4) | collective-permute-done | bytes 196640 | tf_op jit(solution)/shard_map/ppermute | solution.py:188
  133.2 3.8 %collective-permute-done.5.refs_3_ = bf16[128,768]{1,0:T(8,128)(2,1)S(1)} collective-permute-done((bf16[128,768]{1,0:T(8,128)(2,1)S(1)}, bf16[128,768]{1,0:T(8,128)(2,1)S(1)}, u32[]{:S(2)}, u32[]{:S(2)}) %collective-permute-start.5) | collective-permute-done | bytes 196640 | tf_op jit(solution)/shard_map/ppermute | solution.py:188
  137.0 0.0 copy-done
  137.0 0.9 shard_map.71
  138.0 0.0 all-to-all-done.1.refs_0_
  138.0 0.0 copy-done.1
  138.0 0.8 shard_map.72
Async XLA Ops:
  2.7 16.1 %copy-start.6 = (bf16[128,768]{1,0:T(8,128)(2,1)S(1)}, bf16[128,768]{1,0:T(8,128)(2,1)}, u32[]{:S(2)}) copy-start(bf16[128,768]{1,0:T(8,128)(2,1)} %get-tuple-element.11) | copy-start | bytes 589828
  2.7 53.2 %all-to-all-start = ((bf16[32,104,128]{2,1,0:T(8,128)(2,1)}), bf16[32,104,128]{2,1,0:T(8,128)(2,1)S(1)}, u32[]{:S(2)}, u32[]{:S(2)}) async-start(bf16[32,104,128]{2,1,0:T(8,128)(2,1)} %get-tuple-element.12), calls=%async_computation | async-start | bytes 1703936 | tf_op jit(solution)/shard_map/all_to_all | solution.py:197
  33.1 21.9 %collective-permute-start = (bf16[512,768]{1,0:T(8,128)(2,1)S(1)}, bf16[512,768]{1,0:T(8,128)(2,1)S(1)}, u32[]{:S(2)}, u32[]{:S(2)}) collective-permute-start(bf16[512,768]{1,0:T(8,128)(2,1)S(1)} %all_gather.3.own_ref), channel_id=1, source_target_pairs={{0,8},{8,0},{1,9},{9,1},{2,10},{10,2},{3,11},{11,3},{4,12},{12,4},... | collective-permute-start | bytes 2359304 | tf_op jit(solution)/shard_map/ppermute | solution.py:188
  55.0 0.9 copy-start.2
  55.9 4.3 %collective-permute-start.1 = (bf16[32,104,128]{2,1,0:T(8,128)(2,1)S(1)}, bf16[32,104,128]{2,1,0:T(8,128)(2,1)S(1)}, u32[]{:S(2)}, u32[]{:S(2)}) collective-permute-start(bf16[32,104,128]{2,1,0:T(8,128)(2,1)S(1)} %all-to-all-done.own_packet_ref), channel_id=1, source_target_pairs={{0,1},{1,0},{2,3},{3,2},{4,5},{5,4},{6,7},{7,6},{8,9},{9,8},{10,11... | collective-permute-start | bytes 2555912 | tf_op jit(solution)/shard_map/ppermute | solution.py:188
  60.2 1.1 copy-start.3
  66.6 4.2 %collective-permute-start.6 = (bf16[512,768]{1,0:T(8,128)(2,1)S(1)}, bf16[512,768]{1,0:T(8,128)(2,1)S(1)}, u32[]{:S(2)}, u32[]{:S(2)}) collective-permute-start(bf16[512,768]{1,0:T(8,128)(2,1)S(1)} %get-tuple-element.19), channel_id=1, source_target_pairs={{0,1},{1,0},{2,3},{3,2},{4,5},{5,4},{6,7},{7,6},{8,9},{9,8},{10,11... | collective-permute-start | bytes 2359304 | tf_op jit(solution)/shard_map/ppermute | solution.py:188
  71.9 66.1 %all-to-all-start.1 = ((bf16[32,16,768]{2,1,0:T(8,128)(2,1)}), bf16[32,16,768]{2,1,0:T(8,128)(2,1)S(1)}, u32[]{:S(2)}, u32[]{:S(2)}) async-start(bf16[32,16,768]{2,1,0:T(8,128)(2,1)} %bitcast.13), calls=%async_computation.1 | async-start | bytes 1572864 | tf_op jit(solution)/shard_map/all_to_all | solution.py:213
  83.7 1.6 %copy-start.4 = (bf16[1024,1024]{1,0:T(8,128)(2,1)S(1)}, bf16[1024,1024]{1,0:T(8,128)(2,1)}, u32[]{:S(2)}) copy-start(bf16[1024,1024]{1,0:T(8,128)(2,1)} %get-tuple-element.15.weight_ref) | copy-start | bytes 6291460
  88.2 30.7 %collective-permute-start.2 = (bf16[512,768]{1,0:T(8,128)(2,1)}, bf16[512,768]{1,0:T(8,128)(2,1)S(1)}, u32[]{:S(2)}, u32[]{:S(2)}) collective-permute-start(bf16[512,768]{1,0:T(8,128)(2,1)} %get-tuple-element.17), channel_id=1, source_target_pairs={{0,8},{8,0},{1,9},{9,1},{2,10},{10,2},{3,11},{11,3},{4,12},{12,4},... | collective-permute-start | bytes 2359304 | tf_op jit(solution)/shard_map/ppermute | solution.py:188
  118.8 0.9 copy-start.5
  119.7 17.3 %copy-start = (bf16[128,768]{1,0:T(8,128)(2,1)S(1)}, bf16[128,768]{1,0:T(8,128)(2,1)}, u32[]{:S(2)}) copy-start(bf16[128,768]{1,0:T(8,128)(2,1)} %embed_ref.2) | copy-start | bytes 589828
  121.1 16.9 %copy-start.1 = (bf16[16,768]{1,0:T(8,128)(2,1)S(1)}, bf16[16,768]{1,0:T(8,128)(2,1)}, u32[]{:S(2)}) copy-start(bf16[16,768]{1,0:T(8,128)(2,1)} %embed_ref.3) | copy-start | bytes 73732
  121.2 9.7 %collective-permute-start.3 = (bf16[128,768]{1,0:T(8,128)(2,1)S(1)}, bf16[128,768]{1,0:T(8,128)(2,1)S(1)}, u32[]{:S(2)}, u32[]{:S(2)}) collective-permute-start(bf16[128,768]{1,0:T(8,128)(2,1)S(1)} %get-tuple-element.22), channel_id=1, source_target_pairs={{0,2},{2,4},{4,6},{6,0},{1,3},{3,5},{5,7},{7,1},{8,10},{10,12},{12... | collective-permute-start | bytes 589832 | tf_op jit(solution)/shard_map/ppermute | solution.py:188
  123.6 9.7 %collective-permute-start.4 = (bf16[128,768]{1,0:T(8,128)(2,1)S(1)}, bf16[128,768]{1,0:T(8,128)(2,1)S(1)}, u32[]{:S(2)}, u32[]{:S(2)}) collective-permute-start(bf16[128,768]{1,0:T(8,128)(2,1)S(1)} %get-tuple-element.21), channel_id=1, source_target_pairs={{0,4},{2,6},{4,0},{6,2},{1,5},{3,7},{5,1},{7,3},{8,12},{10,14},{12... | collective-permute-start | bytes 589832 | tf_op jit(solution)/shard_map/ppermute | solution.py:188
  127.9 9.1 %collective-permute-start.5 = (bf16[128,768]{1,0:T(8,128)(2,1)S(1)}, bf16[128,768]{1,0:T(8,128)(2,1)S(1)}, u32[]{:S(2)}, u32[]{:S(2)}) collective-permute-start(bf16[128,768]{1,0:T(8,128)(2,1)S(1)} %get-tuple-element.20), channel_id=1, source_target_pairs={{0,6},{2,0},{4,2},{6,4},{1,7},{3,1},{5,3},{7,5},{8,14},{10,8},{12,... | collective-permute-start | bytes 589832 | tf_op jit(solution)/shard_map/ppermute | solution.py:188

commit v16 on v12

--- a/solution.py
+++ b/solution.py
@@ -71,63 +71,104 @@
     )(pair_index, embed)
 
 
-def pair_kernel(first_ref, scalars_ref, images_ref, own_ref, other_ref, *refs):
-    image_grads_ref, own_grad_ref, other_grad_ref, image_ref, text_ref, grad_ref, sems = refs
-    height, width = image_ref.shape
-    size = height // PIECES
+def copies_of(source_ref, target_ref, sems, first):
+    size = target_ref.shape[0] // PIECES
     pieces = [pl.ds(i * size, size) for i in range(PIECES)]
-    arriving = [pltpu.make_async_copy(images_ref.at[p], image_ref.at[p], sems.at[i]) for i, p in enumerate(pieces)]
+    return [pltpu.make_async_copy(source_ref.at[p], target_ref.at[p], sems.at[first + i]) for i, p in enumerate(pieces)]
+
+
+def weight_kernel(first_ref, scalars_ref, images_ref, own_ref, other_ref, *refs):
+    weights_ref, grads_ref, image_ref, text_ref, weight_ref, grad_ref, sems = refs
+    arriving = copies_of(images_ref, image_ref, sems, 0)
     for copy in arriving:
         copy.start()
+    height, width = image_ref.shape
     count = own_ref.shape[0]
     text_ref[:count, :] = own_ref[...]
     text_ref[count:, :] = other_ref[...]
     digits = text_ref[:, width:].astype(jnp.float32).T
     pairs = (digits[0:1] * 256.0 + digits[1:2]).astype(jnp.int32)
     row = lax.broadcasted_iota(jnp.int32, (128, 1), 0)
-    rows = jnp.concatenate([row + first_ref[p] for p in range(image_ref.shape[0] // 128)], axis=0)
     texts = text_ref[:, :width]
-    for copy in arriving:
+    half = height // 2
+    weights = copies_of(weight_ref, weights_ref, sems, PIECES)
+    grads = copies_of(grad_ref, grads_ref, sems, 2 * PIECES)
+    pieces = PIECES // 2
+    for i in range(2):
+        for copy in arriving[i * pieces : (i + 1) * pieces]:
+            copy.wait()
+        images = image_ref[i * half : (i + 1) * half, :]
+        rows = jnp.concatenate([row + first_ref[i * half // 128 + p] for p in range(half // 128)], axis=0)
+        dots = lax.dot_general(images, texts, ROWS_BY_ROWS, preferred_element_type=jnp.float32)
+        chance = 1.0 / (1.0 + jnp.exp2(dots * scalars_ref[1] + scalars_ref[2]))
+        weight = (scalars_ref[0] * jnp.where(pairs == rows, chance - 1.0, chance)).astype(jnp.bfloat16)
+        weight_ref[i * half : (i + 1) * half, :] = weight
+        for copy in weights[i * pieces : (i + 1) * pieces]:
+            copy.start()
+        grad = jnp.dot(weight, texts, preferred_element_type=jnp.float32)
+        grad_ref[i * half : (i + 1) * half, :] = grad.astype(grad_ref.dtype)
+        for copy in grads[i * pieces : (i + 1) * pieces]:
+            copy.start()
+    for copy in weights + grads:
         copy.wait()
-    images = image_ref[...]
-    dots = lax.dot_general(images, texts, ROWS_BY_ROWS, preferred_element_type=jnp.float32)
-    chance = 1.0 / (1.0 + jnp.exp2(dots * scalars_ref[1] + scalars_ref[2]))
-    weight = (scalars_ref[0] * jnp.where(pairs == rows, chance - 1.0, chance)).astype(jnp.bfloat16)
-    grad_ref[...] = jnp.dot(weight, texts, preferred_element_type=jnp.float32).astype(grad_ref.dtype)
-    leaving = [pltpu.make_async_copy(grad_ref.at[p], image_grads_ref.at[p], sems.at[i]) for i, p in enumerate(pieces)]
-    for copy in leaving:
-        copy.start()
-    text_grad = lax.dot_general(weight, images, COLUMNS_BY_ROWS, preferred_element_type=jnp.float32)
-    own_grad_ref[...] = text_grad[:count].astype(own_grad_ref.dtype)
-    other_grad_ref[...] = text_grad[count:].astype(other_grad_ref.dtype)
-    for copy in leaving:
-        copy.wait()
-
-
-def pair_terms(first, scalars, images, own, other):
+
+
+def weights_and_image_terms(first, scalars, images, own, other):
     rows, width = images.shape
     count, wide = own.shape
     texts = 2 * count
     return pl.pallas_call(
-        pair_kernel,
+        weight_kernel,
         in_specs=[smem, smem, hbm, vmem, vmem],
-        out_specs=[hbm, vmem, vmem],
+        out_specs=[hbm, hbm],
         out_shape=[
+            jax.ShapeDtypeStruct((rows, texts), jnp.bfloat16),
             jax.ShapeDtypeStruct((rows, width), jnp.bfloat16),
-            jax.ShapeDtypeStruct((count, width), jnp.bfloat16),
-            jax.ShapeDtypeStruct((count, width), jnp.bfloat16),
         ],
         scratch_shapes=[
             pltpu.VMEM((rows, width), jnp.bfloat16),
             pltpu.VMEM((texts, wide), jnp.bfloat16),
+            pltpu.VMEM((rows, texts), jnp.bfloat16),
             pltpu.VMEM((rows, width), jnp.bfloat16),
-            pltpu.SemaphoreType.DMA((PIECES,)),
-        ],
-        compiler_params=params(48),
+            pltpu.SemaphoreType.DMA((3 * PIECES,)),
+        ],
+        compiler_params=params(51),
         cost_estimate=pl.CostEstimate(
-            flops=6 * rows * texts * width, bytes_accessed=4 * (rows + texts) * width, transcendentals=2 * rows * texts
+            flops=4 * rows * texts * width, bytes_accessed=4 * (rows + texts) * width, transcendentals=2 * rows * texts
         ),
     )(first, scalars, images, own, other)
+
+
+def text_kernel(weights_ref, images_ref, own_grad_ref, other_grad_ref, weight_ref, image_ref, sems):
+    arriving = copies_of(weights_ref, weight_ref, sems, 0) + copies_of(images_ref, image_ref, sems, PIECES)
+    for copy in arriving:
+        copy.start()
+    for copy in arriving:
+        copy.wait()
+    count = own_grad_ref.shape[0]
+    grad = lax.dot_general(weight_ref[...], image_ref[...], COLUMNS_BY_ROWS, preferred_element_type=jnp.float32)
+    own_grad_ref[...] = grad[:count].astype(own_grad_ref.dtype)
+    other_grad_ref[...] = grad[count:].astype(other_grad_ref.dtype)
+
+
+def text_terms(weights, images):
+    rows, texts = weights.shape
+    width = images.shape[1]
+    return pl.pallas_call(
+        text_kernel,
+        in_specs=[hbm] * 2,
+        out_specs=[vmem] * 2,
+        out_shape=[jax.ShapeDtypeStruct((texts // 2, width), jnp.bfloat16)] * 2,
+        scratch_shapes=[
+            pltpu.VMEM(weights.shape, jnp.bfloat16),
+            pltpu.VMEM(images.shape, jnp.bfloat16),
+            pltpu.SemaphoreType.DMA((2 * PIECES,)),
+        ],
+        compiler_params=params(58),
+        cost_estimate=pl.CostEstimate(
+            flops=2 * rows * texts * width, bytes_accessed=2 * (rows + texts) * width, transcendentals=0
+        ),
+    )(weights, images)
 
 
 def project(embed_ref, grad, out_ref):
@@ -199,9 +240,10 @@
     place = jnp.where(c == 0, place, SIZES[1] - 1 - place)
     first = (((z * SIZES[1] + place) * SIZES[2] + x) * SIZES[3] + c) * own_images
 
-    image_part, own_part, other_part = pair_terms(first.astype(jnp.int32), scalars, images, own, other)
+    weights, image_part = weights_and_image_terms(first.astype(jnp.int32), scalars, images, own, other)
     image_grad = lax.psum_scatter(image_part, AXES, scatter_dimension=0, tiled=True, axis_index_groups=rings)
 
+    own_part, other_part = text_terms(weights, images)
     text_part = own_part.astype(jnp.float32) + exchanged(other_part).astype(jnp.float32)
     text_part = jnp.sum(parted(text_part.astype(jnp.bfloat16), "x").astype(jnp.float32), axis=0)
     text_grads = parted(text_part.astype(jnp.bfloat16), "z")

time: 117 us -> 118 us (level)
  waiting for transfers between devices: 14.9 us -> 10 us
  Pallas kernels: 12.2 us -> 16 us
    reduce_scatter x1, waiting for transfers between devices: 5.1 us -> 0.01 us  [on_device(): lax.psum_scatter(image_part, AXES, scatter_dimension=0, tiled=True, axis_...]
    pallas_call x1 -> x2, Pallas kernels: 8.01 us -> 11.8 us  [the longest x1 6.85 us: weights_and_image_terms(): pl.pallas_call(weight_kernel, in_specs=[smem, smem, hbm, vmem, vmem], out...]
  transfers between devices with their start and end apart: 4 -> 4, of which waited for: 4 -> 3; matrix products, arithmetic and copies ran while one was open for 0% -> 1% of each run, Pallas kernels for 1% -> 6%
where the time goes in v16:
time: 118 us; the launch traced here: 116 us
  blocking collectives  68.3 us (58%)
  Pallas kernels  16 us (14%)
  between operations  15.5 us (13%)
  waiting for transfers between devices  10 us (8%)
  starting transfers between devices  3.91 us (3%)
  other arithmetic  1.52 us (1%)
    all_to_all x2, blocking collectives, spread(): lax.all_to_all(copies, axis, split_axis=0, concat_axis=0, tiled=True)  36 us
    all_to_all x2, blocking collectives, parted(): return lax.all_to_all(parts, axis, split_axis=0, concat_axis=0, tiled=True)  32.4 us
    pallas_call x1, Pallas kernels, weights_and_image_terms(): pl.pallas_call(weight_kernel, in_specs=[smem, smem, hbm, vmem, vmem], out...  6.85 us
    all_gather x1, waiting for transfers between devices, on_device(): lax.all_gather(units(image_embed), AXES, axis=0, tiled=True, axis_index_g...  6.53 us
    pallas_call x1, Pallas kernels, text_terms(): pl.pallas_call(text_kernel, in_specs=[hbm] * 2, out_specs=[vmem] * 2, out...  4.99 us
    ppermute x2, starting transfers between devices, exchanged(): return lax.ppermute(array, 'c', [(0, 1), (1, 0)])  3.83 us
    ppermute x2, waiting for transfers between devices, exchanged(): return lax.ppermute(array, 'c', [(0, 1), (1, 0)])  3.46 us
  transfers between devices with their start and end apart: 4, of which 3 were waited for; matrix products, arithmetic and copies ran while one was open for 1% of the time, Pallas kernels for 6%

profile of v16, /device:TPU:6, one launch (start us, length us, event | category | flops | bytes accessed | tf_op | source)
XLA Modules:
  0.0 116.3 jit_solution(9825168674192352152)
XLA Ops:
  7.2 0.0 all-gather.2.cloned.1.call-start
  7.2 1.7 %shard_map.68 = bf16[128,768]{1,0:T(8,128)(2,1)} custom-call(bf16[128,768]{1,0:T(8,128)(2,1)} %image_ref.1), custom_call_target="tpu_custom_call" | custom-call | tf_op jit(solution)/shard_map/pallas_call | solution.py:38
  8.9 0.0 all-gather.2.cloned.1.call-update
  9.0 0.0 reduce-scatter.2.cloned.1.call-start
  9.0 1.5 %shard_map.69 = bf16[8,16,896]{2,1,0:T(8,128)(2,1)} custom-call(s32[16]{0:T(128)} %pair_ref.1, bf16[16,768]{1,0:T(8,128)(2,1)} %text_ref.3), custom_call_target="tpu_custom_call" | custom-call | tf_op jit(solution)/shard_map/pallas_call | solution.py:65
  10.6 21.5 %all_to_all.20 = bf16[8,16,896]{2,1,0:T(8,128)(2,1)S(1)} all-to-all(bf16[8,16,896]{2,1,0:T(8,128)(2,1)} %shard_map.69), channel_id=1, replica_groups=mesh['z'=8,'y'=8,'x'=4,'c'=2] {'z'}, dimensions={0} | all-to-all | bytes 458752 | tf_op jit(solution)/shard_map/all_to_all | solution.py:219
  32.0 0.1 broadcast_in_dim.8
  32.1 14.5 %all_to_all.21 = bf16[4,128,896]{2,1,0:T(8,128)(2,1)S(1)} all-to-all(bf16[4,128,896]{2,1,0:T(8,128)(2,1)S(1)} %broadcast_in_dim.8), channel_id=1, replica_groups=mesh['z'=8,'y'=8,'x'=4,'c'=2] {'x'}, dimensions={0} | all-to-all | bytes 1835008 | tf_op jit(solution)/shard_map/all_to_all | solution.py:219
  46.6 1.9 %collective-permute-start = (bf16[512,896]{1,0:T(8,128)(2,1)S(1)}, bf16[512,896]{1,0:T(8,128)(2,1)S(1)}, u32[]{:S(2)}, u32[]{:S(2)}) collective-permute-start(bf16[512,896]{1,0:T(8,128)(2,1)S(1)} %bitcast.4), channel_id=1, source_target_pairs={{0,1},{1,0},{2,3},{3,2},{4,5},{5,4},{6,7},{7,6},{8,9},{9,8},{10,11... | collective-permute-start | bytes 2752520 | tf_op jit(solution)/shard_map/ppermute | solution.py:215
  49.9 0.1 pad_maximum_fusion.scalars_ref
  50.0 1.0 collective-permute-done.other_ref
  51.0 6.5 %all-gather.2.cloned.1.call-done.images_ref = bf16[1024,768]{1,0:T(8,128)(2,1)} async-done(((bf16[128,768]{1,0:T(8,128)(2,1)}), bf16[1024,768]{1,0:T(8,128)(2,1)}) %all-gather.2.cloned.1.call-update) | async-done | bytes 1572880 | tf_op jit(solution)/shard_map/all_gather | solution.py:230
  57.5 6.9 %shard_map.70 = (bf16[1024,1024]{1,0:T(8,128)(2,1)}, bf16[1024,768]{1,0:T(8,128)(2,1)}) custom-call(s32[8]{0:T(128)S(1)} %add_multiply_fusion.first_ref, f32[3]{0:T(128)S(1)} %pad_maximum_fusion.scalars_ref, bf16[1024,768]{1,0:T(8,128)(2,1)} %all-gather.2.cloned.1.call-done.images_ref, bf16[512,896]{1,0:T(8,128)(2,1)S(1)} %bitcast.5, ...), custom_call_target="tpu_custom_call" | custom-call | flops 3221225472 | bytes 6291456 | tf_op jit(solution)/shard_map/pallas_call | solution.py:120
  64.4 0.0 reduce-scatter.2.cloned.1.call-update
  64.4 5.0 %shard_map.71 = (bf16[512,768]{1,0:T(8,128)(2,1)}, bf16[512,768]{1,0:T(8,128)(2,1)}) custom-call(bf16[1024,1024]{1,0:T(8,128)(2,1)} %get-tuple-element.7.weights_ref, bf16[1024,768]{1,0:T(8,128)(2,1)} %all-gather.2.cloned.1.call-done.images_ref), custom_call_target="tpu_custom_call" | custom-call | flops 1610612736 | bytes 3145728 | tf_op jit(solution)/shard_map/pallas_call | solution.py:157
  69.4 1.9 %collective-permute-start.1 = (bf16[512,768]{1,0:T(8,128)(2,1)}, bf16[512,768]{1,0:T(8,128)(2,1)S(1)}, u32[]{:S(2)}, u32[]{:S(2)}) collective-permute-start(bf16[512,768]{1,0:T(8,128)(2,1)} %get-tuple-element.9), channel_id=1, source_target_pairs={{0,1},{1,0},{2,3},{3,2},{4,5},{5,4},{6,7},{7,6},{8,9},{9,8},{10,11... | collective-permute-start | bytes 2359304 | tf_op jit(solution)/shard_map/ppermute | solution.py:215
  71.3 2.5 %collective-permute-done.1 = bf16[512,768]{1,0:T(8,128)(2,1)S(1)} collective-permute-done((bf16[512,768]{1,0:T(8,128)(2,1)}, bf16[512,768]{1,0:T(8,128)(2,1)S(1)}, u32[]{:S(2)}, u32[]{:S(2)}) %collective-permute-start.1) | collective-permute-done | bytes 786464 | tf_op jit(solution)/shard_map/ppermute | solution.py:215
  73.8 1.3 %add_convert_fusion = bf16[512,768]{1,0:T(8,128)(2,1)S(1)} fusion(bf16[512,768]{1,0:T(8,128)(2,1)S(1)} %collective-permute-done.1, bf16[512,768]{1,0:T(8,128)(2,1)} %get-tuple-element.8), kind=kLoop, calls=%fused_computation | loop fusion | flops 1572864 | bytes 2359296 | tf_op jit(solution)/shard_map/convert_element_type | solution.py:248
  75.1 0.0 copy-start
  75.1 0.0 copy-start.2
  75.1 15.2 %all_to_all.22 = bf16[4,128,768]{2,1,0:T(8,128)(2,1)S(1)} all-to-all(bf16[4,128,768]{2,1,0:T(8,128)(2,1)S(1)} %bitcast.6), channel_id=1, replica_groups=mesh['z'=8,'y'=8,'x'=4,'c'=2] {'x'}, dimensions={0} | all-to-all | bytes 1572864 | tf_op jit(solution)/shard_map/all_to_all | solution.py:224
  90.4 0.1 reduce_sum.12
  90.5 17.1 %all_to_all.23.text_grads_ref = bf16[8,16,768]{2,1,0:T(8,128)(2,1)S(1)} all-to-all(bf16[8,16,768]{2,1,0:T(8,128)(2,1)S(1)} %bitcast.8), channel_id=1, replica_groups=mesh['z'=8,'y'=8,'x'=4,'c'=2] {'z'}, dimensions={0} | all-to-all | bytes 393216 | tf_op jit(solution)/shard_map/all_to_all | solution.py:224
  107.6 0.0 reduce-scatter.2.cloned.1.call-done.image_grad_ref
  107.6 0.0 copy-done
  107.6 0.0 copy-done.2
  107.6 0.0 copy-start.1
  107.6 0.9 copy-done.1
  108.5 0.9 shard_map.72
  (1 shorter events, 0.0 us)
Async XLA Ops:
  7.2 50.3 %all-gather.2.cloned.1.call-start = ((), (), s32[]{:S(2)}) async-start(), calls=%async_computation.5 | async-start | bytes 1769472 | tf_op jit(solution)/shard_map/all_gather | solution.py:230
  9.0 98.6 %reduce-scatter.2.cloned.1.call-start = ((), (), s32[]{:S(2)}) async-start(), calls=%async_computation.6 | async-start | bytes 1769472 | tf_op jit(solution)/shard_map/reduce_scatter | solution.py:244
  46.6 4.4 %collective-permute-start = (bf16[512,896]{1,0:T(8,128)(2,1)S(1)}, bf16[512,896]{1,0:T(8,128)(2,1)S(1)}, u32[]{:S(2)}, u32[]{:S(2)}) collective-permute-start(bf16[512,896]{1,0:T(8,128)(2,1)S(1)} %bitcast.4), channel_id=1, source_target_pairs={{0,1},{1,0},{2,3},{3,2},{4,5},{5,4},{6,7},{7,6},{8,9},{9,8},{10,11... | collective-permute-start | bytes 2752520 | tf_op jit(solution)/shard_map/ppermute | solution.py:215
  69.4 4.4 %collective-permute-start.1 = (bf16[512,768]{1,0:T(8,128)(2,1)}, bf16[512,768]{1,0:T(8,128)(2,1)S(1)}, u32[]{:S(2)}, u32[]{:S(2)}) collective-permute-start(bf16[512,768]{1,0:T(8,128)(2,1)} %get-tuple-element.9), channel_id=1, source_target_pairs={{0,1},{1,0},{2,3},{3,2},{4,5},{5,4},{6,7},{7,6},{8,9},{9,8},{10,11... | collective-permute-start | bytes 2359304 | tf_op jit(solution)/shard_map/ppermute | solution.py:215
  75.1 32.5 %copy-start = (bf16[128,768]{1,0:T(8,128)(2,1)S(1)}, bf16[128,768]{1,0:T(8,128)(2,1)}, u32[]{:S(2)}) copy-start(bf16[128,768]{1,0:T(8,128)(2,1)} %image_ref.1) | copy-start | bytes 589828
  75.1 32.5 %copy-start.2 = (bf16[16,768]{1,0:T(8,128)(2,1)S(1)}, bf16[16,768]{1,0:T(8,128)(2,1)}, u32[]{:S(2)}) copy-start(bf16[16,768]{1,0:T(8,128)(2,1)} %text_ref.3) | copy-start | bytes 73732
  107.6 0.9 copy-start.1
Sparse Core Ops, SparseCore 0:
  10.7 46.8 all-gather.1
  64.5 41.9 reduce-scatter.1

commit v17 on v12

--- a/solution.py
+++ b/solution.py
@@ -71,33 +71,42 @@
     )(pair_index, embed)
 
 
+def copies_of(source_ref, target_ref, sems, first):
+    size = target_ref.shape[0] // PIECES
+    pieces = [pl.ds(i * size, size) for i in range(PIECES)]
+    return [pltpu.make_async_copy(source_ref.at[p], target_ref.at[p], sems.at[first + i]) for i, p in enumerate(pieces)]
+
+
 def pair_kernel(first_ref, scalars_ref, images_ref, own_ref, other_ref, *refs):
     image_grads_ref, own_grad_ref, other_grad_ref, image_ref, text_ref, grad_ref, sems = refs
-    height, width = image_ref.shape
-    size = height // PIECES
-    pieces = [pl.ds(i * size, size) for i in range(PIECES)]
-    arriving = [pltpu.make_async_copy(images_ref.at[p], image_ref.at[p], sems.at[i]) for i, p in enumerate(pieces)]
+    arriving = copies_of(images_ref, image_ref, sems, 0)
     for copy in arriving:
         copy.start()
+    leaving = copies_of(grad_ref, image_grads_ref, sems, PIECES)
+    height, width = image_ref.shape
     count = own_ref.shape[0]
     text_ref[:count, :] = own_ref[...]
     text_ref[count:, :] = other_ref[...]
     digits = text_ref[:, width:].astype(jnp.float32).T
     pairs = (digits[0:1] * 256.0 + digits[1:2]).astype(jnp.int32)
     row = lax.broadcasted_iota(jnp.int32, (128, 1), 0)
-    rows = jnp.concatenate([row + first_ref[p] for p in range(image_ref.shape[0] // 128)], axis=0)
     texts = text_ref[:, :width]
-    for copy in arriving:
-        copy.wait()
-    images = image_ref[...]
-    dots = lax.dot_general(images, texts, ROWS_BY_ROWS, preferred_element_type=jnp.float32)
-    chance = 1.0 / (1.0 + jnp.exp2(dots * scalars_ref[1] + scalars_ref[2]))
-    weight = (scalars_ref[0] * jnp.where(pairs == rows, chance - 1.0, chance)).astype(jnp.bfloat16)
-    grad_ref[...] = jnp.dot(weight, texts, preferred_element_type=jnp.float32).astype(grad_ref.dtype)
-    leaving = [pltpu.make_async_copy(grad_ref.at[p], image_grads_ref.at[p], sems.at[i]) for i, p in enumerate(pieces)]
-    for copy in leaving:
-        copy.start()
-    text_grad = lax.dot_general(weight, images, COLUMNS_BY_ROWS, preferred_element_type=jnp.float32)
+    half, pieces = height // 2, PIECES // 2
+    weights = []
+    for i in range(2):
+        for copy in arriving[i * pieces : (i + 1) * pieces]:
+            copy.wait()
+        images = image_ref[i * half : (i + 1) * half, :]
+        rows = jnp.concatenate([row + first_ref[i * half // 128 + p] for p in range(half // 128)], axis=0)
+        dots = lax.dot_general(images, texts, ROWS_BY_ROWS, preferred_element_type=jnp.float32)
+        chance = 1.0 / (1.0 + jnp.exp2(dots * scalars_ref[1] + scalars_ref[2]))
+        weights.append((scalars_ref[0] * jnp.where(pairs == rows, chance - 1.0, chance)).astype(jnp.bfloat16))
+        grad = jnp.dot(weights[i], texts, preferred_element_type=jnp.float32)
+        grad_ref[i * half : (i + 1) * half, :] = grad.astype(grad_ref.dtype)
+        for copy in leaving[i * pieces : (i + 1) * pieces]:
+            copy.start()
+    weight = jnp.concatenate(weights, axis=0)
+    text_grad = lax.dot_general(weight, image_ref[...], COLUMNS_BY_ROWS, preferred_element_type=jnp.float32)
     own_grad_ref[...] = text_grad[:count].astype(own_grad_ref.dtype)
     other_grad_ref[...] = text_grad[count:].astype(other_grad_ref.dtype)
     for copy in leaving:
@@ -121,7 +130,7 @@
             pltpu.VMEM((rows, width), jnp.bfloat16),
             pltpu.VMEM((texts, wide), jnp.bfloat16),
             pltpu.VMEM((rows, width), jnp.bfloat16),
-            pltpu.SemaphoreType.DMA((PIECES,)),
+            pltpu.SemaphoreType.DMA((2 * PIECES,)),
         ],
         compiler_params=params(48),
         cost_estimate=pl.CostEstimate(

time: 117 us -> 117 us (level)
  no operation moved by 1% of the time
where the time goes in v17:
time: 117 us; the launch traced here: 116 us
  blocking collectives  68.3 us (58%)
  between operations  15.4 us (13%)
  waiting for transfers between devices  15 us (13%)
  Pallas kernels  12.2 us (10%)
  starting transfers between devices  3.91 us (3%)
    all_to_all x2, blocking collectives, spread(): lax.all_to_all(copies, axis, split_axis=0, concat_axis=0, tiled=True)  36 us
    all_to_all x2, blocking collectives, parted(): return lax.all_to_all(parts, axis, split_axis=0, concat_axis=0, tiled=True)  32.4 us
    pallas_call x1, Pallas kernels, pair_terms(): pl.pallas_call(pair_kernel, in_specs=[smem, smem, hbm, vmem, vmem], out_s...  7.99 us
    all_gather x1, waiting for transfers between devices, on_device(): lax.all_gather(units(image_embed), AXES, axis=0, tiled=True, axis_index_g...  6.53 us
    reduce_scatter x1, waiting for transfers between devices, on_device(): lax.psum_scatter(image_part, AXES, scatter_dimension=0, tiled=True, axis_...  5.15 us
    ppermute x2, starting transfers between devices, exchanged(): return lax.ppermute(array, 'c', [(0, 1), (1, 0)])  3.83 us
    ppermute x2, waiting for transfers between devices, exchanged(): return lax.ppermute(array, 'c', [(0, 1), (1, 0)])  3.25 us
  transfers between devices with their start and end apart: 4, of which 4 were waited for; matrix products, arithmetic and copies ran while one was open for 0% of the time, Pallas kernels for 1%

profile of v17, /device:TPU:6, one launch (start us, length us, event | category | flops | bytes accessed | tf_op | source)
XLA Modules:
  0.0 116.3 jit_solution(7825432583763542287)
XLA Ops:
  7.2 0.0 all-gather.2.cloned.1.call-start
  7.2 1.7 %shard_map.68 = bf16[128,768]{1,0:T(8,128)(2,1)} custom-call(bf16[128,768]{1,0:T(8,128)(2,1)} %image_ref.1), custom_call_target="tpu_custom_call" | custom-call | tf_op jit(solution)/shard_map/pallas_call | solution.py:38
  8.9 0.0 all-gather.2.cloned.1.call-update
  9.0 0.0 reduce-scatter.2.cloned.1.call-start
  9.0 1.5 %shard_map.69 = bf16[8,16,896]{2,1,0:T(8,128)(2,1)} custom-call(s32[16]{0:T(128)} %pair_ref.1, bf16[16,768]{1,0:T(8,128)(2,1)} %text_ref.3), custom_call_target="tpu_custom_call" | custom-call | tf_op jit(solution)/shard_map/pallas_call | solution.py:65
  10.6 21.5 %all_to_all.20 = bf16[8,16,896]{2,1,0:T(8,128)(2,1)S(1)} all-to-all(bf16[8,16,896]{2,1,0:T(8,128)(2,1)} %shard_map.69), channel_id=1, replica_groups=mesh['z'=8,'y'=8,'x'=4,'c'=2] {'z'}, dimensions={0} | all-to-all | bytes 458752 | tf_op jit(solution)/shard_map/all_to_all | solution.py:187
  32.0 0.1 broadcast_in_dim.8
  32.1 14.5 %all_to_all.21 = bf16[4,128,896]{2,1,0:T(8,128)(2,1)S(1)} all-to-all(bf16[4,128,896]{2,1,0:T(8,128)(2,1)S(1)} %broadcast_in_dim.8), channel_id=1, replica_groups=mesh['z'=8,'y'=8,'x'=4,'c'=2] {'x'}, dimensions={0} | all-to-all | bytes 1835008 | tf_op jit(solution)/shard_map/all_to_all | solution.py:187
  46.6 1.9 %collective-permute-start = (bf16[512,896]{1,0:T(8,128)(2,1)S(1)}, bf16[512,896]{1,0:T(8,128)(2,1)S(1)}, u32[]{:S(2)}, u32[]{:S(2)}) collective-permute-start(bf16[512,896]{1,0:T(8,128)(2,1)S(1)} %bitcast.4), channel_id=1, source_target_pairs={{0,1},{1,0},{2,3},{3,2},{4,5},{5,4},{6,7},{7,6},{8,9},{9,8},{10,11... | collective-permute-start | bytes 2752520 | tf_op jit(solution)/shard_map/ppermute | solution.py:183
  49.9 0.1 pad_maximum_fusion.scalars_ref
  50.0 1.0 collective-permute-done.other_ref
  51.0 6.5 %all-gather.2.cloned.1.call-done.images_ref = bf16[1024,768]{1,0:T(8,128)(2,1)} async-done(((bf16[128,768]{1,0:T(8,128)(2,1)}), bf16[1024,768]{1,0:T(8,128)(2,1)}) %all-gather.2.cloned.1.call-update) | async-done | bytes 1572880 | tf_op jit(solution)/shard_map/all_gather | solution.py:198
  57.5 8.0 %shard_map.70 = (bf16[1024,768]{1,0:T(8,128)(2,1)}, bf16[512,768]{1,0:T(8,128)(2,1)S(1)}, bf16[512,768]{1,0:T(8,128)(2,1)S(1)}) custom-call(s32[8]{0:T(128)S(1)} %add_multiply_fusion.first_ref, f32[3]{0:T(128)S(1)} %pad_maximum_fusion.scalars_ref, bf16[1024,768]{1,0:T(8,128)(2,1)} %all-gather.2.cloned.1.call-done.images_ref, bf16[512,896]{1,0:T(8,128)(2,1)S(1)} %bitcast.5, ...), custom_call_target="tpu_custom_call" | custom-call | flops 4831838208 | bytes 6291456 | tf_op jit(solution)/shard_map/pallas_call | solution.py:120
  65.5 0.0 reduce-scatter.2.cloned.1.call-update
  65.5 1.9 %collective-permute-start.1 = (bf16[512,768]{1,0:T(8,128)(2,1)S(1)}, bf16[512,768]{1,0:T(8,128)(2,1)S(1)}, u32[]{:S(2)}, u32[]{:S(2)}) collective-permute-start(bf16[512,768]{1,0:T(8,128)(2,1)S(1)} %get-tuple-element.7), channel_id=1, source_target_pairs={{0,1},{1,0},{2,3},{3,2},{4,5},{5,4},{6,7},{7,6},{8,9},{9,8},{10,11... | collective-permute-start | bytes 2359304 | tf_op jit(solution)/shard_map/ppermute | solution.py:183
  67.4 2.3 %collective-permute-done.1 = bf16[512,768]{1,0:T(8,128)(2,1)S(1)} collective-permute-done((bf16[512,768]{1,0:T(8,128)(2,1)S(1)}, bf16[512,768]{1,0:T(8,128)(2,1)S(1)}, u32[]{:S(2)}, u32[]{:S(2)}) %collective-permute-start.1) | collective-permute-done | bytes 786464 | tf_op jit(solution)/shard_map/ppermute | solution.py:183
  69.7 0.2 add_convert_fusion
  69.9 0.0 copy-start
  69.9 0.0 copy-start.2
  69.9 15.3 %all_to_all.22 = bf16[4,128,768]{2,1,0:T(8,128)(2,1)S(1)} all-to-all(bf16[4,128,768]{2,1,0:T(8,128)(2,1)S(1)} %bitcast.6), channel_id=1, replica_groups=mesh['z'=8,'y'=8,'x'=4,'c'=2] {'x'}, dimensions={0} | all-to-all | bytes 1572864 | tf_op jit(solution)/shard_map/all_to_all | solution.py:192
  85.2 0.1 reduce_sum.12
  85.3 17.1 %all_to_all.23.text_grads_ref = bf16[8,16,768]{2,1,0:T(8,128)(2,1)S(1)} all-to-all(bf16[8,16,768]{2,1,0:T(8,128)(2,1)S(1)} %bitcast.8), channel_id=1, replica_groups=mesh['z'=8,'y'=8,'x'=4,'c'=2] {'z'}, dimensions={0} | all-to-all | bytes 393216 | tf_op jit(solution)/shard_map/all_to_all | solution.py:192
  102.4 5.2 %reduce-scatter.2.cloned.1.call-done.image_grad_ref = bf16[128,768]{1,0:T(8,128)(2,1)} async-done(((bf16[1024,768]{1,0:T(8,128)(2,1)}), bf16[128,768]{1,0:T(8,128)(2,1)}) %reduce-scatter.2.cloned.1.call-update) | async-done | bytes 196624 | tf_op jit(solution)/shard_map/reduce_scatter | solution.py:212
  107.6 0.0 copy-done
  107.6 0.0 copy-done.2
  107.6 0.0 copy-start.1
  107.6 0.9 copy-done.1
  108.5 0.9 shard_map.71
  (1 shorter events, 0.0 us)
Async XLA Ops:
  7.2 50.3 %all-gather.2.cloned.1.call-start = ((), (), s32[]{:S(2)}) async-start(), calls=%async_computation.5 | async-start | bytes 1769472 | tf_op jit(solution)/shard_map/all_gather | solution.py:198
  9.0 98.6 %reduce-scatter.2.cloned.1.call-start = ((), (), s32[]{:S(2)}) async-start(), calls=%async_computation.6 | async-start | bytes 1769472 | tf_op jit(solution)/shard_map/reduce_scatter | solution.py:212
  46.6 4.4 %collective-permute-start = (bf16[512,896]{1,0:T(8,128)(2,1)S(1)}, bf16[512,896]{1,0:T(8,128)(2,1)S(1)}, u32[]{:S(2)}, u32[]{:S(2)}) collective-permute-start(bf16[512,896]{1,0:T(8,128)(2,1)S(1)} %bitcast.4), channel_id=1, source_target_pairs={{0,1},{1,0},{2,3},{3,2},{4,5},{5,4},{6,7},{7,6},{8,9},{9,8},{10,11... | collective-permute-start | bytes 2752520 | tf_op jit(solution)/shard_map/ppermute | solution.py:183
  65.5 4.2 %collective-permute-start.1 = (bf16[512,768]{1,0:T(8,128)(2,1)S(1)}, bf16[512,768]{1,0:T(8,128)(2,1)S(1)}, u32[]{:S(2)}, u32[]{:S(2)}) collective-permute-start(bf16[512,768]{1,0:T(8,128)(2,1)S(1)} %get-tuple-element.7), channel_id=1, source_target_pairs={{0,1},{1,0},{2,3},{3,2},{4,5},{5,4},{6,7},{7,6},{8,9},{9,8},{10,11... | collective-permute-start | bytes 2359304 | tf_op jit(solution)/shard_map/ppermute | solution.py:183
  69.9 37.7 %copy-start = (bf16[128,768]{1,0:T(8,128)(2,1)S(1)}, bf16[128,768]{1,0:T(8,128)(2,1)}, u32[]{:S(2)}) copy-start(bf16[128,768]{1,0:T(8,128)(2,1)} %image_ref.1) | copy-start | bytes 589828
  69.9 37.7 %copy-start.2 = (bf16[16,768]{1,0:T(8,128)(2,1)S(1)}, bf16[16,768]{1,0:T(8,128)(2,1)}, u32[]{:S(2)}) copy-start(bf16[16,768]{1,0:T(8,128)(2,1)} %text_ref.3) | copy-start | bytes 73732
  107.6 0.9 copy-start.1
Sparse Core Ops, SparseCore 0:
  10.7 46.8 all-gather.1
  65.6 41.9 reduce-scatter.1

commit v18 on v7

--- a/solution.py
+++ b/solution.py
@@ -69,10 +69,8 @@
     )(pair_index, embed)
 
 
-def pair_kernel(first_ref, scalars_ref, images_ref, own_ref, other_ref, *refs):
-    image_grad_ref, own_grad_ref, other_grad_ref, image_ref, text_ref, sem = refs
-    copy = pltpu.make_async_copy(images_ref, image_ref, sem)
-    copy.start()
+def pair_kernel(first_ref, scalars_ref, image_ref, own_ref, other_ref, *refs):
+    image_grad_ref, own_grad_ref, other_grad_ref, text_ref = refs
     width = image_ref.shape[1]
     count = own_ref.shape[0]
     text_ref[:count, :] = own_ref[...]
@@ -82,7 +80,6 @@
     row = lax.broadcasted_iota(jnp.int32, (128, 1), 0)
     rows = jnp.concatenate([row + first_ref[p] for p in range(image_ref.shape[0] // 128)], axis=0)
     texts = text_ref[:, :width]
-    copy.wait()
     images = image_ref[...]
     dots = lax.dot_general(images, texts, ROWS_BY_ROWS, preferred_element_type=jnp.float32)
     chance = 1.0 / (1.0 + jnp.exp2(dots * scalars_ref[1] + scalars_ref[2]))
@@ -99,18 +96,14 @@
     texts = 2 * count
     return pl.pallas_call(
         pair_kernel,
-        in_specs=[smem, smem, pl.BlockSpec(memory_space=pl.ANY), vmem, vmem],
+        in_specs=[smem, smem, vmem, vmem, vmem],
         out_specs=[vmem] * 3,
         out_shape=[
             jax.ShapeDtypeStruct((rows, width), jnp.bfloat16),
             jax.ShapeDtypeStruct((count, width), jnp.bfloat16),
             jax.ShapeDtypeStruct((count, width), jnp.bfloat16),
         ],
-        scratch_shapes=[
-            pltpu.VMEM((rows, width), jnp.bfloat16),
-            pltpu.VMEM((texts, wide), jnp.bfloat16),
-            pltpu.SemaphoreType.DMA,
-        ],
+        scratch_shapes=[pltpu.VMEM((texts, wide), jnp.bfloat16)],
         compiler_params=params(32),
         cost_estimate=pl.CostEstimate(
             flops=6 * rows * texts * width, bytes_accessed=4 * (rows + texts) * width, transcendentals=2 * rows * texts
@@ -143,7 +136,7 @@
             jax.ShapeDtypeStruct(image_embed.shape, jnp.bfloat16),
             jax.ShapeDtypeStruct(text_embed.shape, jnp.bfloat16),
         ],
-        compiler_params=params(8),
+        compiler_params=params(58),
     )(image_embed, text_embed, image_grad, text_grads)
 
 

time: 117 us -> 116 us (level)
    unnamed x8 -> x2, local copies, waits for them, and re-layouts: 2.35 us -> 1.41 us
where the time goes in v18:
time: 116 us
  blocking collectives  68.3 us (59%)
  between operations  15.4 us (13%)
  waiting for transfers between devices  15.1 us (13%)
  Pallas kernels  11.3 us (10%)
  starting transfers between devices  3.91 us (3%)
  local copies, waits for them, and re-layouts  1.48 us (1%)
    all_to_all x2, blocking collectives, spread(): lax.all_to_all(copies, axis, split_axis=0, concat_axis=0, tiled=True)  36 us
    all_to_all x2, blocking collectives, parted(): return lax.all_to_all(parts, axis, split_axis=0, concat_axis=0, tiled=True)  32.3 us
    all_gather x1, waiting for transfers between devices, on_device(): lax.all_gather(units(image_embed), AXES, axis=0, tiled=True, axis_index_g...  6.53 us
    pallas_call x1, Pallas kernels, pair_terms(): pl.pallas_call(pair_kernel, in_specs=[smem, smem, vmem, vmem, vmem], out_...  5.97 us
    reduce_scatter x1, waiting for transfers between devices, on_device(): lax.psum_scatter(image_part, AXES, scatter_dimension=0, tiled=True, axis_...  5.27 us
    ppermute x2, starting transfers between devices, exchanged(): return lax.ppermute(array, 'c', [(0, 1), (1, 0)])  3.83 us
    ppermute x2, waiting for transfers between devices, exchanged(): return lax.ppermute(array, 'c', [(0, 1), (1, 0)])  3.25 us
  transfers between devices with their start and end apart: 4, of which 4 were waited for; matrix products, arithmetic and copies ran while one was open for 0% of the time, Pallas kernels for 1%

profile of v18, /device:TPU:6, one launch (start us, length us, event | category | flops | bytes accessed | tf_op | source)
XLA Modules:
  0.0 115.9 jit_solution(17845131656736739881)
XLA Ops:
  7.2 0.0 all-gather.2.cloned.1.call-start
  7.2 1.7 %shard_map.68 = bf16[128,768]{1,0:T(8,128)(2,1)} custom-call(bf16[128,768]{1,0:T(8,128)(2,1)} %image_ref.1), custom_call_target="tpu_custom_call" | custom-call | tf_op jit(solution)/shard_map/pallas_call | solution.py:36
  8.9 0.0 all-gather.2.cloned.1.call-update
  9.0 0.0 reduce-scatter.2.cloned.1.call-start
  9.0 1.5 %shard_map.69 = bf16[8,16,896]{2,1,0:T(8,128)(2,1)} custom-call(s32[16]{0:T(128)} %pair_ref.1, bf16[16,768]{1,0:T(8,128)(2,1)} %text_ref.3), custom_call_target="tpu_custom_call" | custom-call | tf_op jit(solution)/shard_map/pallas_call | solution.py:63
  10.6 21.5 %all_to_all.20 = bf16[8,16,896]{2,1,0:T(8,128)(2,1)S(1)} all-to-all(bf16[8,16,896]{2,1,0:T(8,128)(2,1)} %shard_map.69), channel_id=1, replica_groups=mesh['z'=8,'y'=8,'x'=4,'c'=2] {'z'}, dimensions={0} | all-to-all | bytes 458752 | tf_op jit(solution)/shard_map/all_to_all | solution.py:159
  32.0 0.1 broadcast_in_dim.8
  32.1 14.5 %all_to_all.21 = bf16[4,128,896]{2,1,0:T(8,128)(2,1)S(1)} all-to-all(bf16[4,128,896]{2,1,0:T(8,128)(2,1)S(1)} %broadcast_in_dim.8), channel_id=1, replica_groups=mesh['z'=8,'y'=8,'x'=4,'c'=2] {'x'}, dimensions={0} | all-to-all | bytes 1835008 | tf_op jit(solution)/shard_map/all_to_all | solution.py:159
  46.6 1.9 %collective-permute-start = (bf16[512,896]{1,0:T(8,128)(2,1)S(1)}, bf16[512,896]{1,0:T(8,128)(2,1)S(1)}, u32[]{:S(2)}, u32[]{:S(2)}) collective-permute-start(bf16[512,896]{1,0:T(8,128)(2,1)S(1)} %bitcast.4), channel_id=1, source_target_pairs={{0,1},{1,0},{2,3},{3,2},{4,5},{5,4},{6,7},{7,6},{8,9},{9,8},{10,11... | collective-permute-start | bytes 2752520 | tf_op jit(solution)/shard_map/ppermute | solution.py:155
  49.9 0.1 pad_maximum_fusion.scalars_ref
  50.0 1.0 collective-permute-done.other_ref
  51.0 6.5 %all-gather.2.cloned.1.call-done.image_ref = bf16[1024,768]{1,0:T(8,128)(2,1)} async-done(((bf16[128,768]{1,0:T(8,128)(2,1)}), bf16[1024,768]{1,0:T(8,128)(2,1)}) %all-gather.2.cloned.1.call-update) | async-done | bytes 1572880 | tf_op jit(solution)/shard_map/all_gather | solution.py:170
  57.5 0.0 copy-start
  57.5 1.4 %copy-done = bf16[1024,768]{1,0:T(8,128)(2,1)S(1)} copy-done((bf16[1024,768]{1,0:T(8,128)(2,1)S(1)}, bf16[1024,768]{1,0:T(8,128)(2,1)}, u32[]{:S(2)}) %copy-start) | copy-done | bytes 1572888
  58.9 6.0 %shard_map.70 = (bf16[1024,768]{1,0:T(8,128)(2,1)}, bf16[512,768]{1,0:T(8,128)(2,1)S(1)}, bf16[512,768]{1,0:T(8,128)(2,1)S(1)}) custom-call(s32[8]{0:T(128)S(1)} %add_multiply_fusion.first_ref, f32[3]{0:T(128)S(1)} %pad_maximum_fusion.scalars_ref, bf16[1024,768]{1,0:T(8,128)(2,1)S(1)} %copy-done, bf16[512,896]{1,0:T(8,128)(2,1)S(1)} %bitcast.5, ...), custom_call_target="tpu_custom_call" | custom-call | flops 4831838208 | bytes 6291456 | tf_op jit(solution)/shard_map/pallas_call | solution.py:97
  64.9 0.0 reduce-scatter.2.cloned.1.call-update
  64.9 1.9 %collective-permute-start.1 = (bf16[512,768]{1,0:T(8,128)(2,1)S(1)}, bf16[512,768]{1,0:T(8,128)(2,1)S(1)}, u32[]{:S(2)}, u32[]{:S(2)}) collective-permute-start(bf16[512,768]{1,0:T(8,128)(2,1)S(1)} %get-tuple-element.7), channel_id=1, source_target_pairs={{0,1},{1,0},{2,3},{3,2},{4,5},{5,4},{6,7},{7,6},{8,9},{9,8},{10,11... | collective-permute-start | bytes 2359304 | tf_op jit(solution)/shard_map/ppermute | solution.py:155
  66.8 2.3 %collective-permute-done.1 = bf16[512,768]{1,0:T(8,128)(2,1)S(1)} collective-permute-done((bf16[512,768]{1,0:T(8,128)(2,1)S(1)}, bf16[512,768]{1,0:T(8,128)(2,1)S(1)}, u32[]{:S(2)}, u32[]{:S(2)}) %collective-permute-start.1) | collective-permute-done | bytes 786464 | tf_op jit(solution)/shard_map/ppermute | solution.py:155
  69.1 0.2 add_convert_fusion
  69.3 15.1 %all_to_all.22 = bf16[4,128,768]{2,1,0:T(8,128)(2,1)S(1)} all-to-all(bf16[4,128,768]{2,1,0:T(8,128)(2,1)S(1)} %bitcast.6), channel_id=1, replica_groups=mesh['z'=8,'y'=8,'x'=4,'c'=2] {'x'}, dimensions={0} | all-to-all | bytes 1572864 | tf_op jit(solution)/shard_map/all_to_all | solution.py:164
  84.4 0.1 reduce_sum.12
  84.5 17.2 %all_to_all.23.text_grads_ref = bf16[8,16,768]{2,1,0:T(8,128)(2,1)} all-to-all(bf16[8,16,768]{2,1,0:T(8,128)(2,1)S(1)} %bitcast.8), channel_id=1, replica_groups=mesh['z'=8,'y'=8,'x'=4,'c'=2] {'z'}, dimensions={0} | all-to-all | bytes 393216 | tf_op jit(solution)/shard_map/all_to_all | solution.py:164
  101.7 5.3 %reduce-scatter.2.cloned.1.call-done.image_grad_ref = bf16[128,768]{1,0:T(8,128)(2,1)} async-done(((bf16[1024,768]{1,0:T(8,128)(2,1)}), bf16[128,768]{1,0:T(8,128)(2,1)}) %reduce-scatter.2.cloned.1.call-update) | async-done | bytes 196624 | tf_op jit(solution)/shard_map/reduce_scatter | solution.py:184
  107.0 2.0 %shard_map.71 = (bf16[128,768]{1,0:T(8,128)(2,1)}, bf16[16,768]{1,0:T(8,128)(2,1)}) custom-call(bf16[128,768]{1,0:T(8,128)(2,1)} %image_ref.1, bf16[16,768]{1,0:T(8,128)(2,1)} %text_ref.3, bf16[128,768]{1,0:T(8,128)(2,1)} %reduce-scatter.2.cloned.1.call-done.image_grad_ref, bf16[8,16,768]{2,1,0:T(8,128)(2,1)} %all_to_all.23.text_grads_ref), custom_call_target="tpu_custom_call" | custom-call | tf_op jit(solution)/shard_map/pallas_call | solution.py:131
  (1 shorter events, 0.0 us)
Async XLA Ops:
  7.2 50.3 %all-gather.2.cloned.1.call-start = ((), (), s32[]{:S(2)}) async-start(), calls=%async_computation.5 | async-start | bytes 1769472 | tf_op jit(solution)/shard_map/all_gather | solution.py:170
  9.0 98.0 %reduce-scatter.2.cloned.1.call-start = ((), (), s32[]{:S(2)}) async-start(), calls=%async_computation.6 | async-start | bytes 1769472 | tf_op jit(solution)/shard_map/reduce_scatter | solution.py:184
  46.6 4.4 %collective-permute-start = (bf16[512,896]{1,0:T(8,128)(2,1)S(1)}, bf16[512,896]{1,0:T(8,128)(2,1)S(1)}, u32[]{:S(2)}, u32[]{:S(2)}) collective-permute-start(bf16[512,896]{1,0:T(8,128)(2,1)S(1)} %bitcast.4), channel_id=1, source_target_pairs={{0,1},{1,0},{2,3},{3,2},{4,5},{5,4},{6,7},{7,6},{8,9},{9,8},{10,11... | collective-permute-start | bytes 2752520 | tf_op jit(solution)/shard_map/ppermute | solution.py:155
  57.5 1.4 %copy-start = (bf16[1024,768]{1,0:T(8,128)(2,1)S(1)}, bf16[1024,768]{1,0:T(8,128)(2,1)}, u32[]{:S(2)}) copy-start(bf16[1024,768]{1,0:T(8,128)(2,1)} %all-gather.2.cloned.1.call-done.image_ref) | copy-start | bytes 4718596
  64.9 4.2 %collective-permute-start.1 = (bf16[512,768]{1,0:T(8,128)(2,1)S(1)}, bf16[512,768]{1,0:T(8,128)(2,1)S(1)}, u32[]{:S(2)}, u32[]{:S(2)}) collective-permute-start(bf16[512,768]{1,0:T(8,128)(2,1)S(1)} %get-tuple-element.7), channel_id=1, source_target_pairs={{0,1},{1,0},{2,3},{3,2},{4,5},{5,4},{6,7},{7,6},{8,9},{9,8},{10,11... | collective-permute-start | bytes 2359304 | tf_op jit(solution)/shard_map/ppermute | solution.py:155
Sparse Core Ops, SparseCore 0:
  10.7 46.8 all-gather.1
  65.0 41.9 reduce-scatter.1

commit v19 on v18

--- a/solution.py
+++ b/solution.py
@@ -25,21 +25,6 @@
 
 def inverse_norm(floats):
     return lax.rsqrt(jnp.sum(floats * floats, axis=-1, keepdims=True) + 1e-06)
-
-
-def unit_kernel(embed_ref, unit_ref):
-    floats = embed_ref[...].astype(jnp.float32)
-    unit_ref[...] = (floats * inverse_norm(floats)).astype(unit_ref.dtype)
-
-
-def units(embed):
-    return pl.pallas_call(
-        unit_kernel,
-        in_specs=[vmem],
-        out_specs=vmem,
-        out_shape=jax.ShapeDtypeStruct(embed.shape, jnp.bfloat16),
-        compiler_params=params(56),
-    )(embed)
 
 
 def packet_kernel(pair_ref, text_ref, packet_ref):
@@ -81,11 +66,14 @@
     rows = jnp.concatenate([row + first_ref[p] for p in range(image_ref.shape[0] // 128)], axis=0)
     texts = text_ref[:, :width]
     images = image_ref[...]
+    inverse = inverse_norm(images.astype(jnp.float32))
     dots = lax.dot_general(images, texts, ROWS_BY_ROWS, preferred_element_type=jnp.float32)
-    chance = 1.0 / (1.0 + jnp.exp2(dots * scalars_ref[1] + scalars_ref[2]))
-    weight = (scalars_ref[0] * jnp.where(pairs == rows, chance - 1.0, chance)).astype(jnp.bfloat16)
+    chance = 1.0 / (1.0 + jnp.exp2(dots * (inverse * scalars_ref[1]) + scalars_ref[2]))
+    floats = scalars_ref[0] * jnp.where(pairs == rows, chance - 1.0, chance)
+    weight = floats.astype(jnp.bfloat16)
+    scaled = (floats * inverse).astype(jnp.bfloat16)
     image_grad_ref[...] = jnp.dot(weight, texts, preferred_element_type=jnp.float32).astype(image_grad_ref.dtype)
-    text_grad = lax.dot_general(weight, images, COLUMNS_BY_ROWS, preferred_element_type=jnp.float32)
+    text_grad = lax.dot_general(scaled, images, COLUMNS_BY_ROWS, preferred_element_type=jnp.float32)
     own_grad_ref[...] = text_grad[:count].astype(own_grad_ref.dtype)
     other_grad_ref[...] = text_grad[count:].astype(other_grad_ref.dtype)
 
@@ -136,7 +124,7 @@
             jax.ShapeDtypeStruct(image_embed.shape, jnp.bfloat16),
             jax.ShapeDtypeStruct(text_embed.shape, jnp.bfloat16),
         ],
-        compiler_params=params(58),
+        compiler_params=params(8),
     )(image_embed, text_embed, image_grad, text_grads)
 
 
@@ -167,7 +155,7 @@
 def on_device(image_embed, text_embed, log_scale, logit_bias, pair_index):
     own_images = image_embed.shape[0]
     rings = image_rings()
-    images = lax.all_gather(units(image_embed), AXES, axis=0, tiled=True, axis_index_groups=rings)
+    images = lax.all_gather(image_embed, AXES, axis=0, tiled=True, axis_index_groups=rings)
 
     texts = spread(text_packets(pair_index, text_embed, lax.axis_size("z")), "z")
     own = spread(jnp.broadcast_to(texts[None], (lax.axis_size("x"),) + texts.shape), "x")

time: 116 us -> 116 us (level)
  Pallas kernels: 11.3 us -> 8.44 us
    pallas_call x1 -> x0, Pallas kernels: 1.73 us -> none  [units(): pl.pallas_call(unit_kernel, in_specs=[vmem], out_specs=vmem, out_shape=ja...]
    unnamed x2 -> x8, local copies, waits for them, and re-layouts: 1.41 us -> 2.35 us
where the time goes in v19:
time: 116 us; the launch traced here: 115 us
  blocking collectives  68.2 us (59%)
  waiting for transfers between devices  16.2 us (14%)
  between operations  15.4 us (13%)
  Pallas kernels  8.44 us (7%)
  starting transfers between devices  3.9 us (3%)
  local copies, waits for them, and re-layouts  2.42 us (2%)
    all_to_all x2, blocking collectives, spread(): lax.all_to_all(copies, axis, split_axis=0, concat_axis=0, tiled=True)  36 us
    all_to_all x2, blocking collectives, parted(): return lax.all_to_all(parts, axis, split_axis=0, concat_axis=0, tiled=True)  32.2 us
    all_gather x1, waiting for transfers between devices, on_device(): lax.all_gather(image_embed, AXES, axis=0, tiled=True, axis_index_groups=r...  7.19 us
    pallas_call x1, Pallas kernels, pair_terms(): pl.pallas_call(pair_kernel, in_specs=[smem, smem, vmem, vmem, vmem], out_...  5.99 us
    reduce_scatter x1, waiting for transfers between devices, on_device(): lax.psum_scatter(image_part, AXES, scatter_dimension=0, tiled=True, axis_...  5.1 us
    ppermute x2, starting transfers between devices, exchanged(): return lax.ppermute(array, 'c', [(0, 1), (1, 0)])  3.83 us
    ppermute x2, waiting for transfers between devices, exchanged(): return lax.ppermute(array, 'c', [(0, 1), (1, 0)])  3.25 us
    unnamed x8, local copies, waits for them, and re-layouts  2.35 us
  transfers between devices with their start and end apart: 4, of which 4 were waited for; matrix products, arithmetic and copies ran while one was open for 0% of the time, Pallas kernels for 1%

profile of v19, /device:TPU:6, one launch (start us, length us, event | category | flops | bytes accessed | tf_op | source)
XLA Modules:
  0.0 115.1 jit_solution(7170059207138149767)
XLA Ops:
  7.2 0.0 all-gather.2.cloned.1.call-start
  7.2 0.7 all-gather.2.cloned.1.call-update
  7.9 0.0 reduce-scatter.2.cloned.1.call-start
  7.9 1.5 %shard_map.68 = bf16[8,16,896]{2,1,0:T(8,128)(2,1)} custom-call(s32[16]{0:T(128)} %pair_ref.1, bf16[16,768]{1,0:T(8,128)(2,1)} %text_ref.3), custom_call_target="tpu_custom_call" | custom-call | tf_op jit(solution)/shard_map/pallas_call | solution.py:48
  9.5 21.5 %all_to_all.20 = bf16[8,16,896]{2,1,0:T(8,128)(2,1)S(1)} all-to-all(bf16[8,16,896]{2,1,0:T(8,128)(2,1)} %shard_map.68), channel_id=1, replica_groups=mesh['z'=8,'y'=8,'x'=4,'c'=2] {'z'}, dimensions={0} | all-to-all | bytes 458752 | tf_op jit(solution)/shard_map/all_to_all | solution.py:147
  31.0 0.1 broadcast_in_dim.8
  31.0 14.5 %all_to_all.21 = bf16[4,128,896]{2,1,0:T(8,128)(2,1)S(1)} all-to-all(bf16[4,128,896]{2,1,0:T(8,128)(2,1)S(1)} %broadcast_in_dim.8), channel_id=1, replica_groups=mesh['z'=8,'y'=8,'x'=4,'c'=2] {'x'}, dimensions={0} | all-to-all | bytes 1835008 | tf_op jit(solution)/shard_map/all_to_all | solution.py:147
  45.5 1.9 %collective-permute-start = (bf16[512,896]{1,0:T(8,128)(2,1)S(1)}, bf16[512,896]{1,0:T(8,128)(2,1)S(1)}, u32[]{:S(2)}, u32[]{:S(2)}) collective-permute-start(bf16[512,896]{1,0:T(8,128)(2,1)S(1)} %bitcast.4), channel_id=1, source_target_pairs={{0,1},{1,0},{2,3},{3,2},{4,5},{5,4},{6,7},{7,6},{8,9},{9,8},{10,11... | collective-permute-start | bytes 2752520 | tf_op jit(solution)/shard_map/ppermute | solution.py:143
  48.8 0.1 pad_maximum_fusion.scalars_ref
  48.9 1.0 collective-permute-done.other_ref
  49.9 7.2 %all-gather.2.cloned.1.call-done.image_ref = bf16[1024,768]{1,0:T(8,128)(2,1)} async-done(((bf16[128,768]{1,0:T(8,128)(2,1)}), bf16[1024,768]{1,0:T(8,128)(2,1)}) %all-gather.2.cloned.1.call-update) | async-done | bytes 1572880 | tf_op jit(solution)/shard_map/all_gather | solution.py:158
  57.1 0.0 copy-start.3
  57.1 1.4 %copy-done.3 = bf16[1024,768]{1,0:T(8,128)(2,1)S(1)} copy-done((bf16[1024,768]{1,0:T(8,128)(2,1)S(1)}, bf16[1024,768]{1,0:T(8,128)(2,1)}, u32[]{:S(2)}) %copy-start.3) | copy-done | bytes 1572888
  58.5 6.0 %shard_map.69 = (bf16[1024,768]{1,0:T(8,128)(2,1)}, bf16[512,768]{1,0:T(8,128)(2,1)S(1)}, bf16[512,768]{1,0:T(8,128)(2,1)S(1)}) custom-call(s32[8]{0:T(128)S(1)} %add_multiply_fusion.first_ref, f32[3]{0:T(128)S(1)} %pad_maximum_fusion.scalars_ref, bf16[1024,768]{1,0:T(8,128)(2,1)S(1)} %copy-done.3, bf16[512,896]{1,0:T(8,128)(2,1)S(1)} %bitcast.5, ...), custom_call_target="tpu_custom_call" | custom-call | flops 4831838208 | bytes 6291456 | tf_op jit(solution)/shard_map/pallas_call | solution.py:85
  64.5 0.0 reduce-scatter.2.cloned.1.call-update
  64.5 1.9 %collective-permute-start.1 = (bf16[512,768]{1,0:T(8,128)(2,1)S(1)}, bf16[512,768]{1,0:T(8,128)(2,1)S(1)}, u32[]{:S(2)}, u32[]{:S(2)}) collective-permute-start(bf16[512,768]{1,0:T(8,128)(2,1)S(1)} %get-tuple-element.7), channel_id=1, source_target_pairs={{0,1},{1,0},{2,3},{3,2},{4,5},{5,4},{6,7},{7,6},{8,9},{9,8},{10,11... | collective-permute-start | bytes 2359304 | tf_op jit(solution)/shard_map/ppermute | solution.py:143
  66.4 2.3 %collective-permute-done.1 = bf16[512,768]{1,0:T(8,128)(2,1)S(1)} collective-permute-done((bf16[512,768]{1,0:T(8,128)(2,1)S(1)}, bf16[512,768]{1,0:T(8,128)(2,1)S(1)}, u32[]{:S(2)}, u32[]{:S(2)}) %collective-permute-start.1) | collective-permute-done | bytes 786464 | tf_op jit(solution)/shard_map/ppermute | solution.py:143
  68.7 0.2 add_convert_fusion
  68.9 0.0 copy-start
  68.9 0.0 copy-start.2
  68.9 15.1 %all_to_all.22 = bf16[4,128,768]{2,1,0:T(8,128)(2,1)S(1)} all-to-all(bf16[4,128,768]{2,1,0:T(8,128)(2,1)S(1)} %bitcast.6), channel_id=1, replica_groups=mesh['z'=8,'y'=8,'x'=4,'c'=2] {'x'}, dimensions={0} | all-to-all | bytes 1572864 | tf_op jit(solution)/shard_map/all_to_all | solution.py:152
  84.0 0.1 reduce_sum.12
  84.1 17.1 %all_to_all.23.text_grads_ref = bf16[8,16,768]{2,1,0:T(8,128)(2,1)S(1)} all-to-all(bf16[8,16,768]{2,1,0:T(8,128)(2,1)S(1)} %bitcast.8), channel_id=1, replica_groups=mesh['z'=8,'y'=8,'x'=4,'c'=2] {'z'}, dimensions={0} | all-to-all | bytes 393216 | tf_op jit(solution)/shard_map/all_to_all | solution.py:152
  101.3 5.1 %reduce-scatter.2.cloned.1.call-done.image_grad_ref = bf16[128,768]{1,0:T(8,128)(2,1)} async-done(((bf16[1024,768]{1,0:T(8,128)(2,1)}), bf16[128,768]{1,0:T(8,128)(2,1)}) %reduce-scatter.2.cloned.1.call-update) | async-done | bytes 196624 | tf_op jit(solution)/shard_map/reduce_scatter | solution.py:172
  106.4 0.0 copy-done
  106.4 0.0 copy-done.2
  106.4 0.0 copy-start.1
  106.4 0.9 copy-done.1
  107.3 0.9 shard_map.70
  (1 shorter events, 0.0 us)
Async XLA Ops:
  7.2 49.9 %all-gather.2.cloned.1.call-start = ((), (), s32[]{:S(2)}) async-start(), calls=%async_computation.5 | async-start | bytes 1769472 | tf_op jit(solution)/shard_map/all_gather | solution.py:158
  7.9 98.5 %reduce-scatter.2.cloned.1.call-start = ((), (), s32[]{:S(2)}) async-start(), calls=%async_computation.6 | async-start | bytes 1769472 | tf_op jit(solution)/shard_map/reduce_scatter | solution.py:172
  45.5 4.4 %collective-permute-start = (bf16[512,896]{1,0:T(8,128)(2,1)S(1)}, bf16[512,896]{1,0:T(8,128)(2,1)S(1)}, u32[]{:S(2)}, u32[]{:S(2)}) collective-permute-start(bf16[512,896]{1,0:T(8,128)(2,1)S(1)} %bitcast.4), channel_id=1, source_target_pairs={{0,1},{1,0},{2,3},{3,2},{4,5},{5,4},{6,7},{7,6},{8,9},{9,8},{10,11... | collective-permute-start | bytes 2752520 | tf_op jit(solution)/shard_map/ppermute | solution.py:143
  57.1 1.4 %copy-start.3 = (bf16[1024,768]{1,0:T(8,128)(2,1)S(1)}, bf16[1024,768]{1,0:T(8,128)(2,1)}, u32[]{:S(2)}) copy-start(bf16[1024,768]{1,0:T(8,128)(2,1)} %all-gather.2.cloned.1.call-done.image_ref) | copy-start | bytes 4718596
  64.5 4.2 %collective-permute-start.1 = (bf16[512,768]{1,0:T(8,128)(2,1)S(1)}, bf16[512,768]{1,0:T(8,128)(2,1)S(1)}, u32[]{:S(2)}, u32[]{:S(2)}) collective-permute-start(bf16[512,768]{1,0:T(8,128)(2,1)S(1)} %get-tuple-element.7), channel_id=1, source_target_pairs={{0,1},{1,0},{2,3},{3,2},{4,5},{5,4},{6,7},{7,6},{8,9},{9,8},{10,11... | collective-permute-start | bytes 2359304 | tf_op jit(solution)/shard_map/ppermute | solution.py:143
  68.9 37.5 %copy-start = (bf16[128,768]{1,0:T(8,128)(2,1)S(1)}, bf16[128,768]{1,0:T(8,128)(2,1)}, u32[]{:S(2)}) copy-start(bf16[128,768]{1,0:T(8,128)(2,1)} %image_ref.1) | copy-start | bytes 589828
  68.9 37.5 %copy-start.2 = (bf16[16,768]{1,0:T(8,128)(2,1)S(1)}, bf16[16,768]{1,0:T(8,128)(2,1)}, u32[]{:S(2)}) copy-start(bf16[16,768]{1,0:T(8,128)(2,1)} %text_ref.3) | copy-start | bytes 73732
  106.4 0.9 copy-start.1
Sparse Core Ops, SparseCore 0:
  10.1 46.9 all-gather.1
  64.6 41.7 reduce-scatter.1
